TPU v7x, 32 devices: a whole 2x2x4 slice. The times are simulated.
32 devices in a mesh: dp: 4 (over y, x), ctx: 2 (over core), tensor: 4 (over z).
Axes of the slice: x: 2, y: 2, z: 4, core: 2. Of those that a mesh axis runs over, the one named last changes fastest.
Arguments:
- token_ids: int32 [4, 2048], P('dp', 'ctx'), may hold values from 0 to 31999
- targets: int32 [4, 2048, 2], P('dp', 'ctx'), may hold values from 0 to 31999
- counted: int32 [4, 2048, 2], P('dp', 'ctx'), may hold values from 0 to 1, as said below
- routes: int32 [4, 2048, 2], P('dp', 'ctx'), may hold values from 0 to 7, all different within a row
- priority: int32 [8, 1024], P(('dp', 'ctx')), may hold values from 0 to 1023, each once within a row
- owner_of: int32 [137, 1], replicated, may hold values from 0 to 7, as said below
- master: float32 [4, 8, 21, 64, 768], P('tensor', ('dp', 'ctx')), as said below
- master_first: float32 [4, 8, 21, 64, 768], P('tensor', ('dp', 'ctx')), as said below
- master_second: float32 [4, 8, 21, 64, 768], P('tensor', ('dp', 'ctx')), as said below
- expert_in: float32 [8, 768, 3072], P(('dp', 'ctx'), None, 'tensor'), may hold values from -0.21875 to 0.21875
- expert_in_first: float32 [8, 768, 3072], P(('dp', 'ctx'), None, 'tensor'), may hold values from -0.00012207031 to 0.00012207031
- expert_in_second: float32 [8, 768, 3072], P(('dp', 'ctx'), None, 'tensor'), may hold values from 1.6052246e-10 to 2.5683593e-09
- expert_out: float32 [8, 3072, 768], P(('dp', 'ctx'), 'tensor'), may hold values from -0.109375 to 0.109375
- expert_out_first: float32 [8, 3072, 768], P(('dp', 'ctx'), 'tensor'), may hold values from -0.00024414062 to 0.00024414062
- expert_out_second: float32 [8, 3072, 768], P(('dp', 'ctx'), 'tensor'), may hold values from 6.420898e-10 to 1.0273437e-08
- norm_gains: float32 [3, 768], replicated, may hold values from 0.5 to 1.5
- norm_gains_first: float32 [3, 768], replicated, may hold values from -0.00390625 to 0.00390625
- norm_gains_second: float32 [3, 768], replicated, may hold values from 1.2841797e-07 to 2.0546875e-06
- router: float32 [768, 8], replicated, may hold values from -0.21875 to 0.21875
- router_first: float32 [768, 8], replicated, may hold values from -0.001953125 to 0.001953125
- router_second: float32 [768, 8], replicated, may hold values from 3.210449e-08 to 5.1367186e-07
- rel_bias: float32 [12, 8], P('tensor'), may hold values from -3 to 3
- rel_bias_first: float32 [12, 8], P('tensor'), may hold values from -0.015625 to 0.015625
- rel_bias_second: float32 [12, 8], P('tensor'), may hold values from 2.0546875e-06 to 3.2875e-05
Outputs:
- loss_totals: float32 [2], replicated
- master_new: float32 [4, 8, 21, 64, 768], P('tensor', ('dp', 'ctx'))
- master_first_new: float32 [4, 8, 21, 64, 768], P('tensor', ('dp', 'ctx'))
- master_second_new: float32 [4, 8, 21, 64, 768], P('tensor', ('dp', 'ctx'))
- expert_in_new: float32 [8, 768, 3072], P(('dp', 'ctx'), None, 'tensor')
- expert_in_first_new: float32 [8, 768, 3072], P(('dp', 'ctx'), None, 'tensor')
- expert_in_second_new: float32 [8, 768, 3072], P(('dp', 'ctx'), None, 'tensor')
- expert_out_new: float32 [8, 3072, 768], P(('dp', 'ctx'), 'tensor')
- expert_out_first_new: float32 [8, 3072, 768], P(('dp', 'ctx'), 'tensor')
- expert_out_second_new: float32 [8, 3072, 768], P(('dp', 'ctx'), 'tensor')
- norm_gains_new: float32 [3, 768], replicated
- norm_gains_first_new: float32 [3, 768], replicated
- norm_gains_second_new: float32 [3, 768], replicated
- router_new: float32 [768, 8], replicated
- router_first_new: float32 [768, 8], replicated
- router_second_new: float32 [768, 8], replicated
- rel_bias_new: float32 [12, 8], P('tensor')
- rel_bias_first_new: float32 [12, 8], P('tensor')
- rel_bias_second_new: float32 [12, 8], P('tensor')
Inputs may be any that keep to these rules, and one draw needn't show every extreme that they name: `owner_of`: no owner holds more than 21 units, and one holds exactly 21. `counted`: position 0 of every sequence counts for both targets; the last position never counts for the first target and the last two never for the second. `master`: slots that hold no unit are zero. `master_first`: slots that hold no unit are zero. `master_second`: slots that hold no unit are zero. `routes`: the two experts of a token differ. `priority`: each row holds each of 0 to 1023 once.
All inputs are finite; a program needn't handle non-finite values.
Results may differ from a plain program's by a relative error of at most 0.0055.
The roundings to bfloat16 on the way count: a program that leaves them out, or rounds other values in their place, can miss the bound.
Values may be sent and summed in bfloat16 or wider, within the bound.
A program may use at most 320 MiB of HBM per device.

v0:
```python
import math

import jax
import jax.numpy as jnp
from jax import lax
from jax.sharding import PartitionSpec as P

VOCAB = 32000
BLOCK = 256
STEP = 10


highest_precision = lax.Precision.HIGHEST
beta_first = 0.9
beta_second = 0.95
adam_epsilon = 1e-08
norm_epsilon = 1e-06
ahead_weight = 0.3
masked_score = -1e30
rate_table = 0.1
rate_query = 0.05
rate_values = 0.05
rate_project = 0.5
rate_inner = 0.05
rate_outer = 0.03
rate_gains = 0.5
rate_router = 0.05
rate_biases = 0.5
decay_rate = 0.1


def passed_along(value, axis, steps):
    count = lax.axis_size(axis)
    initial, last = (max(0, -steps), min(count, count - steps))
    return lax.ppermute(value, axis, [(source, source + steps) for source in range(initial, last)])


def combined_all(x, axis, combine):
    everything = jax.tree.map(lambda part: lax.all_gather(part, axis), x)
    initial = jax.tree.map(lambda part: part[0], everything)

    def lap(k, so_far):
        return combine(so_far, jax.tree.map(lambda part: part[k], everything))

    return lax.fori_loop(1, lax.axis_size(axis), lap, initial)


def adam_update(weight, moment_one, moment_two, gradient, step_rate, decay_factor):
    moment_new = beta_first * moment_one + (1.0 - beta_first) * gradient
    square_new = beta_second * moment_two + (1.0 - beta_second) * gradient * gradient
    moment_hat = moment_new / (1.0 - beta_first**STEP)
    square_hat = square_new / (1.0 - beta_second**STEP)
    weight_new = weight - step_rate * (
        moment_hat / (jnp.sqrt(square_hat) + adam_epsilon) + decay_factor * weight
    )
    return (weight_new, moment_new, square_new)


def norm_forward(values, gain_row):
    inverse = lax.rsqrt(jnp.mean(values * values, -1, keepdims=True) + norm_epsilon)
    return (values * inverse * gain_row, inverse)


def norm_backward(values, inverse, gain_row, upstream):
    normed = values * inverse
    scaled = upstream * gain_row
    gain_grad = jnp.sum(upstream * normed, 0)
    inputs_grad = inverse * (scaled - normed * jnp.mean(scaled * normed, -1, keepdims=True))
    return (inputs_grad, gain_grad)


def slot_tables(owner_ids, owners, most_units):
    unit_count = owner_ids.shape[0]
    unit_index = jnp.arange(unit_count, dtype=jnp.int32)
    earlier = (owner_ids[None, :] == owner_ids[:, None]) & (
        unit_index[None, :] < unit_index[:, None]
    )
    unit_rank = jnp.sum(earlier.astype(jnp.int32), 1)
    placed = (owner_ids[None, None, :] == jnp.arange(owners, dtype=jnp.int32)[:, None, None]) & (
        unit_rank[None, None, :] == jnp.arange(most_units, dtype=jnp.int32)[None, :, None]
    )
    slot_filled = jnp.any(placed, 2)
    slot_unit = jnp.sum(jnp.where(placed, unit_index[None, None, :], 0), 2)
    return (unit_rank, slot_unit, slot_filled)


def unit_rates(unit_ids, table_units, query_units, value_units):
    return jnp.where(
        unit_ids < table_units,
        rate_table,
        jnp.where(
            unit_ids < query_units,
            rate_query,
            jnp.where(unit_ids < value_units, rate_values, rate_project),
        ),
    )


def pair_slots(route_pairs, priorities, experts, capacity):
    tokens_here = priorities.shape[0]
    pair_expert = route_pairs.T.reshape(-1)
    pair_key = (
        jnp.arange(2, dtype=jnp.int32)[:, None] * tokens_here + priorities[None, :]
    ).reshape(-1)
    before = (pair_expert[None, :] == pair_expert[:, None]) & (
        pair_key[None, :] < pair_key[:, None]
    )
    pair_rank = jnp.sum(before.astype(jnp.int32), 1)
    pair_kept = pair_rank < capacity
    pair_dest = pair_expert * capacity + jnp.minimum(pair_rank, capacity - 1)
    target_slot = jnp.where(pair_kept, pair_dest, experts * capacity)
    slot_source = (
        jnp.full((experts * capacity,), 2 * tokens_here, jnp.int32)
        .at[target_slot]
        .set(jnp.arange(2 * tokens_here, dtype=jnp.int32), mode="drop")
    )
    return (pair_kept, pair_dest, slot_source)


def gelu_tanh(values):
    return jax.nn.gelu(values, approximate=True)


def over_tensor(partial_sums):
    return lax.psum(partial_sums, "tensor")


def to_experts(buffer):
    return lax.all_to_all(buffer, ("dp", "ctx"), split_axis=0, concat_axis=0, tiled=True)


def from_experts(buffer):
    return lax.all_to_all(buffer, ("dp", "ctx"), split_axis=0, concat_axis=0, tiled=True)


def block_bias(bias_table, query_blocks, key_blocks, key_allowed):
    distance = query_blocks[:, None] - key_blocks[None, :]
    allowed = (distance >= 0) & key_allowed[None, :]
    buckets = bias_table.shape[1]
    onehot = (
        jnp.clip(distance, 0, buckets - 1)[:, :, None] == jnp.arange(buckets, dtype=jnp.int32)
    ).astype(jnp.float32)
    bias_block = jnp.einsum("qkr,hr->hqk", onehot, bias_table, precision=highest_precision)
    return (bias_block, allowed, onehot)


def tile_scores(query_tile, keys, bias_block, allowed):
    scores = jnp.einsum(
        "qhd,khd->hqk", query_tile, keys, preferred_element_type=jnp.float32
    ) * query_tile.shape[-1] ** (-0.5)
    head_count, row_count, column_count = scores.shape
    shaped = (
        scores.reshape(head_count, row_count // BLOCK, BLOCK, column_count // BLOCK, BLOCK)
        + bias_block[:, :, None, :, None]
    )
    return jnp.where(allowed[None, :, None, :, None], shaped, masked_score)


def tile_forward(query_tile, keys, values, bias_block, allowed):
    shaped = tile_scores(query_tile, keys, bias_block, allowed)
    peak_value = jnp.max(shaped, axis=(3, 4), keepdims=True)
    exp_scores = jnp.exp(shaped - peak_value)
    exp_total = jnp.sum(exp_scores, axis=(3, 4), keepdims=True)
    head_count = shaped.shape[0]
    softmax_low = (
        (exp_scores / exp_total)
        .astype(jnp.bfloat16)
        .reshape(head_count, query_tile.shape[0], keys.shape[0])
    )
    output = jnp.einsum("hqk,khd->qhd", softmax_low, values, preferred_element_type=jnp.float32)
    return (output.astype(jnp.bfloat16), peak_value + jnp.log(exp_total))


def tile_backward(query_tile, keys, values, grad_out, logsum, bias_block, allowed, onehot):
    shaped = tile_scores(query_tile, keys, bias_block, allowed)
    softmax_full = jnp.exp(shaped - logsum)
    head_count = shaped.shape[0]
    flat_shape = (head_count, query_tile.shape[0], keys.shape[0])
    softmax_low = softmax_full.reshape(flat_shape).astype(jnp.bfloat16)
    grad_softmax = jnp.einsum(
        "qhd,khd->hqk", grad_out, values, preferred_element_type=jnp.float32
    ).reshape(shaped.shape)
    row_inner = jnp.sum(softmax_full * grad_softmax, axis=(3, 4), keepdims=True)
    grad_scores = (softmax_full * (grad_softmax - row_inner)).astype(jnp.bfloat16)
    score_scale = query_tile.shape[-1] ** (-0.5)
    flat_scores = grad_scores.reshape(flat_shape)
    grad_query = (
        jnp.einsum("hqk,khd->qhd", flat_scores, keys, preferred_element_type=jnp.float32)
        * score_scale
    )
    grad_keys = (
        jnp.einsum("hqk,qhd->khd", flat_scores, query_tile, preferred_element_type=jnp.float32)
        * score_scale
    )
    grad_values = jnp.einsum(
        "hqk,qhd->khd", softmax_low, grad_out, preferred_element_type=jnp.float32
    )
    block_sums = jnp.sum(grad_scores.astype(jnp.float32), axis=(2, 4))
    grad_bias = jnp.einsum("hqk,qkr->hr", block_sums, onehot, precision=highest_precision)
    return (grad_query, grad_keys, grad_values, grad_bias)


def on_device(
    token_ids,
    targets,
    counted,
    routes,
    priority,
    owner_of,
    master,
    master_first,
    master_second,
    expert_in,
    expert_in_first,
    expert_in_second,
    expert_out,
    expert_out_first,
    expert_out_second,
    norm_gains,
    norm_gains_first,
    norm_gains_second,
    router,
    router_first,
    router_second,
    rel_bias,
    rel_bias_first,
    rel_bias_second,
):
    owners = lax.axis_size(("dp", "ctx"))
    tensor_ranks = lax.axis_size("tensor")
    my_owner = lax.axis_index(("dp", "ctx"))
    my_rank = lax.axis_index("tensor")
    my_context = lax.axis_index("ctx")
    sequences, half_length = token_ids.shape
    tokens_here = sequences * half_length
    most_units = master.shape[2]
    unit_rows = master.shape[3]
    model_width = master.shape[4]
    vocab_here = VOCAB // tensor_ranks
    heads_here = rel_bias.shape[0]
    head_size = model_width // (heads_here * tensor_ranks)
    hidden_here = heads_here * head_size
    experts = router.shape[1]
    experts_here = expert_in.shape[0]
    capacity = (18 * tokens_here + 8 * experts - 1) // (8 * experts)
    tile_rows = min(half_length, 512)
    head_rows_count = min(tokens_here, 512)
    table_units = vocab_here // unit_rows
    query_units = table_units + 2 * hidden_here // unit_rows
    value_units = table_units + 3 * hidden_here // unit_rows
    embed_scale = math.sqrt(model_width)
    owner_ids = owner_of[:, 0]
    unit_rank, slot_unit, slot_filled = slot_tables(owner_ids, owners, most_units)
    gathered = lax.all_gather(master[0, 0], ("dp", "ctx"), axis=0, tiled=True)
    weights_flat = jnp.take(gathered, owner_ids * most_units + unit_rank, axis=0).reshape(
        -1, model_width
    )
    table_low = weights_flat[:vocab_here].astype(jnp.bfloat16)
    joint_low = weights_flat[vocab_here : vocab_here + 3 * hidden_here].astype(jnp.bfloat16)
    project_low = weights_flat[vocab_here + 3 * hidden_here :].astype(jnp.bfloat16)
    local_ids = token_ids.reshape(-1) - my_rank * vocab_here
    inside = ((local_ids >= 0) & (local_ids < vocab_here)).astype(jnp.float32)
    clipped_ids = jnp.clip(local_ids, 0, vocab_here - 1)
    looked = (
        jnp.take(table_low, clipped_ids, axis=0).astype(jnp.float32)
        * (embed_scale * inside)[:, None]
    )
    stream_zero = over_tensor(looked)
    first_normalized, inverse_one = norm_forward(stream_zero, norm_gains[0])
    normed_one_low = first_normalized.astype(jnp.bfloat16)
    joint = lax.dot_general(
        normed_one_low, joint_low, (((1,), (1,)), ((), ())), preferred_element_type=jnp.float32
    ).astype(jnp.bfloat16)
    queries = joint[:, :hidden_here].reshape(sequences, half_length, heads_here, head_size)
    pairs_here = joint[:, hidden_here:].reshape(sequences, half_length, 2 * hidden_here)
    pairs_before = passed_along(pairs_here, "ctx", 1)
    keyvals = jnp.concatenate([pairs_before, pairs_here], 1).reshape(
        sequences, 2 * half_length, 2, heads_here, head_size
    )
    keys_all = keyvals[:, :, 0]
    values_all = keyvals[:, :, 1]
    blocks_half = half_length // BLOCK
    tile_blocks = tile_rows // BLOCK
    tiles_sequence = half_length // tile_rows
    key_blocks = jnp.arange(2 * blocks_half, dtype=jnp.int32) + (my_context - 1) * blocks_half
    key_allowed = (jnp.arange(2 * blocks_half) >= blocks_half) | (my_context > 0)
    frames = [
        block_bias(
            rel_bias,
            my_context * blocks_half
            + tile_index * tile_blocks
            + jnp.arange(tile_blocks, dtype=jnp.int32),
            key_blocks,
            key_allowed,
        )
        for tile_index in range(tiles_sequence)
    ]

    def attend_forward(seq_items):
        seq_queries, seq_keys, seq_values = seq_items
        outputs = []
        logsums = []
        for tile_index in range(tiles_sequence):
            bias_block, allowed, onehot = frames[tile_index]
            output, logsum = tile_forward(
                seq_queries[tile_index * tile_rows : (tile_index + 1) * tile_rows],
                seq_keys,
                seq_values,
                bias_block,
                allowed,
            )
            outputs.append(output)
            logsums.append(logsum)
        return (jnp.concatenate(outputs, 0), jnp.concatenate(logsums, 1))

    attention_output, logsum_all = lax.map(attend_forward, (queries, keys_all, values_all))
    attended_flat = attention_output.reshape(tokens_here, hidden_here)
    stream_one = stream_zero + over_tensor(
        jnp.dot(attended_flat, project_low, preferred_element_type=jnp.float32)
    )
    second_normalized, inverse_two = norm_forward(stream_one, norm_gains[1])
    normed_two_low = second_normalized.astype(jnp.bfloat16)
    router_low = router.astype(jnp.bfloat16)
    router_scores_raw = jnp.dot(normed_two_low, router_low, preferred_element_type=jnp.float32)
    route_pairs = routes.reshape(tokens_here, 2)
    route_onehot = (route_pairs[:, :, None] == jnp.arange(experts, dtype=jnp.int32)).astype(
        jnp.float32
    )
    chosen = jnp.einsum("tke,te->tk", route_onehot, router_scores_raw, precision=highest_precision)
    gate_values = jax.nn.softmax(chosen, -1)
    pair_kept, pair_dest, slot_source = pair_slots(route_pairs, priority[0], experts, capacity)
    kept_rows = pair_kept.astype(jnp.float32)
    slot_full = (slot_source < 2 * tokens_here).astype(jnp.float32)
    slot_token = slot_source % tokens_here
    dispatch_rows = (
        jnp.take(normed_two_low, slot_token, axis=0) * slot_full[:, None].astype(jnp.bfloat16)
    ).reshape(owners, experts_here * capacity, model_width)
    arrived = to_experts(dispatch_rows).reshape(owners, experts_here, capacity, model_width)
    inner_low = expert_in.astype(jnp.bfloat16)
    outer_low = expert_out.astype(jnp.bfloat16)
    hidden_pre = jnp.einsum(
        "oecd,edf->oecf", arrived, inner_low, preferred_element_type=jnp.float32
    )
    active_low = gelu_tanh(hidden_pre).astype(jnp.bfloat16)
    expert_part = jnp.einsum(
        "oecf,efd->oecd", active_low, outer_low, preferred_element_type=jnp.float32
    ).astype(jnp.bfloat16)
    returned = from_experts(
        expert_part.reshape(owners, experts_here * capacity, model_width)
    ).reshape(experts * capacity, model_width)
    pair_rows = (
        jnp.take(returned, pair_dest, axis=0).astype(jnp.float32) * kept_rows[:, None]
    ).reshape(2, tokens_here, model_width)
    moe_partial = gate_values[:, 0:1] * pair_rows[0] + gate_values[:, 1:2] * pair_rows[1]
    stream_two = stream_one + over_tensor(moe_partial)
    normed_three, inverse_three = norm_forward(stream_two, norm_gains[2])
    head_low = normed_three.astype(jnp.bfloat16)
    head_tiles = tokens_here // head_rows_count
    head_rows = head_low.reshape(head_tiles, head_rows_count, model_width)
    local_targets = (targets.reshape(tokens_here, 2) - my_rank * vocab_here).reshape(
        head_tiles, head_rows_count, 2
    )
    columns = jnp.arange(vocab_here, dtype=jnp.int32)

    def head_forward(tile_items):
        rows_low, wanted = tile_items
        logits = lax.dot_general(
            rows_low, table_low, (((1,), (1,)), ((), ())), preferred_element_type=jnp.float32
        )
        peak_value = jnp.max(logits, 1)
        exp_total = jnp.sum(jnp.exp(logits - peak_value[:, None]), 1)
        picked = jnp.stack(
            [
                jnp.sum(jnp.where(columns[None, :] == wanted[:, which : which + 1], logits, 0.0), 1)
                for which in range(2)
            ],
            1,
        )
        return (peak_value, exp_total, picked)

    peaks, totals, picked = lax.map(head_forward, (head_rows, local_targets))

    def merge_totals(left_part, right_part):
        top_value = jnp.maximum(left_part[0], right_part[0])
        summed = left_part[1] * jnp.exp(left_part[0] - top_value) + right_part[1] * jnp.exp(
            right_part[0] - top_value
        )
        return (top_value, summed, left_part[2] + right_part[2])

    top_value, exp_total, target_logits = combined_all(
        (peaks.reshape(-1), totals.reshape(-1), picked.reshape(tokens_here, 2)),
        "tensor",
        merge_totals,
    )
    logsum_vocab = top_value + jnp.log(exp_total)
    loss_weights = counted.reshape(tokens_here, 2).astype(jnp.float32) * jnp.array(
        [1.0, ahead_weight], jnp.float32
    )
    loss_local = jnp.sum(loss_weights * (logsum_vocab[:, None] - target_logits))
    loss_totals = lax.psum(jnp.stack([loss_local, jnp.sum(loss_weights)]), ("dp", "ctx"))
    inverse_weight = 1.0 / loss_totals[1]

    def head_backward(running, tile_items):
        rows_low, wanted, logsum_rows, weight_rows = tile_items
        logits = lax.dot_general(
            rows_low, table_low, (((1,), (1,)), ((), ())), preferred_element_type=jnp.float32
        )
        softmax_full = jnp.exp(logits - logsum_rows[:, None])
        target_hits = jnp.where(
            columns[None, :] == wanted[:, 0:1], weight_rows[:, 0:1], 0.0
        ) + jnp.where(columns[None, :] == wanted[:, 1:2], weight_rows[:, 1:2], 0.0)
        grad_logits = (
            (jnp.sum(weight_rows, 1, keepdims=True) * softmax_full - target_hits) * inverse_weight
        ).astype(jnp.bfloat16)
        grad_rows = jnp.dot(grad_logits, table_low, preferred_element_type=jnp.float32)
        running = running + lax.dot_general(
            grad_logits, rows_low, (((0,), (0,)), ((), ())), preferred_element_type=jnp.float32
        )
        return (running, grad_rows)

    table_grad, grad_head = lax.scan(
        head_backward,
        jnp.zeros((vocab_here, model_width), jnp.float32),
        (
            head_rows,
            local_targets,
            logsum_vocab.reshape(head_tiles, head_rows_count),
            loss_weights.reshape(head_tiles, head_rows_count, 2),
        ),
    )
    grad_head = over_tensor(grad_head.reshape(tokens_here, model_width))
    grad_two, gain_grad_three = norm_backward(stream_two, inverse_three, norm_gains[2], grad_head)
    gate_flat = gate_values.T.reshape(-1)
    slot_scale = jnp.take(gate_flat, jnp.minimum(slot_source, 2 * tokens_here - 1)) * slot_full
    grad_dispatch = (
        (jnp.take(grad_two, slot_token, axis=0) * slot_scale[:, None])
        .astype(jnp.bfloat16)
        .reshape(owners, experts_here * capacity, model_width)
    )
    grad_arrived = to_experts(grad_dispatch).reshape(owners, experts_here, capacity, model_width)
    grad_active = jnp.einsum(
        "oecd,efd->oecf", grad_arrived, outer_low, preferred_element_type=jnp.float32
    )
    outer_grad = jnp.einsum(
        "oecf,oecd->efd", active_low, grad_arrived, preferred_element_type=jnp.float32
    )
    gelu_values, gelu_back = jax.vjp(gelu_tanh, hidden_pre)
    grad_hidden = gelu_back(grad_active)[0].astype(jnp.bfloat16)
    inner_grad = jnp.einsum(
        "oecd,oecf->edf", arrived, grad_hidden, preferred_element_type=jnp.float32
    )
    grad_back = jnp.einsum(
        "oecf,edf->oecd", grad_hidden, inner_low, preferred_element_type=jnp.float32
    ).astype(jnp.bfloat16)
    grad_returned = from_experts(
        grad_back.reshape(owners, experts_here * capacity, model_width)
    ).reshape(experts * capacity, model_width)
    grad_pairs = (
        jnp.take(grad_returned, pair_dest, axis=0).astype(jnp.float32) * kept_rows[:, None]
    ).reshape(2, tokens_here, model_width)
    gate_partial = jnp.sum(pair_rows * grad_two[None], 2).T
    moe_input_grad, gate_grad = over_tensor((grad_pairs[0] + grad_pairs[1], gate_partial))
    chosen_grad = gate_values * (gate_grad - jnp.sum(gate_values * gate_grad, 1, keepdims=True))
    logit_grad = jnp.einsum(
        "tk,tke->te", chosen_grad, route_onehot, precision=highest_precision
    ).astype(jnp.bfloat16)
    router_grad = lax.dot_general(
        normed_two_low, logit_grad, (((0,), (0,)), ((), ())), preferred_element_type=jnp.float32
    )
    normed_two_grad = moe_input_grad + lax.dot_general(
        logit_grad, router_low, (((1,), (1,)), ((), ())), preferred_element_type=jnp.float32
    )
    grad_one_part, gain_grad_two = norm_backward(
        stream_one, inverse_two, norm_gains[1], normed_two_grad
    )
    grad_one = grad_two + grad_one_part
    grad_one_low = grad_one.astype(jnp.bfloat16)
    project_grad = lax.dot_general(
        attended_flat, grad_one_low, (((0,), (0,)), ((), ())), preferred_element_type=jnp.float32
    )
    grad_attended = lax.dot_general(
        grad_one_low, project_low, (((1,), (1,)), ((), ())), preferred_element_type=jnp.float32
    ).astype(jnp.bfloat16)

    def attend_backward(seq_items):
        seq_queries, seq_keys, seq_values, seq_grad, seq_logsum = seq_items
        query_grads = []
        key_grad = jnp.zeros(seq_keys.shape, jnp.float32)
        value_grad = jnp.zeros(seq_values.shape, jnp.float32)
        bias_grad = jnp.zeros(rel_bias.shape, jnp.float32)
        for tile_index in range(tiles_sequence):
            bias_block, allowed, onehot = frames[tile_index]
            row_range = slice(tile_index * tile_rows, (tile_index + 1) * tile_rows)
            tile_logsum = seq_logsum[:, tile_index * tile_blocks : (tile_index + 1) * tile_blocks]
            grad_query, grad_keys, grad_values, grad_bias = tile_backward(
                seq_queries[row_range],
                seq_keys,
                seq_values,
                seq_grad[row_range],
                tile_logsum,
                bias_block,
                allowed,
                onehot,
            )
            query_grads.append(grad_query)
            key_grad = key_grad + grad_keys
            value_grad = value_grad + grad_values
            bias_grad = bias_grad + grad_bias
        return (jnp.concatenate(query_grads, 0), key_grad, value_grad, bias_grad)

    query_grad, key_grad, value_grad, bias_grads = lax.map(
        attend_backward,
        (
            queries,
            keys_all,
            values_all,
            grad_attended.reshape(sequences, half_length, heads_here, head_size),
            logsum_all,
        ),
    )
    bias_grad = jnp.sum(bias_grads, 0)
    pair_grad = jnp.stack([key_grad, value_grad], 2).reshape(
        sequences, 2 * half_length, 2 * hidden_here
    )
    grad_before = passed_along(pair_grad[:, :half_length].astype(jnp.bfloat16), "ctx", -1)
    pair_grad_here = pair_grad[:, half_length:] + grad_before.astype(jnp.float32)
    joint_grad = jnp.concatenate(
        [
            query_grad.reshape(tokens_here, hidden_here),
            pair_grad_here.reshape(tokens_here, 2 * hidden_here),
        ],
        1,
    ).astype(jnp.bfloat16)
    joint_weight_grad = lax.dot_general(
        joint_grad, normed_one_low, (((0,), (0,)), ((), ())), preferred_element_type=jnp.float32
    )
    normed_one_grad = over_tensor(
        jnp.dot(joint_grad, joint_low, preferred_element_type=jnp.float32)
    )
    grad_zero_part, gain_grad_one = norm_backward(
        stream_zero, inverse_one, norm_gains[0], normed_one_grad
    )
    grad_zero = grad_one + grad_zero_part
    table_grad = table_grad + jax.ops.segment_sum(
        grad_zero * (embed_scale * inside)[:, None], clipped_ids, num_segments=vocab_here
    )
    unit_grads = jnp.concatenate([table_grad, joint_weight_grad, project_grad], 0).reshape(
        -1, unit_rows, model_width
    )
    my_units = jnp.take(slot_unit, my_owner, axis=0)
    my_filled = jnp.take(slot_filled, my_owner, axis=0).astype(jnp.float32)[:, None, None]
    outgoing = (
        jnp.take(unit_grads, slot_unit.reshape(-1), axis=0)
        * slot_filled.reshape(-1).astype(jnp.float32)[:, None, None]
    )
    mine = lax.psum_scatter(outgoing, ("dp", "ctx"), scatter_dimension=0, tiled=True) * my_filled
    gains_grad, router_grad, bias_grad = lax.psum(
        (jnp.stack([gain_grad_one, gain_grad_two, gain_grad_three]), router_grad, bias_grad),
        ("dp", "ctx"),
    )
    slot_rates = unit_rates(my_units, table_units, query_units, value_units)[:, None, None]
    master_new, master_first_new, master_second_new = adam_update(
        master[0, 0], master_first[0, 0], master_second[0, 0], mine, slot_rates, decay_rate
    )
    inner_new, inner_first_new, inner_second_new = adam_update(
        expert_in, expert_in_first, expert_in_second, inner_grad, rate_inner, decay_rate
    )
    outer_new, outer_first_new, outer_second_new = adam_update(
        expert_out, expert_out_first, expert_out_second, outer_grad, rate_outer, decay_rate
    )
    gains_new, gains_first_new, gains_second_new = adam_update(
        norm_gains, norm_gains_first, norm_gains_second, gains_grad, rate_gains, 0.0
    )
    router_new, router_first_new, router_second_new = adam_update(
        router, router_first, router_second, router_grad, rate_router, decay_rate
    )
    biases_new, biases_first_new, biases_second_new = adam_update(
        rel_bias, rel_bias_first, rel_bias_second, bias_grad, rate_biases, 0.0
    )
    return (
        loss_totals,
        master_new[None, None],
        master_first_new[None, None],
        master_second_new[None, None],
        inner_new,
        inner_first_new,
        inner_second_new,
        outer_new,
        outer_first_new,
        outer_second_new,
        gains_new,
        gains_first_new,
        gains_second_new,
        router_new,
        router_first_new,
        router_second_new,
        biases_new,
        biases_first_new,
        biases_second_new,
    )


def solution(mesh):
    in_specs = (
        P("dp", "ctx"),
        P("dp", "ctx", None),
        P("dp", "ctx", None),
        P("dp", "ctx", None),
        P(("dp", "ctx"), None),
        P(),
        P("tensor", ("dp", "ctx"), None, None, None),
        P("tensor", ("dp", "ctx"), None, None, None),
        P("tensor", ("dp", "ctx"), None, None, None),
        P(("dp", "ctx"), None, "tensor"),
        P(("dp", "ctx"), None, "tensor"),
        P(("dp", "ctx"), None, "tensor"),
        P(("dp", "ctx"), "tensor", None),
        P(("dp", "ctx"), "tensor", None),
        P(("dp", "ctx"), "tensor", None),
        P(),
        P(),
        P(),
        P(),
        P(),
        P(),
        P("tensor", None),
        P("tensor", None),
        P("tensor", None),
    )
    out_specs = (
        P(),
        P("tensor", ("dp", "ctx"), None, None, None),
        P("tensor", ("dp", "ctx"), None, None, None),
        P("tensor", ("dp", "ctx"), None, None, None),
        P(("dp", "ctx"), None, "tensor"),
        P(("dp", "ctx"), None, "tensor"),
        P(("dp", "ctx"), None, "tensor"),
        P(("dp", "ctx"), "tensor", None),
        P(("dp", "ctx"), "tensor", None),
        P(("dp", "ctx"), "tensor", None),
        P(),
        P(),
        P(),
        P(),
        P(),
        P(),
        P("tensor", None),
        P("tensor", None),
        P("tensor", None),
    )
    return jax.shard_map(
        on_device, mesh=mesh, in_specs=in_specs, out_specs=out_specs, check_vma=False
    )
```

profile of v0, /device:TPU:0, one launch (start us, length us, event | category | flops | bytes accessed | tf_op | source)
XLA Modules:
  0.0 1838.7 jit_solution(11607745685048301446)
XLA Ops:
  12.5 90.1 %all-gather.5.cloned.1.call-done = bf16[1,1,168,64,768]{4,3,1,0,2:T(8,128)(2,1)} async-done(((bf16[1,1,21,64,768]{4,3,1,0,2:T(8,128)(2,1)}), bf16[1,1,168,64,768]{4,3,1,0,2:T(8,128)(2,1)}) %all-gather.5.cloned.1.call-update) | async-done | bytes 16515088 | tf_op jit(solution)/shard_map/all_gather | solution.py:254
  148.5 118.9 %all-reduce.8.cloned.1.call-done = f32[1024,768]{1,0:T(8,128)} async-done(((f32[1024,768]{1,0:T(8,128)}), f32[1024,768]{1,0:T(8,128)}) %all-reduce.8.cloned.1.call-update) | async-done | bytes 3145744 | tf_op jit(solution)/shard_map/psum | solution.py:125
  387.5 106.1 %all-reduce.10.cloned.1.call-done = f32[1024,768]{1,0:T(8,128)} async-done(((f32[1024,768]{1,0:T(8,128)}), f32[1024,768]{1,0:T(8,128)}) %all-reduce.10.cloned.1.call-update) | async-done | bytes 3145744 | tf_op jit(solution)/shard_map/psum | solution.py:125
  536.8 45.6 %all_to_all.20 = bf16[8,288,768]{2,1,0:T(8,128)(2,1)S(1)} all-to-all(bf16[8,288,768]{2,1,0:T(8,128)(2,1)S(1)} %select_multiply_fusion.1), channel_id=1, replica_groups=mesh['dp'=4,'ctx'=2,'tensor'=4] {'dp','ctx'}, dimensions={0} | all-to-all | bytes 7077888 | tf_op jit(solution)/shard_map/all_to_all | solution.py:129
  600.2 41.3 %all-to-all-done.1 = bf16[8,288,768]{2,1,0:T(8,128)(2,1)S(1)} async-done(((bf16[8,288,768]{2,1,0:T(8,128)(2,1)}), bf16[8,288,768]{2,1,0:T(8,128)(2,1)S(1)}, u32[]{:S(2)}, u32[]{:S(2)}) %all-to-all-start.1) | async-done | bytes 3538976 | tf_op jit(solution)/shard_map/all_to_all | solution.py:133
  656.6 118.2 %all-reduce.12.cloned.1.call-done = f32[1024,768]{1,0:T(8,128)} async-done(((f32[1024,768]{1,0:T(8,128)}), f32[1024,768]{1,0:T(8,128)}) %all-reduce.12.cloned.1.call-update) | async-done | bytes 3145744 | tf_op jit(solution)/shard_map/psum | solution.py:125
  779.1 30.6 %while.64 = (s32[]{:T(128)}, f32[2,512]{1,0:T(2,128)S(1)}, f32[2,512]{1,0:T(2,128)S(1)}, f32[2,512,2]{1,2,0:T(2,128)S(1)}, bf16[2,512,768]{2,1,0:T(8,128)(2,1)S(...) while((s32[]{:T(128)}, f32[2,512]{1,0:T(2,128)S(1)}, ...), condition=%wide.region_20.22_spmd.clone.clone, body=%wide.region_15.21_spmd.clone.clone.sunk | while | flops 6328318976 | bytes 45889656 | solution.py:381
  864.7 92.1 %while.65 = (s32[]{:T(128)}, f32[8000,768]{1,0:T(8,128)}, f32[2,512,768]{2,1,0:T(8,128)}, f32[2,512,2]{1,2,0:T(2,128)S(1)}, bf16[2,512,768]{2,1,0:T(8,128)(2,1)S...) while((s32[]{:T(128)}, f32[8000,768]{1,0:T(8,128)}, ...), condition=%wide.region_29.31_spmd.clone.clone, body=%wide.region_27.30_spmd.clone.clone.sunk | while | flops 18927616000 | bytes 183421136 | solution.py:421
  933.9 22.7 %select_add_fusion.2 = f32[8000,768]{1,0:T(8,128)} fusion(f32[8000,768]{1,0:T(8,128)} %get-tuple-element.890, bf16[512,8000]{0,1:T(8,128)(2,1)} %copy-done.4, pred[]{:T(512)S(6)} %compare.6, bf16[2,512,768]{2,1,0:T(8,128)(2,1)S(1)} %get-tuple-element.904, s32[]{:T(128)S(6)} %copy.159), kind=kOutput, calls=%fused_computation.30.clone.1 | convolution fusion | flops 6303744000 | bytes 58130436 | tf_op jit(solution)/shard_map/while/body/eval_jaxpr/dot_general | solution.py:416
  956.9 119.1 %all-reduce.14.cloned.1.call-done = f32[1024,768]{1,0:T(8,128)} async-done(((f32[1024,768]{1,0:T(8,128)}), f32[1024,768]{1,0:T(8,128)}) %all-reduce.14.cloned.1.call-update) | async-done | bytes 3145744 | tf_op jit(solution)/shard_map/psum | solution.py:125
  1092.1 45.6 %all_to_all.21 = bf16[8,288,768]{2,1,0:T(8,128)(2,1)S(1)} all-to-all(bf16[8,288,768]{2,1,0:T(8,128)(2,1)S(1)} %multiply_convert_fusion.5), channel_id=1, replica_groups=mesh['dp'=4,'ctx'=2,'tensor'=4] {'dp','ctx'}, dimensions={0} | all-to-all | bytes 7077888 | tf_op jit(solution)/shard_map/all_to_all | solution.py:129
  1152.1 45.3 %all_to_all.22 = bf16[8,288,768]{2,1,0:T(8,128)(2,1)} all-to-all(bf16[8,288,768]{2,1,0:T(8,128)(2,1)S(1)} %fusion.71), channel_id=1, replica_groups=mesh['dp'=4,'ctx'=2,'tensor'=4] {'dp','ctx'}, dimensions={0} | all-to-all | bytes 7077888 | tf_op jit(solution)/shard_map/all_to_all | solution.py:133
  1234.9 99.8 %all-reduce.16.cloned.1.call-done = f32[1024,768]{1,0:T(8,128)} async-done(((f32[1024,768]{1,0:T(8,128)}), f32[1024,768]{1,0:T(8,128)}) %all-reduce.16.cloned.1.call-update) | async-done | bytes 3145744 | tf_op jit(solution)/shard_map/psum | solution.py:125
  1415.1 99.8 %all-reduce.18.cloned.1.call-done = f32[1024,768]{1,0:T(8,128)} async-done(((f32[1024,768]{1,0:T(8,128)}), f32[1024,768]{1,0:T(8,128)}) %all-reduce.18.cloned.1.call-update) | async-done | bytes 3145744 | tf_op jit(solution)/shard_map/psum | solution.py:125
  1517.6 25.7 %scatter_custom_fusion.1 = f32[8000,768]{1,0:T(8,128)} fusion(f32[8000,768]{1,0:T(8,128)} %get-tuple-element.385, s32[1024]{0:T(1024)} %bitcast.504, f32[1024,768]{1,0:T(8,128)} %copy-done.15, f32[1024,768]{1,0:T(8,128)} %all-reduce.18.cloned.1.call-done, f32[1024,768]{1,0:T(8,128)S(1)} %copy-done.14, f32[1024]{0:T(1024)S(1)} %broadcast_multiply_fusion.3, ...), kind=kCustom, calls=%fused_computation.123 | custom fusion | flops 6291456 | bytes 34028544 | tf_op jit(solution)/shard_map/scatter-add | solution.py:544
  1543.3 24.2 %pad_maximum_fusion = f32[8768,768]{1,0:T(8,128)} fusion(f32[192,768]{1,0:T(8,128)} %fusion.105, f32[576,768]{1,0:T(8,128)} %fusion.108, f32[8000,768]{1,0:T(8,128)} %scatter_custom_fusion.1), kind=kLoop, calls=%fused_computation.44 | loop fusion | flops 13467648 | bytes 53870592 | tf_op jit(solution)/shard_map/concatenate | solution.py:547
  1567.5 27.1 %gather_fusion.5 = f32[168,64,768]{2,1,0:T(8,128)} fusion(f32[137,64,768]{2,1,0:T(8,128)} %bitcast.432, s32[1024]{0:T(1024)} %pad_clamp_fusion.2), kind=kCustom, calls=%fused_computation.7 | custom fusion | bytes 66060960 | tf_op jit(solution)/shard_map/jit(_take)/gather | solution.py:553
  1594.6 23.5 %select_multiply_fusion = f32[168,64,768]{2,1,0:T(8,128)} fusion(f32[168,64,768]{2,1,0:T(8,128)} %gather_fusion.5, f32[168]{0:T(256)S(1)} %copy-done.118, pred[168]{0:T(512)(128)(4,1)S(1)} %copy-done.128), kind=kLoop, calls=%fused_computation.43 | loop fusion | flops 16515072 | bytes 66061128 | tf_op jit(solution)/shard_map/mul | solution.py:553
  1619.1 18.2 copy.107
  1637.4 20.2 %copy.105 = f32[192,8,8,256]{3,2,1,0:T(8,128)} copy(f32[192,8,8,256]{3,1,2,0:T(8,128)} %bitcast.445) | data formatting | bytes 25165824
  1680.9 15.9 copy.106
  1696.9 16.1 copy.108
  1735.8 25.2 %all-reduce = (f32[3,768]{1,0:T(4,128)S(1)}, f32[768,8]{0,1:T(8,128)S(1)}, f32[3,8]{1,0:T(4,128)S(1)}) all-reduce(f32[3,768]{1,0:T(4,128)S(1)} %pad_maximum_fusion.8, f32[768,8]{0,1:T(8,128)S(1)} %fusion.117, f32[3,8]{1,0:T(4,128)S(1)} %fusion.96), channel_id=1, replica_groups=mesh['dp'=4,'ctx'=2,'tensor'=4] {'dp','ctx'}, use_global_device_ids=true, to_apply=%region_47.49 | all-reduce | flops 8472 | bytes 67776 | tf_op jit(solution)/shard_map/psum | solution.py:557
  1762.9 58.4 %reduce-scatter.2.cloned.1.call-done = f32[21,64,768]{2,1,0:T(8,128)} async-done(((f32[168,64,768]{2,1,0:T(8,128)}), f32[21,64,768]{2,1,0:T(8,128)}) %reduce-scatter.2.cloned.1.call-update) | async-done | bytes 4128784 | tf_op jit(solution)/shard_map/reduce_scatter | solution.py:556
  (561 shorter events, 613.8 us)
Async XLA Ops:
  7.2 95.4 %all-gather.5.cloned.1.call-start = ((), (), s32[]{:S(2)}) async-start(), calls=%async_computation.12 | async-start | bytes 18579456 | tf_op jit(solution)/shard_map/all_gather | solution.py:254
  11.0 256.4 %all-reduce.8.cloned.1.call-start = ((), (), s32[]{:S(2)}) async-start(), calls=%async_computation.5 | async-start | bytes 6291456 | tf_op jit(solution)/shard_map/psum | solution.py:125
  12.5 131.5 %copy-start.84 = (f32[1,1024]{1,0:T(1,128)}, f32[1,1024]{1,0:T(1,128)S(1)}, u32[]{:S(2)}) copy-start(f32[1,1024]{1,0:T(1,128)S(1)} %and_select_fusion.1) | copy-start | bytes 12292
  146.2 347.5 %all-reduce.10.cloned.1.call-start = ((), (), s32[]{:S(2)}) async-start(), calls=%async_computation.6 | async-start | bytes 6291456 | tf_op jit(solution)/shard_map/psum | solution.py:125
  146.3 126.4 %copy-start.124 = (s32[2,8]{1,0:T(2,128)}, s32[2,8]{1,0:T(2,128)S(1)}, u32[]{:S(2)}) copy-start(s32[2,8]{1,0:T(2,128)S(1)} %get-tuple-element.631) | copy-start | bytes 196
  146.3 130.3 %copy-start.126 = (s32[2,8]{1,0:T(2,128)}, s32[2,8]{1,0:T(2,128)S(1)}, u32[]{:S(2)}) copy-start(s32[2,8]{1,0:T(2,128)S(1)} %get-tuple-element.632) | copy-start | bytes 196
  146.6 151.9 %copy-start.93 = (f32[3,2,8]{2,1,0:T(2,128)}, f32[3,2,8]{2,1,0:T(2,128)S(1)}, u32[]{:S(2)}) copy-start(f32[3,2,8]{2,1,0:T(2,128)S(1)} %copy.79) | copy-start | bytes 580
  147.2 125.5 %copy-start.81 = (f32[768]{0:T(1024)}, f32[768]{0:T(1024)S(1)}, u32[]{:S(2)}) copy-start(f32[768]{0:T(1024)S(1)} %get-tuple-element.512) | copy-start | bytes 9220
  147.2 348.8 %copy-start.70 = (f32[768]{0:T(1024)}, f32[768]{0:T(1024)S(1)}, u32[]{:S(2)}) copy-start(f32[768]{0:T(1024)S(1)} %get-tuple-element.511) | copy-start | bytes 9220
  148.5 124.2 %copy-start.32 = (bf16[9,64,768]{2,1,0:T(8,128)(2,1)}, bf16[9,64,768]{2,1,0:T(8,128)(2,1)S(1)}, u32[]{:S(2)}) copy-start(bf16[9,64,768]{2,1,0:T(8,128)(2,1)S(1)} %slice.213) | copy-start | bytes 2654212
  274.0 44.7 %collective-permute-start = (bf16[1,1024,384]{1,2,0:T(8,128)(2,1)}, bf16[1,1024,384]{1,2,0:T(8,128)(2,1)}, u32[]{:S(2)}, u32[]{:S(2)}) collective-permute-start(bf16[1,1024,384]{1,2,0:T(8,128)(2,1)} %get-tuple-element.619), channel_id=1, source_target_pairs={{0,4},{1,5},{2,6},{3,7},{8,12},{9,13},{10,14},{11,15},{16,20},{17,... | collective-permute-start | bytes 2359304 | tf_op jit(solution)/shard_map/ppermute | solution.py:35
  369.9 123.8 %copy-start.13 = (f32[1024,768]{1,0:T(8,128)S(1)}, f32[1024,768]{1,0:T(8,128)}, u32[]{:S(2)}) copy-start(f32[1024,768]{1,0:T(8,128)} %all-reduce.8.cloned.1.call-done) | copy-start | bytes 9437188
  386.5 147.9 %copy-start.91 = (pred[8,288]{1,0:T(8,128)(4,1)}, pred[8,288]{1,0:T(8,128)(4,1)S(1)}, u32[]{:S(2)}) copy-start(pred[8,288]{1,0:T(8,128)(4,1)S(1)} %broadcast_in_dim.330) | copy-start | bytes 6916
  387.5 139.0 %copy-start.50 = (s32[3072]{0:T(1024)}, s32[3072]{0:T(1024)S(1)}, u32[]{:S(2)}) copy-start(s32[3072]{0:T(1024)S(1)} %pad_clamp_fusion.1) | copy-start | bytes 36868
  595.8 45.7 %all-to-all-start.1 = ((bf16[8,288,768]{2,1,0:T(8,128)(2,1)}), bf16[8,288,768]{2,1,0:T(8,128)(2,1)S(1)}, u32[]{:S(2)}, u32[]{:S(2)}) async-start(bf16[8,288,768]{2,1,0:T(8,128)(2,1)} %fusion.68), calls=%async_computation.1 | async-start | bytes 7077888 | tf_op jit(solution)/shard_map/all_to_all | solution.py:133
  599.5 175.3 %all-reduce.12.cloned.1.call-start = ((), (), s32[]{:S(2)}) async-start(), calls=%async_computation.7 | async-start | bytes 6291456 | tf_op jit(solution)/shard_map/psum | solution.py:125
  656.4 419.7 %all-reduce.14.cloned.1.call-start = ((), (), s32[]{:S(2)}) async-start(), calls=%async_computation.8 | async-start | bytes 6291456 | tf_op jit(solution)/shard_map/psum | solution.py:125
  656.6 122.2 %copy-start.72 = (f32[768]{0:T(1024)S(1)}, f32[768]{0:T(1024)}, u32[]{:S(2)}) copy-start(f32[768]{0:T(1024)} %get-tuple-element.510) | copy-start | bytes 9220
  864.6 211.4 %copy-start.69 = (f32[1024]{0:T(1024)S(1)}, f32[1024]{0:T(1024)}, u32[]{:S(2)}) copy-start(f32[1024]{0:T(1024)} %copy-done.68) | copy-start | bytes 12292
  864.6 211.4 %copy-start.73 = (f32[768]{0:T(1024)S(1)}, f32[768]{0:T(1024)}, u32[]{:S(2)}) copy-start(f32[768]{0:T(1024)} %get-tuple-element.510) | copy-start | bytes 9220
  956.8 377.9 %all-reduce.16.cloned.1.call-start = ((), (), s32[]{:S(2)}) async-start(), calls=%async_computation.9 | async-start | bytes 6291456 | tf_op jit(solution)/shard_map/psum | solution.py:125
  1216.2 298.7 %all-reduce.18.cloned.1.call-start = ((), (), s32[]{:S(2)}) async-start(), calls=%async_computation.10 | async-start | bytes 6291456 | tf_op jit(solution)/shard_map/psum | solution.py:125
  1383.4 5.9 collective-permute-start.1
  1393.8 427.5 %reduce-scatter.2.cloned.1.call-start = ((), (), s32[]{:S(2)}) async-start(), calls=%async_computation.11 | async-start | bytes 37158912 | tf_op jit(solution)/shard_map/reduce_scatter | solution.py:556
  (141 other events, 2661.1 us)
Sparse Core Ops, SparseCore 0:
  11.2 91.4 all-gather.4
  146.3 121.0 all-reduce.7
  373.4 120.2 all-reduce.9
  656.5 118.2 all-reduce.11
  956.9 119.0 all-reduce.13
  1216.3 118.4 all-reduce.15
  1393.9 120.8 all-reduce.17
  1618.3 202.9 reduce-scatter.1
where the time goes:
time: 1850 us; the launch traced here: 1840 us
  waiting for transfers between devices  852 us (46%)
  local copies, waits for them, and re-layouts  275 us (15%)
  matrix products  237 us (13%)
  other arithmetic  226 us (12%)
  blocking collectives  223 us (12%)
    psum x6, waiting for transfers between devices, over_tensor(): return lax.psum(partial_sums, 'tensor')  662 us
    unnamed x310, local copies, waits for them, and re-layouts  95.5 us
    all_to_all x2, blocking collectives, to_experts(): lax.all_to_all(buffer, ('dp', 'ctx'), split_axis=0, concat_axis=0, tiled=...  91.3 us
    all_gather x1, waiting for transfers between devices, on_device(): gathered = lax.all_gather(master[0, 0], ('dp', 'ctx'), axis=0, tiled=True)  90.1 us
    reduce_scatter x1, waiting for transfers between devices, on_device(): lax.psum_scatter(outgoing, ('dp', 'ctx'), scatter_dimension=0, tiled=True)  58.4 us
    all_to_all x1, blocking collectives, from_experts(): lax.all_to_all(buffer, ('dp', 'ctx'), split_axis=0, concat_axis=0, tiled=...  45.3 us
    all_to_all x1, waiting for transfers between devices, from_experts(): lax.all_to_all(buffer, ('dp', 'ctx'), split_axis=0, concat_axis=0, tiled=...  41.3 us
    all_gather x3, blocking collectives, combined_all(): everything = jax.tree.map(lambda part: lax.all_gather(part, axis), x)  39.4 us
  transfers between devices with their start and end apart: 11, of which 9 were waited for; matrix products, arithmetic and copies ran while one was open for 11% of the time, Pallas kernels for 0%

commit v1 on v0

--- a/solution.py
+++ b/solution.py
@@ -1,8 +1,11 @@
+import functools
 import math
 
 import jax
 import jax.numpy as jnp
 from jax import lax
+from jax.experimental import pallas as pl
+from jax.experimental.pallas import tpu as pltpu
 from jax.sharding import PartitionSpec as P
 
 VOCAB = 32000
@@ -34,6 +37,333 @@
     initial, last = (max(0, -steps), min(count, count - steps))
     return lax.ppermute(value, axis, [(source, source + steps) for source in range(initial, last)])
 
+MESH_ID = pl.DeviceIdType.MESH
+whole_vmem = pl.BlockSpec(memory_space=pltpu.VMEM)
+whole_any = pl.BlockSpec(memory_space=pl.ANY)
+line_rows = 128
+line_lag = 3
+
+
+def sum_line_kernel(
+    count, meets_all, prologue, epilogue, n_extra, n_aux, n_scratch, part_ref, *refs
+):
+    extras = refs[:n_extra]
+    out_ref = refs[n_extra]
+    aux = refs[n_extra + 1 : n_extra + 1 + n_aux]
+    rest = refs[n_extra + 1 + n_aux :]
+    scratch = rest[:n_scratch]
+    stage, from_end, from_mid, send_sem, end_sem, mid_sem, back_sem, back_recv = rest[n_scratch:]
+    rank = lax.axis_index("tensor")
+    inner = (rank == 1) | (rank == 2)
+    end_peer = jnp.where(rank < 2, 1 - rank, 5 - rank)
+    mid_peer = 3 - rank
+    barrier = pltpu.get_barrier_semaphore()
+    if not meets_all:
+        pl.semaphore_signal(barrier, inc=1, device_id={"tensor": end_peer}, device_id_type=MESH_ID)
+
+        @pl.when(inner)
+        def _():
+            pl.semaphore_signal(
+                barrier, inc=1, device_id={"tensor": mid_peer}, device_id_type=MESH_ID
+            )
+            pl.semaphore_wait(barrier, 2)
+
+        @pl.when(jnp.logical_not(inner))
+        def _():
+            pl.semaphore_wait(barrier, 1)
+    else:
+        for step in (1, 2, 3):
+            other = lax.rem(rank + step, 4)
+            pl.semaphore_signal(barrier, inc=1, device_id={"tensor": other}, device_id_type=MESH_ID)
+        pl.semaphore_wait(barrier, 3)
+
+    rows = line_rows
+
+    def span(i):
+        return pl.ds(pl.multiple_of(i * rows, rows), rows)
+
+    def to_inner(i):
+        return pltpu.make_async_remote_copy(
+            src_ref=stage.at[i],
+            dst_ref=from_end.at[i],
+            send_sem=send_sem.at[i],
+            recv_sem=end_sem.at[i],
+            device_id={"tensor": end_peer},
+            device_id_type=MESH_ID,
+        )
+
+    def to_middle(i):
+        return pltpu.make_async_remote_copy(
+            src_ref=stage.at[i],
+            dst_ref=from_mid.at[i],
+            send_sem=send_sem.at[i],
+            recv_sem=mid_sem.at[i],
+            device_id={"tensor": mid_peer},
+            device_id_type=MESH_ID,
+        )
+
+    def to_end(i):
+        return pltpu.make_async_remote_copy(
+            src_ref=out_ref.at[span(i)],
+            dst_ref=out_ref.at[span(i)],
+            send_sem=back_sem.at[i],
+            recv_sem=back_recv.at[i],
+            device_id={"tensor": end_peer},
+            device_id_type=MESH_ID,
+        )
+
+    @pl.when(jnp.logical_not(inner))
+    def _():
+        def push(i, carry):
+            stage[i] = part_ref[span(i)].astype(jnp.bfloat16)
+            to_inner(i).start()
+            return carry
+
+        lax.fori_loop(0, count, push, 0)
+
+    if prologue is not None:
+        prologue(rank, extras, aux, scratch)
+
+    @pl.when(inner)
+    def _():
+        def step(i, carry):
+            @pl.when(i < count)
+            def _():
+                to_inner(i).wait_recv()
+                mine = part_ref[span(i)].astype(jnp.float32) + from_end[i].astype(jnp.float32)
+                stage[i] = mine.astype(jnp.bfloat16)
+                to_middle(i).start()
+
+            @pl.when(i >= line_lag)
+            def _():
+                j = i - line_lag
+                to_middle(j).wait_recv()
+                total = stage[j].astype(jnp.float32) + from_mid[j].astype(jnp.float32)
+                out_ref[span(j)] = epilogue(total, span(j), rank, extras, aux, scratch)
+                to_end(j).start()
+
+            return carry
+
+        lax.fori_loop(0, count + line_lag, step, 0)
+
+        def drain(i, carry):
+            to_middle(i).wait_send()
+            to_end(i).wait_send()
+            return carry
+
+        lax.fori_loop(0, count, drain, 0)
+
+    @pl.when(jnp.logical_not(inner))
+    def _():
+        def finish(i, carry):
+            to_end(i).wait_recv()
+            to_inner(i).wait_send()
+            return carry
+
+        lax.fori_loop(0, count, finish, 0)
+
+
+def sum_line(
+    part, extras, aux_shapes, epilogue, collective_id, prologue=None, scratch=(), meets_all=False
+):
+    tokens, width = part.shape
+    count = tokens // line_rows
+    chunks = pltpu.VMEM((count, line_rows, width), jnp.bfloat16)
+    return pl.pallas_call(
+        functools.partial(
+            sum_line_kernel,
+            count,
+            meets_all,
+            prologue,
+            epilogue,
+            len(extras),
+            len(aux_shapes),
+            len(scratch),
+        ),
+        out_shape=[jax.ShapeDtypeStruct((tokens, width), jnp.bfloat16)] + list(aux_shapes),
+        in_specs=[whole_vmem] * (1 + len(extras)),
+        out_specs=[whole_vmem] * (1 + len(aux_shapes)),
+        scratch_shapes=list(scratch)
+        + [chunks, chunks, chunks]
+        + [pltpu.SemaphoreType.DMA((count,))] * 5,
+        compiler_params=pltpu.CompilerParams(
+            collective_id=collective_id, has_side_effects=True, vmem_limit_bytes=48 << 20
+        ),
+    )(part, *extras)
+
+
+def keep_total(total, span, rank, extras, aux, scratch):
+    return total.astype(jnp.bfloat16)
+
+
+def inverse_rms(values):
+    return lax.rsqrt(jnp.mean(values * values, -1, keepdims=True) + norm_epsilon)
+
+
+def finish_mixture(total, span, rank, extras, aux, scratch):
+    stream_one, gain = extras
+    stream_two = stream_one[span] + total
+    aux[0][span] = stream_two
+    return (stream_two * inverse_rms(stream_two) * gain[...]).astype(jnp.bfloat16)
+
+
+def norm_back_rows(values, gain, upstream):
+    inverse = inverse_rms(values)
+    normed = values * inverse
+    scaled = upstream * gain
+    gain_grad = jnp.sum(upstream * normed, 0, keepdims=True)
+    inputs_grad = inverse * (scaled - normed * jnp.mean(scaled * normed, -1, keepdims=True))
+    return (inputs_grad, gain_grad)
+
+
+def clear_gain(rank, extras, aux, scratch):
+    aux[-1][...] = jnp.zeros_like(aux[-1])
+
+
+def add_gain(rank, ref, gain_grad):
+    ref[...] += jnp.where(rank == 1, gain_grad, 0.0)
+
+
+def finish_head_grad(total, span, rank, extras, aux, scratch):
+    stream_two, gain = extras
+    grad_two, gain_grad = norm_back_rows(stream_two[span], gain[...], total)
+    aux[0][span] = grad_two
+    add_gain(rank, aux[1], gain_grad)
+    return grad_two.astype(jnp.bfloat16)
+
+
+def start_router_grad(rank, extras, aux, scratch):
+    stream_one, gain, grad_two, gate_part, gates, routes, router_low = extras
+    grad_one, logit_grad, gain_grad = aux
+    landed, gate_send, gate_recv = scratch
+    gain_grad[...] = jnp.zeros_like(gain_grad)
+    copies = []
+    for step in (1, 2, 3):
+        copy = pltpu.make_async_remote_copy(
+            src_ref=gate_part,
+            dst_ref=landed.at[step - 1],
+            send_sem=gate_send.at[step - 1],
+            recv_sem=gate_recv.at[step - 1],
+            device_id={"tensor": lax.rem(rank + step, 4)},
+            device_id_type=MESH_ID,
+        )
+        copy.start()
+        copies.append(copy)
+    for copy in copies:
+        copy.wait()
+    gate_grad = jnp.zeros(gate_part.shape, jnp.float32)
+    for source in range(4):
+        piece = jnp.zeros(gate_part.shape, jnp.float32)
+        for step in (1, 2, 3):
+            piece = jnp.where(lax.rem(source + step, 4) == rank, landed[step - 1], piece)
+        gate_grad = gate_grad + jnp.where(rank == source, gate_part[...], piece)
+    weighted = gates[...] * gate_grad
+    chosen = gates[...] * (gate_grad - (weighted[0:1] + weighted[1:2]))
+    experts, tokens = logit_grad.shape
+    row = lax.broadcasted_iota(jnp.int32, (experts, tokens), 0)
+    placed = jnp.where(row == routes[0:1], chosen[0:1], 0.0) + jnp.where(
+        row == routes[1:2], chosen[1:2], 0.0
+    )
+    logit_grad[...] = placed.astype(jnp.bfloat16)
+
+
+def finish_expert_grad(total, span, rank, extras, aux, scratch):
+    stream_one, gain, grad_two, gate_part, gates, routes, router_low = extras
+    grad_one, logit_grad, gain_grad = aux
+    upstream = total + lax.dot_general(
+        logit_grad[:, span],
+        router_low[...],
+        (((0,), (1,)), ((), ())),
+        preferred_element_type=jnp.float32,
+    )
+    part, gain_part = norm_back_rows(stream_one[span], gain[...], upstream)
+    result = grad_two[span] + part
+    grad_one[span] = result
+    add_gain(rank, gain_grad, gain_part)
+    return result.astype(jnp.bfloat16)
+
+
+def finish_input_grad(scale, total, span, rank, extras, aux, scratch):
+    embedded, gain, grad_one = extras
+    stream_zero = embedded[span].astype(jnp.float32) * scale
+    part, gain_part = norm_back_rows(stream_zero, gain[...], total)
+    add_gain(rank, aux[0], gain_part)
+    return ((grad_one[span] + part) * scale).astype(jnp.bfloat16)
+
+
+def gather_line_kernel(count, *refs):
+    ins = refs[:count]
+    outs = refs[count : 2 * count]
+    local_sem, send_sem, recv_sem = refs[2 * count :]
+    rank = lax.axis_index("tensor")
+    barrier = pltpu.get_barrier_semaphore()
+    for step in (1, 2, 3):
+        other = lax.rem(rank + step, 4)
+        pl.semaphore_signal(barrier, inc=1, device_id={"tensor": other}, device_id_type=MESH_ID)
+    pl.semaphore_wait(barrier, 3)
+    copies = []
+    for k in range(count):
+        for step in (1, 2, 3):
+            copy = pltpu.make_async_remote_copy(
+                src_ref=ins[k],
+                dst_ref=outs[k].at[rank],
+                send_sem=send_sem.at[k, step - 1],
+                recv_sem=recv_sem.at[k, step - 1],
+                device_id={"tensor": lax.rem(rank + step, 4)},
+                device_id_type=MESH_ID,
+            )
+            copy.start()
+            copies.append(copy)
+        own = pltpu.make_async_copy(ins[k], outs[k].at[rank], local_sem.at[k])
+        own.start()
+        own.wait()
+    for copy in copies:
+        copy.wait()
+
+
+def gather_line(arrays, collective_id):
+    count = len(arrays)
+    return pl.pallas_call(
+        functools.partial(gather_line_kernel, count),
+        out_shape=[jax.ShapeDtypeStruct((4,) + x.shape, x.dtype) for x in arrays],
+        in_specs=[whole_vmem] * count,
+        out_specs=[whole_vmem] * count,
+        scratch_shapes=[
+            pltpu.SemaphoreType.DMA((count,)),
+            pltpu.SemaphoreType.DMA((count, 3)),
+            pltpu.SemaphoreType.DMA((count, 3)),
+        ],
+        compiler_params=pltpu.CompilerParams(
+            collective_id=collective_id, has_side_effects=True, vmem_limit_bytes=40 << 20
+        ),
+    )(*arrays)
+
+
+def pull_units_kernel(group, slots_ref, source_ref, out_ref, sem):
+    start = pl.program_id(0) * group
+
+    def push(u, carry):
+        pltpu.make_async_copy(source_ref.at[slots_ref[start + u]], out_ref.at[u], sem).start()
+        return carry
+
+    lax.fori_loop(0, group, push, 0)
+    pltpu.make_async_copy(out_ref, out_ref, sem).wait()
+
+
+def pull_units(source, slots):
+    count = slots.shape[0]
+    unit_bytes = math.prod(source.shape[1:]) * source.dtype.itemsize
+    group = max(k for k in range(1, count + 1) if count % k == 0 and (k <= 32 or k * unit_bytes < 15 << 20))
+    return pl.pallas_call(
+        functools.partial(pull_units_kernel, group),
+        grid=(count // group,),
+        out_shape=jax.ShapeDtypeStruct((count,) + source.shape[1:], source.dtype),
+        in_specs=[pl.BlockSpec(memory_space=pltpu.SMEM), whole_any],
+        out_specs=pl.BlockSpec((group,) + source.shape[1:], lambda k: (k,) + (0,) * (source.ndim - 1)),
+        scratch_shapes=[pltpu.SemaphoreType.DMA],
+        compiler_params=pltpu.CompilerParams(vmem_limit_bytes=40 << 20),
+    )(slots, source)
+
 
 def combined_all(x, axis, combine):
     everything = jax.tree.map(lambda part: lax.all_gather(part, axis), x)
@@ -57,16 +387,7 @@
 
 
 def norm_forward(values, gain_row):
-    inverse = lax.rsqrt(jnp.mean(values * values, -1, keepdims=True) + norm_epsilon)
-    return (values * inverse * gain_row, inverse)
-
-
-def norm_backward(values, inverse, gain_row, upstream):
-    normed = values * inverse
-    scaled = upstream * gain_row
-    gain_grad = jnp.sum(upstream * normed, 0)
-    inputs_grad = inverse * (scaled - normed * jnp.mean(scaled * normed, -1, keepdims=True))
-    return (inputs_grad, gain_grad)
+    return values * inverse_rms(values) * gain_row
 
 
 def slot_tables(owner_ids, owners, most_units):
@@ -108,21 +429,11 @@
     pair_rank = jnp.sum(before.astype(jnp.int32), 1)
     pair_kept = pair_rank < capacity
     pair_dest = pair_expert * capacity + jnp.minimum(pair_rank, capacity - 1)
-    target_slot = jnp.where(pair_kept, pair_dest, experts * capacity)
-    slot_source = (
-        jnp.full((experts * capacity,), 2 * tokens_here, jnp.int32)
-        .at[target_slot]
-        .set(jnp.arange(2 * tokens_here, dtype=jnp.int32), mode="drop")
-    )
-    return (pair_kept, pair_dest, slot_source)
+    return (pair_kept, pair_dest)
 
 
 def gelu_tanh(values):
     return jax.nn.gelu(values, approximate=True)
-
-
-def over_tensor(partial_sums):
-    return lax.psum(partial_sums, "tensor")
 
 
 def to_experts(buffer):
@@ -251,22 +562,28 @@
     embed_scale = math.sqrt(model_width)
     owner_ids = owner_of[:, 0]
     unit_rank, slot_unit, slot_filled = slot_tables(owner_ids, owners, most_units)
-    gathered = lax.all_gather(master[0, 0], ("dp", "ctx"), axis=0, tiled=True)
-    weights_flat = jnp.take(gathered, owner_ids * most_units + unit_rank, axis=0).reshape(
-        -1, model_width
-    )
-    table_low = weights_flat[:vocab_here].astype(jnp.bfloat16)
-    joint_low = weights_flat[vocab_here : vocab_here + 3 * hidden_here].astype(jnp.bfloat16)
-    project_low = weights_flat[vocab_here + 3 * hidden_here :].astype(jnp.bfloat16)
+    gathered = lax.all_gather(master[0, 0].astype(jnp.bfloat16), ("dp", "ctx"), axis=0, tiled=True)
+    weights_low = pull_units(gathered, owner_ids * most_units + unit_rank).reshape(-1, model_width)
+    table_low = weights_low[:vocab_here]
+    joint_low = weights_low[vocab_here : vocab_here + 3 * hidden_here]
+    project_low = weights_low[vocab_here + 3 * hidden_here :]
+    rolled = [project_low] + [
+        lax.ppermute(project_low, "tensor", [(source, (source + step) % 4) for source in range(4)])
+        for step in (1, 2, 3)
+    ]
+    project_full = lax.dynamic_slice_in_dim(
+        jnp.concatenate(rolled[::-1] + rolled[::-1], 0), (3 - my_rank) * hidden_here, model_width, 0
+    )
     local_ids = token_ids.reshape(-1) - my_rank * vocab_here
-    inside = ((local_ids >= 0) & (local_ids < vocab_here)).astype(jnp.float32)
+    inside = (local_ids >= 0) & (local_ids < vocab_here)
     clipped_ids = jnp.clip(local_ids, 0, vocab_here - 1)
-    looked = (
-        jnp.take(table_low, clipped_ids, axis=0).astype(jnp.float32)
-        * (embed_scale * inside)[:, None]
-    )
-    stream_zero = over_tensor(looked)
-    first_normalized, inverse_one = norm_forward(stream_zero, norm_gains[0])
+    looked = jnp.where(inside[:, None], jnp.take(table_low, clipped_ids, axis=0), 0)
+    gain_rows = [norm_gains[k : k + 1] for k in range(3)]
+    stream_shape = jax.ShapeDtypeStruct((tokens_here, model_width), jnp.float32)
+    gain_shape = jax.ShapeDtypeStruct((1, model_width), jnp.float32)
+    (embedded,) = sum_line(looked, [], [], keep_total, 1)
+    stream_zero = embedded.astype(jnp.float32) * embed_scale
+    first_normalized = norm_forward(stream_zero, norm_gains[0])
     normed_one_low = first_normalized.astype(jnp.bfloat16)
     joint = lax.dot_general(
         normed_one_low, joint_low, (((1,), (1,)), ((), ())), preferred_element_type=jnp.float32
@@ -315,10 +632,14 @@
 
     attention_output, logsum_all = lax.map(attend_forward, (queries, keys_all, values_all))
     attended_flat = attention_output.reshape(tokens_here, hidden_here)
-    stream_one = stream_zero + over_tensor(
-        jnp.dot(attended_flat, project_low, preferred_element_type=jnp.float32)
-    )
-    second_normalized, inverse_two = norm_forward(stream_one, norm_gains[1])
+    (attended_all,) = gather_line([attended_flat.T], 2)
+    stream_one = stream_zero + lax.dot_general(
+        attended_all.reshape(model_width, tokens_here),
+        project_full,
+        (((0,), (0,)), ((), ())),
+        preferred_element_type=jnp.float32,
+    )
+    second_normalized = norm_forward(stream_one, norm_gains[1])
     normed_two_low = second_normalized.astype(jnp.bfloat16)
     router_low = router.astype(jnp.bfloat16)
     router_scores_raw = jnp.dot(normed_two_low, router_low, preferred_element_type=jnp.float32)
@@ -328,13 +649,18 @@
     )
     chosen = jnp.einsum("tke,te->tk", route_onehot, router_scores_raw, precision=highest_precision)
     gate_values = jax.nn.softmax(chosen, -1)
-    pair_kept, pair_dest, slot_source = pair_slots(route_pairs, priority[0], experts, capacity)
-    kept_rows = pair_kept.astype(jnp.float32)
-    slot_full = (slot_source < 2 * tokens_here).astype(jnp.float32)
-    slot_token = slot_source % tokens_here
-    dispatch_rows = (
-        jnp.take(normed_two_low, slot_token, axis=0) * slot_full[:, None].astype(jnp.bfloat16)
-    ).reshape(owners, experts_here * capacity, model_width)
+    pair_kept, pair_dest = pair_slots(route_pairs, priority[0], experts, capacity)
+    slots = lax.broadcasted_iota(jnp.int32, (experts * capacity, tokens_here), 0)
+    hits = [
+        (slots == pair_dest[k * tokens_here : (k + 1) * tokens_here][None, :])
+        & pair_kept[k * tokens_here : (k + 1) * tokens_here][None, :]
+        for k in range(2)
+    ]
+    hit_low = [hit.astype(jnp.bfloat16) for hit in hits]
+    both_low = (hits[0] | hits[1]).astype(jnp.bfloat16)
+    dispatch_rows = jnp.dot(
+        both_low, normed_two_low, preferred_element_type=jnp.float32
+    ).astype(jnp.bfloat16).reshape(owners, experts_here * capacity, model_width)
     arrived = to_experts(dispatch_rows).reshape(owners, experts_here, capacity, model_width)
     inner_low = expert_in.astype(jnp.bfloat16)
     outer_low = expert_out.astype(jnp.bfloat16)
@@ -348,13 +674,16 @@
     returned = from_experts(
         expert_part.reshape(owners, experts_here * capacity, model_width)
     ).reshape(experts * capacity, model_width)
-    pair_rows = (
-        jnp.take(returned, pair_dest, axis=0).astype(jnp.float32) * kept_rows[:, None]
-    ).reshape(2, tokens_here, model_width)
+    pair_rows = [
+        lax.dot_general(
+            hit_low[k], returned, (((0,), (0,)), ((), ())), preferred_element_type=jnp.float32
+        )
+        for k in range(2)
+    ]
     moe_partial = gate_values[:, 0:1] * pair_rows[0] + gate_values[:, 1:2] * pair_rows[1]
-    stream_two = stream_one + over_tensor(moe_partial)
-    normed_three, inverse_three = norm_forward(stream_two, norm_gains[2])
-    head_low = normed_three.astype(jnp.bfloat16)
+    head_low, stream_two = sum_line(
+        moe_partial, [stream_one, gain_rows[2]], [stream_shape], finish_mixture, 3
+    )
     head_tiles = tokens_here // head_rows_count
     head_rows = head_low.reshape(head_tiles, head_rows_count, model_width)
     local_targets = (targets.reshape(tokens_here, 2) - my_rank * vocab_here).reshape(
@@ -428,15 +757,27 @@
             loss_weights.reshape(head_tiles, head_rows_count, 2),
         ),
     )
-    grad_head = over_tensor(grad_head.reshape(tokens_here, model_width))
-    grad_two, gain_grad_three = norm_backward(stream_two, inverse_three, norm_gains[2], grad_head)
-    gate_flat = gate_values.T.reshape(-1)
-    slot_scale = jnp.take(gate_flat, jnp.minimum(slot_source, 2 * tokens_here - 1)) * slot_full
+    grad_two_low, grad_two, gain_grad_three = sum_line(
+        grad_head.reshape(tokens_here, model_width),
+        [stream_two, gain_rows[2]],
+        [stream_shape, gain_shape],
+        finish_head_grad,
+        4,
+        prologue=clear_gain,
+    )
+    slot_scale = jnp.sum(
+        jnp.where(hits[0], gate_values[:, 0][None, :], 0.0)
+        + jnp.where(hits[1], gate_values[:, 1][None, :], 0.0),
+        1,
+    )
+    slot_grads = jnp.dot(both_low, grad_two_low, preferred_element_type=jnp.float32)
     grad_dispatch = (
-        (jnp.take(grad_two, slot_token, axis=0) * slot_scale[:, None])
+        (slot_grads * slot_scale[:, None])
         .astype(jnp.bfloat16)
         .reshape(owners, experts_here * capacity, model_width)
     )
+    slot_dots = jnp.sum(slot_grads * returned.astype(jnp.float32), 1)
+    gate_part = jnp.stack([jnp.sum(jnp.where(hit, slot_dots[:, None], 0.0), 0) for hit in hits])
     grad_arrived = to_experts(grad_dispatch).reshape(owners, experts_here, capacity, model_width)
     grad_active = jnp.einsum(
         "oecd,efd->oecf", grad_arrived, outer_low, preferred_element_type=jnp.float32
@@ -455,26 +796,35 @@
     grad_returned = from_experts(
         grad_back.reshape(owners, experts_here * capacity, model_width)
     ).reshape(experts * capacity, model_width)
-    grad_pairs = (
-        jnp.take(grad_returned, pair_dest, axis=0).astype(jnp.float32) * kept_rows[:, None]
-    ).reshape(2, tokens_here, model_width)
-    gate_partial = jnp.sum(pair_rows * grad_two[None], 2).T
-    moe_input_grad, gate_grad = over_tensor((grad_pairs[0] + grad_pairs[1], gate_partial))
-    chosen_grad = gate_values * (gate_grad - jnp.sum(gate_values * gate_grad, 1, keepdims=True))
-    logit_grad = jnp.einsum(
-        "tk,tke->te", chosen_grad, route_onehot, precision=highest_precision
-    ).astype(jnp.bfloat16)
+    moe_grad_part = lax.dot_general(
+        both_low, grad_returned, (((0,), (0,)), ((), ())), preferred_element_type=jnp.float32
+    )
+    gate_block = pltpu.VMEM((3, 2, tokens_here), jnp.float32)
+    grad_one_low, grad_one, logit_grad, gain_grad_two = sum_line(
+        moe_grad_part,
+        [
+            stream_one,
+            gain_rows[1],
+            grad_two,
+            gate_part,
+            gate_values.T,
+            route_pairs.T,
+            router_low,
+        ],
+        [
+            stream_shape,
+            jax.ShapeDtypeStruct((experts, tokens_here), jnp.bfloat16),
+            gain_shape,
+        ],
+        finish_expert_grad,
+        5,
+        prologue=start_router_grad,
+        scratch=(gate_block, pltpu.SemaphoreType.DMA((3,)), pltpu.SemaphoreType.DMA((3,))),
+        meets_all=True,
+    )
     router_grad = lax.dot_general(
-        normed_two_low, logit_grad, (((0,), (0,)), ((), ())), preferred_element_type=jnp.float32
-    )
-    normed_two_grad = moe_input_grad + lax.dot_general(
-        logit_grad, router_low, (((1,), (1,)), ((), ())), preferred_element_type=jnp.float32
-    )
-    grad_one_part, gain_grad_two = norm_backward(
-        stream_one, inverse_two, norm_gains[1], normed_two_grad
-    )
-    grad_one = grad_two + grad_one_part
-    grad_one_low = grad_one.astype(jnp.bfloat16)
+        normed_two_low, logit_grad, (((0,), (1,)), ((), ())), preferred_element_type=jnp.float32
+    )
     project_grad = lax.dot_general(
         attended_flat, grad_one_low, (((0,), (0,)), ((), ())), preferred_element_type=jnp.float32
     )
@@ -534,30 +884,38 @@
     joint_weight_grad = lax.dot_general(
         joint_grad, normed_one_low, (((0,), (0,)), ((), ())), preferred_element_type=jnp.float32
     )
-    normed_one_grad = over_tensor(
-        jnp.dot(joint_grad, joint_low, preferred_element_type=jnp.float32)
-    )
-    grad_zero_part, gain_grad_one = norm_backward(
-        stream_zero, inverse_one, norm_gains[0], normed_one_grad
-    )
-    grad_zero = grad_one + grad_zero_part
-    table_grad = table_grad + jax.ops.segment_sum(
-        grad_zero * (embed_scale * inside)[:, None], clipped_ids, num_segments=vocab_here
-    )
-    unit_grads = jnp.concatenate([table_grad, joint_weight_grad, project_grad], 0).reshape(
-        -1, unit_rows, model_width
-    )
+    zero_grad_low, gain_grad_one = sum_line(
+        jnp.dot(joint_grad, joint_low, preferred_element_type=jnp.float32),
+        [embedded, gain_rows[0], grad_one],
+        [gain_shape],
+        functools.partial(finish_input_grad, embed_scale),
+        6,
+        prologue=clear_gain,
+    )
+    onehot_ids = (
+        (lax.broadcasted_iota(jnp.int32, (vocab_here, tokens_here), 0) == local_ids[None, :])
+    ).astype(jnp.bfloat16)
+    table_grad = table_grad + jnp.dot(
+        onehot_ids, zero_grad_low, preferred_element_type=jnp.float32
+    )
+    unit_grads = jnp.concatenate(
+        [
+            table_grad,
+            joint_weight_grad,
+            project_grad,
+        ],
+        0,
+    ).reshape(-1, unit_rows, model_width)
     my_units = jnp.take(slot_unit, my_owner, axis=0)
-    my_filled = jnp.take(slot_filled, my_owner, axis=0).astype(jnp.float32)[:, None, None]
-    outgoing = (
-        jnp.take(unit_grads, slot_unit.reshape(-1), axis=0)
-        * slot_filled.reshape(-1).astype(jnp.float32)[:, None, None]
-    )
-    mine = lax.psum_scatter(outgoing, ("dp", "ctx"), scatter_dimension=0, tiled=True) * my_filled
-    gains_grad, router_grad, bias_grad = lax.psum(
-        (jnp.stack([gain_grad_one, gain_grad_two, gain_grad_three]), router_grad, bias_grad),
-        ("dp", "ctx"),
-    )
+    my_filled = jnp.take(slot_filled, my_owner, axis=0)[:, None, None]
+    outgoing = pull_units(unit_grads, slot_unit.reshape(-1))
+    summed = lax.psum_scatter(outgoing, ("dp", "ctx"), scatter_dimension=0, tiled=True)
+    mine = jnp.where(my_filled, summed, 0.0)
+    gains_grad = lax.psum(
+        jnp.concatenate([gain_grad_one, gain_grad_two, gain_grad_three], 0),
+        ("dp", "ctx", "tensor"),
+    )
+    router_grad, bias_grad = lax.psum((router_grad, bias_grad), ("dp", "ctx"))
     slot_rates = unit_rates(my_units, table_units, query_units, value_units)[:, None, None]
     master_new, master_first_new, master_second_new = adam_update(
         master[0, 0], master_first[0, 0], master_second[0, 0], mine, slot_rates, decay_rate

time: 1850 us -> 1340 us (0.72)
  waiting for transfers between devices: 852 us -> 130 us
  Pallas kernels: 0 us -> 372 us
  local copies, waits for them, and re-layouts: 275 us -> 156 us
  other arithmetic: 226 us -> 132 us
  matrix products: 237 us -> 298 us
    psum x6 -> x0, waiting for transfers between devices: 662 us -> none  [over_tensor(): return lax.psum(partial_sums, 'tensor')]
    pallas_call x0 -> x8, Pallas kernels: none -> 372 us  [the longest x5 311 us: sum_line(): pl.pallas_call(functools.partial(sum_line_kernel, count, meets_all, prolo...]
    gather x8 -> x1, local copies, waits for them, and re-layouts: 103 us -> 10.5 us  [on_device(): jnp.take(table_low, clipped_ids, axis=0)]
    dot_general x4 -> x8, matrix products: 14.9 us -> 64.5 us  [the longest x1 23.4 us: on_device(): jnp.dot(onehot_ids, zero_grad_low, preferred_element_type=jnp.float32)]
    all_gather x1, waiting for transfers between devices: 90.1 us -> 42.9 us  [on_device(): lax.all_gather(master[0, 0].astype(jnp.bfloat16), ('dp', 'ctx'), axis=0,...]
    all_to_all x1 -> x0, blocking collectives: 45.3 us -> none  [from_experts(): lax.all_to_all(buffer, ('dp', 'ctx'), split_axis=0, concat_axis=0, tiled=...]
    reduce_scatter x1, waiting for transfers between devices: 58.4 us -> 20.1 us  [on_device(): lax.psum_scatter(outgoing, ('dp', 'ctx'), scatter_dimension=0, tiled=True)]
    psum x2, blocking collectives: 35.5 us -> 67.7 us  [the longest x1 38.6 us: on_device(): lax.psum(jnp.concatenate([gain_grad_one, gain_grad_two, gain_grad_three],...]
  transfers between devices with their start and end apart: 11 -> 9, of which waited for: 9 -> 5; matrix products, arithmetic and copies ran while one was open for 11% -> 15% of each run, Pallas kernels for 0% -> 4%
where the time goes in v1:
time: 1340 us; the launch traced here: 1330 us
  Pallas kernels  372 us (28%)
  matrix products  298 us (22%)
  blocking collectives  209 us (16%)
  local copies, waits for them, and re-layouts  156 us (12%)
  other arithmetic  132 us (10%)
  waiting for transfers between devices  130 us (10%)
  starting transfers between devices  18.2 us (1%)
  between operations  17 us (1%)
    pallas_call x5, Pallas kernels, sum_line(): pl.pallas_call(functools.partial(sum_line_kernel, count, meets_all, prolo...  311 us
    unnamed x268, local copies, waits for them, and re-layouts  90.9 us
    all_to_all x2, blocking collectives, to_experts(): lax.all_to_all(buffer, ('dp', 'ctx'), split_axis=0, concat_axis=0, tiled=...  89.6 us
    all_to_all x2, waiting for transfers between devices, from_experts(): lax.all_to_all(buffer, ('dp', 'ctx'), split_axis=0, concat_axis=0, tiled=...  67 us
    all_gather x1, waiting for transfers between devices, on_device(): lax.all_gather(master[0, 0].astype(jnp.bfloat16), ('dp', 'ctx'), axis=0,...  42.9 us
    all_gather x3, blocking collectives, combined_all(): everything = jax.tree.map(lambda part: lax.all_gather(part, axis), x)  39.4 us
    add x4, local copies, waits for them, and re-layouts, tile_scores(): scores.reshape(head_count, row_count // BLOCK, BLOCK, column_count // BLO...  38.9 us
    psum x1, blocking collectives, on_device(): lax.psum(jnp.concatenate([gain_grad_one, gain_grad_two, gain_grad_three],...  38.6 us
  transfers between devices with their start and end apart: 9, of which 5 were waited for; matrix products, arithmetic and copies ran while one was open for 15% of the time, Pallas kernels for 4%

profile of v1, /device:TPU:0, one launch (start us, length us, event | category | flops | bytes accessed | tf_op | source)
XLA Modules:
  0.0 1333.0 jit_solution(871131205928111611)
XLA Ops:
  59.8 42.9 %all-gather.4.cloned.1.call-done.source_ref = bf16[168,64,768]{2,1,0:T(8,128)(2,1)} async-done(((bf16[21,64,768]{2,1,0:T(8,128)(2,1)}), bf16[168,64,768]{2,1,0:T(8,128)(2,1)}) %all-gather.4.cloned.1.call-update) | async-done | bytes 16515088 | tf_op jit(solution)/shard_map/all_gather | solution.py:565
  131.7 54.7 %shard_map.385.refs_0_ = bf16[1024,768]{1,0:T(8,128)(2,1)S(1)} custom-call(bf16[1024,768]{1,0:T(8,128)(2,1)S(1)} %select_select_fusion.part_ref), custom_call_target="tpu_custom_call" | custom-call | tf_op jit(solution)/shard_map/pallas_call | solution.py:172
  246.5 29.1 %shard_map.386 = bf16[4,192,1024]{2,1,0:T(8,128)(2,1)S(1)} custom-call(bf16[192,1024]{1,0:T(8,128)(2,1)S(1)} %bitcast.406), custom_call_target="tpu_custom_call" | custom-call | tf_op jit(solution)/shard_map/pallas_call | solution.py:326
  284.4 44.7 %all_to_all.20 = bf16[8,288,768]{2,1,0:T(8,128)(2,1)S(1)} all-to-all(bf16[8,288,768]{2,1,0:T(8,128)(2,1)S(1)} %bitcast.436), channel_id=1, replica_groups=mesh['dp'=4,'ctx'=2,'tensor'=4] {'dp','ctx'}, dimensions={0} | all-to-all | bytes 7077888 | tf_op jit(solution)/shard_map/all_to_all | solution.py:440
  363.6 25.9 %all-to-all-done.1 = bf16[8,288,768]{2,1,0:T(8,128)(2,1)} async-done(((bf16[8,288,768]{2,1,0:T(8,128)(2,1)}), bf16[8,288,768]{2,1,0:T(8,128)(2,1)}, u32[]{:S(2)}, u32[]{:S(2)}) %all-to-all-start.1) | async-done | bytes 3538976 | tf_op jit(solution)/shard_map/all_to_all | solution.py:444
  404.0 62.4 %shard_map.387 = (bf16[1024,768]{1,0:T(8,128)(2,1)S(1)}, f32[1024,768]{1,0:T(8,128)S(1)}) custom-call(f32[1024,768]{1,0:T(8,128)} %multiply_add_fusion.1.part_ref, f32[1024,768]{1,0:T(8,128)} %copy-done.11, f32[1,768]{1,0:T(1,128)S(1)} %get-tuple-element.628.refs_1_), custom_call_target="tpu_custom_call" | custom-call | tf_op jit(solution)/shard_map/pallas_call | solution.py:172
  468.1 31.0 %while.64 = (s32[]{:T(128)}, f32[2,512]{1,0:T(2,128)S(1)}, f32[2,512]{1,0:T(2,128)S(1)}, f32[2,512,2]{1,2,0:T(2,128)S(1)}, bf16[2,512,768]{2,1,0:T(8,128)(2,1)S(...) while((s32[]{:T(128)}, f32[2,512]{1,0:T(2,128)S(1)}, ...), condition=%wide.region_15.16_spmd.clone.clone, body=%wide.region_10.15_spmd.clone.clone.sunk | while | flops 6328318976 | bytes 45889656 | solution.py:710
  554.0 94.1 %while.65 = (s32[]{:T(128)}, f32[8000,768]{1,0:T(8,128)}, f32[2,512,768]{2,1,0:T(8,128)}, f32[2,512,2]{1,2,0:T(2,128)S(1)}, bf16[2,512,768]{2,1,0:T(8,128)(2,1)S...) while((s32[]{:T(128)}, f32[8000,768]{1,0:T(8,128)}, ...), condition=%wide.region_25.26_spmd.clone.clone, body=%wide.region_23.25_spmd.clone.clone.sunk | while | flops 18927616000 | bytes 134269104 | solution.py:750
  625.5 22.7 %select_add_fusion.2 = f32[8000,768]{1,0:T(8,128)} fusion(f32[8000,768]{1,0:T(8,128)} %get-tuple-element.897, bf16[512,8000]{0,1:T(8,128)(2,1)} %copy-done.8, pred[]{:T(512)S(6)} %compare.5, bf16[2,512,768]{2,1,0:T(8,128)(2,1)S(1)} %get-tuple-element.911, s32[]{:T(128)S(6)} %copy.151), kind=kOutput, calls=%fused_computation.21.clone.1 | convolution fusion | flops 6303744000 | bytes 58130436 | tf_op jit(solution)/shard_map/while/body/eval_jaxpr/dot_general | solution.py:745
  648.2 58.3 %shard_map.388 = (bf16[1024,768]{1,0:T(8,128)(2,1)S(1)}, f32[1024,768]{1,0:T(8,128)S(1)}, f32[1,768]{1,0:T(1,128)S(1)}) custom-call(f32[1024,768]{1,0:T(8,128)} %bitcast.57.part_ref, f32[1024,768]{1,0:T(8,128)} %copy-done.4, f32[1,768]{1,0:T(1,128)S(1)} %get-tuple-element.628.refs_1_), custom_call_target="tpu_custom_call" | custom-call | tf_op jit(solution)/shard_map/pallas_call | solution.py:172
  724.6 44.9 %all_to_all.21 = bf16[8,288,768]{2,1,0:T(8,128)(2,1)S(1)} all-to-all(bf16[8,288,768]{2,1,0:T(8,128)(2,1)S(1)} %bitcast.428), channel_id=1, replica_groups=mesh['dp'=4,'ctx'=2,'tensor'=4] {'dp','ctx'}, dimensions={0} | all-to-all | bytes 7077888 | tf_op jit(solution)/shard_map/all_to_all | solution.py:440
  788.2 41.1 %all-to-all-done.3 = bf16[8,288,768]{2,1,0:T(8,128)(2,1)} async-done(((bf16[8,288,768]{2,1,0:T(8,128)(2,1)}), bf16[8,288,768]{2,1,0:T(8,128)(2,1)}, u32[]{:S(2)}, u32[]{:S(2)}) %all-to-all-start.3) | async-done | bytes 3538976 | tf_op jit(solution)/shard_map/all_to_all | solution.py:444
  837.9 77.2 %shard_map.389 = (bf16[1024,768]{1,0:T(8,128)(2,1)S(1)}, f32[1024,768]{1,0:T(8,128)S(1)}, bf16[8,1024]{1,0:T(8,128)(2,1)S(1)}, f32[1,768]{1,0:T(1,128)S(1)}) custom-call(f32[1024,768]{1,0:T(8,128)} %fusion.149.part_ref, f32[1024,768]{1,0:T(8,128)} %copy-done.11, f32[1,768]{1,0:T(1,128)S(1)} %get-tuple-element.627.refs_1_, f32[1024,768]{1,0:T(8,128)} %copy-done.6, ...), custom_call_target="tpu_custom_call" | custom-call | tf_op jit(solution)/shard_map/pallas_call | solution.py:172
  975.1 58.8 %shard_map.390 = (bf16[1024,768]{1,0:T(8,128)(2,1)S(1)}, f32[1,768]{1,0:T(1,128)S(1)}) custom-call(f32[1024,768]{1,0:T(8,128)} %fusion.113.part_ref, bf16[1024,768]{1,0:T(8,128)(2,1)S(1)} %copy-done.1, f32[1,768]{1,0:T(1,128)S(1)} %get-tuple-element.626.refs_1_, f32[1024,768]{1,0:T(8,128)} %copy-done.5), custom_call_target="tpu_custom_call" | custom-call | tf_op jit(solution)/shard_map/pallas_call | solution.py:172
  1033.9 23.4 %fusion.17 = f32[8000,768]{1,0:T(8,128)} fusion(f32[8000,768]{1,0:T(8,128)} %get-tuple-element.396, bf16[1024,768]{1,0:T(8,128)(2,1)S(1)} %get-tuple-element.403, s32[1024]{0:T(1024)S(1)} %bitcast.475), kind=kOutput, calls=%fused_computation.39 | convolution fusion | flops 12597248000 | bytes 50728960 | tf_op jit(solution)/shard_map/dot_general | solution.py:898
  1057.3 23.7 %pad_maximum_fusion = f32[8768,768]{1,0:T(8,128)} fusion(f32[192,768]{1,0:T(8,128)S(1)} %fusion.173, f32[576,768]{1,0:T(8,128)S(1)} %fusion.112, f32[8000,768]{1,0:T(8,128)} %fusion.17), kind=kLoop, calls=%fused_computation.36 | loop fusion | flops 13467648 | bytes 53870592 | tf_op jit(solution)/shard_map/concatenate | solution.py:901
  1081.0 25.4 %shard_map.391 = f32[168,64,768]{2,1,0:T(8,128)} custom-call(s32[168]{0:T(256)S(1)} %reshape.668.slots_ref, f32[137,64,768]{2,1,0:T(8,128)} %bitcast.417), custom_call_target="tpu_custom_call" | custom-call | tf_op jit(solution)/shard_map/pallas_call | solution.py:357
  1108.0 17.8 %copy.99 = f32[192,8,8,256]{3,2,1,0:T(8,128)} copy(f32[192,8,8,256]{3,1,2,0:T(8,128)} %bitcast.426) | data formatting | bytes 25165824
  1125.8 20.4 %copy.97 = f32[192,8,8,256]{3,2,1,0:T(8,128)} copy(f32[192,8,8,256]{3,1,2,0:T(8,128)} %bitcast.427) | data formatting | bytes 25165824
  1171.1 15.8 %copy.98 = f32[192,8,8,256]{3,2,1,0:T(8,128)} copy(f32[192,8,8,256]{3,1,2,0:T(8,128)} %bitcast.415) | data formatting | bytes 25165824
  1186.9 16.0 %copy.100 = f32[192,8,8,256]{3,2,1,0:T(8,128)} copy(f32[192,8,8,256]{3,1,2,0:T(8,128)} %bitcast.416) | data formatting | bytes 25165824
  1225.9 29.0 %all-reduce = (f32[768,8]{0,1:T(8,128)S(1)}, f32[3,8]{1,0:T(4,128)S(1)}) all-reduce(f32[768,8]{0,1:T(8,128)S(1)} %fusion.174, f32[3,8]{1,0:T(4,128)S(1)} %fusion.104), channel_id=1, replica_groups=mesh['dp'=4,'ctx'=2,'tensor'=4] {'dp','ctx'}, use_global_device_ids=true, to_apply=%region_34.35 | all-reduce | flops 6168 | bytes 49344 | tf_op jit(solution)/shard_map/psum | solution.py:918
  1256.2 38.6 %psum.29 = f32[3,768]{1,0:T(4,128)S(1)} all-reduce(f32[3,768]{1,0:T(4,128)S(1)} %pad_maximum_fusion.8), channel_id=1, replica_groups=mesh['dp'=4,'ctx'=2,'tensor'=4] {'dp','ctx','tensor'}, use_global_device_ids=true, to_apply=%region_33.34 | all-reduce | flops 2304 | bytes 18432 | tf_op jit(solution)/shard_map/psum | solution.py:914
  1295.5 20.1 %reduce-scatter.2.cloned.1.call-done = f32[21,64,768]{2,1,0:T(8,128)} async-done(((f32[168,64,768]{2,1,0:T(8,128)}), f32[21,64,768]{2,1,0:T(8,128)}) %reduce-scatter.2.cloned.1.call-update) | async-done | bytes 4128784 | tf_op jit(solution)/shard_map/reduce_scatter | solution.py:912
  (467 shorter events, 522.7 us)
Async XLA Ops:
  7.2 95.4 %all-gather.4.cloned.1.call-start = ((), (), s32[]{:S(2)}) async-start(), calls=%async_computation.5 | async-start | bytes 18579456 | tf_op jit(solution)/shard_map/all_gather | solution.py:565
  59.7 329.8 %copy-start.85 = (s32[1024]{0:T(1024)}, s32[1024]{0:T(1024)S(1)}, u32[]{:S(2)}) copy-start(s32[1024]{0:T(1024)S(1)} %get-tuple-element.631) | copy-start | bytes 12292
  59.7 336.2 %copy-start.87 = (s32[1024]{0:T(1024)}, s32[1024]{0:T(1024)S(1)}, u32[]{:S(2)}) copy-start(s32[1024]{0:T(1024)S(1)} %get-tuple-element.632) | copy-start | bytes 12292
  59.8 127.1 %copy-start.83 = (f32[768]{0:T(1024)}, f32[768]{0:T(1024)S(1)}, u32[]{:S(2)}) copy-start(f32[768]{0:T(1024)S(1)} %get-tuple-element.528) | copy-start | bytes 9220
  108.3 84.0 %copy-start.23 = (bf16[3,64,768]{2,1,0:T(8,128)(2,1)}, bf16[3,64,768]{2,1,0:T(8,128)(2,1)S(1)}, u32[]{:S(2)}) copy-start(bf16[3,64,768]{2,1,0:T(8,128)(2,1)S(1)} %slice.209) | copy-start | bytes 884740
  108.3 82.8 %collective-permute-start.3 = (bf16[192,768]{1,0:T(8,128)(2,1)S(1)}, bf16[192,768]{1,0:T(8,128)(2,1)S(1)}, u32[]{:S(2)}, u32[]{:S(2)}) collective-permute-start(bf16[192,768]{1,0:T(8,128)(2,1)S(1)} %bitcast.438), channel_id=1, source_target_pairs={{0,1},{1,2},{2,3},{3,0},{4,5},{5,6},{6,7},{7,4},{8,9},{9,10},{10,1... | collective-permute-start | bytes 884744 | tf_op jit(solution)/shard_map/ppermute | solution.py:571
  109.8 81.3 %collective-permute-start.2 = (bf16[192,768]{1,0:T(8,128)(2,1)S(1)}, bf16[192,768]{1,0:T(8,128)(2,1)S(1)}, u32[]{:S(2)}, u32[]{:S(2)}) collective-permute-start(bf16[192,768]{1,0:T(8,128)(2,1)S(1)} %bitcast.439), channel_id=1, source_target_pairs={{0,2},{1,3},{2,0},{3,1},{4,6},{5,7},{6,4},{7,5},{8,10},{9,11},{10,... | collective-permute-start | bytes 884744 | tf_op jit(solution)/shard_map/ppermute | solution.py:571
  112.3 77.9 %collective-permute-start.1 = (bf16[192,768]{1,0:T(8,128)(2,1)S(1)}, bf16[192,768]{1,0:T(8,128)(2,1)}, u32[]{:S(2)}, u32[]{:S(2)}) collective-permute-start(bf16[192,768]{1,0:T(8,128)(2,1)S(1)} %bitcast.440), channel_id=1, source_target_pairs={{0,3},{1,0},{2,1},{3,2},{4,7},{5,4},{6,5},{7,6},{8,11},{9,8},{10,9... | collective-permute-start | bytes 884744 | tf_op jit(solution)/shard_map/ppermute | solution.py:571
  186.4 89.2 %copy-start = (bf16[1024,768]{1,0:T(8,128)(2,1)}, bf16[1024,768]{1,0:T(8,128)(2,1)S(1)}, u32[]{:S(2)}) copy-start(bf16[1024,768]{1,0:T(8,128)(2,1)S(1)} %shard_map.385.refs_0_) | copy-start | bytes 4718596
  188.4 3.9 collective-permute-start
  342.6 46.9 %all-to-all-start.1 = ((bf16[8,288,768]{2,1,0:T(8,128)(2,1)}), bf16[8,288,768]{2,1,0:T(8,128)(2,1)}, u32[]{:S(2)}, u32[]{:S(2)}) async-start(bf16[8,288,768]{2,1,0:T(8,128)(2,1)} %fusion.77), calls=%async_computation.1 | async-start | bytes 7077888 | tf_op jit(solution)/shard_map/all_to_all | solution.py:444
  648.2 58.4 %copy-start.103 = (pred[1024]{0:T(1024)(128)(4,1)S(1)}, pred[1024]{0:T(1024)(128)(4,1)}, u32[]{:S(2)}) copy-start(pred[1024]{0:T(1024)(128)(4,1)} %get-tuple-element.633) | copy-start | bytes 3076
  648.2 58.4 %copy-start.105 = (pred[1024]{0:T(1024)(128)(4,1)S(1)}, pred[1024]{0:T(1024)(128)(4,1)}, u32[]{:S(2)}) copy-start(pred[1024]{0:T(1024)(128)(4,1)} %get-tuple-element.634) | copy-start | bytes 3076
  648.2 121.3 %slice-start.6 = ((s8[7077888]{0:T(1024)(128)(4,1)}), s8[4194304]{0:T(1024)(128)(4,1)S(1)}, s32[]{:S(2)}) async-start(s8[7077888]{0:T(1024)(128)(4,1)} %bitcast.490), calls=%async_computation.13 | async-start | bytes 8388608
  706.6 62.9 %slice-start.7 = ((s8[7077888]{0:T(1024)(128)(4,1)}), s8[2883584]{0:T(1024)(128)(4,1)S(1)}, s32[]{:S(2)}) async-start(s8[7077888]{0:T(1024)(128)(4,1)} %bitcast.490), calls=%async_computation.14 | async-start | bytes 5767168
  782.5 46.7 %all-to-all-start.3 = ((bf16[8,288,768]{2,1,0:T(8,128)(2,1)}), bf16[8,288,768]{2,1,0:T(8,128)(2,1)}, u32[]{:S(2)}, u32[]{:S(2)}) async-start(bf16[8,288,768]{2,1,0:T(8,128)(2,1)} %fusion.80), calls=%async_computation.3 | async-start | bytes 7077888 | tf_op jit(solution)/shard_map/all_to_all | solution.py:444
  787.1 528.4 %reduce-scatter.2.cloned.1.call-start = ((), (), s32[]{:S(2)}) async-start(), calls=%async_computation.6 | async-start | bytes 37158912 | tf_op jit(solution)/shard_map/reduce_scatter | solution.py:912
  837.9 77.2 %copy-start.24 = (bf16[3,64,768]{2,1,0:T(8,128)(2,1)S(1)}, bf16[3,64,768]{2,1,0:T(8,128)(2,1)}, u32[]{:S(2)}) copy-start(bf16[3,64,768]{2,1,0:T(8,128)(2,1)} %copy-done.23) | copy-start | bytes 884740
  837.9 77.9 %copy-start.18 = (bf16[2048,3,64]{0,2,1:T(8,128)(2,1)S(1)}, bf16[2048,3,64]{0,2,1:T(8,128)(2,1)}, u32[]{:S(2)}) copy-start(bf16[2048,3,64]{0,2,1:T(8,128)(2,1)} %copy-done.17) | copy-start | bytes 2359300
  965.6 4.3 collective-permute-start.4
  975.1 58.8 %copy-start.52 = (s32[1,1024]{1,0:T(1,128)S(1)}, s32[1,1024]{1,0:T(1,128)}, u32[]{:S(2)}) copy-start(s32[1,1024]{1,0:T(1,128)} %copy-done.51) | copy-start | bytes 12292
  1220.0 74.8 %copy-start.48 = (f32[3,768]{1,0:T(4,128)S(1)}, f32[3,768]{1,0:T(4,128)}, u32[]{:S(2)}) copy-start(f32[3,768]{1,0:T(4,128)} %param.46) | copy-start | bytes 27652
  1220.0 74.8 %copy-start.70 = (f32[3,768]{1,0:T(4,128)S(1)}, f32[3,768]{1,0:T(4,128)}, u32[]{:S(2)}) copy-start(f32[3,768]{1,0:T(4,128)} %param.47) | copy-start | bytes 27652
  1220.0 74.8 %copy-start.71 = (f32[3,768]{1,0:T(4,128)S(1)}, f32[3,768]{1,0:T(4,128)}, u32[]{:S(2)}) copy-start(f32[3,768]{1,0:T(4,128)} %param.48) | copy-start | bytes 27652
  (112 other events, 1572.9 us)
Sparse Core Ops, SparseCore 0:
  11.1 91.4 all-gather.3
  1106.6 208.8 reduce-scatter.1

commit v2 on v1

--- a/solution.py
+++ b/solution.py
@@ -365,14 +365,455 @@
     )(slots, source)
 
 
-def combined_all(x, axis, combine):
-    everything = jax.tree.map(lambda part: lax.all_gather(part, axis), x)
-    initial = jax.tree.map(lambda part: part[0], everything)
-
-    def lap(k, so_far):
-        return combine(so_far, jax.tree.map(lambda part: part[k], everything))
-
-    return lax.fori_loop(1, lax.axis_size(axis), lap, initial)
+def attention_kernel(heads, size, bias_ref, own_ref, before_ref, out_ref, logsum_ref, scores, peak, total):
+    tokens = own_ref.shape[1]
+    blocks = tokens // BLOCK
+    hidden = heads * size
+    later = lax.axis_index("ctx") > 0
+
+    for head in range(heads):
+        query = own_ref[head * size : (head + 1) * size, :].astype(jnp.float32).T * size**-0.5
+        query = query.astype(jnp.bfloat16)
+        own_keys = own_ref[hidden + head * size : hidden + (head + 1) * size, :]
+        old_keys = before_ref[head * size : (head + 1) * size, :]
+        own_values = own_ref[2 * hidden + head * size : 2 * hidden + (head + 1) * size, :]
+        own_values = own_values.astype(jnp.float32).T.astype(jnp.bfloat16)
+        old_values = before_ref[hidden + head * size : hidden + (head + 1) * size, :]
+        old_values = old_values.astype(jnp.float32).T.astype(jnp.bfloat16)
+        for block in range(blocks):
+            rows = query[block * BLOCK : (block + 1) * BLOCK]
+            width = (block + 1) * BLOCK
+            mine = jnp.dot(rows, own_keys[:, :width], preferred_element_type=jnp.float32)
+            top = None
+            parts = []
+            for k in range(block + 1):
+                part = mine[:, k * BLOCK : (k + 1) * BLOCK] + bias_ref[head, block - k]
+                parts.append(part)
+                high = jnp.max(part, 1, keepdims=True)
+                top = high if top is None else jnp.maximum(top, high)
+            peak[...] = top
+
+            @pl.when(later)
+            def _():
+                old = jnp.dot(rows, old_keys, preferred_element_type=jnp.float32)
+                top_old = None
+                for k in range(blocks):
+                    part = old[:, k * BLOCK : (k + 1) * BLOCK] + bias_ref[head, block + blocks - k]
+                    scores[:, k * BLOCK : (k + 1) * BLOCK] = part
+                    high = jnp.max(part, 1, keepdims=True)
+                    top_old = high if top_old is None else jnp.maximum(top_old, high)
+                peak[...] = jnp.maximum(peak[...], top_old)
+
+            top = peak[...]
+            parts = [jnp.exp(part - top) for part in parts]
+            own_sum = None
+            for part in parts:
+                part_sum = jnp.sum(part, 1, keepdims=True)
+                own_sum = part_sum if own_sum is None else own_sum + part_sum
+            total[...] = own_sum
+
+            @pl.when(later)
+            def _():
+                old_exp = jnp.exp(scores[...] - top)
+                scores[...] = old_exp
+                total[...] += jnp.sum(old_exp, 1, keepdims=True)
+
+            full = total[...]
+            inverse = 1.0 / full
+            low = jnp.concatenate([(part * inverse).astype(jnp.bfloat16) for part in parts], 1)
+            result = jnp.dot(low, own_values[:width], preferred_element_type=jnp.float32)
+            peak[...] = top + jnp.log(full)
+            logsum_ref[head, block * BLOCK : (block + 1) * BLOCK, :] = peak[...]
+            place = (slice(head * size, (head + 1) * size), slice(block * BLOCK, (block + 1) * BLOCK))
+
+            @pl.when(later)
+            def _():
+                low_old = (scores[...] * inverse).astype(jnp.bfloat16)
+                both = result + jnp.dot(low_old, old_values, preferred_element_type=jnp.float32)
+                out_ref[place] = both.T.astype(jnp.bfloat16)
+
+            @pl.when(jnp.logical_not(later))
+            def _():
+                out_ref[place] = result.T.astype(jnp.bfloat16)
+
+
+def attention(biases, own, before, heads, size):
+    tokens = own.shape[1]
+    return pl.pallas_call(
+        functools.partial(attention_kernel, heads, size),
+        out_shape=[
+            jax.ShapeDtypeStruct((heads * size, tokens), jnp.bfloat16),
+            jax.ShapeDtypeStruct((heads, tokens, 1), jnp.float32),
+        ],
+        in_specs=[pl.BlockSpec(memory_space=pltpu.SMEM), whole_vmem, whole_vmem],
+        out_specs=[whole_vmem, whole_vmem],
+        scratch_shapes=[
+            pltpu.VMEM((BLOCK, tokens), jnp.float32),
+            pltpu.VMEM((BLOCK, 1), jnp.float32),
+            pltpu.VMEM((BLOCK, 1), jnp.float32),
+        ],
+        compiler_params=pltpu.CompilerParams(vmem_limit_bytes=40 << 20),
+    )(biases, own, before)
+
+
+def attention_back_kernel(
+    heads, size, bias_ref, own_ref, before_ref, logsum_ref, grad_ref, project_ref,
+    query_out, own_out, before_out, bias_out, probs, slopes, inner, query_sum, own_sum, before_sum,
+):
+    tokens = own_ref.shape[1]
+    blocks = tokens // BLOCK
+    hidden = heads * size
+    later = lax.axis_index("ctx") > 0
+    bias_out[...] = jnp.zeros_like(bias_out)
+
+    def flipped(rows):
+        return rows.astype(jnp.float32).T.astype(jnp.bfloat16)
+
+    for head in range(heads):
+        span = slice(head * size, (head + 1) * size)
+        value_span = slice(hidden + head * size, hidden + (head + 1) * size)
+        query_rows = own_ref[span, :]
+        query = flipped(query_rows) * jnp.bfloat16(size**-0.5)
+        own_keys = own_ref[hidden + head * size : hidden + (head + 1) * size, :]
+        own_values = own_ref[2 * hidden + head * size : 2 * hidden + (head + 1) * size, :]
+        old_keys = before_ref[span, :]
+        old_values = before_ref[value_span, :]
+        own_keys_flip = flipped(own_keys)
+        grad = lax.dot_general(
+            grad_ref[...], project_ref[span, :], (((1,), (1,)), ((), ())), preferred_element_type=jnp.float32
+        )
+        grad_rows = grad.T.astype(jnp.bfloat16)
+        grad = grad.astype(jnp.bfloat16)
+        own_sum[...] = jnp.zeros_like(own_sum)
+
+        @pl.when(later)
+        def _():
+            before_sum[...] = jnp.zeros_like(before_sum)
+
+        for block in range(blocks):
+            at = slice(block * BLOCK, (block + 1) * BLOCK)
+            width = (block + 1) * BLOCK
+            rows, up = query[at], grad[at]
+            lse = logsum_ref[head, at, :]
+            score = jnp.dot(rows, own_keys[:, :width], preferred_element_type=jnp.float32)
+            prob = jnp.concatenate(
+                [
+                    jnp.exp(score[:, k * BLOCK : (k + 1) * BLOCK] + (bias_ref[head, block - k] - lse))
+                    for k in range(block + 1)
+                ],
+                1,
+            )
+            slope = jnp.dot(up, own_values[:, :width], preferred_element_type=jnp.float32)
+            inner[...] = jnp.sum(prob * slope, 1, keepdims=True)
+
+            @pl.when(later)
+            def _():
+                score = jnp.dot(rows, old_keys, preferred_element_type=jnp.float32)
+                old_slope = jnp.dot(up, old_values, preferred_element_type=jnp.float32)
+                old_prob = jnp.concatenate(
+                    [
+                        jnp.exp(
+                            score[:, k * BLOCK : (k + 1) * BLOCK]
+                            + (bias_ref[head, block + blocks - k] - lse)
+                        )
+                        for k in range(blocks)
+                    ],
+                    1,
+                )
+                probs[...] = old_prob
+                slopes[...] = old_slope
+                inner[...] += jnp.sum(old_prob * old_slope, 1, keepdims=True)
+
+            row_inner = inner[...]
+            low_grad = (prob * (slope - row_inner)).astype(jnp.bfloat16)
+            query_sum[...] = jnp.dot(
+                low_grad, own_keys_flip[:width], preferred_element_type=jnp.float32
+            )
+            own_sum[:size, :width] += jnp.dot(
+                query_rows[:, at], low_grad, preferred_element_type=jnp.float32
+            )
+            own_sum[size:, :width] += jnp.dot(
+                grad_rows[:, at], prob.astype(jnp.bfloat16), preferred_element_type=jnp.float32
+            )
+            for k in range(block + 1):
+                line = head * 2 * blocks + block - k
+                bias_out[line : line + 1, :] += jnp.sum(
+                    low_grad[:, k * BLOCK : (k + 1) * BLOCK].astype(jnp.float32), 0, keepdims=True
+                )
+
+            @pl.when(later)
+            def _():
+                old_prob = probs[...]
+                low_old = (old_prob * (slopes[...] - row_inner)).astype(jnp.bfloat16)
+                query_sum[...] += jnp.dot(
+                    low_old, flipped(old_keys), preferred_element_type=jnp.float32
+                )
+                before_sum[:size, :] += jnp.dot(
+                    query_rows[:, at], low_old, preferred_element_type=jnp.float32
+                )
+                before_sum[size:, :] += jnp.dot(
+                    grad_rows[:, at], old_prob.astype(jnp.bfloat16), preferred_element_type=jnp.float32
+                )
+                for k in range(blocks):
+                    line = head * 2 * blocks + block + blocks - k
+                    bias_out[line : line + 1, :] += jnp.sum(
+                        low_old[:, k * BLOCK : (k + 1) * BLOCK].astype(jnp.float32), 0, keepdims=True
+                    )
+
+            query_out[span, at] = (query_sum[...].T * size**-0.5).astype(jnp.bfloat16)
+
+        own_out[span, :] = own_sum[:size, :] * size**-0.5
+        own_out[value_span, :] = own_sum[size:, :]
+
+        @pl.when(later)
+        def _():
+            before_out[span, :] = (before_sum[:size, :] * size**-0.5).astype(jnp.bfloat16)
+            before_out[value_span, :] = before_sum[size:, :].astype(jnp.bfloat16)
+
+    @pl.when(jnp.logical_not(later))
+    def _():
+        before_out[...] = jnp.zeros_like(before_out)
+
+
+def attention_back(biases, own, before, logsum, grad, project, heads, size):
+    tokens = own.shape[1]
+    hidden = heads * size
+    return pl.pallas_call(
+        functools.partial(attention_back_kernel, heads, size),
+        out_shape=[
+            jax.ShapeDtypeStruct((hidden, tokens), jnp.bfloat16),
+            jax.ShapeDtypeStruct((2 * hidden, tokens), jnp.float32),
+            jax.ShapeDtypeStruct((2 * hidden, tokens), jnp.bfloat16),
+            jax.ShapeDtypeStruct((heads * 2 * (tokens // BLOCK), BLOCK), jnp.float32),
+        ],
+        in_specs=[pl.BlockSpec(memory_space=pltpu.SMEM)] + [whole_vmem] * 5,
+        out_specs=[whole_vmem] * 4,
+        scratch_shapes=[
+            pltpu.VMEM((BLOCK, tokens), jnp.float32),
+            pltpu.VMEM((BLOCK, tokens), jnp.float32),
+            pltpu.VMEM((BLOCK, 1), jnp.float32),
+            pltpu.VMEM((BLOCK, size), jnp.float32),
+            pltpu.VMEM((2 * size, tokens), jnp.float32),
+            pltpu.VMEM((2 * size, tokens), jnp.float32),
+        ],
+        compiler_params=pltpu.CompilerParams(vmem_limit_bytes=48 << 20),
+    )(biases, own, before, logsum, grad, project)
+
+
+def head_sums_kernel(table_ref, rows_ref, stats_ref, turned):
+    @pl.when(pl.program_id(0) == 0)
+    def _():
+        turned[...] = rows_ref[...].astype(jnp.float32).T.astype(jnp.bfloat16)
+        stats_ref[0:1, :] = jnp.full_like(stats_ref[0:1, :], masked_score)
+        stats_ref[1:2, :] = jnp.zeros_like(stats_ref[1:2, :])
+
+    logits = jnp.dot(table_ref[...], turned[...], preferred_element_type=jnp.float32)
+    before = stats_ref[0:1, :]
+    top = jnp.maximum(before, jnp.max(logits, 0, keepdims=True))
+    stats_ref[1:2, :] = stats_ref[1:2, :] * jnp.exp(before - top) + jnp.sum(
+        jnp.exp(logits - top), 0, keepdims=True
+    )
+    stats_ref[0:1, :] = top
+
+
+def vocab_tile(vocab):
+    return max(k for k in range(16, 1601, 16) if vocab % k == 0)
+
+
+def head_sums(weights, rows, vocab):
+    tokens, width = rows.shape
+    tile = vocab_tile(vocab)
+    return pl.pallas_call(
+        head_sums_kernel,
+        grid=(vocab // tile,),
+        out_shape=jax.ShapeDtypeStruct((2, tokens), jnp.float32),
+        in_specs=[pl.BlockSpec((tile, width), lambda k: (k, 0)), pl.BlockSpec((tokens, width), lambda k: (0, 0))],
+        out_specs=pl.BlockSpec((2, tokens), lambda k: (0, 0)),
+        scratch_shapes=[pltpu.VMEM((width, tokens), jnp.bfloat16)],
+        compiler_params=pltpu.CompilerParams(vmem_limit_bytes=56 << 20),
+    )(weights, rows)
+
+
+def join_sums_kernel(stats_ref, logsum_ref, landed, send_sem, recv_sem):
+    rank = lax.axis_index("tensor")
+    barrier = pltpu.get_barrier_semaphore()
+    for step in (1, 2, 3):
+        other = lax.rem(rank + step, 4)
+        pl.semaphore_signal(barrier, inc=1, device_id={"tensor": other}, device_id_type=MESH_ID)
+    pl.semaphore_wait(barrier, 3)
+    copies = []
+    for step in (1, 2, 3):
+        copy = pltpu.make_async_remote_copy(
+            src_ref=stats_ref,
+            dst_ref=landed.at[step - 1],
+            send_sem=send_sem.at[step - 1],
+            recv_sem=recv_sem.at[step - 1],
+            device_id={"tensor": lax.rem(rank + step, 4)},
+            device_id_type=MESH_ID,
+        )
+        copy.start()
+        copies.append(copy)
+    for copy in copies:
+        copy.wait()
+    tops, sums = [], []
+    for source in range(4):
+        piece = stats_ref[...]
+        for step in (1, 2, 3):
+            piece = jnp.where(lax.rem(source + step, 4) == rank, landed[step - 1], piece)
+        tops.append(piece[0:1])
+        sums.append(piece[1:2])
+    top = jnp.maximum(jnp.maximum(tops[0], tops[1]), jnp.maximum(tops[2], tops[3]))
+    total = sums[0] * jnp.exp(tops[0] - top)
+    for source in (1, 2, 3):
+        total = total + sums[source] * jnp.exp(tops[source] - top)
+    logsum_ref[...] = top + jnp.log(total)
+
+
+def join_sums(stats, collective_id):
+    tokens = stats.shape[1]
+    return pl.pallas_call(
+        join_sums_kernel,
+        out_shape=jax.ShapeDtypeStruct((1, tokens), jnp.float32),
+        in_specs=[whole_vmem],
+        out_specs=whole_vmem,
+        scratch_shapes=[
+            pltpu.VMEM((3, 2, tokens), jnp.float32),
+            pltpu.SemaphoreType.DMA((3,)),
+            pltpu.SemaphoreType.DMA((3,)),
+        ],
+        compiler_params=pltpu.CompilerParams(collective_id=collective_id, has_side_effects=True),
+    )(stats)
+
+
+def head_back_kernel(
+    tile, table_ref, rows_ref, logsum_ref, wanted_ref, weight_ref, slope_ref, grad_ref, picked_ref, turned
+):
+    step = pl.program_id(0)
+
+    @pl.when(step == 0)
+    def _():
+        turned[...] = rows_ref[...].astype(jnp.float32).T.astype(jnp.bfloat16)
+        picked_ref[...] = jnp.zeros_like(picked_ref)
+        grad_ref[...] = jnp.zeros_like(grad_ref)
+
+    logits = jnp.dot(table_ref[...], turned[...], preferred_element_type=jnp.float32)
+    row = lax.broadcasted_iota(jnp.int32, logits.shape, 0)
+    base = step * tile
+    hits = jnp.where(row == wanted_ref[0:1, :] - base, weight_ref[0:1, :], 0.0) + jnp.where(
+        row == wanted_ref[1:2, :] - base, weight_ref[1:2, :], 0.0
+    )
+    picked_ref[...] += jnp.sum(hits * logits, 0, keepdims=True)
+    softmax = jnp.exp(logits - logsum_ref[...])
+    slope = ((weight_ref[2:3, :] * softmax - hits) * weight_ref[3:4, :]).astype(jnp.bfloat16)
+    slope_ref[...] = slope
+    grad_ref[...] += lax.dot_general(
+        slope, table_ref[...], (((0,), (0,)), ((), ())), preferred_element_type=jnp.float32
+    )
+
+
+def head_back(weights, rows, logsum, wanted, weight_rows, vocab):
+    tokens, width = rows.shape
+    tile = vocab_tile(vocab)
+    fixed = lambda k: (0, 0)
+    return pl.pallas_call(
+        functools.partial(head_back_kernel, tile),
+        grid=(vocab // tile,),
+        out_shape=[
+            jax.ShapeDtypeStruct((vocab, tokens), jnp.bfloat16),
+            jax.ShapeDtypeStruct((tokens, width), jnp.float32),
+            jax.ShapeDtypeStruct((1, tokens), jnp.float32),
+        ],
+        in_specs=[
+            pl.BlockSpec((tile, width), lambda k: (k, 0)),
+            pl.BlockSpec((tokens, width), fixed),
+            pl.BlockSpec((1, tokens), fixed),
+            pl.BlockSpec((2, tokens), fixed),
+            pl.BlockSpec((4, tokens), fixed),
+        ],
+        out_specs=[
+            pl.BlockSpec((tile, tokens), lambda k: (k, 0)),
+            pl.BlockSpec((tokens, width), fixed),
+            pl.BlockSpec((1, tokens), fixed),
+        ],
+        scratch_shapes=[pltpu.VMEM((width, tokens), jnp.bfloat16)],
+        compiler_params=pltpu.CompilerParams(vmem_limit_bytes=60 << 20),
+    )(weights, rows, logsum, wanted, weight_rows)
+
+
+def weight_grads_kernel(
+    tile_units, tiles, place_ref, slope_ref, rows_ref, ids_ref, zero_ref, joint_ref, normed_ref,
+    attended_ref, grad_ref, out_ref, made, sem,
+):
+    step = pl.program_id(0)
+    unit_rows = out_ref.shape[1]
+    buffer = lax.rem(step, 2)
+    last_units = joint_ref.shape[0] // unit_rows + attended_ref.shape[0] // unit_rows
+
+    def settle(which, count):
+        pltpu.make_async_copy(
+            made.at[which, pl.ds(0, count)], made.at[which, pl.ds(0, count)], sem.at[which]
+        ).wait()
+
+    def send(first, count):
+        def push(u, carry):
+            pltpu.make_async_copy(
+                made.at[buffer, u], out_ref.at[place_ref[first + u]], sem.at[buffer]
+            ).start()
+            return carry
+
+        lax.fori_loop(0, count, push, 0)
+
+    @pl.when(step >= 2)
+    def _():
+        settle(buffer, tile_units)
+
+    @pl.when(step < tiles)
+    def _():
+        row = lax.broadcasted_iota(jnp.int32, slope_ref.shape, 0)
+        seen = jnp.where(row == ids_ref[...] - step * slope_ref.shape[0], 1.0, 0.0).astype(jnp.bfloat16)
+        made[buffer] = (
+            jnp.dot(slope_ref[...], rows_ref[...], preferred_element_type=jnp.float32)
+            + jnp.dot(seen, zero_ref[...], preferred_element_type=jnp.float32)
+        ).reshape(tile_units, unit_rows, -1)
+        send(step * tile_units, tile_units)
+
+    @pl.when(step == tiles)
+    def _():
+        joint_units = joint_ref.shape[0] // unit_rows
+        made[buffer, pl.ds(0, joint_units)] = jnp.dot(
+            joint_ref[...], normed_ref[...], preferred_element_type=jnp.float32
+        ).reshape(joint_units, unit_rows, -1)
+        made[buffer, pl.ds(joint_units, last_units - joint_units)] = jnp.dot(
+            attended_ref[...], grad_ref[...], preferred_element_type=jnp.float32
+        ).reshape(last_units - joint_units, unit_rows, -1)
+        send(tiles * tile_units, last_units)
+        settle(1 - buffer, tile_units)
+        settle(buffer, last_units)
+
+
+def weight_grads(place, slots, unit_rows, slope, rows, ids, zero, joint, normed, attended, grad):
+    vocab, tokens = slope.shape
+    width = rows.shape[1]
+    tile = vocab_tile(vocab)
+    tiles = vocab // tile
+    fixed = lambda k: (0, 0)
+    whole = lambda x: pl.BlockSpec(x.shape, fixed)
+    return pl.pallas_call(
+        functools.partial(weight_grads_kernel, tile // unit_rows, tiles),
+        grid=(tiles + 1,),
+        out_shape=jax.ShapeDtypeStruct((slots, unit_rows, width), jnp.float32),
+        in_specs=[
+            pl.BlockSpec(memory_space=pltpu.SMEM),
+            pl.BlockSpec((tile, tokens), lambda k: (jnp.minimum(k, tiles - 1), 0)),
+        ]
+        + [whole(x) for x in (rows, ids, zero, joint, normed, attended, grad)],
+        out_specs=whole_any,
+        scratch_shapes=[
+            pltpu.VMEM((2, tile // unit_rows, unit_rows, width), jnp.float32),
+            pltpu.SemaphoreType.DMA((2,)),
+        ],
+        compiler_params=pltpu.CompilerParams(vmem_limit_bytes=60 << 20),
+    )(place, slope, rows, ids, zero, joint, normed, attended, grad)
 
 
 def adam_update(weight, moment_one, moment_two, gradient, step_rate, decay_factor):
@@ -442,73 +883,6 @@
 
 def from_experts(buffer):
     return lax.all_to_all(buffer, ("dp", "ctx"), split_axis=0, concat_axis=0, tiled=True)
-
-
-def block_bias(bias_table, query_blocks, key_blocks, key_allowed):
-    distance = query_blocks[:, None] - key_blocks[None, :]
-    allowed = (distance >= 0) & key_allowed[None, :]
-    buckets = bias_table.shape[1]
-    onehot = (
-        jnp.clip(distance, 0, buckets - 1)[:, :, None] == jnp.arange(buckets, dtype=jnp.int32)
-    ).astype(jnp.float32)
-    bias_block = jnp.einsum("qkr,hr->hqk", onehot, bias_table, precision=highest_precision)
-    return (bias_block, allowed, onehot)
-
-
-def tile_scores(query_tile, keys, bias_block, allowed):
-    scores = jnp.einsum(
-        "qhd,khd->hqk", query_tile, keys, preferred_element_type=jnp.float32
-    ) * query_tile.shape[-1] ** (-0.5)
-    head_count, row_count, column_count = scores.shape
-    shaped = (
-        scores.reshape(head_count, row_count // BLOCK, BLOCK, column_count // BLOCK, BLOCK)
-        + bias_block[:, :, None, :, None]
-    )
-    return jnp.where(allowed[None, :, None, :, None], shaped, masked_score)
-
-
-def tile_forward(query_tile, keys, values, bias_block, allowed):
-    shaped = tile_scores(query_tile, keys, bias_block, allowed)
-    peak_value = jnp.max(shaped, axis=(3, 4), keepdims=True)
-    exp_scores = jnp.exp(shaped - peak_value)
-    exp_total = jnp.sum(exp_scores, axis=(3, 4), keepdims=True)
-    head_count = shaped.shape[0]
-    softmax_low = (
-        (exp_scores / exp_total)
-        .astype(jnp.bfloat16)
-        .reshape(head_count, query_tile.shape[0], keys.shape[0])
-    )
-    output = jnp.einsum("hqk,khd->qhd", softmax_low, values, preferred_element_type=jnp.float32)
-    return (output.astype(jnp.bfloat16), peak_value + jnp.log(exp_total))
-
-
-def tile_backward(query_tile, keys, values, grad_out, logsum, bias_block, allowed, onehot):
-    shaped = tile_scores(query_tile, keys, bias_block, allowed)
-    softmax_full = jnp.exp(shaped - logsum)
-    head_count = shaped.shape[0]
-    flat_shape = (head_count, query_tile.shape[0], keys.shape[0])
-    softmax_low = softmax_full.reshape(flat_shape).astype(jnp.bfloat16)
-    grad_softmax = jnp.einsum(
-        "qhd,khd->hqk", grad_out, values, preferred_element_type=jnp.float32
-    ).reshape(shaped.shape)
-    row_inner = jnp.sum(softmax_full * grad_softmax, axis=(3, 4), keepdims=True)
-    grad_scores = (softmax_full * (grad_softmax - row_inner)).astype(jnp.bfloat16)
-    score_scale = query_tile.shape[-1] ** (-0.5)
-    flat_scores = grad_scores.reshape(flat_shape)
-    grad_query = (
-        jnp.einsum("hqk,khd->qhd", flat_scores, keys, preferred_element_type=jnp.float32)
-        * score_scale
-    )
-    grad_keys = (
-        jnp.einsum("hqk,qhd->khd", flat_scores, query_tile, preferred_element_type=jnp.float32)
-        * score_scale
-    )
-    grad_values = jnp.einsum(
-        "hqk,qhd->khd", softmax_low, grad_out, preferred_element_type=jnp.float32
-    )
-    block_sums = jnp.sum(grad_scores.astype(jnp.float32), axis=(2, 4))
-    grad_bias = jnp.einsum("hqk,qkr->hr", block_sums, onehot, precision=highest_precision)
-    return (grad_query, grad_keys, grad_values, grad_bias)
 
 
 def on_device(
@@ -554,17 +928,19 @@
     experts = router.shape[1]
     experts_here = expert_in.shape[0]
     capacity = (18 * tokens_here + 8 * experts - 1) // (8 * experts)
-    tile_rows = min(half_length, 512)
-    head_rows_count = min(tokens_here, 512)
     table_units = vocab_here // unit_rows
     query_units = table_units + 2 * hidden_here // unit_rows
     value_units = table_units + 3 * hidden_here // unit_rows
     embed_scale = math.sqrt(model_width)
     owner_ids = owner_of[:, 0]
     unit_rank, slot_unit, slot_filled = slot_tables(owner_ids, owners, most_units)
+    loss_weights = counted.reshape(tokens_here, 2).T.astype(jnp.float32) * jnp.array(
+        [[1.0], [ahead_weight]], jnp.float32
+    )
+    weight_total = lax.psum(jnp.sum(loss_weights), ("dp", "ctx"))
     gathered = lax.all_gather(master[0, 0].astype(jnp.bfloat16), ("dp", "ctx"), axis=0, tiled=True)
-    weights_low = pull_units(gathered, owner_ids * most_units + unit_rank).reshape(-1, model_width)
-    table_low = weights_low[:vocab_here]
+    unit_slots = owner_ids * most_units + unit_rank
+    weights_low = pull_units(gathered, unit_slots).reshape(-1, model_width)
     joint_low = weights_low[vocab_here : vocab_here + 3 * hidden_here]
     project_low = weights_low[vocab_here + 3 * hidden_here :]
     rolled = [project_low] + [
@@ -577,7 +953,7 @@
     local_ids = token_ids.reshape(-1) - my_rank * vocab_here
     inside = (local_ids >= 0) & (local_ids < vocab_here)
     clipped_ids = jnp.clip(local_ids, 0, vocab_here - 1)
-    looked = jnp.where(inside[:, None], jnp.take(table_low, clipped_ids, axis=0), 0)
+    looked = jnp.where(inside[:, None], jnp.take(weights_low, clipped_ids, axis=0), 0)
     gain_rows = [norm_gains[k : k + 1] for k in range(3)]
     stream_shape = jax.ShapeDtypeStruct((tokens_here, model_width), jnp.float32)
     gain_shape = jax.ShapeDtypeStruct((1, model_width), jnp.float32)
@@ -586,53 +962,11 @@
     first_normalized = norm_forward(stream_zero, norm_gains[0])
     normed_one_low = first_normalized.astype(jnp.bfloat16)
     joint = lax.dot_general(
-        normed_one_low, joint_low, (((1,), (1,)), ((), ())), preferred_element_type=jnp.float32
+        joint_low, normed_one_low, (((1,), (1,)), ((), ())), preferred_element_type=jnp.float32
     ).astype(jnp.bfloat16)
-    queries = joint[:, :hidden_here].reshape(sequences, half_length, heads_here, head_size)
-    pairs_here = joint[:, hidden_here:].reshape(sequences, half_length, 2 * hidden_here)
-    pairs_before = passed_along(pairs_here, "ctx", 1)
-    keyvals = jnp.concatenate([pairs_before, pairs_here], 1).reshape(
-        sequences, 2 * half_length, 2, heads_here, head_size
-    )
-    keys_all = keyvals[:, :, 0]
-    values_all = keyvals[:, :, 1]
-    blocks_half = half_length // BLOCK
-    tile_blocks = tile_rows // BLOCK
-    tiles_sequence = half_length // tile_rows
-    key_blocks = jnp.arange(2 * blocks_half, dtype=jnp.int32) + (my_context - 1) * blocks_half
-    key_allowed = (jnp.arange(2 * blocks_half) >= blocks_half) | (my_context > 0)
-    frames = [
-        block_bias(
-            rel_bias,
-            my_context * blocks_half
-            + tile_index * tile_blocks
-            + jnp.arange(tile_blocks, dtype=jnp.int32),
-            key_blocks,
-            key_allowed,
-        )
-        for tile_index in range(tiles_sequence)
-    ]
-
-    def attend_forward(seq_items):
-        seq_queries, seq_keys, seq_values = seq_items
-        outputs = []
-        logsums = []
-        for tile_index in range(tiles_sequence):
-            bias_block, allowed, onehot = frames[tile_index]
-            output, logsum = tile_forward(
-                seq_queries[tile_index * tile_rows : (tile_index + 1) * tile_rows],
-                seq_keys,
-                seq_values,
-                bias_block,
-                allowed,
-            )
-            outputs.append(output)
-            logsums.append(logsum)
-        return (jnp.concatenate(outputs, 0), jnp.concatenate(logsums, 1))
-
-    attention_output, logsum_all = lax.map(attend_forward, (queries, keys_all, values_all))
-    attended_flat = attention_output.reshape(tokens_here, hidden_here)
-    (attended_all,) = gather_line([attended_flat.T], 2)
+    pairs_before = passed_along(joint[hidden_here:], "ctx", 1)
+    attended, logsum_rows = attention(rel_bias, joint, pairs_before, heads_here, head_size)
+    (attended_all,) = gather_line([attended], 2)
     stream_one = stream_zero + lax.dot_general(
         attended_all.reshape(model_width, tokens_here),
         project_full,
@@ -684,81 +1018,25 @@
     head_low, stream_two = sum_line(
         moe_partial, [stream_one, gain_rows[2]], [stream_shape], finish_mixture, 3
     )
-    head_tiles = tokens_here // head_rows_count
-    head_rows = head_low.reshape(head_tiles, head_rows_count, model_width)
-    local_targets = (targets.reshape(tokens_here, 2) - my_rank * vocab_here).reshape(
-        head_tiles, head_rows_count, 2
-    )
-    columns = jnp.arange(vocab_here, dtype=jnp.int32)
-
-    def head_forward(tile_items):
-        rows_low, wanted = tile_items
-        logits = lax.dot_general(
-            rows_low, table_low, (((1,), (1,)), ((), ())), preferred_element_type=jnp.float32
-        )
-        peak_value = jnp.max(logits, 1)
-        exp_total = jnp.sum(jnp.exp(logits - peak_value[:, None]), 1)
-        picked = jnp.stack(
-            [
-                jnp.sum(jnp.where(columns[None, :] == wanted[:, which : which + 1], logits, 0.0), 1)
-                for which in range(2)
-            ],
-            1,
-        )
-        return (peak_value, exp_total, picked)
-
-    peaks, totals, picked = lax.map(head_forward, (head_rows, local_targets))
-
-    def merge_totals(left_part, right_part):
-        top_value = jnp.maximum(left_part[0], right_part[0])
-        summed = left_part[1] * jnp.exp(left_part[0] - top_value) + right_part[1] * jnp.exp(
-            right_part[0] - top_value
-        )
-        return (top_value, summed, left_part[2] + right_part[2])
-
-    top_value, exp_total, target_logits = combined_all(
-        (peaks.reshape(-1), totals.reshape(-1), picked.reshape(tokens_here, 2)),
-        "tensor",
-        merge_totals,
-    )
-    logsum_vocab = top_value + jnp.log(exp_total)
-    loss_weights = counted.reshape(tokens_here, 2).astype(jnp.float32) * jnp.array(
-        [1.0, ahead_weight], jnp.float32
-    )
-    loss_local = jnp.sum(loss_weights * (logsum_vocab[:, None] - target_logits))
-    loss_totals = lax.psum(jnp.stack([loss_local, jnp.sum(loss_weights)]), ("dp", "ctx"))
-    inverse_weight = 1.0 / loss_totals[1]
-
-    def head_backward(running, tile_items):
-        rows_low, wanted, logsum_rows, weight_rows = tile_items
-        logits = lax.dot_general(
-            rows_low, table_low, (((1,), (1,)), ((), ())), preferred_element_type=jnp.float32
-        )
-        softmax_full = jnp.exp(logits - logsum_rows[:, None])
-        target_hits = jnp.where(
-            columns[None, :] == wanted[:, 0:1], weight_rows[:, 0:1], 0.0
-        ) + jnp.where(columns[None, :] == wanted[:, 1:2], weight_rows[:, 1:2], 0.0)
-        grad_logits = (
-            (jnp.sum(weight_rows, 1, keepdims=True) * softmax_full - target_hits) * inverse_weight
-        ).astype(jnp.bfloat16)
-        grad_rows = jnp.dot(grad_logits, table_low, preferred_element_type=jnp.float32)
-        running = running + lax.dot_general(
-            grad_logits, rows_low, (((0,), (0,)), ((), ())), preferred_element_type=jnp.float32
-        )
-        return (running, grad_rows)
-
-    table_grad, grad_head = lax.scan(
-        head_backward,
-        jnp.zeros((vocab_here, model_width), jnp.float32),
-        (
-            head_rows,
-            local_targets,
-            logsum_vocab.reshape(head_tiles, head_rows_count),
-            loss_weights.reshape(head_tiles, head_rows_count, 2),
-        ),
+    stats = head_sums(weights_low, head_low, vocab_here)
+    logsum_vocab = join_sums(stats, 7)
+    local_targets = targets.reshape(tokens_here, 2).T - my_rank * vocab_here
+    weight_rows = jnp.concatenate(
+        [
+            loss_weights,
+            loss_weights[0:1] + loss_weights[1:2],
+            jnp.broadcast_to(1.0 / weight_total, (1, tokens_here)),
+        ],
+        0,
+    )
+    slopes, grad_head, target_sums = head_back(
+        weights_low, head_low, logsum_vocab, local_targets, weight_rows, vocab_here
+    )
+    loss_local = (
+        jnp.sum(weight_rows[2] * logsum_vocab[0]) * (my_rank == 0) - jnp.sum(target_sums)
     )
     grad_two_low, grad_two, gain_grad_three = sum_line(
-        grad_head.reshape(tokens_here, model_width),
+        grad_head,
         [stream_two, gain_rows[2]],
         [stream_shape, gain_shape],
         finish_head_grad,
@@ -825,97 +1103,54 @@
     router_grad = lax.dot_general(
         normed_two_low, logit_grad, (((0,), (1,)), ((), ())), preferred_element_type=jnp.float32
     )
-    project_grad = lax.dot_general(
-        attended_flat, grad_one_low, (((0,), (0,)), ((), ())), preferred_element_type=jnp.float32
-    )
-    grad_attended = lax.dot_general(
-        grad_one_low, project_low, (((1,), (1,)), ((), ())), preferred_element_type=jnp.float32
-    ).astype(jnp.bfloat16)
-
-    def attend_backward(seq_items):
-        seq_queries, seq_keys, seq_values, seq_grad, seq_logsum = seq_items
-        query_grads = []
-        key_grad = jnp.zeros(seq_keys.shape, jnp.float32)
-        value_grad = jnp.zeros(seq_values.shape, jnp.float32)
-        bias_grad = jnp.zeros(rel_bias.shape, jnp.float32)
-        for tile_index in range(tiles_sequence):
-            bias_block, allowed, onehot = frames[tile_index]
-            row_range = slice(tile_index * tile_rows, (tile_index + 1) * tile_rows)
-            tile_logsum = seq_logsum[:, tile_index * tile_blocks : (tile_index + 1) * tile_blocks]
-            grad_query, grad_keys, grad_values, grad_bias = tile_backward(
-                seq_queries[row_range],
-                seq_keys,
-                seq_values,
-                seq_grad[row_range],
-                tile_logsum,
-                bias_block,
-                allowed,
-                onehot,
-            )
-            query_grads.append(grad_query)
-            key_grad = key_grad + grad_keys
-            value_grad = value_grad + grad_values
-            bias_grad = bias_grad + grad_bias
-        return (jnp.concatenate(query_grads, 0), key_grad, value_grad, bias_grad)
-
-    query_grad, key_grad, value_grad, bias_grads = lax.map(
-        attend_backward,
-        (
-            queries,
-            keys_all,
-            values_all,
-            grad_attended.reshape(sequences, half_length, heads_here, head_size),
-            logsum_all,
+    query_grad, pair_grad, before_grad, bias_lines = attention_back(
+        rel_bias,
+        joint,
+        pairs_before,
+        logsum_rows,
+        grad_one_low,
+        project_low,
+        heads_here,
+        head_size,
+    )
+    grad_after = passed_along(before_grad, "ctx", -1)
+    pair_grad_low = (pair_grad + grad_after.astype(jnp.float32)).astype(jnp.bfloat16)
+    joint_grad = jnp.concatenate([query_grad, pair_grad_low], 0)
+    distances = 2 * (half_length // BLOCK)
+    bias_grad = jnp.sum(bias_lines, 1).reshape(heads_here, distances)
+    zero_grad_low, gain_grad_one = sum_line(
+        lax.dot_general(
+            joint_grad, joint_low, (((0,), (0,)), ((), ())), preferred_element_type=jnp.float32
         ),
-    )
-    bias_grad = jnp.sum(bias_grads, 0)
-    pair_grad = jnp.stack([key_grad, value_grad], 2).reshape(
-        sequences, 2 * half_length, 2 * hidden_here
-    )
-    grad_before = passed_along(pair_grad[:, :half_length].astype(jnp.bfloat16), "ctx", -1)
-    pair_grad_here = pair_grad[:, half_length:] + grad_before.astype(jnp.float32)
-    joint_grad = jnp.concatenate(
-        [
-            query_grad.reshape(tokens_here, hidden_here),
-            pair_grad_here.reshape(tokens_here, 2 * hidden_here),
-        ],
-        1,
-    ).astype(jnp.bfloat16)
-    joint_weight_grad = lax.dot_general(
-        joint_grad, normed_one_low, (((0,), (0,)), ((), ())), preferred_element_type=jnp.float32
-    )
-    zero_grad_low, gain_grad_one = sum_line(
-        jnp.dot(joint_grad, joint_low, preferred_element_type=jnp.float32),
         [embedded, gain_rows[0], grad_one],
         [gain_shape],
         functools.partial(finish_input_grad, embed_scale),
         6,
         prologue=clear_gain,
     )
-    onehot_ids = (
-        (lax.broadcasted_iota(jnp.int32, (vocab_here, tokens_here), 0) == local_ids[None, :])
-    ).astype(jnp.bfloat16)
-    table_grad = table_grad + jnp.dot(
-        onehot_ids, zero_grad_low, preferred_element_type=jnp.float32
-    )
-    unit_grads = jnp.concatenate(
-        [
-            table_grad,
-            joint_weight_grad,
-            project_grad,
-        ],
-        0,
-    ).reshape(-1, unit_rows, model_width)
     my_units = jnp.take(slot_unit, my_owner, axis=0)
     my_filled = jnp.take(slot_filled, my_owner, axis=0)[:, None, None]
-    outgoing = pull_units(unit_grads, slot_unit.reshape(-1))
+    outgoing = weight_grads(
+        unit_slots,
+        owners * most_units,
+        unit_rows,
+        slopes,
+        head_low,
+        local_ids[None, :],
+        zero_grad_low,
+        joint_grad,
+        normed_one_low,
+        attended,
+        grad_one_low,
+    )
     summed = lax.psum_scatter(outgoing, ("dp", "ctx"), scatter_dimension=0, tiled=True)
     mine = jnp.where(my_filled, summed, 0.0)
-    gains_grad = lax.psum(
-        jnp.concatenate([gain_grad_one, gain_grad_two, gain_grad_three], 0),
+    gains_grad, loss_total = lax.psum(
+        (jnp.concatenate([gain_grad_one, gain_grad_two, gain_grad_three], 0), loss_local),
         ("dp", "ctx", "tensor"),
     )
     router_grad, bias_grad = lax.psum((router_grad, bias_grad), ("dp", "ctx"))
+    loss_totals = jnp.stack([loss_total, weight_total])
     slot_rates = unit_rates(my_units, table_units, query_units, value_units)[:, None, None]
     master_new, master_first_new, master_second_new = adam_update(
         master[0, 0], master_first[0, 0], master_second[0, 0], mine, slot_rates, decay_rate

time: 1340 us -> 1180 us (0.88)
  matrix products: 298 us -> 96.1 us
  Pallas kernels: 372 us -> 489 us
  local copies, waits for them, and re-layouts: 156 us -> 39.5 us
  waiting for transfers between devices: 130 us -> 241 us
  other arithmetic: 132 us -> 56.2 us
    dot_general x30 -> x2, matrix products: 212 us -> 4.2 us  [the longest x1 3.1 us: on_device(): lax.dot_general(joint_grad, joint_low, (((0,), (0,)), ((), ())), preferre...]
    pallas_call x0 -> x6, Pallas kernels: none -> 139 us  [the longest x1 44 us: head_back(): pl.pallas_call(functools.partial(head_back_kernel, tile), grid=(vocab //...]
    reduce_scatter x1, waiting for transfers between devices: 20.1 us -> 106 us  [on_device(): lax.psum_scatter(outgoing, ('dp', 'ctx'), scatter_dimension=0, tiled=True)]
    unnamed x268 -> x114, local copies, waits for them, and re-layouts: 90.9 us -> 24.9 us
    all_gather x1, waiting for transfers between devices: 42.9 us -> 87.1 us  [on_device(): lax.all_gather(master[0, 0].astype(jnp.bfloat16), ('dp', 'ctx'), axis=0,...]
    reduce_sum x9 -> x3, other arithmetic: 44.2 us -> 2.02 us  [the longest x1 1.29 us: on_device(): jnp.sum(weight_rows[2] * logsum_vocab[0]) * (my_rank == 0)]
    all_gather x3 -> x0, blocking collectives: 39.4 us -> none  [combined_all(): everything = jax.tree.map(lambda part: lax.all_gather(part, axis), x)]
    add x6 -> x0, local copies, waits for them, and re-layouts: 38.9 us -> none  [the longest x4 38.9 us: tile_scores(): scores.reshape(head_count, row_count // BLOCK, BLOCK, column_count // BLO...]
  transfers between devices with their start and end apart: 9 -> 9, of which waited for: 5 -> 4; matrix products, arithmetic and copies ran while one was open for 15% -> 7% of each run, Pallas kernels for 4% -> 5%
where the time goes in v2:
time: 1180 us; the launch traced here: 1170 us
  Pallas kernels  489 us (41%)
  waiting for transfers between devices  241 us (20%)
  blocking collectives  212 us (18%)
  matrix products  96.1 us (8%)
  other arithmetic  56.2 us (5%)
  local copies, waits for them, and re-layouts  39.5 us (3%)
  between operations  17.5 us (1%)
  starting transfers between devices  16.4 us (1%)
    pallas_call x5, Pallas kernels, sum_line(): pl.pallas_call(functools.partial(sum_line_kernel, count, meets_all, prolo...  316 us
    reduce_scatter x1, waiting for transfers between devices, on_device(): lax.psum_scatter(outgoing, ('dp', 'ctx'), scatter_dimension=0, tiled=True)  106 us
    all_to_all x2, blocking collectives, to_experts(): lax.all_to_all(buffer, ('dp', 'ctx'), split_axis=0, concat_axis=0, tiled=...  91.1 us
    all_gather x1, waiting for transfers between devices, on_device(): lax.all_gather(master[0, 0].astype(jnp.bfloat16), ('dp', 'ctx'), axis=0,...  87.1 us
    psum x1, blocking collectives, on_device(): weight_total = lax.psum(jnp.sum(loss_weights), ('dp', 'ctx'))  48.3 us
    pallas_call x1, Pallas kernels, head_back(): pl.pallas_call(functools.partial(head_back_kernel, tile), grid=(vocab //...  44 us
    all_to_all x2, waiting for transfers between devices, from_experts(): lax.all_to_all(buffer, ('dp', 'ctx'), split_axis=0, concat_axis=0, tiled=...  42 us
    psum x1, blocking collectives, on_device(): lax.psum((jnp.concatenate([gain_grad_one, gain_grad_two, gain_grad_three]...  39.4 us
  transfers between devices with their start and end apart: 9, of which 4 were waited for; matrix products, arithmetic and copies ran while one was open for 7% of the time, Pallas kernels for 5%

profile of v2, /device:TPU:0, one launch (start us, length us, event | category | flops | bytes accessed | tf_op | source)
XLA Modules:
  0.0 1167.5 jit_solution(7984700120179548639)
XLA Ops:
  15.6 87.1 %all-gather.2.cloned.1.call-done.source_ref = bf16[168,64,768]{2,1,0:T(8,128)(2,1)} async-done(((bf16[21,64,768]{2,1,0:T(8,128)(2,1)}), bf16[168,64,768]{2,1,0:T(8,128)(2,1)}) %all-gather.2.cloned.1.call-update) | async-done | bytes 16515088 | tf_op jit(solution)/shard_map/all_gather | solution.py:941
  117.9 11.0 gather_fusion
  129.8 60.2 %shard_map.385.refs_0_ = bf16[1024,768]{1,0:T(8,128)(2,1)S(1)} custom-call(bf16[1024,768]{1,0:T(8,128)(2,1)S(1)} %select_select_fusion.part_ref), custom_call_target="tpu_custom_call" | custom-call | tf_op jit(solution)/shard_map/pallas_call | solution.py:172
  197.9 12.6 %shard_map.386 = (bf16[192,1024]{1,0:T(8,128)(2,1)S(1)}, f32[3,1024,1]{2,1,0:T(8,128)S(1)}) custom-call(f32[3,8]{1,0:T(4,128)S(1)} %copy-done.12, bf16[576,1024]{1,0:T(8,128)(2,1)S(1)} %convolution_convert_fusion.1.own_ref, bf16[384,1024]{1,0:T(8,128)(2,1)S(1)} %collective-permute-done.before_ref), custom_call_target="tpu_custom_call" | custom-call | tf_op jit(solution)/shard_map/pallas_call | solution.py:442
  212.6 28.8 %shard_map.387 = bf16[4,192,1024]{2,1,0:T(8,128)(2,1)S(1)} custom-call(bf16[192,1024]{1,0:T(8,128)(2,1)S(1)} %get-tuple-element.39.refs_0_.attended_ref), custom_call_target="tpu_custom_call" | custom-call | tf_op jit(solution)/shard_map/pallas_call | solution.py:326
  249.8 46.3 %all_to_all.20 = bf16[8,288,768]{2,1,0:T(8,128)(2,1)S(1)} all-to-all(bf16[8,288,768]{2,1,0:T(8,128)(2,1)S(1)} %bitcast.216), channel_id=1, replica_groups=mesh['dp'=4,'ctx'=2,'tensor'=4] {'dp','ctx'}, dimensions={0} | all-to-all | bytes 7077888 | tf_op jit(solution)/shard_map/all_to_all | solution.py:881
  314.7 48.3 %psum.35 = f32[]{:T(128)} all-reduce(f32[]{:T(128)} %get-tuple-element.116), channel_id=1, replica_groups=mesh['dp'=4,'ctx'=2,'tensor'=4] {'dp','ctx'}, use_global_device_ids=true, to_apply=%region_8.9 | all-reduce | flops 1 | bytes 8 | tf_op jit(solution)/shard_map/psum | solution.py:940
  367.6 16.1 %fusion.57 = f32[1024,2]{1,0:T(8,128)} fusion(f32[1024,8]{1,0:T(8,128)S(1)} %fusion.98, s32[1024,2]{1,0:T(8,128)} %copy.56), kind=kLoop, calls=%fused_computation.87 | loop fusion | flops 47104 | bytes 49152
  400.4 65.1 %shard_map.388 = (bf16[1024,768]{1,0:T(8,128)(2,1)S(1)}, f32[1024,768]{1,0:T(8,128)S(1)}) custom-call(f32[1024,768]{1,0:T(8,128)} %multiply_add_fusion.part_ref, f32[1024,768]{1,0:T(8,128)} %copy-done.14, f32[1,768]{1,0:T(1,128)S(1)} %get-tuple-element.114.refs_1_), custom_call_target="tpu_custom_call" | custom-call | tf_op jit(solution)/shard_map/pallas_call | solution.py:172
  468.3 23.3 %shard_map.389.stats_ref = f32[2,1024]{1,0:T(2,128)} custom-call(bf16[8768,768]{1,0:T(8,128)(2,1)} %bitcast.202, bf16[1024,768]{1,0:T(8,128)(2,1)} %copy-done.1), custom_call_target="tpu_custom_call" | custom-call | tf_op jit(solution)/shard_map/pallas_call | solution.py:626
  500.4 44.0 %shard_map.391 = (bf16[8000,1024]{1,0:T(8,128)(2,1)}, f32[1024,768]{1,0:T(8,128)}, f32[1,1024]{1,0:T(1,128)}) custom-call(bf16[8768,768]{1,0:T(8,128)(2,1)} %bitcast.203, bf16[1024,768]{1,0:T(8,128)(2,1)} %copy-done.1, f32[1,1024]{1,0:T(1,128)} %shard_map.390.logsum_ref, s32[2,1024]{1,0:T(2,128)} %subtract_bitcast_fusion.wanted_ref, ...), custom_call_target="tpu_custom_call" | custom-call | tf_op jit(solution)/shard_map/pallas_call | solution.py:718
  544.4 56.0 %shard_map.392 = (bf16[1024,768]{1,0:T(8,128)(2,1)S(1)}, f32[1024,768]{1,0:T(8,128)S(1)}, f32[1,768]{1,0:T(1,128)S(1)}) custom-call(f32[1024,768]{1,0:T(8,128)} %get-tuple-element.44.part_ref, f32[1024,768]{1,0:T(8,128)} %copy-done.6, f32[1,768]{1,0:T(1,128)S(1)} %get-tuple-element.114.refs_1_), custom_call_target="tpu_custom_call" | custom-call | tf_op jit(solution)/shard_map/pallas_call | solution.py:172
  618.3 44.8 %all_to_all.21 = bf16[8,288,768]{2,1,0:T(8,128)(2,1)S(1)} all-to-all(bf16[8,288,768]{2,1,0:T(8,128)(2,1)S(1)} %bitcast.215), channel_id=1, replica_groups=mesh['dp'=4,'ctx'=2,'tensor'=4] {'dp','ctx'}, dimensions={0} | all-to-all | bytes 7077888 | tf_op jit(solution)/shard_map/all_to_all | solution.py:881
  663.1 11.0 fusion.13
  685.0 42.0 %all-to-all-done.3 = bf16[8,288,768]{2,1,0:T(8,128)(2,1)} async-done(((bf16[8,288,768]{2,1,0:T(8,128)(2,1)}), bf16[8,288,768]{2,1,0:T(8,128)(2,1)}, u32[]{:S(2)}, u32[]{:S(2)}) %all-to-all-start.3) | async-done | bytes 3538976 | tf_op jit(solution)/shard_map/all_to_all | solution.py:885
  735.6 76.7 %shard_map.393 = (bf16[1024,768]{1,0:T(8,128)(2,1)S(1)}, f32[1024,768]{1,0:T(8,128)S(1)}, bf16[8,1024]{1,0:T(8,128)(2,1)S(1)}, f32[1,768]{1,0:T(1,128)S(1)}) custom-call(f32[1024,768]{1,0:T(8,128)} %fusion.85.part_ref, f32[1024,768]{1,0:T(8,128)} %copy-done.14, f32[1,768]{1,0:T(1,128)S(1)} %get-tuple-element.113.refs_1_, f32[1024,768]{1,0:T(8,128)} %copy-done.7, ...), custom_call_target="tpu_custom_call" | custom-call | tf_op jit(solution)/shard_map/pallas_call | solution.py:172
  815.1 18.1 %shard_map.394 = (bf16[192,1024]{1,0:T(8,128)(2,1)S(1)}, f32[384,1024]{1,0:T(8,128)S(1)}, bf16[384,1024]{1,0:T(8,128)(2,1)S(1)}, f32[24,256]{1,0:T(8,128)S(1)}) custom-call(f32[3,8]{1,0:T(4,128)S(1)} %copy-done.12, bf16[576,1024]{1,0:T(8,128)(2,1)S(1)} %convolution_convert_fusion.1.own_ref, bf16[384,1024]{1,0:T(8,128)(2,1)S(1)} %copy-done.4, ...), custom_call_target="tpu_custom_call" | custom-call | tf_op jit(solution)/shard_map/pallas_call | solution.py:581
  844.7 57.6 %shard_map.395 = (bf16[1024,768]{1,0:T(8,128)(2,1)S(1)}, f32[1,768]{1,0:T(1,128)S(1)}) custom-call(f32[1024,768]{1,0:T(8,128)} %fusion.84.part_ref, bf16[1024,768]{1,0:T(8,128)(2,1)S(1)} %shard_map.385.refs_0_, f32[1,768]{1,0:T(1,128)S(1)} %get-tuple-element.112.refs_1_, f32[1024,768]{1,0:T(8,128)} %copy-done.5), custom_call_target="tpu_custom_call" | custom-call | tf_op jit(solution)/shard_map/pallas_call | solution.py:172
  903.4 34.6 %shard_map.396 = f32[168,64,768]{2,1,0:T(8,128)} custom-call(s32[137]{0:T(256)} %copy-done.13, bf16[8000,1024]{1,0:T(8,128)(2,1)} %get-tuple-element.42.slope_ref, bf16[1024,768]{1,0:T(8,128)(2,1)} %copy-done.1, s32[1,1024]{1,0:T(1,128)} %copy-done.24, bf16[1024,768]{1,0:T(8,128)(2,1)} %copy-done.10, bf16[576,1024]{1,0:T(8,128)(2,1)} %pad_maximum_fusion.joint_ref, ...), custom_call_target="tpu_custom_call" | custom-call | tf_op jit(solution)/shard_map/pallas_call | solution.py:801
  942.0 12.1 %multiply_subtract_fusion.1 = (f32[1,768,768]{2,1,0:T(8,128)}, f32[1,768,768]{2,1,0:T(8,128)}, f32[1,768,768]{2,1,0:T(8,128)}) fusion(f32[1,768,768]{2,1,0:T(8,128)S(1)} %copy-done.45, f32[1,768,768]{2,1,0:T(8,128)} %param.35, f32[1,768,768]{2,1,0:T(8,128)} %param.36, bf16[8,288,768]{2,1,0:T(8,128)(2,1)} %copy-done.18, bf16[8,1,288,768]{3,2,0,1:T(8,128)(2,1)} %copy-done.52), kind=kOutput, calls=%fused_computation.75 | convolution fusion | flops 2726756352 | bytes 21233664 | tf_op jit(solution)/shard_map/oecd,oecf->edf/dot_general | solution.py:1068
  954.2 13.2 %multiply_subtract_fusion = (f32[1,768,768]{2,1,0:T(8,128)}, f32[1,768,768]{2,1,0:T(8,128)}, f32[1,768,768]{2,1,0:T(8,128)}) fusion(f32[1,768,768]{2,1,0:T(8,128)S(1)} %copy-done.48, f32[1,768,768]{2,1,0:T(8,128)S(1)} %copy-done.49, f32[1,768,768]{2,1,0:T(8,128)S(1)} %copy-done.50, bf16[8,288,768]{2,1,0:T(8,128)(2,1)S(1)} %copy-done.20, ...), kind=kOutput, calls=%fused_computation.74 | convolution fusion | flops 2742681600 | bytes 24772608 | tf_op jit(solution)/shard_map/oecf,oecd->efd/dot_general | solution.py:1063
  967.9 32.9 %all-reduce.1 = (f32[768,8]{0,1:T(8,128)S(1)}, f32[3,8]{1,0:T(4,128)S(1)}) all-reduce(f32[768,8]{0,1:T(8,128)S(1)} %fusion.99, f32[3,8]{1,0:T(4,128)S(1)} %reshape.302), channel_id=1, replica_groups=mesh['dp'=4,'ctx'=2,'tensor'=4] {'dp','ctx'}, use_global_device_ids=true, to_apply=%region_19.20 | all-reduce | flops 6168 | bytes 49344 | tf_op jit(solution)/shard_map/psum | solution.py:1152
  1002.1 39.4 %all-reduce = (f32[1]{0:T(128)}, f32[3,768]{1,0:T(4,128)S(1)}) all-reduce(f32[1]{0:T(128)} %bitcast.31, f32[3,768]{1,0:T(4,128)S(1)} %pad_maximum_fusion.1), channel_id=1, replica_groups=mesh['dp'=4,'ctx'=2,'tensor'=4] {'dp','ctx','tensor'}, use_global_device_ids=true, to_apply=%region_10.11 | all-reduce | flops 2305 | bytes 18440 | tf_op jit(solution)/shard_map/psum | solution.py:1148
  1044.1 105.8 %reduce-scatter.2.cloned.1.call-done = f32[21,64,768]{2,1,0:T(8,128)} async-done(((f32[168,64,768]{2,1,0:T(8,128)}), f32[21,64,768]{2,1,0:T(8,128)}) %reduce-scatter.2.cloned.1.call-update) | async-done | bytes 4128784 | tf_op jit(solution)/shard_map/reduce_scatter | solution.py:1146
  (205 shorter events, 162.9 us)
Async XLA Ops:
  7.2 95.4 %all-gather.2.cloned.1.call-start = ((), (), s32[]{:S(2)}) async-start(), calls=%async_computation.5 | async-start | bytes 18579456 | tf_op jit(solution)/shard_map/all_gather | solution.py:941
  11.9 96.5 %copy-start.13 = (s32[137]{0:T(256)}, s32[137]{0:T(256)S(1)}, u32[]{:S(2)}) copy-start(s32[137]{0:T(256)S(1)} %multiply_add_fusion.4.slots_ref.place_ref) | copy-start | bytes 1648
  15.4 92.9 %copy-start.24 = (s32[1,1024]{1,0:T(1,128)}, s32[1,1024]{1,0:T(1,128)S(1)}, u32[]{:S(2)}) copy-start(s32[1,1024]{1,0:T(1,128)S(1)} %get-tuple-element.108.ids_ref) | copy-start | bytes 12292
  113.4 80.3 %collective-permute-start.1 = (bf16[192,768]{1,0:T(8,128)(2,1)S(1)}, bf16[192,768]{1,0:T(8,128)(2,1)S(1)}, u32[]{:S(2)}, u32[]{:S(2)}) collective-permute-start(bf16[192,768]{1,0:T(8,128)(2,1)S(1)} %bitcast.204), channel_id=1, source_target_pairs={{0,3},{1,0},{2,1},{3,2},{4,7},{5,4},{6,5},{7,6},{8,11},{9,8},{10,9... | collective-permute-start | bytes 884744 | tf_op jit(solution)/shard_map/ppermute | solution.py:947
  116.8 77.0 %collective-permute-start.2 = (bf16[192,768]{1,0:T(8,128)(2,1)S(1)}, bf16[192,768]{1,0:T(8,128)(2,1)}, u32[]{:S(2)}, u32[]{:S(2)}) collective-permute-start(bf16[192,768]{1,0:T(8,128)(2,1)S(1)} %bitcast.205), channel_id=1, source_target_pairs={{0,2},{1,3},{2,0},{3,1},{4,6},{5,7},{6,4},{7,5},{8,10},{9,11},{10,... | collective-permute-start | bytes 884744 | tf_op jit(solution)/shard_map/ppermute | solution.py:947
  116.8 78.0 %collective-permute-start.3 = (bf16[192,768]{1,0:T(8,128)(2,1)S(1)}, bf16[192,768]{1,0:T(8,128)(2,1)}, u32[]{:S(2)}, u32[]{:S(2)}) collective-permute-start(bf16[192,768]{1,0:T(8,128)(2,1)S(1)} %bitcast.206), channel_id=1, source_target_pairs={{0,1},{1,2},{2,3},{3,0},{4,5},{5,6},{6,7},{7,4},{8,9},{9,10},{10,1... | collective-permute-start | bytes 884744 | tf_op jit(solution)/shard_map/ppermute | solution.py:947
  192.4 5.4 collective-permute-start
  212.6 30.6 %copy-start.8 = (bf16[192,1024]{1,0:T(8,128)(2,1)}, bf16[192,1024]{1,0:T(8,128)(2,1)S(1)}, u32[]{:S(2)}) copy-start(bf16[192,1024]{1,0:T(8,128)(2,1)S(1)} %get-tuple-element.39.refs_0_.attended_ref) | copy-start | bytes 1179652
  249.8 48.1 %copy-start.43 = (f32[1,768,768]{2,1,0:T(8,128)S(1)}, f32[1,768,768]{2,1,0:T(8,128)}, u32[]{:S(2)}) copy-start(f32[1,768,768]{2,1,0:T(8,128)} %param.34) | copy-start | bytes 7077892
  309.4 53.6 %copy-start.23 = (f32[768,8]{0,1:T(8,128)S(1)}, f32[768,8]{0,1:T(8,128)}, u32[]{:S(2)}) copy-start(f32[768,8]{0,1:T(8,128)} %param.43) | copy-start | bytes 73732
  309.4 55.6 %copy-start.36 = (s32[1,1024,2]{1,2,0:T(2,128)S(1)}, s32[1,1024,2]{1,2,0:T(2,128)}, u32[]{:S(2)}) copy-start(s32[1,1024,2]{1,2,0:T(2,128)} %param.26) | copy-start | bytes 24580
  309.4 76.9 %all-to-all-start.1 = ((bf16[8,288,768]{2,1,0:T(8,128)(2,1)}), bf16[8,288,768]{2,1,0:T(8,128)(2,1)}, u32[]{:S(2)}, u32[]{:S(2)}) async-start(bf16[8,288,768]{2,1,0:T(8,128)(2,1)} %fusion.39), calls=%async_computation.1 | async-start | bytes 7077888 | tf_op jit(solution)/shard_map/all_to_all | solution.py:885
  618.3 44.8 %copy-start.47 = (f32[1,768,768]{2,1,0:T(8,128)S(1)}, f32[1,768,768]{2,1,0:T(8,128)}, u32[]{:S(2)}) copy-start(f32[1,768,768]{2,1,0:T(8,128)} %param.37) | copy-start | bytes 7077892
  680.4 46.6 %all-to-all-start.3 = ((bf16[8,288,768]{2,1,0:T(8,128)(2,1)}), bf16[8,288,768]{2,1,0:T(8,128)(2,1)}, u32[]{:S(2)}, u32[]{:S(2)}) async-start(bf16[8,288,768]{2,1,0:T(8,128)(2,1)} %fusion.42), calls=%async_computation.3 | async-start | bytes 7077888 | tf_op jit(solution)/shard_map/all_to_all | solution.py:885
  684.9 465.0 %reduce-scatter.2.cloned.1.call-start = ((), (), s32[]{:S(2)}) async-start(), calls=%async_computation.6 | async-start | bytes 37158912 | tf_op jit(solution)/shard_map/reduce_scatter | solution.py:1146
  735.6 79.5 %copy-start.4 = (bf16[384,1024]{1,0:T(8,128)(2,1)S(1)}, bf16[384,1024]{1,0:T(8,128)(2,1)}, u32[]{:S(2)}) copy-start(bf16[384,1024]{1,0:T(8,128)(2,1)} %copy-done.3) | copy-start | bytes 2359300
  833.2 7.1 collective-permute-start.4
  954.1 46.7 %copy-start.40 = (f32[3,8]{1,0:T(4,128)S(1)}, f32[3,8]{1,0:T(4,128)}, u32[]{:S(2)}) copy-start(f32[3,8]{1,0:T(4,128)} %param.47) | copy-start | bytes 292
  954.1 46.7 %copy-start.41 = (f32[3,8]{1,0:T(4,128)S(1)}, f32[3,8]{1,0:T(4,128)}, u32[]{:S(2)}) copy-start(f32[3,8]{1,0:T(4,128)} %param.48) | copy-start | bytes 292
  954.2 47.3 %copy-start.27 = (f32[768,8]{0,1:T(8,128)S(1)}, f32[768,8]{0,1:T(8,128)}, u32[]{:S(2)}) copy-start(f32[768,8]{0,1:T(8,128)} %param.44) | copy-start | bytes 73732
  954.2 47.3 %copy-start.28 = (f32[768,8]{0,1:T(8,128)S(1)}, f32[768,8]{0,1:T(8,128)}, u32[]{:S(2)}) copy-start(f32[768,8]{0,1:T(8,128)} %param.45) | copy-start | bytes 73732
  954.2 89.3 %copy-start.26 = (f32[3,768]{1,0:T(4,128)S(1)}, f32[3,768]{1,0:T(4,128)}, u32[]{:S(2)}) copy-start(f32[3,768]{1,0:T(4,128)} %param.40) | copy-start | bytes 27652
  954.2 89.3 %copy-start.31 = (f32[3,768]{1,0:T(4,128)S(1)}, f32[3,768]{1,0:T(4,128)}, u32[]{:S(2)}) copy-start(f32[3,768]{1,0:T(4,128)} %param.41) | copy-start | bytes 27652
  954.2 89.2 %copy-start.32 = (f32[3,768]{1,0:T(4,128)S(1)}, f32[3,768]{1,0:T(4,128)}, u32[]{:S(2)}) copy-start(f32[3,768]{1,0:T(4,128)} %param.42) | copy-start | bytes 27652
  (38 other events, 197.8 us)
Sparse Core Ops, SparseCore 0:
  11.2 91.4 all-gather.1
  938.2 211.6 reduce-scatter.1

commit v3 on v2

--- a/solution.py
+++ b/solution.py
@@ -40,12 +40,12 @@
 MESH_ID = pl.DeviceIdType.MESH
 whole_vmem = pl.BlockSpec(memory_space=pltpu.VMEM)
 whole_any = pl.BlockSpec(memory_space=pl.ANY)
-line_rows = 128
-line_lag = 3
+line_rows = 64
+line_lag = 2
 
 
 def sum_line_kernel(
-    count, meets_all, prologue, epilogue, n_extra, n_aux, n_scratch, part_ref, *refs
+    count, meets_all, prologue, epilogue, ending, n_extra, n_aux, n_scratch, part_ref, *refs
 ):
     extras = refs[:n_extra]
     out_ref = refs[n_extra]
@@ -122,7 +122,7 @@
         lax.fori_loop(0, count, push, 0)
 
     if prologue is not None:
-        prologue(rank, extras, aux, scratch)
+        prologue(rank, inner, extras, aux, scratch)
 
     @pl.when(inner)
     def _():
@@ -162,9 +162,20 @@
 
         lax.fori_loop(0, count, finish, 0)
 
+    if ending is not None:
+        ending(inner, end_peer, extras, aux, scratch)
+
 
 def sum_line(
-    part, extras, aux_shapes, epilogue, collective_id, prologue=None, scratch=(), meets_all=False
+    part,
+    extras,
+    aux_shapes,
+    epilogue,
+    collective_id,
+    prologue=None,
+    scratch=(),
+    meets_all=False,
+    ending=None,
 ):
     tokens, width = part.shape
     count = tokens // line_rows
@@ -176,6 +187,7 @@
             meets_all,
             prologue,
             epilogue,
+            ending,
             len(extras),
             len(aux_shapes),
             len(scratch),
@@ -216,27 +228,48 @@
     return (inputs_grad, gain_grad)
 
 
-def clear_gain(rank, extras, aux, scratch):
-    aux[-1][...] = jnp.zeros_like(aux[-1])
-
-
-def add_gain(rank, ref, gain_grad):
-    ref[...] += jnp.where(rank == 1, gain_grad, 0.0)
+def clear_gain(rank, inner, extras, aux, scratch):
+    @pl.when(inner)
+    def _():
+        aux[-1][...] = jnp.zeros_like(aux[-1])
+
+
+def share_gains(inner, end_peer, extras, aux, scratch):
+    gains = aux[0]
+    copy = pltpu.make_async_remote_copy(
+        src_ref=gains,
+        dst_ref=gains,
+        send_sem=scratch[0],
+        recv_sem=scratch[1],
+        device_id={"tensor": end_peer},
+        device_id_type=MESH_ID,
+    )
+
+    @pl.when(inner)
+    def _():
+        gains[1:2, :] = extras[3][...]
+        gains[2:3, :] = extras[4][...]
+        copy.start()
+        copy.wait_send()
+
+    @pl.when(jnp.logical_not(inner))
+    def _():
+        copy.wait_recv()
 
 
 def finish_head_grad(total, span, rank, extras, aux, scratch):
     stream_two, gain = extras
     grad_two, gain_grad = norm_back_rows(stream_two[span], gain[...], total)
     aux[0][span] = grad_two
-    add_gain(rank, aux[1], gain_grad)
+    aux[1][...] += gain_grad
     return grad_two.astype(jnp.bfloat16)
 
 
-def start_router_grad(rank, extras, aux, scratch):
+def start_router_grad(rank, inner, extras, aux, scratch):
     stream_one, gain, grad_two, gate_part, gates, routes, router_low = extras
-    grad_one, logit_grad, gain_grad = aux
+    grad_one, logit_grad, target_total, gain_grad = aux
     landed, gate_send, gate_recv = scratch
-    gain_grad[...] = jnp.zeros_like(gain_grad)
+    clear_gain(rank, inner, extras, aux, scratch)
     copies = []
     for step in (1, 2, 3):
         copy = pltpu.make_async_remote_copy(
@@ -257,6 +290,8 @@
         for step in (1, 2, 3):
             piece = jnp.where(lax.rem(source + step, 4) == rank, landed[step - 1], piece)
         gate_grad = gate_grad + jnp.where(rank == source, gate_part[...], piece)
+    target_total[...] = gate_grad[2:3]
+    gate_grad = gate_grad[0:2]
     weighted = gates[...] * gate_grad
     chosen = gates[...] * (gate_grad - (weighted[0:1] + weighted[1:2]))
     experts, tokens = logit_grad.shape
@@ -266,28 +301,33 @@
     )
     logit_grad[...] = placed.astype(jnp.bfloat16)
 
+    @pl.when(inner)
+    def _():
+        grad_one[...] = lax.dot_general(
+            logit_grad[...],
+            router_low[...],
+            (((0,), (1,)), ((), ())),
+            preferred_element_type=jnp.float32,
+        )
+
 
 def finish_expert_grad(total, span, rank, extras, aux, scratch):
     stream_one, gain, grad_two, gate_part, gates, routes, router_low = extras
-    grad_one, logit_grad, gain_grad = aux
-    upstream = total + lax.dot_general(
-        logit_grad[:, span],
-        router_low[...],
-        (((0,), (1,)), ((), ())),
-        preferred_element_type=jnp.float32,
-    )
-    part, gain_part = norm_back_rows(stream_one[span], gain[...], upstream)
+    grad_one, logit_grad, target_total, gain_grad = aux
+    part, gain_part = norm_back_rows(
+        stream_one[span], gain[...], total + grad_one[span]
+    )
     result = grad_two[span] + part
     grad_one[span] = result
-    add_gain(rank, gain_grad, gain_part)
+    gain_grad[...] += gain_part
     return result.astype(jnp.bfloat16)
 
 
 def finish_input_grad(scale, total, span, rank, extras, aux, scratch):
-    embedded, gain, grad_one = extras
+    embedded, gain, grad_one = extras[:3]
     stream_zero = embedded[span].astype(jnp.float32) * scale
     part, gain_part = norm_back_rows(stream_zero, gain[...], total)
-    add_gain(rank, aux[0], gain_part)
+    aux[0][0:1, :] += gain_part
     return ((grad_one[span] + part) * scale).astype(jnp.bfloat16)
 
 
@@ -774,7 +814,7 @@
         made[buffer] = (
             jnp.dot(slope_ref[...], rows_ref[...], preferred_element_type=jnp.float32)
             + jnp.dot(seen, zero_ref[...], preferred_element_type=jnp.float32)
-        ).reshape(tile_units, unit_rows, -1)
+        ).astype(jnp.bfloat16).reshape(tile_units, unit_rows, -1)
         send(step * tile_units, tile_units)
 
     @pl.when(step == tiles)
@@ -782,10 +822,10 @@
         joint_units = joint_ref.shape[0] // unit_rows
         made[buffer, pl.ds(0, joint_units)] = jnp.dot(
             joint_ref[...], normed_ref[...], preferred_element_type=jnp.float32
-        ).reshape(joint_units, unit_rows, -1)
+        ).astype(jnp.bfloat16).reshape(joint_units, unit_rows, -1)
         made[buffer, pl.ds(joint_units, last_units - joint_units)] = jnp.dot(
             attended_ref[...], grad_ref[...], preferred_element_type=jnp.float32
-        ).reshape(last_units - joint_units, unit_rows, -1)
+        ).astype(jnp.bfloat16).reshape(last_units - joint_units, unit_rows, -1)
         send(tiles * tile_units, last_units)
         settle(1 - buffer, tile_units)
         settle(buffer, last_units)
@@ -801,7 +841,7 @@
     return pl.pallas_call(
         functools.partial(weight_grads_kernel, tile // unit_rows, tiles),
         grid=(tiles + 1,),
-        out_shape=jax.ShapeDtypeStruct((slots, unit_rows, width), jnp.float32),
+        out_shape=jax.ShapeDtypeStruct((slots, unit_rows, width), jnp.bfloat16),
         in_specs=[
             pl.BlockSpec(memory_space=pltpu.SMEM),
             pl.BlockSpec((tile, tokens), lambda k: (jnp.minimum(k, tiles - 1), 0)),
@@ -809,7 +849,7 @@
         + [whole(x) for x in (rows, ids, zero, joint, normed, attended, grad)],
         out_specs=whole_any,
         scratch_shapes=[
-            pltpu.VMEM((2, tile // unit_rows, unit_rows, width), jnp.float32),
+            pltpu.VMEM((2, tile // unit_rows, unit_rows, width), jnp.bfloat16),
             pltpu.SemaphoreType.DMA((2,)),
         ],
         compiler_params=pltpu.CompilerParams(vmem_limit_bytes=60 << 20),
@@ -877,12 +917,575 @@
     return jax.nn.gelu(values, approximate=True)
 
 
-def to_experts(buffer):
+def gelu_slope(values):
+    root = math.sqrt(2.0 / math.pi)
+    bent = jnp.tanh(root * (values + 0.044715 * values * values * values))
+    return 0.5 * (1.0 + bent) + 0.5 * values * (1.0 - bent * bent) * root * (
+        1.0 + 3.0 * 0.044715 * values * values
+    )
+
+
+def plane_peer(step):
+    chip, core = lax.axis_index("dp"), lax.axis_index("ctx")
+    row = lax.rem(chip // 2 + step // 4, 2)
+    column = lax.rem(lax.rem(chip, 2) + lax.rem(step // 2, 2), 2)
+    place = {"dp": row * 2 + column, "ctx": lax.rem(core + lax.rem(step, 2), 2)}
+    return place, place["dp"] * 2 + place["ctx"]
+
+
+def greet_plane():
+    barrier = pltpu.get_barrier_semaphore()
+    for step in range(1, 8):
+        place, _ = plane_peer(step)
+        pl.semaphore_signal(barrier, inc=1, device_id=place, device_id_type=MESH_ID)
+    pl.semaphore_wait(barrier, 7)
+
+
+def plane_copy(source, target, send_sem, recv_sem, step):
+    place, _ = plane_peer(step)
+    return pltpu.make_async_remote_copy(
+        src_ref=source.at[step],
+        dst_ref=target.at[step],
+        send_sem=send_sem.at[step],
+        recv_sem=recv_sem.at[step],
+        device_id=place,
+        device_id_type=MESH_ID,
+    )
+
+
+def slot_hits(dest_rows, expert, capacity, tokens):
+    slot = lax.broadcasted_iota(jnp.int32, (capacity, tokens), 0) + expert * capacity
+    return (slot == dest_rows[0:1, :]) | (slot == dest_rows[1:2, :])
+
+
+def token_hits(dest_columns, expert, capacity, tokens):
+    slot = lax.broadcasted_iota(jnp.int32, (tokens, capacity), 1) + expert * capacity
+    hit = (slot == dest_columns[:, 0:1]) | (slot == dest_columns[:, 1:2])
+    return jnp.where(hit, 1.0, 0.0).astype(jnp.bfloat16)
+
+
+def gate_of(routes, gates, expert, axis):
+    pick = (lambda a, k: a[k : k + 1, :]) if axis == 0 else (lambda a, k: a[:, k : k + 1])
+    return jnp.where(pick(routes, 0) == expert, pick(gates, 0), 0.0) + jnp.where(
+        pick(routes, 1) == expert, pick(gates, 1), 0.0
+    )
+
+
+def arrival(i):
+    return jnp.where(i < 2, i, 9 - i)
+
+
+def experts_kernel(
+    rows_ref, dest_rows, dest_columns, gates, routes, inner_ref, outer_ref, counts_ref,
+    mix_ref, arrived, hidden, returned, totals_ref,
+    outgoing, results, counts, send_one, recv_one, send_two, recv_two, send_count, recv_count,
+):
+    capacity = arrived.shape[1]
+    tokens = rows_ref.shape[0]
+    greet_plane()
+    counts[0] = counts_ref[...]
+
+    def send_counts(step, carry):
+        place, _ = plane_peer(step)
+        pltpu.make_async_remote_copy(
+            src_ref=counts_ref,
+            dst_ref=counts.at[step],
+            send_sem=send_count.at[step],
+            recv_sem=recv_count.at[step],
+            device_id=place,
+            device_id_type=MESH_ID,
+        ).start()
+        return carry
+
+    def dispatch(i, carry):
+        step = 7 - i
+        _, expert = plane_peer(step)
+        hit = jnp.where(slot_hits(dest_rows, expert, capacity, tokens), 1.0, 0.0).astype(jnp.bfloat16)
+        rows = jnp.dot(hit, rows_ref[...], preferred_element_type=jnp.float32).astype(jnp.bfloat16)
+
+        @pl.when(step > 0)
+        def _():
+            outgoing[step] = rows
+            plane_copy(outgoing, arrived, send_one, recv_one, step).start()
+
+        @pl.when(step == 0)
+        def _():
+            arrived[0] = rows
+
+        return carry
+
+    def work(i, carry):
+        step = arrival(i)
+
+        @pl.when(step > 0)
+        def _():
+            plane_copy(outgoing, arrived, send_one, recv_one, step).wait_recv()
+
+        before = jnp.dot(arrived[step], inner_ref[...], preferred_element_type=jnp.float32)
+        hidden[step] = before
+        active = gelu_tanh(before).astype(jnp.bfloat16)
+        part = jnp.dot(active, outer_ref[...], preferred_element_type=jnp.float32).astype(jnp.bfloat16)
+
+        @pl.when(step > 0)
+        def _():
+            results[step] = part
+            plane_copy(results, returned, send_two, recv_two, step).start()
+
+        @pl.when(step == 0)
+        def _():
+            returned[0] = part
+
+        return carry
+
+    def combine(i, carry):
+        step = arrival(i)
+        _, expert = plane_peer(step)
+        hit = token_hits(dest_columns, expert, capacity, tokens)
+        gate = gate_of(routes, gates, expert, 1)
+
+        @pl.when(step > 0)
+        def _():
+            plane_copy(results, returned, send_two, recv_two, step).wait_recv()
+
+        part = gate * jnp.dot(hit, returned[step], preferred_element_type=jnp.float32)
+
+        @pl.when(i == 0)
+        def _():
+            mix_ref[...] = part
+
+        @pl.when(i > 0)
+        def _():
+            mix_ref[...] += part
+
+        return carry
+
+    def finish(step, carry):
+        plane_copy(outgoing, arrived, send_one, recv_one, step).wait_send()
+        plane_copy(results, returned, send_two, recv_two, step).wait_send()
+        place, _ = plane_peer(step)
+        pltpu.make_async_remote_copy(
+            src_ref=counts_ref,
+            dst_ref=counts.at[step],
+            send_sem=send_count.at[step],
+            recv_sem=recv_count.at[step],
+            device_id=place,
+            device_id_type=MESH_ID,
+        ).wait()
+        return carry
+
+    lax.fori_loop(0, 8, dispatch, 0)
+    lax.fori_loop(1, 8, send_counts, 0)
+    lax.fori_loop(0, 8, work, 0)
+    lax.fori_loop(0, 8, combine, 0)
+    lax.fori_loop(1, 8, finish, 0)
+    totals_ref[...] = jnp.sum(counts[...], 0)
+
+
+def experts_forward(rows, dest, gates, routes, inner, outer, counts, capacity, collective_id):
+    tokens, width = rows.shape
+    hidden = inner.shape[1]
+    buffer = pltpu.VMEM((8, capacity, width), jnp.bfloat16)
+    return pl.pallas_call(
+        experts_kernel,
+        out_shape=[
+            jax.ShapeDtypeStruct((tokens, width), jnp.float32),
+            jax.ShapeDtypeStruct((8, capacity, width), jnp.bfloat16),
+            jax.ShapeDtypeStruct((8, capacity, hidden), jnp.float32),
+            jax.ShapeDtypeStruct((8, capacity, width), jnp.bfloat16),
+            jax.ShapeDtypeStruct(counts.shape, jnp.float32),
+        ],
+        in_specs=[whole_vmem] * 8,
+        out_specs=[whole_vmem] * 5,
+        scratch_shapes=[buffer, buffer, pltpu.VMEM((8,) + counts.shape, jnp.float32)]
+        + [pltpu.SemaphoreType.DMA((8,))] * 6,
+        compiler_params=pltpu.CompilerParams(
+            collective_id=collective_id, has_side_effects=True, vmem_limit_bytes=60 << 20
+        ),
+    )(rows, dest, dest.T, gates, routes, inner, outer, counts)
+
+
+def experts_back_kernel(
+    rows_ref, dest_rows, dest_columns, gates, routes, returned, arrived, hidden, inner_ref, outer_ref,
+    grad_ref, gate_ref, inner_grad, outer_grad,
+    outgoing, landed, results, landed_two, active, slopes, send_one, recv_one, send_two, recv_two,
+):
+    capacity = arrived.shape[1]
+    tokens = rows_ref.shape[0]
+    greet_plane()
+    gate_ref[...] = jnp.zeros_like(gate_ref)
+
+    def dispatch(i, carry):
+        step = 7 - i
+        _, expert = plane_peer(step)
+        hit = slot_hits(dest_rows, expert, capacity, tokens)
+        rows = jnp.dot(
+            jnp.where(hit, 1.0, 0.0).astype(jnp.bfloat16), rows_ref[...], preferred_element_type=jnp.float32
+        )
+        scale = jnp.sum(jnp.where(hit, gate_of(routes, gates, expert, 0), 0.0), 1, keepdims=True)
+        sent = (rows * scale).astype(jnp.bfloat16)
+
+        @pl.when(step > 0)
+        def _():
+            outgoing[step] = sent
+            plane_copy(outgoing, landed, send_one, recv_one, step).start()
+
+        @pl.when(step == 0)
+        def _():
+            landed[0] = sent
+
+        dots = jnp.sum(rows * returned[step].astype(jnp.float32), 1, keepdims=True)
+        part = jnp.sum(jnp.where(hit, dots, 0.0), 0, keepdims=True)
+        for k in range(2):
+            gate_ref[k : k + 1, :] += jnp.where(routes[k : k + 1, :] == expert, part, 0.0)
+        return carry
+
+    def work(i, carry):
+        step = arrival(i)
+
+        @pl.when(step > 0)
+        def _():
+            plane_copy(outgoing, landed, send_one, recv_one, step).wait_recv()
+
+        grad_active = lax.dot_general(
+            landed[step], outer_ref[...], (((1,), (1,)), ((), ())), preferred_element_type=jnp.float32
+        )
+        before = hidden[step]
+        slope = (grad_active * gelu_slope(before)).astype(jnp.bfloat16)
+        back = lax.dot_general(
+            slope, inner_ref[...], (((1,), (1,)), ((), ())), preferred_element_type=jnp.float32
+        ).astype(jnp.bfloat16)
+
+        @pl.when(step > 0)
+        def _():
+            results[step] = back
+            plane_copy(results, landed_two, send_two, recv_two, step).start()
+
+        @pl.when(step == 0)
+        def _():
+            landed_two[0] = back
+
+        slopes[step] = slope
+        active[step] = gelu_tanh(before).astype(jnp.bfloat16)
+        return carry
+
+    def weigh(step, carry):
+        outer_part = lax.dot_general(
+            active[step], landed[step], (((0,), (0,)), ((), ())), preferred_element_type=jnp.float32
+        )
+        inner_part = lax.dot_general(
+            arrived[step], slopes[step], (((0,), (0,)), ((), ())), preferred_element_type=jnp.float32
+        )
+
+        @pl.when(step == 0)
+        def _():
+            outer_grad[...] = outer_part
+            inner_grad[...] = inner_part
+
+        @pl.when(step > 0)
+        def _():
+            outer_grad[...] += outer_part
+            inner_grad[...] += inner_part
+
+        return carry
+
+    def combine(i, carry):
+        step = arrival(i)
+        _, expert = plane_peer(step)
+        hit = token_hits(dest_columns, expert, capacity, tokens)
+
+        @pl.when(step > 0)
+        def _():
+            plane_copy(results, landed_two, send_two, recv_two, step).wait_recv()
+
+        part = jnp.dot(hit, landed_two[step], preferred_element_type=jnp.float32)
+
+        @pl.when(i == 0)
+        def _():
+            grad_ref[...] = part
+
+        @pl.when(i > 0)
+        def _():
+            grad_ref[...] += part
+
+        return carry
+
+    def finish(step, carry):
+        plane_copy(outgoing, landed, send_one, recv_one, step).wait_send()
+        plane_copy(results, landed_two, send_two, recv_two, step).wait_send()
+        return carry
+
+    lax.fori_loop(0, 8, dispatch, 0)
+    lax.fori_loop(0, 8, work, 0)
+    lax.fori_loop(0, 8, weigh, 0)
+    lax.fori_loop(0, 8, combine, 0)
+    lax.fori_loop(1, 8, finish, 0)
+
+
+def experts_backward(rows, dest, gates, routes, returned, arrived, hidden, inner, outer, collective_id):
+    tokens, width = rows.shape
+    capacity = arrived.shape[1]
+    inside = inner.shape[1]
+    buffer = pltpu.VMEM((8, capacity, width), jnp.bfloat16)
+    inside_buffer = pltpu.VMEM((8, capacity, inside), jnp.bfloat16)
+    return pl.pallas_call(
+        experts_back_kernel,
+        out_shape=[
+            jax.ShapeDtypeStruct((tokens, width), jnp.float32),
+            jax.ShapeDtypeStruct((2, tokens), jnp.float32),
+            jax.ShapeDtypeStruct((width, inside), jnp.float32),
+            jax.ShapeDtypeStruct((inside, width), jnp.float32),
+        ],
+        in_specs=[whole_vmem] * 10,
+        out_specs=[whole_vmem] * 4,
+        scratch_shapes=[buffer] * 4
+        + [inside_buffer] * 2
+        + [pltpu.SemaphoreType.DMA((8,))] * 4,
+        compiler_params=pltpu.CompilerParams(
+            collective_id=collective_id, has_side_effects=True, vmem_limit_bytes=63 << 20
+        ),
+    )(rows, dest, dest.T, gates, routes, returned, arrived, hidden, inner, outer)
+
+
+def own_units_kernel(
+    chunks, parts_ref, small_ref, grads_ref, small_out,
+    own, other, relay, landed, small_landed,
+    own_sem, other_send, other_recv, relay_send, relay_recv, landed_send, landed_recv, small_send, small_recv,
+):
+    chip, core = lax.axis_index("dp"), lax.axis_index("ctx")
+    beside = chip + 1 - 2 * lax.rem(chip, 2)
+    across = lax.rem(chip + 2, 4)
+    opposite = across + 1 - 2 * lax.rem(across, 2)
+    places = (opposite, beside, across, chip)
+    slots = grads_ref.shape[0]
+    size = slots // chunks
+    split = (chunks + 1) // 2
+    greet_plane()
+
+    def span(q):
+        return pl.ds(q * size, size)
+
+    def fetch(k):
+        first = (places[k] * 2 + core) * slots
+        return pltpu.make_async_copy(parts_ref.at[pl.ds(first, slots)], own.at[k], own_sem.at[k])
+
+    def pass_over(k, q):
+        first = (places[k] * 2 + 1 - core) * slots + q * size
+        return pltpu.make_async_remote_copy(
+            src_ref=parts_ref.at[pl.ds(first, size)],
+            dst_ref=other.at[k, span(q)],
+            send_sem=other_send.at[k, q],
+            recv_sem=other_recv.at[k, q],
+            device_id={"ctx": 1 - core},
+            device_id_type=MESH_ID,
+        )
+
+    def to_relay(q, place):
+        return pltpu.make_async_remote_copy(
+            src_ref=own.at[0, span(q)],
+            dst_ref=relay.at[span(q)],
+            send_sem=relay_send.at[q],
+            recv_sem=relay_recv.at[q],
+            device_id={"dp": place},
+            device_id_type=MESH_ID,
+        )
+
+    def to_owner(k, q):
+        return pltpu.make_async_remote_copy(
+            src_ref=own.at[k, span(q)],
+            dst_ref=landed.at[k - 1, span(q)],
+            send_sem=landed_send.at[k - 1, q],
+            recv_sem=landed_recv.at[k - 1, q],
+            device_id={"dp": places[k]},
+            device_id_type=MESH_ID,
+        )
+
+    def small_copy(step):
+        place, _ = plane_peer(step)
+        return pltpu.make_async_remote_copy(
+            src_ref=small_ref,
+            dst_ref=small_landed.at[chip * 2 + core],
+            send_sem=small_send.at[step],
+            recv_sem=small_recv.at[step],
+            device_id=place,
+            device_id_type=MESH_ID,
+        )
+
+    for k in range(4):
+        fetch(k).start()
+
+        def start(q, carry):
+            pass_over(k, q).start()
+            return carry
+
+        lax.fori_loop(0, chunks, start, 0)
+
+    def joined(k, q):
+        pass_over(k, q).wait_recv()
+        return own[k, span(q)].astype(jnp.float32) + other[k, span(q)].astype(jnp.float32)
+
+    fetch(0).wait()
+
+    def first_leg(place):
+        def leg(q, carry):
+            own[0, span(q)] = joined(0, q).astype(jnp.bfloat16)
+            to_relay(q, place).start()
+            return carry
+
+        return leg
+
+    lax.fori_loop(0, split, first_leg(beside), 0)
+    lax.fori_loop(split, chunks, first_leg(across), 0)
+    lax.fori_loop(1, 8, lambda step, carry: (small_copy(step).start(), carry)[1], 0)
+    small_landed[chip * 2 + core] = small_ref[...]
+    fetch(1).wait()
+    fetch(2).wait()
+
+    def direct(k):
+        def leg(q, carry):
+            own[k, span(q)] = joined(k, q).astype(jnp.bfloat16)
+            to_owner(k, q).start()
+            return carry
+
+        return leg
+
+    def relayed(k, place):
+        def leg(q, carry):
+            to_relay(q, place).wait_recv()
+            total = joined(k, q) + relay[span(q)].astype(jnp.float32)
+            own[k, span(q)] = total.astype(jnp.bfloat16)
+            to_owner(k, q).start()
+            return carry
+
+        return leg
+
+    lax.fori_loop(0, split, direct(1), 0)
+    lax.fori_loop(split, chunks, direct(2), 0)
+    lax.fori_loop(0, split, relayed(2, beside), 0)
+    lax.fori_loop(split, chunks, relayed(1, across), 0)
+    fetch(3).wait()
+
+    def keep(q, carry):
+        total = joined(3, q)
+        to_owner(1, q).wait_recv()
+        to_owner(2, q).wait_recv()
+        grads_ref[span(q)] = (
+            total + landed[0, span(q)].astype(jnp.float32) + landed[1, span(q)].astype(jnp.float32)
+        )
+        return carry
+
+    lax.fori_loop(0, split, keep, 0)
+    lax.fori_loop(split, chunks, keep, 0)
+
+    def finish(q, carry):
+        for k in range(4):
+            pass_over(k, q).wait_send()
+        to_owner(1, q).wait_send()
+        to_owner(2, q).wait_send()
+        return carry
+
+    lax.fori_loop(0, chunks, finish, 0)
+    lax.fori_loop(0, split, lambda q, carry: (to_relay(q, beside).wait_send(), carry)[1], 0)
+    lax.fori_loop(split, chunks, lambda q, carry: (to_relay(q, across).wait_send(), carry)[1], 0)
+    lax.fori_loop(1, 8, lambda step, carry: (small_copy(step).wait(), carry)[1], 0)
+    total = small_landed[0]
+    for source in range(1, 8):
+        total = total + small_landed[source]
+    small_out[...] = total
+
+
+def own_units(parts, small, slots, collective_id):
+    unit = parts.shape[1:]
+    chunks = max(k for k in range(1, 8) if slots % k == 0)
+    block = pltpu.VMEM((4, slots) + unit, jnp.bfloat16)
+    return pl.pallas_call(
+        functools.partial(own_units_kernel, chunks),
+        out_shape=[
+            jax.ShapeDtypeStruct((slots,) + unit, jnp.float32),
+            jax.ShapeDtypeStruct(small.shape, jnp.float32),
+        ],
+        in_specs=[whole_any, whole_vmem],
+        out_specs=[whole_vmem] * 2,
+        scratch_shapes=[
+            block,
+            block,
+            pltpu.VMEM((slots,) + unit, jnp.bfloat16),
+            pltpu.VMEM((2, slots) + unit, jnp.bfloat16),
+            pltpu.VMEM((8,) + small.shape, jnp.float32),
+            pltpu.SemaphoreType.DMA((4,)),
+            pltpu.SemaphoreType.DMA((4, chunks)),
+            pltpu.SemaphoreType.DMA((4, chunks)),
+            pltpu.SemaphoreType.DMA((chunks,)),
+            pltpu.SemaphoreType.DMA((chunks,)),
+            pltpu.SemaphoreType.DMA((2, chunks)),
+            pltpu.SemaphoreType.DMA((2, chunks)),
+            pltpu.SemaphoreType.DMA((8,)),
+            pltpu.SemaphoreType.DMA((8,)),
+        ],
+        compiler_params=pltpu.CompilerParams(
+            collective_id=collective_id, has_side_effects=True, vmem_limit_bytes=56 << 20
+        ),
+    )(parts, small)
+
+
+def to_plane(buffer):
     return lax.all_to_all(buffer, ("dp", "ctx"), split_axis=0, concat_axis=0, tiled=True)
 
 
-def from_experts(buffer):
-    return lax.all_to_all(buffer, ("dp", "ctx"), split_axis=0, concat_axis=0, tiled=True)
+def plain_hits(dest, experts, capacity):
+    slots = lax.broadcasted_iota(jnp.int32, (experts * capacity, dest.shape[1]), 0)
+    return [slots == dest[k : k + 1] for k in range(2)]
+
+
+def plain_forward(rows, dest, gates, inner, outer, owners, capacity):
+    width = rows.shape[1]
+    hits = plain_hits(dest, owners, capacity)
+    both = (hits[0] | hits[1]).astype(jnp.bfloat16)
+    sent = jnp.dot(both, rows, preferred_element_type=jnp.float32).astype(jnp.bfloat16)
+    arrived = to_plane(sent.reshape(owners, capacity, width))
+    hidden = jnp.einsum("ocd,df->ocf", arrived, inner, preferred_element_type=jnp.float32)
+    active = gelu_tanh(hidden).astype(jnp.bfloat16)
+    part = jnp.einsum("ocf,fd->ocd", active, outer, preferred_element_type=jnp.float32)
+    returned = to_plane(part.astype(jnp.bfloat16))
+    flat = returned.reshape(owners * capacity, width)
+    mix = sum(
+        gates[:, k : k + 1]
+        * lax.dot_general(
+            hits[k].astype(jnp.bfloat16),
+            flat,
+            (((0,), (0,)), ((), ())),
+            preferred_element_type=jnp.float32,
+        )
+        for k in range(2)
+    )
+    return (mix, arrived, hidden, returned)
+
+
+def plain_backward(rows, dest, gates, returned, arrived, hidden, inner, outer):
+    owners, capacity, width = arrived.shape
+    hits = plain_hits(dest, owners, capacity)
+    both = (hits[0] | hits[1]).astype(jnp.bfloat16)
+    slot_scale = jnp.sum(
+        jnp.where(hits[0], gates[0:1], 0.0) + jnp.where(hits[1], gates[1:2], 0.0), 1, keepdims=True
+    )
+    slot_grads = jnp.dot(both, rows, preferred_element_type=jnp.float32)
+    sent = (slot_grads * slot_scale).astype(jnp.bfloat16)
+    flat = returned.reshape(owners * capacity, width)
+    dots = jnp.sum(slot_grads * flat.astype(jnp.float32), 1, keepdims=True)
+    gate_part = jnp.concatenate(
+        [jnp.sum(jnp.where(hit, dots, 0.0), 0, keepdims=True) for hit in hits], 0
+    )
+    landed = to_plane(sent.reshape(owners, capacity, width))
+    grad_active = jnp.einsum("ocd,fd->ocf", landed, outer, preferred_element_type=jnp.float32)
+    active = gelu_tanh(hidden).astype(jnp.bfloat16)
+    slope = (grad_active * gelu_slope(hidden)).astype(jnp.bfloat16)
+    outer_grad = jnp.einsum("ocf,ocd->fd", active, landed, preferred_element_type=jnp.float32)
+    inner_grad = jnp.einsum("ocd,ocf->df", arrived, slope, preferred_element_type=jnp.float32)
+    back = jnp.einsum("ocf,df->ocd", slope, inner, preferred_element_type=jnp.float32)
+    back = to_plane(back.astype(jnp.bfloat16)).reshape(owners * capacity, width)
+    grad = lax.dot_general(
+        both, back, (((0,), (0,)), ((), ())), preferred_element_type=jnp.float32
+    )
+    return (grad, gate_part, inner_grad, outer_grad)
 
 
 def on_device(
@@ -926,7 +1529,6 @@
     head_size = model_width // (heads_here * tensor_ranks)
     hidden_here = heads_here * head_size
     experts = router.shape[1]
-    experts_here = expert_in.shape[0]
     capacity = (18 * tokens_here + 8 * experts - 1) // (8 * experts)
     table_units = vocab_here // unit_rows
     query_units = table_units + 2 * hidden_here // unit_rows
@@ -934,10 +1536,10 @@
     embed_scale = math.sqrt(model_width)
     owner_ids = owner_of[:, 0]
     unit_rank, slot_unit, slot_filled = slot_tables(owner_ids, owners, most_units)
-    loss_weights = counted.reshape(tokens_here, 2).T.astype(jnp.float32) * jnp.array(
-        [[1.0], [ahead_weight]], jnp.float32
-    )
-    weight_total = lax.psum(jnp.sum(loss_weights), ("dp", "ctx"))
+    on_square = lax.axis_size("dp") == 4 and lax.axis_size("ctx") == 2
+    counted_rows = counted.reshape(tokens_here, 2).T.astype(jnp.float32)
+    loss_weights = counted_rows * jnp.array([[1.0], [ahead_weight]], jnp.float32)
+    counts = jnp.zeros((8, 128), jnp.float32).at[0:2].set(jnp.sum(counted_rows, 1, keepdims=True))
     gathered = lax.all_gather(master[0, 0].astype(jnp.bfloat16), ("dp", "ctx"), axis=0, tiled=True)
     unit_slots = owner_ids * most_units + unit_rank
     weights_low = pull_units(gathered, unit_slots).reshape(-1, model_width)
@@ -984,37 +1586,19 @@
     chosen = jnp.einsum("tke,te->tk", route_onehot, router_scores_raw, precision=highest_precision)
     gate_values = jax.nn.softmax(chosen, -1)
     pair_kept, pair_dest = pair_slots(route_pairs, priority[0], experts, capacity)
-    slots = lax.broadcasted_iota(jnp.int32, (experts * capacity, tokens_here), 0)
-    hits = [
-        (slots == pair_dest[k * tokens_here : (k + 1) * tokens_here][None, :])
-        & pair_kept[k * tokens_here : (k + 1) * tokens_here][None, :]
-        for k in range(2)
-    ]
-    hit_low = [hit.astype(jnp.bfloat16) for hit in hits]
-    both_low = (hits[0] | hits[1]).astype(jnp.bfloat16)
-    dispatch_rows = jnp.dot(
-        both_low, normed_two_low, preferred_element_type=jnp.float32
-    ).astype(jnp.bfloat16).reshape(owners, experts_here * capacity, model_width)
-    arrived = to_experts(dispatch_rows).reshape(owners, experts_here, capacity, model_width)
-    inner_low = expert_in.astype(jnp.bfloat16)
-    outer_low = expert_out.astype(jnp.bfloat16)
-    hidden_pre = jnp.einsum(
-        "oecd,edf->oecf", arrived, inner_low, preferred_element_type=jnp.float32
-    )
-    active_low = gelu_tanh(hidden_pre).astype(jnp.bfloat16)
-    expert_part = jnp.einsum(
-        "oecf,efd->oecd", active_low, outer_low, preferred_element_type=jnp.float32
-    ).astype(jnp.bfloat16)
-    returned = from_experts(
-        expert_part.reshape(owners, experts_here * capacity, model_width)
-    ).reshape(experts * capacity, model_width)
-    pair_rows = [
-        lax.dot_general(
-            hit_low[k], returned, (((0,), (0,)), ((), ())), preferred_element_type=jnp.float32
-        )
-        for k in range(2)
-    ]
-    moe_partial = gate_values[:, 0:1] * pair_rows[0] + gate_values[:, 1:2] * pair_rows[1]
+    dest = jnp.where(pair_kept, pair_dest, -1).reshape(2, tokens_here)
+    inner_low = expert_in[0].astype(jnp.bfloat16)
+    outer_low = expert_out[0].astype(jnp.bfloat16)
+    if on_square:
+        moe_partial, arrived, hidden_pre, returned, counts = experts_forward(
+            normed_two_low, dest, gate_values, route_pairs, inner_low, outer_low, counts, capacity, 8
+        )
+    else:
+        moe_partial, arrived, hidden_pre, returned = plain_forward(
+            normed_two_low, dest, gate_values, inner_low, outer_low, owners, capacity
+        )
+        counts = lax.psum(counts, ("dp", "ctx"))
+    weight_total = counts[0, 0] + ahead_weight * counts[1, 0]
     head_low, stream_two = sum_line(
         moe_partial, [stream_one, gain_rows[2]], [stream_shape], finish_mixture, 3
     )
@@ -1032,9 +1616,6 @@
     slopes, grad_head, target_sums = head_back(
         weights_low, head_low, logsum_vocab, local_targets, weight_rows, vocab_here
     )
-    loss_local = (
-        jnp.sum(weight_rows[2] * logsum_vocab[0]) * (my_rank == 0) - jnp.sum(target_sums)
-    )
     grad_two_low, grad_two, gain_grad_three = sum_line(
         grad_head,
         [stream_two, gain_rows[2]],
@@ -1043,55 +1624,41 @@
         4,
         prologue=clear_gain,
     )
-    slot_scale = jnp.sum(
-        jnp.where(hits[0], gate_values[:, 0][None, :], 0.0)
-        + jnp.where(hits[1], gate_values[:, 1][None, :], 0.0),
-        1,
-    )
-    slot_grads = jnp.dot(both_low, grad_two_low, preferred_element_type=jnp.float32)
-    grad_dispatch = (
-        (slot_grads * slot_scale[:, None])
-        .astype(jnp.bfloat16)
-        .reshape(owners, experts_here * capacity, model_width)
-    )
-    slot_dots = jnp.sum(slot_grads * returned.astype(jnp.float32), 1)
-    gate_part = jnp.stack([jnp.sum(jnp.where(hit, slot_dots[:, None], 0.0), 0) for hit in hits])
-    grad_arrived = to_experts(grad_dispatch).reshape(owners, experts_here, capacity, model_width)
-    grad_active = jnp.einsum(
-        "oecd,efd->oecf", grad_arrived, outer_low, preferred_element_type=jnp.float32
-    )
-    outer_grad = jnp.einsum(
-        "oecf,oecd->efd", active_low, grad_arrived, preferred_element_type=jnp.float32
-    )
-    gelu_values, gelu_back = jax.vjp(gelu_tanh, hidden_pre)
-    grad_hidden = gelu_back(grad_active)[0].astype(jnp.bfloat16)
-    inner_grad = jnp.einsum(
-        "oecd,oecf->edf", arrived, grad_hidden, preferred_element_type=jnp.float32
-    )
-    grad_back = jnp.einsum(
-        "oecf,edf->oecd", grad_hidden, inner_low, preferred_element_type=jnp.float32
-    ).astype(jnp.bfloat16)
-    grad_returned = from_experts(
-        grad_back.reshape(owners, experts_here * capacity, model_width)
-    ).reshape(experts * capacity, model_width)
-    moe_grad_part = lax.dot_general(
-        both_low, grad_returned, (((0,), (0,)), ((), ())), preferred_element_type=jnp.float32
-    )
-    gate_block = pltpu.VMEM((3, 2, tokens_here), jnp.float32)
-    grad_one_low, grad_one, logit_grad, gain_grad_two = sum_line(
+    gate_rows = gate_values.T
+    if on_square:
+        moe_grad_part, gate_part, inner_grad, outer_grad = experts_backward(
+            grad_two_low,
+            dest,
+            gate_rows,
+            route_pairs.T,
+            returned,
+            arrived,
+            hidden_pre,
+            inner_low,
+            outer_low,
+            9,
+        )
+    else:
+        moe_grad_part, gate_part, inner_grad, outer_grad = plain_backward(
+            grad_two_low, dest, gate_rows, returned, arrived, hidden_pre, inner_low, outer_low
+        )
+    gate_part = jnp.concatenate([gate_part, target_sums, jnp.zeros_like(target_sums)], 0)
+    gate_block = pltpu.VMEM((3, 4, tokens_here), jnp.float32)
+    grad_one_low, grad_one, logit_grad, target_total, gain_grad_two = sum_line(
         moe_grad_part,
         [
             stream_one,
             gain_rows[1],
             grad_two,
             gate_part,
-            gate_values.T,
+            gate_rows,
             route_pairs.T,
             router_low,
         ],
         [
             stream_shape,
             jax.ShapeDtypeStruct((experts, tokens_here), jnp.bfloat16),
+            jax.ShapeDtypeStruct((1, tokens_here), jnp.float32),
             gain_shape,
         ],
         finish_expert_grad,
@@ -1100,9 +1667,8 @@
         scratch=(gate_block, pltpu.SemaphoreType.DMA((3,)), pltpu.SemaphoreType.DMA((3,))),
         meets_all=True,
     )
-    router_grad = lax.dot_general(
-        normed_two_low, logit_grad, (((0,), (1,)), ((), ())), preferred_element_type=jnp.float32
-    )
+    router_grad = jnp.dot(logit_grad, normed_two_low, preferred_element_type=jnp.float32)
+    loss_local = jnp.sum(weight_rows[2:3] * logsum_vocab) - jnp.sum(target_total)
     query_grad, pair_grad, before_grad, bias_lines = attention_back(
         rel_bias,
         joint,
@@ -1118,15 +1684,17 @@
     joint_grad = jnp.concatenate([query_grad, pair_grad_low], 0)
     distances = 2 * (half_length // BLOCK)
     bias_grad = jnp.sum(bias_lines, 1).reshape(heads_here, distances)
-    zero_grad_low, gain_grad_one = sum_line(
+    zero_grad_low, gain_grads = sum_line(
         lax.dot_general(
             joint_grad, joint_low, (((0,), (0,)), ((), ())), preferred_element_type=jnp.float32
         ),
-        [embedded, gain_rows[0], grad_one],
-        [gain_shape],
+        [embedded, gain_rows[0], grad_one, gain_grad_two, gain_grad_three],
+        [jax.ShapeDtypeStruct((8, model_width), jnp.float32)],
         functools.partial(finish_input_grad, embed_scale),
         6,
         prologue=clear_gain,
+        scratch=(pltpu.SemaphoreType.DMA, pltpu.SemaphoreType.DMA),
+        ending=share_gains,
     )
     my_units = jnp.take(slot_unit, my_owner, axis=0)
     my_filled = jnp.take(slot_filled, my_owner, axis=0)[:, None, None]
@@ -1143,23 +1711,31 @@
         attended,
         grad_one_low,
     )
-    summed = lax.psum_scatter(outgoing, ("dp", "ctx"), scatter_dimension=0, tiled=True)
-    mine = jnp.where(my_filled, summed, 0.0)
-    gains_grad, loss_total = lax.psum(
-        (jnp.concatenate([gain_grad_one, gain_grad_two, gain_grad_three], 0), loss_local),
-        ("dp", "ctx", "tensor"),
-    )
-    router_grad, bias_grad = lax.psum((router_grad, bias_grad), ("dp", "ctx"))
-    loss_totals = jnp.stack([loss_total, weight_total])
+    bias_row = jnp.concatenate([bias_grad.reshape(-1), loss_local[None]])
+    bias_row = jnp.pad(bias_row, (0, model_width - bias_row.shape[0]))[None]
+    small = jnp.concatenate([gain_grads[:3], router_grad, bias_row], 0)
+    small = jnp.pad(small, ((0, -small.shape[0] % 8), (0, 0)))
+    if on_square:
+        mine, small = own_units(outgoing, small, most_units, 10)
+    else:
+        mine = lax.psum_scatter(
+            outgoing.astype(jnp.float32), ("dp", "ctx"), scatter_dimension=0, tiled=True
+        )
+        small = lax.psum(small, ("dp", "ctx"))
+    mine = jnp.where(my_filled, mine, 0.0)
+    gains_grad = small[:3]
+    router_grad = small[3 : 3 + experts].T
+    bias_grad = small[3 + experts, : rel_bias.size].reshape(rel_bias.shape)
+    loss_totals = jnp.stack([small[3 + experts, rel_bias.size], weight_total])
     slot_rates = unit_rates(my_units, table_units, query_units, value_units)[:, None, None]
     master_new, master_first_new, master_second_new = adam_update(
         master[0, 0], master_first[0, 0], master_second[0, 0], mine, slot_rates, decay_rate
     )
     inner_new, inner_first_new, inner_second_new = adam_update(
-        expert_in, expert_in_first, expert_in_second, inner_grad, rate_inner, decay_rate
+        expert_in, expert_in_first, expert_in_second, inner_grad[None], rate_inner, decay_rate
     )
     outer_new, outer_first_new, outer_second_new = adam_update(
-        expert_out, expert_out_first, expert_out_second, outer_grad, rate_outer, decay_rate
+        expert_out, expert_out_first, expert_out_second, outer_grad[None], rate_outer, decay_rate
     )
     gains_new, gains_first_new, gains_second_new = adam_update(
         norm_gains, norm_gains_first, norm_gains_second, gains_grad, rate_gains, 0.0

time: 1180 us -> 958 us (0.81)
  Pallas kernels: 489 us -> 729 us
  blocking collectives: 212 us -> 0 us
  waiting for transfers between devices: 241 us -> 79.3 us
  matrix products: 96.1 us -> 8.26 us
    pallas_call x0 -> x3, Pallas kernels: none -> 283 us  [the longest x1 96.4 us: experts_forward(): pl.pallas_call(experts_kernel, out_shape=[jax.ShapeDtypeStruct((tokens, w...]
    psum x3 -> x0, blocking collectives: 121 us -> none  [the longest x1 48.3 us: on_device(): weight_total = lax.psum(jnp.sum(loss_weights), ('dp', 'ctx'))]
    reduce_scatter x1 -> x0, waiting for transfers between devices: 106 us -> none  [on_device(): lax.psum_scatter(outgoing, ('dp', 'ctx'), scatter_dimension=0, tiled=True)]
    all_to_all x2 -> x0, blocking collectives: 91.1 us -> none  [to_experts(): lax.all_to_all(buffer, ('dp', 'ctx'), split_axis=0, concat_axis=0, tiled=...]
    dot_general x12 -> x1, matrix products: 88.2 us -> 1.72 us  [on_device(): jnp.dot(logit_grad, normed_two_low, preferred_element_type=jnp.float32)]
    all_to_all x2 -> x0, waiting for transfers between devices: 42 us -> none  [from_experts(): lax.all_to_all(buffer, ('dp', 'ctx'), split_axis=0, concat_axis=0, tiled=...]
    pallas_call x5, Pallas kernels: 316 us -> 277 us  [sum_line(): pl.pallas_call(functools.partial(sum_line_kernel, count, meets_all, prolo...]
    sub x3 -> x5, other arithmetic: 1.88 us -> 15.5 us  [adam_update(): weight - step_rate * (moment_hat / (jnp.sqrt(square_hat) + adam_epsilon)...]
  transfers between devices with their start and end apart: 9 -> 6, of which waited for: 4 -> 1; matrix products, arithmetic and copies ran while one was open for 7% -> 4% of each run, Pallas kernels for 5% -> 5%
where the time goes in v3:
time: 958 us; the launch traced here: 948 us
  Pallas kernels  729 us (76%)
  waiting for transfers between devices  79.3 us (8%)
  other arithmetic  66.7 us (7%)
  local copies, waits for them, and re-layouts  39 us (4%)
  between operations  17.9 us (2%)
    pallas_call x5, Pallas kernels, sum_line(): pl.pallas_call(functools.partial(sum_line_kernel, count, meets_all, prolo...  277 us
    pallas_call x1, Pallas kernels, experts_forward(): pl.pallas_call(experts_kernel, out_shape=[jax.ShapeDtypeStruct((tokens, w...  96.4 us
    pallas_call x1, Pallas kernels, experts_backward(): pl.pallas_call(experts_back_kernel, out_shape=[jax.ShapeDtypeStruct((toke...  95.1 us
    pallas_call x1, Pallas kernels, own_units(): pl.pallas_call(functools.partial(own_units_kernel, chunks), out_shape=[ja...  91.1 us
    all_gather x1, waiting for transfers between devices, on_device(): lax.all_gather(master[0, 0].astype(jnp.bfloat16), ('dp', 'ctx'), axis=0,...  79.3 us
    pallas_call x1, Pallas kernels, head_back(): pl.pallas_call(functools.partial(head_back_kernel, tile), grid=(vocab //...  44 us
    pallas_call x1, Pallas kernels, weight_grads(): pl.pallas_call(functools.partial(weight_grads_kernel, tile // unit_rows,...  34 us
    pallas_call x1, Pallas kernels, gather_line(): pl.pallas_call(functools.partial(gather_line_kernel, count), out_shape=[j...  28.8 us
  transfers between devices with their start and end apart: 6, of which 1 were waited for; matrix products, arithmetic and copies ran while one was open for 4% of the time, Pallas kernels for 5%

profile of v3, /device:TPU:0, one launch (start us, length us, event | category | flops | bytes accessed | tf_op | source)
XLA Modules:
  0.0 948.5 jit_solution(1350844178365970727)
XLA Ops:
  7.3 3.8 bitcast_convert_fusion
  19.6 3.8 convert_bitcast_fusion
  23.5 79.3 %all-gather.2.cloned.1.call-done.source_ref = bf16[168,64,768]{2,1,0:T(8,128)(2,1)} async-done(((bf16[21,64,768]{2,1,0:T(8,128)(2,1)}), bf16[168,64,768]{2,1,0:T(8,128)(2,1)}) %all-gather.2.cloned.1.call-update) | async-done | bytes 16515088 | tf_op jit(solution)/shard_map/all_gather | solution.py:1543
  102.7 5.6 shard_map.384
  113.9 11.4 %gather_fusion = bf16[1024,768]{1,0:T(8,128)(2,1)S(1)} fusion(bf16[8768,768]{1,0:T(8,128)(2,1)} %bitcast.110, s32[1024]{0:T(1024)S(1)} %broadcast_clamp_fusion), kind=kCustom, calls=%fused_computation | custom fusion | bytes 3149824 | tf_op jit(solution)/shard_map/jit(_take)/gather | solution.py:1558
  126.1 50.3 %shard_map.385.refs_0_ = bf16[1024,768]{1,0:T(8,128)(2,1)S(1)} custom-call(bf16[1024,768]{1,0:T(8,128)(2,1)S(1)} %select_select_fusion.part_ref), custom_call_target="tpu_custom_call" | custom-call | tf_op jit(solution)/shard_map/pallas_call | solution.py:183
  184.3 12.7 %shard_map.386 = (bf16[192,1024]{1,0:T(8,128)(2,1)S(1)}, f32[3,1024,1]{2,1,0:T(8,128)S(1)}) custom-call(f32[3,8]{1,0:T(4,128)S(1)} %copy-done.21, bf16[576,1024]{1,0:T(8,128)(2,1)S(1)} %convolution_convert_fusion.own_ref, bf16[384,1024]{1,0:T(8,128)(2,1)S(1)} %collective-permute-done.before_ref), custom_call_target="tpu_custom_call" | custom-call | tf_op jit(solution)/shard_map/pallas_call | solution.py:482
  198.2 28.8 %shard_map.387 = bf16[4,192,1024]{2,1,0:T(8,128)(2,1)S(1)} custom-call(bf16[192,1024]{1,0:T(8,128)(2,1)S(1)} %get-tuple-element.63.refs_0_.attended_ref), custom_call_target="tpu_custom_call" | custom-call | tf_op jit(solution)/shard_map/pallas_call | solution.py:366
  231.0 15.3 %fusion.14 = f32[1024,2]{1,0:T(8,128)} fusion(f32[1024,8]{1,0:T(8,128)S(1)} %fusion.35, s32[1024,2]{1,0:T(8,128)S(1)} %copy-done.29), kind=kLoop, calls=%fused_computation.38 | loop fusion | flops 47104 | bytes 49152
  251.2 96.4 %shard_map.388 = (f32[1024,768]{1,0:T(8,128)}, bf16[8,288,768]{2,1,0:T(8,128)(2,1)}, f32[8,288,768]{2,1,0:T(8,128)}, bf16[8,288,768]{2,1,0:T(8,128)(2,1)}, f32[8,128]{1,0:T(8,128)}) custom-call(bf16[1024,768]{1,0:T(8,128)(2,1)} %copy-done.25, s32[2,1024]{1,0:T(2,128)} %copy-done.35, s32[1024,2]{1,0:T(8,128)} %copy.75.dest_columns, f32[1024,2]{1,0:T(8,128)} %copy.76.gates, ...), custom_call_target="tpu_custom_call" | custom-call | tf_op jit(solution)/shard_map/pallas_call | solution.py:1088
  350.3 55.6 %shard_map.389 = (bf16[1024,768]{1,0:T(8,128)(2,1)S(1)}, f32[1024,768]{1,0:T(8,128)S(1)}) custom-call(f32[1024,768]{1,0:T(8,128)} %get-tuple-element.64.part_ref, f32[1024,768]{1,0:T(8,128)} %copy-done.24, f32[1,768]{1,0:T(1,128)S(1)} %get-tuple-element.143.refs_1_), custom_call_target="tpu_custom_call" | custom-call | tf_op jit(solution)/shard_map/pallas_call | solution.py:183
  408.7 23.3 %shard_map.390.stats_ref = f32[2,1024]{1,0:T(2,128)} custom-call(bf16[8768,768]{1,0:T(8,128)(2,1)} %bitcast.111, bf16[1024,768]{1,0:T(8,128)(2,1)} %copy-done.3), custom_call_target="tpu_custom_call" | custom-call | tf_op jit(solution)/shard_map/pallas_call | solution.py:666
  432.0 6.8 shard_map.391.logsum_ref
  440.8 44.0 %shard_map.392 = (bf16[8000,1024]{1,0:T(8,128)(2,1)}, f32[1024,768]{1,0:T(8,128)}, f32[1,1024]{1,0:T(1,128)}) custom-call(bf16[8768,768]{1,0:T(8,128)(2,1)} %bitcast.112, bf16[1024,768]{1,0:T(8,128)(2,1)} %copy-done.3, f32[1,1024]{1,0:T(1,128)} %shard_map.391.logsum_ref, s32[2,1024]{1,0:T(2,128)} %subtract_bitcast_fusion.wanted_ref, ...), custom_call_target="tpu_custom_call" | custom-call | tf_op jit(solution)/shard_map/pallas_call | solution.py:758
  484.8 45.9 %shard_map.393 = (bf16[1024,768]{1,0:T(8,128)(2,1)S(1)}, f32[1024,768]{1,0:T(8,128)S(1)}, f32[1,768]{1,0:T(1,128)S(1)}) custom-call(f32[1024,768]{1,0:T(8,128)} %get-tuple-element.69.part_ref, f32[1024,768]{1,0:T(8,128)} %copy-done.10, f32[1,768]{1,0:T(1,128)S(1)} %get-tuple-element.143.refs_1_), custom_call_target="tpu_custom_call" | custom-call | tf_op jit(solution)/shard_map/pallas_call | solution.py:183
  533.5 95.1 %shard_map.394 = (f32[1024,768]{1,0:T(8,128)}, f32[2,1024]{1,0:T(2,128)}, f32[768,768]{1,0:T(8,128)}, f32[768,768]{1,0:T(8,128)}) custom-call(bf16[1024,768]{1,0:T(8,128)(2,1)} %copy-done.14, s32[2,1024]{1,0:T(2,128)} %copy-done.35, s32[1024,2]{1,0:T(8,128)} %copy.75.dest_columns, f32[2,1024]{1,0:T(2,128)} %fusion.45.gates.refs_4_, s32[2,1024]{1,0:T(2,128)} %bitcast.120, ...), custom_call_target="tpu_custom_call" | custom-call | tf_op jit(solution)/shard_map/pallas_call | solution.py:1230
  629.5 82.7 %shard_map.395 = (bf16[1024,768]{1,0:T(8,128)(2,1)S(1)}, f32[1024,768]{1,0:T(8,128)S(1)}, bf16[8,1024]{1,0:T(8,128)(2,1)S(1)}, f32[1,1024]{1,0:T(1,128)S(1)}, f32[1,768]{1,0:T(1,128)S(1)}) custom-call(f32[1024,768]{1,0:T(8,128)} %get-tuple-element.75.part_ref, f32[1024,768]{1,0:T(8,128)} %copy-done.24, f32[1,768]{1,0:T(1,128)S(1)} %get-tuple-element.142.refs_1_, ...), custom_call_target="tpu_custom_call" | custom-call | tf_op jit(solution)/shard_map/pallas_call | solution.py:183
  715.6 14.2 %shard_map.396 = (bf16[192,1024]{1,0:T(8,128)(2,1)S(1)}, f32[384,1024]{1,0:T(8,128)S(1)}, bf16[384,1024]{1,0:T(8,128)(2,1)S(1)}, f32[24,256]{1,0:T(8,128)S(1)}) custom-call(f32[3,8]{1,0:T(4,128)S(1)} %copy-done.21, bf16[576,1024]{1,0:T(8,128)(2,1)S(1)} %copy-done.5, bf16[384,1024]{1,0:T(8,128)(2,1)S(1)} %copy-done.9, f32[3,1024,1]{2,1,0:T(8,128)} %copy-done.17, ...), custom_call_target="tpu_custom_call" | custom-call | tf_op jit(solution)/shard_map/pallas_call | solution.py:621
  736.4 8.0 multiply_subtract_fusion.1
  745.1 4.1 multiply_subtract_fusion
  754.9 42.3 %shard_map.397 = (bf16[1024,768]{1,0:T(8,128)(2,1)S(1)}, f32[8,768]{1,0:T(8,128)S(1)}) custom-call(f32[1024,768]{1,0:T(8,128)} %fusion.27.part_ref, bf16[1024,768]{1,0:T(8,128)(2,1)S(1)} %copy-done.2, f32[1,768]{1,0:T(1,128)S(1)} %get-tuple-element.141.refs_1_, f32[1024,768]{1,0:T(8,128)} %copy-done.7, f32[1,768]{1,0:T(1,128)S(1)} %get-tuple-element.84.refs_3_, ...), custom_call_target="tpu_custom_call" | custom-call | tf_op jit(solution)/shard_map/pallas_call | solution.py:183
  798.4 34.0 %shard_map.398.parts_ref = bf16[168,64,768]{2,1,0:T(8,128)(2,1)} custom-call(s32[137]{0:T(256)} %copy-done.22, bf16[8000,1024]{1,0:T(8,128)(2,1)} %get-tuple-element.67.slope_ref, bf16[1024,768]{1,0:T(8,128)(2,1)} %copy-done.3, s32[1,1024]{1,0:T(1,128)} %copy-done.37, bf16[1024,768]{1,0:T(8,128)(2,1)} %copy-done.13, ...), custom_call_target="tpu_custom_call" | custom-call | tf_op jit(solution)/shard_map/pallas_call | solution.py:841
  833.1 91.1 %shard_map.399 = (f32[21,64,768]{2,1,0:T(8,128)}, f32[16,768]{1,0:T(8,128)}) custom-call(bf16[168,64,768]{2,1,0:T(8,128)(2,1)} %shard_map.398.parts_ref, f32[16,768]{1,0:T(8,128)} %select_maximum_fusion.small_ref), custom_call_target="tpu_custom_call" | custom-call | tf_op jit(solution)/shard_map/pallas_call | solution.py:1400
  930.8 10.4 %fusion.26 = (f32[1,1,21,64,768]{4,3,2,1,0:T(8,128)}, f32[1,1,21,64,768]{4,3,2,1,0:T(8,128)}, f32[1,1,21,64,768]{4,3,2,1,0:T(8,128)}) fusion(f32[21,64,768]{2,1,0:T(8,128)} %get-tuple-element.92, pred[21]{0:T(512)(128)(4,1)S(1)} %select_reduce_fusion.1, f32[1,1,21,64,768]{4,3,2,1,0:T(8,128)} %param.35, f32[1,1,21,64,768]{4,3,2,1,0:T(8,128)} %param.34, ...), kind=kLoop, calls=%fused_computation.108 | loop fusion | flops 16515072 | bytes 28901480 | tf_op jit(solution)/shard_map/broadcast_in_dim | solution.py:1753
  (196 shorter events, 65.6 us)
Async XLA Ops:
  7.2 95.5 %all-gather.2.cloned.1.call-start = ((), (), s32[]{:S(2)}) async-start(), calls=%async_computation | async-start | bytes 18579456 | tf_op jit(solution)/shard_map/all_gather | solution.py:1543
  18.8 84.0 %copy-start.22 = (s32[137]{0:T(256)}, s32[137]{0:T(256)S(1)}, u32[]{:S(2)}) copy-start(s32[137]{0:T(256)S(1)} %multiply_add_fusion.2.slots_ref.place_ref) | copy-start | bytes 1648
  108.4 73.8 %collective-permute-start.3 = (bf16[192,768]{1,0:T(8,128)(2,1)S(1)}, bf16[192,768]{1,0:T(8,128)(2,1)S(1)}, u32[]{:S(2)}, u32[]{:S(2)}) collective-permute-start(bf16[192,768]{1,0:T(8,128)(2,1)S(1)} %bitcast.113), channel_id=1, source_target_pairs={{0,1},{1,2},{2,3},{3,0},{4,5},{5,6},{6,7},{7,4},{8,9},{9,10},{10,1... | collective-permute-start | bytes 884744 | tf_op jit(solution)/shard_map/ppermute | solution.py:1549
  109.9 71.2 %collective-permute-start.2 = (bf16[192,768]{1,0:T(8,128)(2,1)S(1)}, bf16[192,768]{1,0:T(8,128)(2,1)}, u32[]{:S(2)}, u32[]{:S(2)}) collective-permute-start(bf16[192,768]{1,0:T(8,128)(2,1)S(1)} %bitcast.114), channel_id=1, source_target_pairs={{0,2},{1,3},{2,0},{3,1},{4,6},{5,7},{6,4},{7,5},{8,10},{9,11},{10,... | collective-permute-start | bytes 884744 | tf_op jit(solution)/shard_map/ppermute | solution.py:1549
  112.3 67.8 %collective-permute-start.1 = (bf16[192,768]{1,0:T(8,128)(2,1)S(1)}, bf16[192,768]{1,0:T(8,128)(2,1)}, u32[]{:S(2)}, u32[]{:S(2)}) collective-permute-start(bf16[192,768]{1,0:T(8,128)(2,1)S(1)} %bitcast.115), channel_id=1, source_target_pairs={{0,3},{1,0},{2,1},{3,2},{4,7},{5,4},{6,5},{7,6},{8,11},{9,8},{10,9... | collective-permute-start | bytes 884744 | tf_op jit(solution)/shard_map/ppermute | solution.py:1549
  113.8 63.5 %copy-start.33 = (bf16[9,64,768]{2,1,0:T(8,128)(2,1)}, bf16[9,64,768]{2,1,0:T(8,128)(2,1)S(1)}, u32[]{:S(2)}) copy-start(bf16[9,64,768]{2,1,0:T(8,128)(2,1)S(1)} %slice.102) | copy-start | bytes 2654212
  176.4 50.6 %copy-start.1 = (bf16[1024,768]{1,0:T(8,128)(2,1)}, bf16[1024,768]{1,0:T(8,128)(2,1)S(1)}, u32[]{:S(2)}) copy-start(bf16[1024,768]{1,0:T(8,128)(2,1)S(1)} %shard_map.385.refs_0_) | copy-start | bytes 4718596
  178.6 5.7 collective-permute-start
  184.3 12.7 %copy-start.8 = (bf16[384,1024]{1,0:T(8,128)(2,1)}, bf16[384,1024]{1,0:T(8,128)(2,1)S(1)}, u32[]{:S(2)}) copy-start(bf16[384,1024]{1,0:T(8,128)(2,1)S(1)} %collective-permute-done.before_ref) | copy-start | bytes 2359300
  198.2 30.6 %copy-start.12 = (bf16[192,1024]{1,0:T(8,128)(2,1)}, bf16[192,1024]{1,0:T(8,128)(2,1)S(1)}, u32[]{:S(2)}) copy-start(bf16[192,1024]{1,0:T(8,128)(2,1)S(1)} %get-tuple-element.63.refs_0_.attended_ref) | copy-start | bytes 1179652
  230.4 18.4 %copy-start.25 = (bf16[1024,768]{1,0:T(8,128)(2,1)}, bf16[1024,768]{1,0:T(8,128)(2,1)S(1)}, u32[]{:S(2)}) copy-start(bf16[1024,768]{1,0:T(8,128)(2,1)S(1)} %multiply_convert_fusion.rows_ref) | copy-start | bytes 4718596
  533.5 95.1 %copy-start.47 = (f32[1,1024]{1,0:T(1,128)S(1)}, f32[1,1024]{1,0:T(1,128)}, u32[]{:S(2)}) copy-start(f32[1,1024]{1,0:T(1,128)} %get-tuple-element.78) | copy-start | bytes 12292
  533.5 95.9 %copy-start.19 = (s32[1,1024,2]{1,2,0:T(2,128)S(1)}, s32[1,1024,2]{1,2,0:T(2,128)}, u32[]{:S(2)}) copy-start(s32[1,1024,2]{1,2,0:T(2,128)} %param.30) | copy-start | bytes 24580
  533.5 95.9 %copy-start.20 = (f32[2,1024]{1,0:T(2,128)S(1)}, f32[2,1024]{1,0:T(2,128)}, u32[]{:S(2)}) copy-start(f32[2,1024]{1,0:T(2,128)} %fusion.45.gates.refs_4_) | copy-start | bytes 24580
  629.5 86.2 %copy-start.5 = (bf16[576,1024]{1,0:T(8,128)(2,1)S(1)}, bf16[576,1024]{1,0:T(8,128)(2,1)}, u32[]{:S(2)}) copy-start(bf16[576,1024]{1,0:T(8,128)(2,1)} %copy-done.4) | copy-start | bytes 3538948
  629.5 86.2 %copy-start.9 = (bf16[384,1024]{1,0:T(8,128)(2,1)S(1)}, bf16[384,1024]{1,0:T(8,128)(2,1)}, u32[]{:S(2)}) copy-start(bf16[384,1024]{1,0:T(8,128)(2,1)} %copy-done.8) | copy-start | bytes 2359300
  733.8 15.4 %collective-permute-start.4 = (bf16[384,1024]{1,0:T(8,128)(2,1)}, bf16[384,1024]{1,0:T(8,128)(2,1)}, u32[]{:S(2)}, u32[]{:S(2)}) collective-permute-start(bf16[384,1024]{1,0:T(8,128)(2,1)} %copy-done.23), channel_id=1, source_target_pairs={{4,0},{5,1},{6,2},{7,3},{12,8},{13,9},{14,10},{15,11},{20,16},{21,... | collective-permute-start | bytes 2359304 | tf_op jit(solution)/shard_map/ppermute | solution.py:38
  736.4 8.7 copy-start.32
  833.0 94.4 %copy-start.43 = (f32[3,768]{1,0:T(4,128)S(1)}, f32[3,768]{1,0:T(4,128)}, u32[]{:S(2)}) copy-start(f32[3,768]{1,0:T(4,128)} %param.43) | copy-start | bytes 27652
  833.1 94.4 %copy-start.44 = (f32[3,768]{1,0:T(4,128)S(1)}, f32[3,768]{1,0:T(4,128)}, u32[]{:S(2)}) copy-start(f32[3,768]{1,0:T(4,128)} %param.44) | copy-start | bytes 27652
  833.1 95.7 %copy-start.40 = (f32[768,8]{0,1:T(8,128)S(1)}, f32[768,8]{0,1:T(8,128)}, u32[]{:S(2)}) copy-start(f32[768,8]{0,1:T(8,128)} %param.46) | copy-start | bytes 73732
  833.1 95.7 %copy-start.41 = (f32[768,8]{0,1:T(8,128)S(1)}, f32[768,8]{0,1:T(8,128)}, u32[]{:S(2)}) copy-start(f32[768,8]{0,1:T(8,128)} %param.47) | copy-start | bytes 73732
  833.1 97.2 %copy-start.49 = (f32[3,8]{1,0:T(4,128)S(1)}, f32[3,8]{1,0:T(4,128)}, u32[]{:S(2)}) copy-start(f32[3,8]{1,0:T(4,128)} %param.49) | copy-start | bytes 292
  833.1 97.2 %copy-start.50 = (f32[3,8]{1,0:T(4,128)S(1)}, f32[3,8]{1,0:T(4,128)}, u32[]{:S(2)}) copy-start(f32[3,8]{1,0:T(4,128)} %param.50) | copy-start | bytes 292
  (34 other events, 150.9 us)
Sparse Core Ops, SparseCore 0:
  11.2 91.4 all-gather.1

commit v4 on v3

--- a/solution.py
+++ b/solution.py
@@ -30,6 +30,7 @@
 rate_router = 0.05
 rate_biases = 0.5
 decay_rate = 0.1
+column_parts = 3
 
 
 def passed_along(value, axis, steps):
@@ -40,12 +41,11 @@
 MESH_ID = pl.DeviceIdType.MESH
 whole_vmem = pl.BlockSpec(memory_space=pltpu.VMEM)
 whole_any = pl.BlockSpec(memory_space=pl.ANY)
-line_rows = 64
 line_lag = 2
 
 
 def sum_line_kernel(
-    count, meets_all, prologue, epilogue, ending, n_extra, n_aux, n_scratch, part_ref, *refs
+    rows, count, opening, prologue, epilogue, ending, n_extra, n_aux, n_scratch, part_ref, *refs
 ):
     extras = refs[:n_extra]
     out_ref = refs[n_extra]
@@ -58,7 +58,7 @@
     end_peer = jnp.where(rank < 2, 1 - rank, 5 - rank)
     mid_peer = 3 - rank
     barrier = pltpu.get_barrier_semaphore()
-    if not meets_all:
+    if opening is None:
         pl.semaphore_signal(barrier, inc=1, device_id={"tensor": end_peer}, device_id_type=MESH_ID)
 
         @pl.when(inner)
@@ -76,8 +76,6 @@
             other = lax.rem(rank + step, 4)
             pl.semaphore_signal(barrier, inc=1, device_id={"tensor": other}, device_id_type=MESH_ID)
         pl.semaphore_wait(barrier, 3)
-
-    rows = line_rows
 
     def span(i):
         return pl.ds(pl.multiple_of(i * rows, rows), rows)
@@ -111,6 +109,9 @@
             device_id={"tensor": end_peer},
             device_id_type=MESH_ID,
         )
+
+    if opening is not None:
+        opening(rank, extras, scratch)
 
     @pl.when(jnp.logical_not(inner))
     def _():
@@ -174,17 +175,19 @@
     collective_id,
     prologue=None,
     scratch=(),
-    meets_all=False,
+    opening=None,
     ending=None,
+    rows=64,
 ):
     tokens, width = part.shape
-    count = tokens // line_rows
-    chunks = pltpu.VMEM((count, line_rows, width), jnp.bfloat16)
+    count = tokens // rows
+    chunks = pltpu.VMEM((count, rows, width), jnp.bfloat16)
     return pl.pallas_call(
         functools.partial(
             sum_line_kernel,
+            rows,
             count,
-            meets_all,
+            opening,
             prologue,
             epilogue,
             ending,
@@ -265,14 +268,11 @@
     return grad_two.astype(jnp.bfloat16)
 
 
-def start_router_grad(rank, inner, extras, aux, scratch):
-    stream_one, gain, grad_two, gate_part, gates, routes, router_low = extras
-    grad_one, logit_grad, target_total, gain_grad = aux
+def gate_copies(rank, extras, scratch):
+    gate_part = extras[3]
     landed, gate_send, gate_recv = scratch
-    clear_gain(rank, inner, extras, aux, scratch)
-    copies = []
-    for step in (1, 2, 3):
-        copy = pltpu.make_async_remote_copy(
+    return [
+        pltpu.make_async_remote_copy(
             src_ref=gate_part,
             dst_ref=landed.at[step - 1],
             send_sem=gate_send.at[step - 1],
@@ -280,9 +280,21 @@
             device_id={"tensor": lax.rem(rank + step, 4)},
             device_id_type=MESH_ID,
         )
+        for step in (1, 2, 3)
+    ]
+
+
+def send_gate_parts(rank, extras, scratch):
+    for copy in gate_copies(rank, extras, scratch):
         copy.start()
-        copies.append(copy)
-    for copy in copies:
+
+
+def start_router_grad(rank, inner, extras, aux, scratch):
+    stream_one, gain, grad_two, gate_part, gates, routes, router_low = extras
+    grad_one, logit_grad, target_total, gain_grad = aux
+    landed = scratch[0]
+    clear_gain(rank, inner, extras, aux, scratch)
+    for copy in gate_copies(rank, extras, scratch):
         copy.wait()
     gate_grad = jnp.zeros(gate_part.shape, jnp.float32)
     for source in range(4):
@@ -379,30 +391,34 @@
     )(*arrays)
 
 
-def pull_units_kernel(group, slots_ref, source_ref, out_ref, sem):
-    start = pl.program_id(0) * group
+def pull_units_kernel(parts, slots_ref, *refs):
+    sources, out_ref, sem = refs[:parts], refs[parts], refs[parts + 1]
+    width = out_ref.shape[-1] // parts
 
     def push(u, carry):
-        pltpu.make_async_copy(source_ref.at[slots_ref[start + u]], out_ref.at[u], sem).start()
+        for part in range(parts):
+            pltpu.make_async_copy(
+                sources[part].at[slots_ref[u]],
+                out_ref.at[u, :, part * width : (part + 1) * width],
+                sem,
+            ).start()
         return carry
 
-    lax.fori_loop(0, group, push, 0)
+    lax.fori_loop(0, out_ref.shape[0], push, 0)
     pltpu.make_async_copy(out_ref, out_ref, sem).wait()
 
 
-def pull_units(source, slots):
+def pull_units(sources, slots):
     count = slots.shape[0]
-    unit_bytes = math.prod(source.shape[1:]) * source.dtype.itemsize
-    group = max(k for k in range(1, count + 1) if count % k == 0 and (k <= 32 or k * unit_bytes < 15 << 20))
+    rows, width = sources[0].shape[1:]
     return pl.pallas_call(
-        functools.partial(pull_units_kernel, group),
-        grid=(count // group,),
-        out_shape=jax.ShapeDtypeStruct((count,) + source.shape[1:], source.dtype),
-        in_specs=[pl.BlockSpec(memory_space=pltpu.SMEM), whole_any],
-        out_specs=pl.BlockSpec((group,) + source.shape[1:], lambda k: (k,) + (0,) * (source.ndim - 1)),
+        functools.partial(pull_units_kernel, len(sources)),
+        out_shape=jax.ShapeDtypeStruct((count, rows, width * len(sources)), sources[0].dtype),
+        in_specs=[pl.BlockSpec(memory_space=pltpu.SMEM)] + [whole_any] * len(sources),
+        out_specs=whole_vmem,
         scratch_shapes=[pltpu.SemaphoreType.DMA],
         compiler_params=pltpu.CompilerParams(vmem_limit_bytes=40 << 20),
-    )(slots, source)
+    )(slots, *sources)
 
 
 def attention_kernel(heads, size, bias_ref, own_ref, before_ref, out_ref, logsum_ref, scores, peak, total):
@@ -977,7 +993,7 @@
 
 def experts_kernel(
     rows_ref, dest_rows, dest_columns, gates, routes, inner_ref, outer_ref, counts_ref,
-    mix_ref, arrived, hidden, returned, totals_ref,
+    mix_ref, arrived, returned, totals_ref,
     outgoing, results, counts, send_one, recv_one, send_two, recv_two, send_count, recv_count,
 ):
     capacity = arrived.shape[1]
@@ -1022,7 +1038,6 @@
             plane_copy(outgoing, arrived, send_one, recv_one, step).wait_recv()
 
         before = jnp.dot(arrived[step], inner_ref[...], preferred_element_type=jnp.float32)
-        hidden[step] = before
         active = gelu_tanh(before).astype(jnp.bfloat16)
         part = jnp.dot(active, outer_ref[...], preferred_element_type=jnp.float32).astype(jnp.bfloat16)
 
@@ -1083,19 +1098,17 @@
 
 def experts_forward(rows, dest, gates, routes, inner, outer, counts, capacity, collective_id):
     tokens, width = rows.shape
-    hidden = inner.shape[1]
     buffer = pltpu.VMEM((8, capacity, width), jnp.bfloat16)
     return pl.pallas_call(
         experts_kernel,
         out_shape=[
             jax.ShapeDtypeStruct((tokens, width), jnp.float32),
             jax.ShapeDtypeStruct((8, capacity, width), jnp.bfloat16),
-            jax.ShapeDtypeStruct((8, capacity, hidden), jnp.float32),
             jax.ShapeDtypeStruct((8, capacity, width), jnp.bfloat16),
             jax.ShapeDtypeStruct(counts.shape, jnp.float32),
         ],
         in_specs=[whole_vmem] * 8,
-        out_specs=[whole_vmem] * 5,
+        out_specs=[whole_vmem] * 4,
         scratch_shapes=[buffer, buffer, pltpu.VMEM((8,) + counts.shape, jnp.float32)]
         + [pltpu.SemaphoreType.DMA((8,))] * 6,
         compiler_params=pltpu.CompilerParams(
@@ -1105,12 +1118,17 @@
 
 
 def experts_back_kernel(
-    rows_ref, dest_rows, dest_columns, gates, routes, returned, arrived, hidden, inner_ref, outer_ref,
-    grad_ref, gate_ref, inner_grad, outer_grad,
-    outgoing, landed, results, landed_two, active, slopes, send_one, recv_one, send_two, recv_two,
+    rows_ref, dest_rows, dest_columns, gates, routes, returned, arrived, *refs
 ):
+    states, (grad_ref, gate_ref), updated = refs[:6], refs[6:8], refs[8:14]
+    held, grads, low, outgoing, landed, results, landed_two, active, slopes = refs[14:23]
+    send_one, recv_one, send_two, recv_two, load_sem, store_sem = refs[23:]
+    inner_ref, outer_ref = low.at[0], low.at[1]
     capacity = arrived.shape[1]
     tokens = rows_ref.shape[0]
+    loads = [pltpu.make_async_copy(states[k], held.at[k], load_sem.at[k]) for k in range(6)]
+    for load in loads:
+        load.start()
     greet_plane()
     gate_ref[...] = jnp.zeros_like(gate_ref)
 
@@ -1149,7 +1167,7 @@
         grad_active = lax.dot_general(
             landed[step], outer_ref[...], (((1,), (1,)), ((), ())), preferred_element_type=jnp.float32
         )
-        before = hidden[step]
+        before = jnp.dot(arrived[step], inner_ref[...], preferred_element_type=jnp.float32)
         slope = (grad_active * gelu_slope(before)).astype(jnp.bfloat16)
         back = lax.dot_general(
             slope, inner_ref[...], (((1,), (1,)), ((), ())), preferred_element_type=jnp.float32
@@ -1178,14 +1196,25 @@
 
         @pl.when(step == 0)
         def _():
-            outer_grad[...] = outer_part
-            inner_grad[...] = inner_part
+            grads[0] = inner_part
+            grads[1] = outer_part
 
         @pl.when(step > 0)
         def _():
-            outer_grad[...] += outer_part
-            inner_grad[...] += inner_part
-
+            grads[0] += inner_part
+            grads[1] += outer_part
+
+        return carry
+
+    def update(i, carry):
+        lines = grads.shape[1] // 8
+        span = pl.ds(pl.multiple_of(i * lines, lines), lines)
+        for k, rate in enumerate((rate_inner, rate_outer)):
+            fresh = adam_update(
+                held[3 * k, span], held[3 * k + 1, span], held[3 * k + 2, span], grads[k, span], rate, decay_rate
+            )
+            for n in range(3):
+                held[3 * k + n, span] = fresh[n]
         return carry
 
     def combine(i, carry):
@@ -1215,48 +1244,66 @@
         return carry
 
     lax.fori_loop(0, 8, dispatch, 0)
+    for load in loads:
+        load.wait()
+    for k in range(2):
+        low[k] = held[3 * k].astype(jnp.bfloat16)
     lax.fori_loop(0, 8, work, 0)
     lax.fori_loop(0, 8, weigh, 0)
+    lax.fori_loop(0, 8, update, 0)
+    stores = [pltpu.make_async_copy(held.at[k], updated[k], store_sem.at[k]) for k in range(6)]
+    for store in stores:
+        store.start()
     lax.fori_loop(0, 8, combine, 0)
     lax.fori_loop(1, 8, finish, 0)
-
-
-def experts_backward(rows, dest, gates, routes, returned, arrived, hidden, inner, outer, collective_id):
+    for store in stores:
+        store.wait()
+
+
+def experts_backward(rows, dest, gates, routes, returned, arrived, states, collective_id):
     tokens, width = rows.shape
     capacity = arrived.shape[1]
-    inside = inner.shape[1]
+    square = states[0].shape
     buffer = pltpu.VMEM((8, capacity, width), jnp.bfloat16)
-    inside_buffer = pltpu.VMEM((8, capacity, inside), jnp.bfloat16)
+    inside_buffer = pltpu.VMEM((8, capacity, square[1]), jnp.bfloat16)
+    state = jax.ShapeDtypeStruct(square, jnp.float32)
     return pl.pallas_call(
         experts_back_kernel,
         out_shape=[
             jax.ShapeDtypeStruct((tokens, width), jnp.float32),
             jax.ShapeDtypeStruct((2, tokens), jnp.float32),
-            jax.ShapeDtypeStruct((width, inside), jnp.float32),
-            jax.ShapeDtypeStruct((inside, width), jnp.float32),
-        ],
-        in_specs=[whole_vmem] * 10,
-        out_specs=[whole_vmem] * 4,
-        scratch_shapes=[buffer] * 4
+        ]
+        + [state] * 6,
+        in_specs=[whole_vmem] * 7 + [whole_any] * 6,
+        out_specs=[whole_vmem] * 2 + [whole_any] * 6,
+        scratch_shapes=[
+            pltpu.VMEM((6,) + square, jnp.float32),
+            pltpu.VMEM((2,) + square, jnp.float32),
+            pltpu.VMEM((2,) + square, jnp.bfloat16),
+        ]
+        + [buffer] * 4
         + [inside_buffer] * 2
-        + [pltpu.SemaphoreType.DMA((8,))] * 4,
+        + [pltpu.SemaphoreType.DMA((8,))] * 4
+        + [pltpu.SemaphoreType.DMA((6,))] * 2,
         compiler_params=pltpu.CompilerParams(
             collective_id=collective_id, has_side_effects=True, vmem_limit_bytes=63 << 20
         ),
-    )(rows, dest, dest.T, gates, routes, returned, arrived, hidden, inner, outer)
+    )(rows, dest, dest.T, gates, routes, returned, arrived, *states)
 
 
 def own_units_kernel(
-    chunks, parts_ref, small_ref, grads_ref, small_out,
-    own, other, relay, landed, small_landed,
-    own_sem, other_send, other_recv, relay_send, relay_recv, landed_send, landed_recv, small_send, small_recv,
+    chunks, parts_ref, small_ref, rates_ref, filled_ref, *refs
 ):
     chip, core = lax.axis_index("dp"), lax.axis_index("ctx")
     beside = chip + 1 - 2 * lax.rem(chip, 2)
     across = lax.rem(chip + 2, 4)
     opposite = across + 1 - 2 * lax.rem(across, 2)
     places = (opposite, beside, across, chip)
-    slots = grads_ref.shape[0]
+    states, (small_out, *updated) = refs[:3], refs[3:7]
+    own, other, relay, landed, small_landed, held = refs[7:13]
+    own_sem, other_send, other_recv, relay_send, relay_recv, landed_send, landed_recv = refs[13:20]
+    small_send, small_recv, load_sem, store_sem = refs[20:]
+    slots = held.shape[1]
     size = slots // chunks
     split = (chunks + 1) // 2
     greet_plane()
@@ -1310,6 +1357,12 @@
             device_id_type=MESH_ID,
         )
 
+    def store(n, q):
+        return pltpu.make_async_copy(
+            held.at[n, span(q)], updated[n].at[span(q)], store_sem.at[n, q]
+        )
+
+    loads = [pltpu.make_async_copy(states[n], held.at[n], load_sem.at[n]) for n in range(3)]
     for k in range(4):
         fetch(k).start()
 
@@ -1323,6 +1376,8 @@
         pass_over(k, q).wait_recv()
         return own[k, span(q)].astype(jnp.float32) + other[k, span(q)].astype(jnp.float32)
 
+    for load in loads:
+        load.start()
     fetch(0).wait()
 
     def first_leg(place):
@@ -1363,14 +1418,21 @@
     lax.fori_loop(0, split, relayed(2, beside), 0)
     lax.fori_loop(split, chunks, relayed(1, across), 0)
     fetch(3).wait()
+    for load in loads:
+        load.wait()
 
     def keep(q, carry):
         total = joined(3, q)
         to_owner(1, q).wait_recv()
         to_owner(2, q).wait_recv()
-        grads_ref[span(q)] = (
-            total + landed[0, span(q)].astype(jnp.float32) + landed[1, span(q)].astype(jnp.float32)
-        )
+        total = total + landed[0, span(q)].astype(jnp.float32) + landed[1, span(q)].astype(jnp.float32)
+        total = jnp.where(filled_ref[span(q)] > 0.5, total, 0.0)
+        fresh = adam_update(
+            held[0, span(q)], held[1, span(q)], held[2, span(q)], total, rates_ref[span(q)], decay_rate
+        )
+        for n in range(3):
+            held[n, span(q)] = fresh[n]
+            store(n, q).start()
         return carry
 
     lax.fori_loop(0, split, keep, 0)
@@ -1381,6 +1443,8 @@
             pass_over(k, q).wait_send()
         to_owner(1, q).wait_send()
         to_owner(2, q).wait_send()
+        for n in range(3):
+            store(n, q).wait()
         return carry
 
     lax.fori_loop(0, chunks, finish, 0)
@@ -1393,24 +1457,24 @@
     small_out[...] = total
 
 
-def own_units(parts, small, slots, collective_id):
+def own_units(parts, small, rates, filled, states, collective_id):
+    slots = states[0].shape[0]
     unit = parts.shape[1:]
     chunks = max(k for k in range(1, 8) if slots % k == 0)
     block = pltpu.VMEM((4, slots) + unit, jnp.bfloat16)
     return pl.pallas_call(
         functools.partial(own_units_kernel, chunks),
-        out_shape=[
-            jax.ShapeDtypeStruct((slots,) + unit, jnp.float32),
-            jax.ShapeDtypeStruct(small.shape, jnp.float32),
-        ],
-        in_specs=[whole_any, whole_vmem],
-        out_specs=[whole_vmem] * 2,
+        out_shape=[jax.ShapeDtypeStruct(small.shape, jnp.float32)]
+        + [jax.ShapeDtypeStruct((slots,) + unit, jnp.float32)] * 3,
+        in_specs=[whole_any] + [whole_vmem] * 3 + [whole_any] * 3,
+        out_specs=[whole_vmem] + [whole_any] * 3,
         scratch_shapes=[
             block,
             block,
             pltpu.VMEM((slots,) + unit, jnp.bfloat16),
             pltpu.VMEM((2, slots) + unit, jnp.bfloat16),
             pltpu.VMEM((8,) + small.shape, jnp.float32),
+            pltpu.VMEM((3, slots) + unit, jnp.float32),
             pltpu.SemaphoreType.DMA((4,)),
             pltpu.SemaphoreType.DMA((4, chunks)),
             pltpu.SemaphoreType.DMA((4, chunks)),
@@ -1420,11 +1484,13 @@
             pltpu.SemaphoreType.DMA((2, chunks)),
             pltpu.SemaphoreType.DMA((8,)),
             pltpu.SemaphoreType.DMA((8,)),
+            pltpu.SemaphoreType.DMA((3,)),
+            pltpu.SemaphoreType.DMA((3, chunks)),
         ],
         compiler_params=pltpu.CompilerParams(
             collective_id=collective_id, has_side_effects=True, vmem_limit_bytes=56 << 20
         ),
-    )(parts, small)
+    )(parts, small, rates, filled, *states)
 
 
 def to_plane(buffer):
@@ -1540,8 +1606,45 @@
     counted_rows = counted.reshape(tokens_here, 2).T.astype(jnp.float32)
     loss_weights = counted_rows * jnp.array([[1.0], [ahead_weight]], jnp.float32)
     counts = jnp.zeros((8, 128), jnp.float32).at[0:2].set(jnp.sum(counted_rows, 1, keepdims=True))
-    gathered = lax.all_gather(master[0, 0].astype(jnp.bfloat16), ("dp", "ctx"), axis=0, tiled=True)
     unit_slots = owner_ids * most_units + unit_rank
+    route_pairs = routes.reshape(tokens_here, 2)
+    pair_kept, pair_dest = pair_slots(route_pairs, priority[0], experts, capacity)
+    dest = jnp.where(pair_kept, pair_dest, -1).reshape(2, tokens_here)
+    unit_slots, dest = lax.optimization_barrier((unit_slots, dest))
+    local_ids = token_ids.reshape(-1) - my_rank * vocab_here
+    inside = (local_ids >= 0) & (local_ids < vocab_here)
+    clipped_ids = jnp.clip(local_ids, 0, vocab_here - 1)
+    master_low = master[0, 0].astype(jnp.bfloat16)
+    part_width = model_width // column_parts
+    unit_starts = jnp.sum(
+        jnp.where(
+            (clipped_ids // unit_rows)[None, :] == jnp.arange(unit_slots.shape[0])[:, None],
+            unit_slots[:, None] * unit_rows,
+            0,
+        ),
+        0,
+    )
+    slot_rows = unit_starts + clipped_ids % unit_rows
+    gathered, embedded = [], []
+
+    def embed(part):
+        if part > 0:
+            gathered[part], embedded[-1] = lax.optimization_barrier((gathered[part], embedded[-1]))
+        table_part = gathered[part].reshape(-1, part_width)
+        looked = jnp.where(inside[:, None], jnp.take(table_part, slot_rows, axis=0), 0)
+        embedded.extend(sum_line(looked, [], [], keep_total, 11 + part, rows=128))
+
+    for part in range(column_parts):
+        columns = master_low[:, :, part * part_width : (part + 1) * part_width]
+        if part > 0:
+            columns, gathered[-1] = lax.optimization_barrier((columns, gathered[-1]))
+        if part > 1:
+            columns, embedded[-1] = lax.optimization_barrier((columns, embedded[-1]))
+        gathered.append(lax.all_gather(columns, ("dp", "ctx"), axis=0, tiled=True))
+        if part > 0:
+            embed(part - 1)
+    embed(column_parts - 1)
+    embedded = jnp.concatenate(embedded, 1)
     weights_low = pull_units(gathered, unit_slots).reshape(-1, model_width)
     joint_low = weights_low[vocab_here : vocab_here + 3 * hidden_here]
     project_low = weights_low[vocab_here + 3 * hidden_here :]
@@ -1552,14 +1655,9 @@
     project_full = lax.dynamic_slice_in_dim(
         jnp.concatenate(rolled[::-1] + rolled[::-1], 0), (3 - my_rank) * hidden_here, model_width, 0
     )
-    local_ids = token_ids.reshape(-1) - my_rank * vocab_here
-    inside = (local_ids >= 0) & (local_ids < vocab_here)
-    clipped_ids = jnp.clip(local_ids, 0, vocab_here - 1)
-    looked = jnp.where(inside[:, None], jnp.take(weights_low, clipped_ids, axis=0), 0)
     gain_rows = [norm_gains[k : k + 1] for k in range(3)]
     stream_shape = jax.ShapeDtypeStruct((tokens_here, model_width), jnp.float32)
     gain_shape = jax.ShapeDtypeStruct((1, model_width), jnp.float32)
-    (embedded,) = sum_line(looked, [], [], keep_total, 1)
     stream_zero = embedded.astype(jnp.float32) * embed_scale
     first_normalized = norm_forward(stream_zero, norm_gains[0])
     normed_one_low = first_normalized.astype(jnp.bfloat16)
@@ -1579,18 +1677,15 @@
     normed_two_low = second_normalized.astype(jnp.bfloat16)
     router_low = router.astype(jnp.bfloat16)
     router_scores_raw = jnp.dot(normed_two_low, router_low, preferred_element_type=jnp.float32)
-    route_pairs = routes.reshape(tokens_here, 2)
     route_onehot = (route_pairs[:, :, None] == jnp.arange(experts, dtype=jnp.int32)).astype(
         jnp.float32
     )
     chosen = jnp.einsum("tke,te->tk", route_onehot, router_scores_raw, precision=highest_precision)
     gate_values = jax.nn.softmax(chosen, -1)
-    pair_kept, pair_dest = pair_slots(route_pairs, priority[0], experts, capacity)
-    dest = jnp.where(pair_kept, pair_dest, -1).reshape(2, tokens_here)
     inner_low = expert_in[0].astype(jnp.bfloat16)
     outer_low = expert_out[0].astype(jnp.bfloat16)
     if on_square:
-        moe_partial, arrived, hidden_pre, returned, counts = experts_forward(
+        moe_partial, arrived, returned, counts = experts_forward(
             normed_two_low, dest, gate_values, route_pairs, inner_low, outer_low, counts, capacity, 8
         )
     else:
@@ -1625,23 +1720,25 @@
         prologue=clear_gain,
     )
     gate_rows = gate_values.T
+    expert_states = (
+        expert_in[0],
+        expert_in_first[0],
+        expert_in_second[0],
+        expert_out[0],
+        expert_out_first[0],
+        expert_out_second[0],
+    )
     if on_square:
-        moe_grad_part, gate_part, inner_grad, outer_grad = experts_backward(
-            grad_two_low,
-            dest,
-            gate_rows,
-            route_pairs.T,
-            returned,
-            arrived,
-            hidden_pre,
-            inner_low,
-            outer_low,
-            9,
+        moe_grad_part, gate_part, *expert_states = experts_backward(
+            grad_two_low, dest, gate_rows, route_pairs.T, returned, arrived, expert_states, 9
         )
     else:
         moe_grad_part, gate_part, inner_grad, outer_grad = plain_backward(
             grad_two_low, dest, gate_rows, returned, arrived, hidden_pre, inner_low, outer_low
         )
+        expert_states = adam_update(
+            *expert_states[:3], inner_grad, rate_inner, decay_rate
+        ) + adam_update(*expert_states[3:], outer_grad, rate_outer, decay_rate)
     gate_part = jnp.concatenate([gate_part, target_sums, jnp.zeros_like(target_sums)], 0)
     gate_block = pltpu.VMEM((3, 4, tokens_here), jnp.float32)
     grad_one_low, grad_one, logit_grad, target_total, gain_grad_two = sum_line(
@@ -1665,7 +1762,7 @@
         5,
         prologue=start_router_grad,
         scratch=(gate_block, pltpu.SemaphoreType.DMA((3,)), pltpu.SemaphoreType.DMA((3,))),
-        meets_all=True,
+        opening=send_gate_parts,
     )
     router_grad = jnp.dot(logit_grad, normed_two_low, preferred_element_type=jnp.float32)
     loss_local = jnp.sum(weight_rows[2:3] * logsum_vocab) - jnp.sum(target_total)
@@ -1715,28 +1812,28 @@
     bias_row = jnp.pad(bias_row, (0, model_width - bias_row.shape[0]))[None]
     small = jnp.concatenate([gain_grads[:3], router_grad, bias_row], 0)
     small = jnp.pad(small, ((0, -small.shape[0] % 8), (0, 0)))
+    slot_rates = unit_rates(my_units, table_units, query_units, value_units)[:, None, None]
+    states = (master[0, 0], master_first[0, 0], master_second[0, 0])
     if on_square:
-        mine, small = own_units(outgoing, small, most_units, 10)
+        spread = (most_units, 1, model_width)
+        small, *states = own_units(
+            outgoing,
+            small,
+            jnp.broadcast_to(slot_rates, spread),
+            jnp.broadcast_to(my_filled.astype(jnp.float32), spread),
+            states,
+            10,
+        )
     else:
         mine = lax.psum_scatter(
             outgoing.astype(jnp.float32), ("dp", "ctx"), scatter_dimension=0, tiled=True
         )
         small = lax.psum(small, ("dp", "ctx"))
-    mine = jnp.where(my_filled, mine, 0.0)
+        states = adam_update(*states, jnp.where(my_filled, mine, 0.0), slot_rates, decay_rate)
     gains_grad = small[:3]
     router_grad = small[3 : 3 + experts].T
     bias_grad = small[3 + experts, : rel_bias.size].reshape(rel_bias.shape)
     loss_totals = jnp.stack([small[3 + experts, rel_bias.size], weight_total])
-    slot_rates = unit_rates(my_units, table_units, query_units, value_units)[:, None, None]
-    master_new, master_first_new, master_second_new = adam_update(
-        master[0, 0], master_first[0, 0], master_second[0, 0], mine, slot_rates, decay_rate
-    )
-    inner_new, inner_first_new, inner_second_new = adam_update(
-        expert_in, expert_in_first, expert_in_second, inner_grad[None], rate_inner, decay_rate
-    )
-    outer_new, outer_first_new, outer_second_new = adam_update(
-        expert_out, expert_out_first, expert_out_second, outer_grad[None], rate_outer, decay_rate
-    )
     gains_new, gains_first_new, gains_second_new = adam_update(
         norm_gains, norm_gains_first, norm_gains_second, gains_grad, rate_gains, 0.0
     )
@@ -1748,15 +1845,8 @@
     )
     return (
         loss_totals,
-        master_new[None, None],
-        master_first_new[None, None],
-        master_second_new[None, None],
-        inner_new,
-        inner_first_new,
-        inner_second_new,
-        outer_new,
-        outer_first_new,
-        outer_second_new,
+        *(state[None, None] for state in states),
+        *(state[None] for state in expert_states),
         gains_new,
         gains_first_new,
         gains_second_new,

time: 958 us -> 966 us (level)
  local copies, waits for them, and re-layouts: 39 us -> 81.9 us
  other arithmetic: 66.7 us -> 43.1 us
    unnamed x112 -> x125, local copies, waits for them, and re-layouts: 19 us -> 48 us
    all_gather x1 -> x3, waiting for transfers between devices: 79.3 us -> 64.8 us  [on_device(): gathered.append(lax.all_gather(columns, ('dp', 'ctx'), axis=0, tiled=True))]
    sub x5 -> x3, other arithmetic: 15.5 us -> 3.41 us  [adam_update(): weight - step_rate * (moment_hat / (jnp.sqrt(square_hat) + adam_epsilon)...]
    broadcast_in_dim x1 -> x0, other arithmetic: 10.4 us -> none  [on_device(): master_second_new[None, None]]
    gather x1 -> x3, local copies, waits for them, and re-layouts: 11.4 us -> 20.2 us  [embed(): jnp.take(table_part, slot_rows, axis=0)]
    pallas_call x6 -> x8, Pallas kernels: 283 us -> 291 us  [the longest x7 281 us: sum_line(): pl.pallas_call(functools.partial(sum_line_kernel, rows, count, opening, p...]
  transfers between devices with their start and end apart: 6 -> 8, of which waited for: 1 -> 4; matrix products, arithmetic and copies ran while one was open for 4% -> 4% of each run, Pallas kernels for 5% -> 8%
where the time goes in v4:
time: 966 us; the launch traced here: 956 us
  Pallas kernels  725 us (75%)
  local copies, waits for them, and re-layouts  81.9 us (8%)
  waiting for transfers between devices  72.8 us (8%)
  other arithmetic  43.1 us (4%)
  between operations  17.7 us (2%)
    pallas_call x7, Pallas kernels, sum_line(): pl.pallas_call(functools.partial(sum_line_kernel, rows, count, opening, p...  281 us
    pallas_call x1, Pallas kernels, experts_forward(): pl.pallas_call(experts_kernel, out_shape=[jax.ShapeDtypeStruct((tokens, w...  94.2 us
    pallas_call x1, Pallas kernels, experts_backward(): pl.pallas_call(experts_back_kernel, out_shape=[jax.ShapeDtypeStruct((toke...  91 us
    pallas_call x1, Pallas kernels, own_units(): pl.pallas_call(functools.partial(own_units_kernel, chunks), out_shape=[ja...  84.3 us
    all_gather x3, waiting for transfers between devices, on_device(): gathered.append(lax.all_gather(columns, ('dp', 'ctx'), axis=0, tiled=True))  64.8 us
    unnamed x125, local copies, waits for them, and re-layouts  48 us
    pallas_call x1, Pallas kernels, head_back(): pl.pallas_call(functools.partial(head_back_kernel, tile), grid=(vocab //...  44 us
    pallas_call x1, Pallas kernels, weight_grads(): pl.pallas_call(functools.partial(weight_grads_kernel, tile // unit_rows,...  34.1 us
  transfers between devices with their start and end apart: 8, of which 4 were waited for; matrix products, arithmetic and copies ran while one was open for 4% of the time, Pallas kernels for 8%

profile of v4, /device:TPU:0, one launch (start us, length us, event | category | flops | bytes accessed | tf_op | source)
XLA Modules:
  0.0 956.1 jit_solution(1636115431264989589)
XLA Ops:
  11.2 45.0 %all-gather.4.cloned.1.call-done.refs_0_ = bf16[168,64,256]{2,1,0:T(8,128)(2,1)} async-done(((bf16[21,64,256]{2,1,0:T(8,128)(2,1)}), bf16[168,64,256]{2,1,0:T(8,128)(2,1)}) %all-gather.4.cloned.1.call-update) | async-done | bytes 5505040 | tf_op jit(solution)/shard_map/all_gather | solution.py:1643
  67.6 22.4 %shard_map.384 = bf16[1024,256]{1,0:T(8,128)(2,1)S(1)} custom-call(bf16[1024,256]{1,0:T(8,128)(2,1)S(1)} %select_select_fusion.2.part_ref), custom_call_target="tpu_custom_call" | custom-call | tf_op jit(solution)/shard_map/pallas_call | solution.py:185
  89.9 11.0 %all-gather.6.cloned.1.call-done.refs_1_ = bf16[168,64,256]{2,1,0:T(8,128)(2,1)} async-done(((bf16[21,64,256]{2,1,0:T(8,128)(2,1)}), bf16[168,64,256]{2,1,0:T(8,128)(2,1)}) %all-gather.6.cloned.1.call-update) | async-done | bytes 5505040 | tf_op jit(solution)/shard_map/all_gather | solution.py:1643
  107.3 6.8 gather_fusion.1
  114.5 22.3 %shard_map.385 = bf16[1024,256]{1,0:T(8,128)(2,1)S(1)} custom-call(bf16[1024,256]{1,0:T(8,128)(2,1)S(1)} %select_select_fusion.1.part_ref), custom_call_target="tpu_custom_call" | custom-call | tf_op jit(solution)/shard_map/pallas_call | solution.py:185
  136.8 8.8 all-gather.8.cloned.1.call-done.refs_2_
  150.7 9.4 shard_map.386
  174.9 33.5 %shard_map.387 = bf16[1024,256]{1,0:T(8,128)(2,1)S(1)} custom-call(bf16[1024,256]{1,0:T(8,128)(2,1)S(1)} %select_select_fusion.part_ref), custom_call_target="tpu_custom_call" | custom-call | tf_op jit(solution)/shard_map/pallas_call | solution.py:185
  215.6 12.7 %shard_map.388 = (bf16[192,1024]{1,0:T(8,128)(2,1)S(1)}, f32[3,1024,1]{2,1,0:T(8,128)S(1)}) custom-call(f32[3,8]{1,0:T(4,128)S(1)} %copy-done.20, bf16[576,1024]{1,0:T(8,128)(2,1)S(1)} %convolution_convert_fusion.own_ref, bf16[384,1024]{1,0:T(8,128)(2,1)S(1)} %collective-permute-done.before_ref), custom_call_target="tpu_custom_call" | custom-call | tf_op jit(solution)/shard_map/pallas_call | solution.py:498
  229.4 28.8 %shard_map.389 = bf16[4,192,1024]{2,1,0:T(8,128)(2,1)S(1)} custom-call(bf16[192,1024]{1,0:T(8,128)(2,1)S(1)} %get-tuple-element.92.refs_0_.attended_ref), custom_call_target="tpu_custom_call" | custom-call | tf_op jit(solution)/shard_map/pallas_call | solution.py:378
  262.3 15.3 %fusion.6 = f32[1024,2]{1,0:T(8,128)} fusion(f32[1024,8]{1,0:T(8,128)S(1)} %fusion.26, s32[1024,2]{1,0:T(8,128)S(1)} %copy.66.routes), kind=kLoop, calls=%fused_computation.19 | loop fusion | flops 47104 | bytes 49152
  282.4 94.2 %shard_map.390 = (f32[1024,768]{1,0:T(8,128)}, bf16[8,288,768]{2,1,0:T(8,128)(2,1)}, bf16[8,288,768]{2,1,0:T(8,128)(2,1)}, f32[8,128]{1,0:T(8,128)}) custom-call(bf16[1024,768]{1,0:T(8,128)(2,1)} %copy-done.23, s32[2,1024]{1,0:T(2,128)} %copy-done.37, s32[1024,2]{1,0:T(8,128)} %copy.68.dest_columns, f32[1024,2]{1,0:T(8,128)} %copy.69.gates, ...), custom_call_target="tpu_custom_call" | custom-call | tf_op jit(solution)/shard_map/pallas_call | solution.py:1102
  377.9 55.6 %shard_map.391 = (bf16[1024,768]{1,0:T(8,128)(2,1)S(1)}, f32[1024,768]{1,0:T(8,128)S(1)}) custom-call(f32[1024,768]{1,0:T(8,128)} %get-tuple-element.94.part_ref, f32[1024,768]{1,0:T(8,128)} %copy-done.22, f32[1,768]{1,0:T(1,128)S(1)} %get-tuple-element.174.refs_1_), custom_call_target="tpu_custom_call" | custom-call | tf_op jit(solution)/shard_map/pallas_call | solution.py:185
  436.3 23.3 %shard_map.392.stats_ref = f32[2,1024]{1,0:T(2,128)} custom-call(bf16[8768,768]{1,0:T(8,128)(2,1)} %bitcast.95, bf16[1024,768]{1,0:T(8,128)(2,1)} %copy-done.2), custom_call_target="tpu_custom_call" | custom-call | tf_op jit(solution)/shard_map/pallas_call | solution.py:682
  459.6 6.8 shard_map.393.logsum_ref
  469.8 44.0 %shard_map.394 = (bf16[8000,1024]{1,0:T(8,128)(2,1)}, f32[1024,768]{1,0:T(8,128)}, f32[1,1024]{1,0:T(1,128)}) custom-call(bf16[8768,768]{1,0:T(8,128)(2,1)} %bitcast.96, bf16[1024,768]{1,0:T(8,128)(2,1)} %copy-done.2, f32[1,1024]{1,0:T(1,128)} %shard_map.393.logsum_ref, s32[2,1024]{1,0:T(2,128)} %subtract_bitcast_fusion.wanted_ref, ...), custom_call_target="tpu_custom_call" | custom-call | tf_op jit(solution)/shard_map/pallas_call | solution.py:774
  513.8 46.5 %shard_map.395 = (bf16[1024,768]{1,0:T(8,128)(2,1)S(1)}, f32[1024,768]{1,0:T(8,128)S(1)}, f32[1,768]{1,0:T(1,128)S(1)}) custom-call(f32[1024,768]{1,0:T(8,128)} %get-tuple-element.99.part_ref, f32[1024,768]{1,0:T(8,128)} %copy-done.11, f32[1,768]{1,0:T(1,128)S(1)} %get-tuple-element.174.refs_1_), custom_call_target="tpu_custom_call" | custom-call | tf_op jit(solution)/shard_map/pallas_call | solution.py:185
  563.2 91.0 %shard_map.396 = (f32[1024,768]{1,0:T(8,128)}, f32[2,1024]{1,0:T(2,128)}, f32[768,768]{1,0:T(8,128)}, f32[768,768]{1,0:T(8,128)}, f32[768,768]{1,0:T(8,128)}, /*...) custom-call(bf16[1024,768]{1,0:T(8,128)(2,1)} %copy-done.15, s32[2,1024]{1,0:T(2,128)} %copy-done.37, ...), custom_call_target="tpu_custom_call" | custom-call | tf_op jit(solution)/shard_map/pallas_call | solution.py:1270
  655.0 51.3 %shard_map.397 = (bf16[1024,768]{1,0:T(8,128)(2,1)S(1)}, f32[1024,768]{1,0:T(8,128)S(1)}, bf16[8,1024]{1,0:T(8,128)(2,1)S(1)}, f32[1,1024]{1,0:T(1,128)S(1)}, f32[1,768]{1,0:T(1,128)S(1)}) custom-call(f32[1024,768]{1,0:T(8,128)} %get-tuple-element.104.part_ref, f32[1024,768]{1,0:T(8,128)} %copy-done.22, f32[1,768]{1,0:T(1,128)S(1)} %get-tuple-element.173.refs_1_, ...), custom_call_target="tpu_custom_call" | custom-call | tf_op jit(solution)/shard_map/pallas_call | solution.py:185
  709.2 15.1 %shard_map.398 = (bf16[192,1024]{1,0:T(8,128)(2,1)S(1)}, f32[384,1024]{1,0:T(8,128)S(1)}, bf16[384,1024]{1,0:T(8,128)(2,1)}, f32[24,256]{1,0:T(8,128)S(1)}) custom-call(f32[3,8]{1,0:T(4,128)S(1)} %copy-done.20, bf16[576,1024]{1,0:T(8,128)(2,1)S(1)} %copy-done.6, bf16[384,1024]{1,0:T(8,128)(2,1)S(1)} %copy-done.10, f32[3,1024,1]{2,1,0:T(8,128)} %copy-done.16, ...), custom_call_target="tpu_custom_call" | custom-call | tf_op jit(solution)/shard_map/pallas_call | solution.py:637
  730.5 8.0 collective-permute-done.4
  745.7 49.5 %shard_map.399 = (bf16[1024,768]{1,0:T(8,128)(2,1)S(1)}, f32[8,768]{1,0:T(8,128)S(1)}) custom-call(f32[1024,768]{1,0:T(8,128)} %fusion.19.part_ref, bf16[1024,768]{1,0:T(8,128)(2,1)S(1)} %copy-done.4, f32[1,768]{1,0:T(1,128)S(1)} %get-tuple-element.172.refs_1_, f32[1024,768]{1,0:T(8,128)} %copy-done.8, f32[1,768]{1,0:T(1,128)S(1)} %get-tuple-element.113.refs_3_, ...), custom_call_target="tpu_custom_call" | custom-call | tf_op jit(solution)/shard_map/pallas_call | solution.py:185
  796.4 34.1 %shard_map.400.parts_ref = bf16[168,64,768]{2,1,0:T(8,128)(2,1)} custom-call(s32[137]{0:T(256)} %copy-done.21, bf16[8000,1024]{1,0:T(8,128)(2,1)} %get-tuple-element.97.slope_ref, bf16[1024,768]{1,0:T(8,128)(2,1)} %copy-done.2, s32[1,1024]{1,0:T(1,128)} %copy-done.40, bf16[1024,768]{1,0:T(8,128)(2,1)} %copy-done.14, ...), custom_call_target="tpu_custom_call" | custom-call | tf_op jit(solution)/shard_map/pallas_call | solution.py:857
  832.6 84.3 %shard_map.401 = (f32[16,768]{1,0:T(8,128)}, f32[21,64,768]{2,1,0:T(8,128)}, f32[21,64,768]{2,1,0:T(8,128)}, f32[21,64,768]{2,1,0:T(8,128)}) custom-call(bf16[168,64,768]{2,1,0:T(8,128)(2,1)} %shard_map.400.parts_ref, f32[16,768]{1,0:T(8,128)} %select_maximum_fusion.small_ref, f32[21,1,768]{2,1,0:T(1,128)} %broadcast_in_dim.173.rates_ref, ...), custom_call_target="tpu_custom_call" | custom-call | tf_op jit(solution)/shard_map/pallas_call | solution.py:1465
  (221 shorter events, 118.7 us)
Async XLA Ops:
  7.2 49.0 %all-gather.4.cloned.1.call-start = ((), (), s32[]{:S(2)}) async-start(), calls=%async_computation | async-start | bytes 6193152 | tf_op jit(solution)/shard_map/all_gather | solution.py:1643
  9.7 50.2 %copy-start.44 = (s32[137,1]{0,1:T(1,128)S(1)}, s32[137,1]{0,1:T(1,128)}, u32[]{:S(2)}) copy-start(s32[137,1]{0,1:T(1,128)} %param.34) | copy-start | bytes 1648
  9.7 50.4 %copy-start.50 = (s32[1,1024]{1,0:T(1,128)S(1)}, s32[1,1024]{1,0:T(1,128)}, u32[]{:S(2)}) copy-start(s32[1,1024]{1,0:T(1,128)} %param.29) | copy-start | bytes 12292
  11.1 89.8 %all-gather.6.cloned.1.call-start = ((), (), s32[]{:S(2)}) async-start(), calls=%async_computation.1 | async-start | bytes 6193152 | tf_op jit(solution)/shard_map/all_gather | solution.py:1643
  56.2 89.4 %all-gather.8.cloned.1.call-start = ((), (), s32[]{:S(2)}) async-start(), calls=%async_computation.2 | async-start | bytes 6193152 | tf_op jit(solution)/shard_map/all_gather | solution.py:1643
  60.1 85.5 %copy-start.21 = (s32[137]{0:T(256)}, s32[137]{0:T(256)S(1)}, u32[]{:S(2)}) copy-start(s32[137]{0:T(256)S(1)} %multiply_add_fusion.2.slots_ref.place_ref) | copy-start | bytes 1648
  102.4 159.9 %copy-start.25 = (s32[1024,2]{1,0:T(8,128)}, s32[1024,2]{1,0:T(8,128)S(1)}, u32[]{:S(2)}) copy-start(s32[1024,2]{1,0:T(8,128)S(1)} %copy.66.routes) | copy-start | bytes 24580
  163.3 50.0 %collective-permute-start.1 = (bf16[192,768]{1,0:T(8,128)(2,1)S(1)}, bf16[192,768]{1,0:T(8,128)(2,1)S(1)}, u32[]{:S(2)}, u32[]{:S(2)}) collective-permute-start(bf16[192,768]{1,0:T(8,128)(2,1)S(1)} %bitcast.84), channel_id=1, source_target_pairs={{0,3},{1,0},{2,1},{3,2},{4,7},{5,4},{6,5},{7,6},{8,11},{9,8},{10,9... | collective-permute-start | bytes 884744 | tf_op jit(solution)/shard_map/ppermute | solution.py:1652
  166.7 46.7 %collective-permute-start.2 = (bf16[192,768]{1,0:T(8,128)(2,1)S(1)}, bf16[192,768]{1,0:T(8,128)(2,1)S(1)}, u32[]{:S(2)}, u32[]{:S(2)}) collective-permute-start(bf16[192,768]{1,0:T(8,128)(2,1)S(1)} %bitcast.85), channel_id=1, source_target_pairs={{0,2},{1,3},{2,0},{3,1},{4,6},{5,7},{6,4},{7,5},{8,10},{9,11},{10,... | collective-permute-start | bytes 884744 | tf_op jit(solution)/shard_map/ppermute | solution.py:1652
  166.7 46.7 %collective-permute-start.3 = (bf16[192,768]{1,0:T(8,128)(2,1)S(1)}, bf16[192,768]{1,0:T(8,128)(2,1)}, u32[]{:S(2)}, u32[]{:S(2)}) collective-permute-start(bf16[192,768]{1,0:T(8,128)(2,1)S(1)} %bitcast.86), channel_id=1, source_target_pairs={{0,1},{1,2},{2,3},{3,0},{4,5},{5,6},{6,7},{7,4},{8,9},{9,10},{10,1... | collective-permute-start | bytes 884744 | tf_op jit(solution)/shard_map/ppermute | solution.py:1652
  208.9 49.4 %copy-start.3 = (bf16[1024,768]{1,0:T(8,128)(2,1)}, bf16[1024,768]{1,0:T(8,128)(2,1)S(1)}, u32[]{:S(2)}) copy-start(bf16[1024,768]{1,0:T(8,128)(2,1)S(1)} %get-tuple-element.166.refs_0_) | copy-start | bytes 4718596
  211.9 3.7 collective-permute-start
  563.2 91.0 %copy-start.49 = (f32[1,1024]{1,0:T(1,128)S(1)}, f32[1,1024]{1,0:T(1,128)}, u32[]{:S(2)}) copy-start(f32[1,1024]{1,0:T(1,128)} %get-tuple-element.107) | copy-start | bytes 12292
  563.2 91.8 %copy-start.18 = (s32[1,1024,2]{1,2,0:T(2,128)S(1)}, s32[1,1024,2]{1,2,0:T(2,128)}, u32[]{:S(2)}) copy-start(s32[1,1024,2]{1,2,0:T(2,128)} %param.32) | copy-start | bytes 24580
  563.2 91.8 %copy-start.19 = (f32[2,1024]{1,0:T(2,128)S(1)}, f32[2,1024]{1,0:T(2,128)}, u32[]{:S(2)}) copy-start(f32[2,1024]{1,0:T(2,128)} %fusion.36.gates.refs_4_) | copy-start | bytes 24580
  655.0 54.1 %copy-start.6 = (bf16[576,1024]{1,0:T(8,128)(2,1)S(1)}, bf16[576,1024]{1,0:T(8,128)(2,1)}, u32[]{:S(2)}) copy-start(bf16[576,1024]{1,0:T(8,128)(2,1)} %copy-done.5) | copy-start | bytes 3538948
  655.0 54.1 %copy-start.10 = (bf16[384,1024]{1,0:T(8,128)(2,1)S(1)}, bf16[384,1024]{1,0:T(8,128)(2,1)}, u32[]{:S(2)}) copy-start(bf16[384,1024]{1,0:T(8,128)(2,1)} %copy-done.9) | copy-start | bytes 2359300
  724.2 14.3 %collective-permute-start.4 = (bf16[384,1024]{1,0:T(8,128)(2,1)}, bf16[384,1024]{1,0:T(8,128)(2,1)S(1)}, u32[]{:S(2)}, u32[]{:S(2)}) collective-permute-start(bf16[384,1024]{1,0:T(8,128)(2,1)} %get-tuple-element.111), channel_id=1, source_target_pairs={{4,0},{5,1},{6,2},{7,3},{12,8},{13,9},{14,10},{15,11},{20,16},{21,... | collective-permute-start | bytes 2359304 | tf_op jit(solution)/shard_map/ppermute | solution.py:39
  832.6 87.7 %copy-start.45 = (f32[3,768]{1,0:T(4,128)S(1)}, f32[3,768]{1,0:T(4,128)}, u32[]{:S(2)}) copy-start(f32[3,768]{1,0:T(4,128)} %param.45) | copy-start | bytes 27652
  832.6 87.7 %copy-start.46 = (f32[3,768]{1,0:T(4,128)S(1)}, f32[3,768]{1,0:T(4,128)}, u32[]{:S(2)}) copy-start(f32[3,768]{1,0:T(4,128)} %param.46) | copy-start | bytes 27652
  832.6 89.0 %copy-start.42 = (f32[768,8]{0,1:T(8,128)S(1)}, f32[768,8]{0,1:T(8,128)}, u32[]{:S(2)}) copy-start(f32[768,8]{0,1:T(8,128)} %param.48) | copy-start | bytes 73732
  832.6 89.0 %copy-start.43 = (f32[768,8]{0,1:T(8,128)S(1)}, f32[768,8]{0,1:T(8,128)}, u32[]{:S(2)}) copy-start(f32[768,8]{0,1:T(8,128)} %param.49) | copy-start | bytes 73732
  832.6 90.5 %copy-start.51 = (f32[3,8]{1,0:T(4,128)S(1)}, f32[3,8]{1,0:T(4,128)}, u32[]{:S(2)}) copy-start(f32[3,8]{1,0:T(4,128)} %param.51) | copy-start | bytes 292
  832.6 90.5 %copy-start.52 = (f32[3,8]{1,0:T(4,128)S(1)}, f32[3,8]{1,0:T(4,128)}, u32[]{:S(2)}) copy-start(f32[3,8]{1,0:T(4,128)} %param.52) | copy-start | bytes 292
  (38 other events, 450.8 us)
Sparse Core Ops, SparseCore 0:
  11.2 44.9 all-gather.3
  58.6 42.2 all-gather.5
  103.4 42.2 all-gather.7

commit v5 on v3

--- a/solution.py
+++ b/solution.py
@@ -40,12 +40,11 @@
 MESH_ID = pl.DeviceIdType.MESH
 whole_vmem = pl.BlockSpec(memory_space=pltpu.VMEM)
 whole_any = pl.BlockSpec(memory_space=pl.ANY)
-line_rows = 64
 line_lag = 2
 
 
 def sum_line_kernel(
-    count, meets_all, prologue, epilogue, ending, n_extra, n_aux, n_scratch, part_ref, *refs
+    rows, count, opening, prologue, epilogue, ending, n_extra, n_aux, n_scratch, part_ref, *refs
 ):
     extras = refs[:n_extra]
     out_ref = refs[n_extra]
@@ -58,7 +57,7 @@
     end_peer = jnp.where(rank < 2, 1 - rank, 5 - rank)
     mid_peer = 3 - rank
     barrier = pltpu.get_barrier_semaphore()
-    if not meets_all:
+    if opening is None:
         pl.semaphore_signal(barrier, inc=1, device_id={"tensor": end_peer}, device_id_type=MESH_ID)
 
         @pl.when(inner)
@@ -76,8 +75,6 @@
             other = lax.rem(rank + step, 4)
             pl.semaphore_signal(barrier, inc=1, device_id={"tensor": other}, device_id_type=MESH_ID)
         pl.semaphore_wait(barrier, 3)
-
-    rows = line_rows
 
     def span(i):
         return pl.ds(pl.multiple_of(i * rows, rows), rows)
@@ -111,6 +108,9 @@
             device_id={"tensor": end_peer},
             device_id_type=MESH_ID,
         )
+
+    if opening is not None:
+        opening(rank, extras, scratch)
 
     @pl.when(jnp.logical_not(inner))
     def _():
@@ -174,17 +174,19 @@
     collective_id,
     prologue=None,
     scratch=(),
-    meets_all=False,
+    opening=None,
     ending=None,
+    rows=64,
 ):
     tokens, width = part.shape
-    count = tokens // line_rows
-    chunks = pltpu.VMEM((count, line_rows, width), jnp.bfloat16)
+    count = tokens // rows
+    chunks = pltpu.VMEM((count, rows, width), jnp.bfloat16)
     return pl.pallas_call(
         functools.partial(
             sum_line_kernel,
+            rows,
             count,
-            meets_all,
+            opening,
             prologue,
             epilogue,
             ending,
@@ -265,14 +267,11 @@
     return grad_two.astype(jnp.bfloat16)
 
 
-def start_router_grad(rank, inner, extras, aux, scratch):
-    stream_one, gain, grad_two, gate_part, gates, routes, router_low = extras
-    grad_one, logit_grad, target_total, gain_grad = aux
+def gate_copies(rank, extras, scratch):
+    gate_part = extras[3]
     landed, gate_send, gate_recv = scratch
-    clear_gain(rank, inner, extras, aux, scratch)
-    copies = []
-    for step in (1, 2, 3):
-        copy = pltpu.make_async_remote_copy(
+    return [
+        pltpu.make_async_remote_copy(
             src_ref=gate_part,
             dst_ref=landed.at[step - 1],
             send_sem=gate_send.at[step - 1],
@@ -280,9 +279,21 @@
             device_id={"tensor": lax.rem(rank + step, 4)},
             device_id_type=MESH_ID,
         )
+        for step in (1, 2, 3)
+    ]
+
+
+def send_gate_parts(rank, extras, scratch):
+    for copy in gate_copies(rank, extras, scratch):
         copy.start()
-        copies.append(copy)
-    for copy in copies:
+
+
+def start_router_grad(rank, inner, extras, aux, scratch):
+    stream_one, gain, grad_two, gate_part, gates, routes, router_low = extras
+    grad_one, logit_grad, target_total, gain_grad = aux
+    landed = scratch[0]
+    clear_gain(rank, inner, extras, aux, scratch)
+    for copy in gate_copies(rank, extras, scratch):
         copy.wait()
     gate_grad = jnp.zeros(gate_part.shape, jnp.float32)
     for source in range(4):
@@ -379,30 +390,247 @@
     )(*arrays)
 
 
-def pull_units_kernel(group, slots_ref, source_ref, out_ref, sem):
-    start = pl.program_id(0) * group
+def middle_kernel(
+    attended_ref, project_ref, embedded_ref, gain_ref, router_ref, routes_ref,
+    stream_ref, normed_ref, rows_ref, columns_ref,
+):
+    scale = math.sqrt(embedded_ref.shape[1])
+    stream = embedded_ref[...].astype(jnp.float32) * scale + lax.dot_general(
+        attended_ref[...], project_ref[...], (((0,), (0,)), ((), ())), preferred_element_type=jnp.float32
+    )
+    stream_ref[...] = stream
+    normed = (stream * inverse_rms(stream) * gain_ref[...]).astype(jnp.bfloat16)
+    normed_ref[...] = normed
+    scores = lax.dot_general(
+        router_ref[...], normed, (((1,), (1,)), ((), ())), preferred_element_type=jnp.float32
+    )
+    expert = lax.broadcasted_iota(jnp.int32, scores.shape, 0)
+    first, second = (
+        jnp.sum(jnp.where(expert == routes_ref[k : k + 1, :], scores, 0.0), 0, keepdims=True)
+        for k in range(2)
+    )
+    top = jnp.maximum(first, second)
+    first, second = jnp.exp(first - top), jnp.exp(second - top)
+    total = first + second
+    gates = jnp.concatenate([first / total, second / total], 0)
+    rows_ref[...] = gates
+    columns_ref[...] = jnp.concatenate([gates, jnp.zeros((6, gates.shape[1]), jnp.float32)], 0).T
+
+
+def middle(attended, project, embedded, gain, router, routes):
+    tokens, width = embedded.shape
+    tile = 256
+    fixed = lambda k: (0, 0)
+    whole = lambda x: pl.BlockSpec(x.shape, fixed)
+    down = lambda n: pl.BlockSpec((tile, n), lambda k: (k, 0))
+    along = lambda n: pl.BlockSpec((n, tile), lambda k: (0, k))
+    return pl.pallas_call(
+        middle_kernel,
+        grid=(tokens // tile,),
+        out_shape=[
+            jax.ShapeDtypeStruct((tokens, width), jnp.float32),
+            jax.ShapeDtypeStruct((tokens, width), jnp.bfloat16),
+            jax.ShapeDtypeStruct((2, tokens), jnp.float32),
+            jax.ShapeDtypeStruct((tokens, 8), jnp.float32),
+        ],
+        in_specs=[along(width), whole(project), down(width), whole(gain), whole(router), along(2)],
+        out_specs=[down(width), down(width), along(2), down(8)],
+        compiler_params=pltpu.CompilerParams(vmem_limit_bytes=40 << 20),
+    )(attended, project, embedded, gain, router, routes)
+
+
+def gather_units_kernel(
+    chunks, slots_ref, mine_ref, rows_ref, units_ref, looked_ref,
+    held, total, send_x, recv_x, send_y, recv_y, send_z, recv_z, send_core, recv_core,
+):
+    chip, core = lax.axis_index("dp"), lax.axis_index("ctx")
+    beside = chip + 1 - 2 * lax.rem(chip, 2)
+    across = lax.rem(chip + 2, 4)
+    opposite = across + 1 - 2 * lax.rem(across, 2)
+    places = (chip, beside, across, opposite)
+    slots, unit_rows, width = mine_ref.shape
+    size = slots // chunks
+    split = (chunks + 1) // 2
+    tokens = rows_ref.shape[0]
+    barrier = pltpu.get_barrier_semaphore()
+    for place in ({"ctx": 1 - core}, {"dp": beside}, {"dp": across}):
+        pl.semaphore_signal(barrier, inc=1, device_id=place, device_id_type=MESH_ID)
+    pl.semaphore_wait(barrier, 3)
+
+    def piece(place, which, q):
+        return held.at[pl.ds((place * 2 + which) * slots + q * size, size)]
+
+    def copy(place, q, send, recv, target):
+        return pltpu.make_async_remote_copy(
+            src_ref=piece(place, core, q),
+            dst_ref=piece(place, core, q),
+            send_sem=send,
+            recv_sem=recv,
+            device_id=target,
+            device_id_type=MESH_ID,
+        )
+
+    def to_beside(q):
+        return copy(chip, q, send_x.at[q], recv_x.at[q], {"dp": beside})
+
+    def to_across(q):
+        return copy(chip, q, send_y.at[q], recv_y.at[q], {"dp": across})
+
+    def passed_on(q, source, target):
+        return copy(source, q, send_z.at[q], recv_z.at[q], {"dp": target})
+
+    def to_core(k, q):
+        return copy(places[k], q, send_core.at[k, q], recv_core.at[k, q], {"ctx": 1 - core})
+
+    held[pl.ds((chip * 2 + core) * slots, slots)] = mine_ref[...]
+
+    def start(i, carry):
+        to_beside(i).start()
+        to_across(lax.rem(i + split, chunks)).start()
+        return carry
+
+    lax.fori_loop(0, chunks, start, 0)
+
+    def start_core(q, carry):
+        to_core(0, q).start()
+        return carry
+
+    lax.fori_loop(0, chunks, start_core, 0)
+    total[...] = jnp.zeros_like(total)
+
+    def look(place, which, first, count):
+        lines = count * unit_rows
+        begin = (place * 2 + which) * slots + first
+        column = lax.broadcasted_iota(jnp.int32, (tokens, lines), 1) + begin * unit_rows
+        hit = jnp.where(column == rows_ref[...], 1.0, 0.0).astype(jnp.bfloat16)
+        block = held[pl.ds(begin, count)].reshape(lines, width)
+        total[...] += jnp.dot(hit, block, preferred_element_type=jnp.float32)
+
+    def look_block(place, which):
+        def one(q, carry):
+            look(place, which, q * size, size)
+            return carry
+
+        lax.fori_loop(0, chunks, one, 0)
+
+    look_block(chip, core)
+
+    def relay(i, carry):
+        to_beside(i).wait_recv()
+
+        @pl.when(i < split)
+        def _():
+            passed_on(i, beside, across).start()
+
+        to_core(1, i).start()
+        j = lax.rem(i + split, chunks)
+        to_across(j).wait_recv()
+
+        @pl.when(j >= split)
+        def _():
+            passed_on(j, across, beside).start()
+
+        to_core(2, j).start()
+        to_core(0, i).wait_recv()
+        look(chip, 1 - core, i * size, size)
+        return carry
+
+    lax.fori_loop(0, chunks, relay, 0)
+    look_block(beside, core)
+    look_block(across, core)
+
+    def last(q, carry):
+        passed_on(q, opposite, opposite).wait_recv()
+        to_core(3, q).start()
+        to_core(1, q).wait_recv()
+        look(beside, 1 - core, q * size, size)
+        to_core(2, q).wait_recv()
+        look(across, 1 - core, q * size, size)
+        look(opposite, core, q * size, size)
+        return carry
+
+    lax.fori_loop(0, chunks, last, 0)
+
+    def ending(q, carry):
+        to_core(3, q).wait_recv()
+        look(opposite, 1 - core, q * size, size)
+        return carry
+
+    lax.fori_loop(0, chunks, ending, 0)
+    looked_ref[...] = total[...].astype(jnp.bfloat16)
+
+    def place_unit(u, carry):
+        units_ref[u] = held[slots_ref[u]]
+        return carry
+
+    lax.fori_loop(0, units_ref.shape[0], place_unit, 0)
+
+    def finish(q, carry):
+        to_beside(q).wait_send()
+        to_across(q).wait_send()
+        for k in range(4):
+            to_core(k, q).wait_send()
+        passed_on(q, opposite, opposite).wait_send()
+        return carry
+
+    lax.fori_loop(0, chunks, finish, 0)
+
+
+def gather_units(unit_slots, mine, slot_rows, collective_id):
+    slots = mine.shape[0]
+    unit = mine.shape[1:]
+    tokens = slot_rows.shape[0]
+    chunks = max(k for k in range(1, 8) if slots % k == 0)
+    sems = pltpu.SemaphoreType.DMA((chunks,))
+    core_sems = pltpu.SemaphoreType.DMA((4, chunks))
+    return pl.pallas_call(
+        functools.partial(gather_units_kernel, chunks),
+        out_shape=[
+            jax.ShapeDtypeStruct((unit_slots.shape[0],) + unit, jnp.bfloat16),
+            jax.ShapeDtypeStruct((tokens, unit[1]), jnp.bfloat16),
+        ],
+        in_specs=[pl.BlockSpec(memory_space=pltpu.SMEM), whole_vmem, whole_vmem],
+        out_specs=[whole_vmem] * 2,
+        scratch_shapes=[
+            pltpu.VMEM((8 * slots,) + unit, jnp.bfloat16),
+            pltpu.VMEM((tokens, unit[1]), jnp.float32),
+        ]
+        + [sems] * 6
+        + [core_sems] * 2,
+        compiler_params=pltpu.CompilerParams(
+            collective_id=collective_id, has_side_effects=True, vmem_limit_bytes=56 << 20
+        ),
+    )(unit_slots, mine, slot_rows)
+
+
+def pull_units_kernel(parts, slots_ref, *refs):
+    sources, out_ref, sem = refs[:parts], refs[parts], refs[parts + 1]
+    width = out_ref.shape[-1] // parts
 
     def push(u, carry):
-        pltpu.make_async_copy(source_ref.at[slots_ref[start + u]], out_ref.at[u], sem).start()
+        for part in range(parts):
+            pltpu.make_async_copy(
+                sources[part].at[slots_ref[u]],
+                out_ref.at[u, :, part * width : (part + 1) * width],
+                sem,
+            ).start()
         return carry
 
-    lax.fori_loop(0, group, push, 0)
+    lax.fori_loop(0, out_ref.shape[0], push, 0)
     pltpu.make_async_copy(out_ref, out_ref, sem).wait()
 
 
-def pull_units(source, slots):
+def pull_units(sources, slots):
     count = slots.shape[0]
-    unit_bytes = math.prod(source.shape[1:]) * source.dtype.itemsize
-    group = max(k for k in range(1, count + 1) if count % k == 0 and (k <= 32 or k * unit_bytes < 15 << 20))
+    rows, width = sources[0].shape[1:]
     return pl.pallas_call(
-        functools.partial(pull_units_kernel, group),
-        grid=(count // group,),
-        out_shape=jax.ShapeDtypeStruct((count,) + source.shape[1:], source.dtype),
-        in_specs=[pl.BlockSpec(memory_space=pltpu.SMEM), whole_any],
-        out_specs=pl.BlockSpec((group,) + source.shape[1:], lambda k: (k,) + (0,) * (source.ndim - 1)),
+        functools.partial(pull_units_kernel, len(sources)),
+        out_shape=jax.ShapeDtypeStruct((count, rows, width * len(sources)), sources[0].dtype),
+        in_specs=[pl.BlockSpec(memory_space=pltpu.SMEM)] + [whole_any] * len(sources),
+        out_specs=whole_vmem,
         scratch_shapes=[pltpu.SemaphoreType.DMA],
         compiler_params=pltpu.CompilerParams(vmem_limit_bytes=40 << 20),
-    )(slots, source)
+    )(slots, *sources)
 
 
 def attention_kernel(heads, size, bias_ref, own_ref, before_ref, out_ref, logsum_ref, scores, peak, total):
@@ -782,9 +1010,14 @@
 
 def weight_grads_kernel(
     tile_units, tiles, place_ref, slope_ref, rows_ref, ids_ref, zero_ref, joint_ref, normed_ref,
-    attended_ref, grad_ref, out_ref, made, sem,
+    attended_ref, grad_ref, *refs
 ):
+    states, (out_ref, *updated), (made, sem) = refs[:8], refs[8:15], refs[15:]
     step = pl.program_id(0)
+    for k, rate in enumerate((rate_inner, rate_outer)):
+        fresh = adam_update(*(state[...] for state in states[4 * k : 4 * k + 4]), rate, decay_rate)
+        for n in range(3):
+            updated[3 * k + n][...] = fresh[n]
     unit_rows = out_ref.shape[1]
     buffer = lax.rem(step, 2)
     last_units = joint_ref.shape[0] // unit_rows + attended_ref.shape[0] // unit_rows
@@ -831,29 +1064,34 @@
         settle(buffer, last_units)
 
 
-def weight_grads(place, slots, unit_rows, slope, rows, ids, zero, joint, normed, attended, grad):
+def weight_grads(
+    place, slots, unit_rows, slope, rows, ids, zero, joint, normed, attended, grad, states
+):
     vocab, tokens = slope.shape
     width = rows.shape[1]
     tile = vocab_tile(vocab)
     tiles = vocab // tile
     fixed = lambda k: (0, 0)
     whole = lambda x: pl.BlockSpec(x.shape, fixed)
+    piece = pl.BlockSpec((states[0].shape[0] // (tiles + 1), states[0].shape[1]), lambda k: (k, 0))
     return pl.pallas_call(
         functools.partial(weight_grads_kernel, tile // unit_rows, tiles),
         grid=(tiles + 1,),
-        out_shape=jax.ShapeDtypeStruct((slots, unit_rows, width), jnp.bfloat16),
+        out_shape=[jax.ShapeDtypeStruct((slots, unit_rows, width), jnp.bfloat16)]
+        + [jax.ShapeDtypeStruct(states[0].shape, jnp.float32)] * 6,
         in_specs=[
             pl.BlockSpec(memory_space=pltpu.SMEM),
             pl.BlockSpec((tile, tokens), lambda k: (jnp.minimum(k, tiles - 1), 0)),
         ]
-        + [whole(x) for x in (rows, ids, zero, joint, normed, attended, grad)],
-        out_specs=whole_any,
+        + [whole(x) for x in (rows, ids, zero, joint, normed, attended, grad)]
+        + [piece] * 8,
+        out_specs=[whole_any] + [piece] * 6,
         scratch_shapes=[
             pltpu.VMEM((2, tile // unit_rows, unit_rows, width), jnp.bfloat16),
             pltpu.SemaphoreType.DMA((2,)),
         ],
         compiler_params=pltpu.CompilerParams(vmem_limit_bytes=60 << 20),
-    )(place, slope, rows, ids, zero, joint, normed, attended, grad)
+    )(place, slope, rows, ids, zero, joint, normed, attended, grad, *states)
 
 
 def adam_update(weight, moment_one, moment_two, gradient, step_rate, decay_factor):
@@ -977,7 +1215,7 @@
 
 def experts_kernel(
     rows_ref, dest_rows, dest_columns, gates, routes, inner_ref, outer_ref, counts_ref,
-    mix_ref, arrived, hidden, returned, totals_ref,
+    mix_ref, arrived, returned, totals_ref,
     outgoing, results, counts, send_one, recv_one, send_two, recv_two, send_count, recv_count,
 ):
     capacity = arrived.shape[1]
@@ -1022,7 +1260,6 @@
             plane_copy(outgoing, arrived, send_one, recv_one, step).wait_recv()
 
         before = jnp.dot(arrived[step], inner_ref[...], preferred_element_type=jnp.float32)
-        hidden[step] = before
         active = gelu_tanh(before).astype(jnp.bfloat16)
         part = jnp.dot(active, outer_ref[...], preferred_element_type=jnp.float32).astype(jnp.bfloat16)
 
@@ -1083,19 +1320,17 @@
 
 def experts_forward(rows, dest, gates, routes, inner, outer, counts, capacity, collective_id):
     tokens, width = rows.shape
-    hidden = inner.shape[1]
     buffer = pltpu.VMEM((8, capacity, width), jnp.bfloat16)
     return pl.pallas_call(
         experts_kernel,
         out_shape=[
             jax.ShapeDtypeStruct((tokens, width), jnp.float32),
             jax.ShapeDtypeStruct((8, capacity, width), jnp.bfloat16),
-            jax.ShapeDtypeStruct((8, capacity, hidden), jnp.float32),
             jax.ShapeDtypeStruct((8, capacity, width), jnp.bfloat16),
             jax.ShapeDtypeStruct(counts.shape, jnp.float32),
         ],
         in_specs=[whole_vmem] * 8,
-        out_specs=[whole_vmem] * 5,
+        out_specs=[whole_vmem] * 4,
         scratch_shapes=[buffer, buffer, pltpu.VMEM((8,) + counts.shape, jnp.float32)]
         + [pltpu.SemaphoreType.DMA((8,))] * 6,
         compiler_params=pltpu.CompilerParams(
@@ -1105,10 +1340,11 @@
 
 
 def experts_back_kernel(
-    rows_ref, dest_rows, dest_columns, gates, routes, returned, arrived, hidden, inner_ref, outer_ref,
-    grad_ref, gate_ref, inner_grad, outer_grad,
-    outgoing, landed, results, landed_two, active, slopes, send_one, recv_one, send_two, recv_two,
+    rows_ref, dest_rows, dest_columns, gates, routes, returned, arrived, *refs
 ):
+    inner_ref, outer_ref, grad_ref, gate_ref, inner_grad, outer_grad = refs[:6]
+    outgoing, landed, results, landed_two, active, slopes = refs[6:12]
+    send_one, recv_one, send_two, recv_two = refs[12:]
     capacity = arrived.shape[1]
     tokens = rows_ref.shape[0]
     greet_plane()
@@ -1149,7 +1385,7 @@
         grad_active = lax.dot_general(
             landed[step], outer_ref[...], (((1,), (1,)), ((), ())), preferred_element_type=jnp.float32
         )
-        before = hidden[step]
+        before = jnp.dot(arrived[step], inner_ref[...], preferred_element_type=jnp.float32)
         slope = (grad_active * gelu_slope(before)).astype(jnp.bfloat16)
         back = lax.dot_general(
             slope, inner_ref[...], (((1,), (1,)), ((), ())), preferred_element_type=jnp.float32
@@ -1178,13 +1414,13 @@
 
         @pl.when(step == 0)
         def _():
+            inner_grad[...] = inner_part
             outer_grad[...] = outer_part
-            inner_grad[...] = inner_part
 
         @pl.when(step > 0)
         def _():
+            inner_grad[...] += inner_part
             outer_grad[...] += outer_part
-            inner_grad[...] += inner_part
 
         return carry
 
@@ -1221,7 +1457,7 @@
     lax.fori_loop(1, 8, finish, 0)
 
 
-def experts_backward(rows, dest, gates, routes, returned, arrived, hidden, inner, outer, collective_id):
+def experts_backward(rows, dest, gates, routes, returned, arrived, inner, outer, collective_id):
     tokens, width = rows.shape
     capacity = arrived.shape[1]
     inside = inner.shape[1]
@@ -1235,15 +1471,13 @@
             jax.ShapeDtypeStruct((width, inside), jnp.float32),
             jax.ShapeDtypeStruct((inside, width), jnp.float32),
         ],
-        in_specs=[whole_vmem] * 10,
+        in_specs=[whole_vmem] * 9,
         out_specs=[whole_vmem] * 4,
-        scratch_shapes=[buffer] * 4
-        + [inside_buffer] * 2
-        + [pltpu.SemaphoreType.DMA((8,))] * 4,
+        scratch_shapes=[buffer] * 4 + [inside_buffer] * 2 + [pltpu.SemaphoreType.DMA((8,))] * 4,
         compiler_params=pltpu.CompilerParams(
-            collective_id=collective_id, has_side_effects=True, vmem_limit_bytes=63 << 20
+            collective_id=collective_id, has_side_effects=True, vmem_limit_bytes=60 << 20
         ),
-    )(rows, dest, dest.T, gates, routes, returned, arrived, hidden, inner, outer)
+    )(rows, dest, dest.T, gates, routes, returned, arrived, inner, outer)
 
 
 def own_units_kernel(
@@ -1457,10 +1691,10 @@
         )
         for k in range(2)
     )
-    return (mix, arrived, hidden, returned)
-
-
-def plain_backward(rows, dest, gates, returned, arrived, hidden, inner, outer):
+    return (mix, arrived, returned)
+
+
+def plain_backward(rows, dest, gates, returned, arrived, inner, outer):
     owners, capacity, width = arrived.shape
     hits = plain_hits(dest, owners, capacity)
     both = (hits[0] | hits[1]).astype(jnp.bfloat16)
@@ -1476,6 +1710,7 @@
     )
     landed = to_plane(sent.reshape(owners, capacity, width))
     grad_active = jnp.einsum("ocd,fd->ocf", landed, outer, preferred_element_type=jnp.float32)
+    hidden = jnp.einsum("ocd,df->ocf", arrived, inner, preferred_element_type=jnp.float32)
     active = gelu_tanh(hidden).astype(jnp.bfloat16)
     slope = (grad_active * gelu_slope(hidden)).astype(jnp.bfloat16)
     outer_grad = jnp.einsum("ocf,ocd->fd", active, landed, preferred_element_type=jnp.float32)
@@ -1535,14 +1770,39 @@
     value_units = table_units + 3 * hidden_here // unit_rows
     embed_scale = math.sqrt(model_width)
     owner_ids = owner_of[:, 0]
+    on_square = lax.axis_size("dp") == 4 and lax.axis_size("ctx") == 2
     unit_rank, slot_unit, slot_filled = slot_tables(owner_ids, owners, most_units)
-    on_square = lax.axis_size("dp") == 4 and lax.axis_size("ctx") == 2
     counted_rows = counted.reshape(tokens_here, 2).T.astype(jnp.float32)
     loss_weights = counted_rows * jnp.array([[1.0], [ahead_weight]], jnp.float32)
     counts = jnp.zeros((8, 128), jnp.float32).at[0:2].set(jnp.sum(counted_rows, 1, keepdims=True))
-    gathered = lax.all_gather(master[0, 0].astype(jnp.bfloat16), ("dp", "ctx"), axis=0, tiled=True)
     unit_slots = owner_ids * most_units + unit_rank
-    weights_low = pull_units(gathered, unit_slots).reshape(-1, model_width)
+    route_pairs = routes.reshape(tokens_here, 2)
+    pair_kept, pair_dest = pair_slots(route_pairs, priority[0], experts, capacity)
+    dest = jnp.where(pair_kept, pair_dest, -1).reshape(2, tokens_here)
+    unit_slots, dest = lax.optimization_barrier((unit_slots, dest))
+    local_ids = token_ids.reshape(-1) - my_rank * vocab_here
+    inside = (local_ids >= 0) & (local_ids < vocab_here)
+    clipped_ids = jnp.clip(local_ids, 0, vocab_here - 1)
+    master_low = master[0, 0].astype(jnp.bfloat16)
+    unit_starts = jnp.sum(
+        jnp.where(
+            (clipped_ids // unit_rows)[None, :] == jnp.arange(unit_slots.shape[0])[:, None],
+            unit_slots[:, None] * unit_rows,
+            0,
+        ),
+        0,
+    )
+    slot_rows = unit_starts + clipped_ids % unit_rows
+    if on_square:
+        slot_rows = jnp.where(inside, slot_rows, -1)[:, None]
+        weights_low, looked = gather_units(unit_slots, master_low, slot_rows, 11)
+    else:
+        gathered = lax.all_gather(master_low, ("dp", "ctx"), axis=0, tiled=True)
+        looked = jnp.take(gathered.reshape(-1, model_width), slot_rows, axis=0)
+        looked = jnp.where(inside[:, None], looked, 0)
+        weights_low = pull_units([gathered], unit_slots)
+    weights_low = weights_low.reshape(-1, model_width)
+    (embedded,) = sum_line(looked, [], [], keep_total, 1)
     joint_low = weights_low[vocab_here : vocab_here + 3 * hidden_here]
     project_low = weights_low[vocab_here + 3 * hidden_here :]
     rolled = [project_low] + [
@@ -1552,14 +1812,9 @@
     project_full = lax.dynamic_slice_in_dim(
         jnp.concatenate(rolled[::-1] + rolled[::-1], 0), (3 - my_rank) * hidden_here, model_width, 0
     )
-    local_ids = token_ids.reshape(-1) - my_rank * vocab_here
-    inside = (local_ids >= 0) & (local_ids < vocab_here)
-    clipped_ids = jnp.clip(local_ids, 0, vocab_here - 1)
-    looked = jnp.where(inside[:, None], jnp.take(weights_low, clipped_ids, axis=0), 0)
     gain_rows = [norm_gains[k : k + 1] for k in range(3)]
     stream_shape = jax.ShapeDtypeStruct((tokens_here, model_width), jnp.float32)
     gain_shape = jax.ShapeDtypeStruct((1, model_width), jnp.float32)
-    (embedded,) = sum_line(looked, [], [], keep_total, 1)
     stream_zero = embedded.astype(jnp.float32) * embed_scale
     first_normalized = norm_forward(stream_zero, norm_gains[0])
     normed_one_low = first_normalized.astype(jnp.bfloat16)
@@ -1569,33 +1824,24 @@
     pairs_before = passed_along(joint[hidden_here:], "ctx", 1)
     attended, logsum_rows = attention(rel_bias, joint, pairs_before, heads_here, head_size)
     (attended_all,) = gather_line([attended], 2)
-    stream_one = stream_zero + lax.dot_general(
+    router_low = router.astype(jnp.bfloat16)
+    stream_one, normed_two_low, gate_rows, gate_columns = middle(
         attended_all.reshape(model_width, tokens_here),
         project_full,
-        (((0,), (0,)), ((), ())),
-        preferred_element_type=jnp.float32,
-    )
-    second_normalized = norm_forward(stream_one, norm_gains[1])
-    normed_two_low = second_normalized.astype(jnp.bfloat16)
-    router_low = router.astype(jnp.bfloat16)
-    router_scores_raw = jnp.dot(normed_two_low, router_low, preferred_element_type=jnp.float32)
-    route_pairs = routes.reshape(tokens_here, 2)
-    route_onehot = (route_pairs[:, :, None] == jnp.arange(experts, dtype=jnp.int32)).astype(
-        jnp.float32
-    )
-    chosen = jnp.einsum("tke,te->tk", route_onehot, router_scores_raw, precision=highest_precision)
-    gate_values = jax.nn.softmax(chosen, -1)
-    pair_kept, pair_dest = pair_slots(route_pairs, priority[0], experts, capacity)
-    dest = jnp.where(pair_kept, pair_dest, -1).reshape(2, tokens_here)
+        embedded,
+        gain_rows[1],
+        router_low.T,
+        route_pairs.T,
+    )
     inner_low = expert_in[0].astype(jnp.bfloat16)
     outer_low = expert_out[0].astype(jnp.bfloat16)
     if on_square:
-        moe_partial, arrived, hidden_pre, returned, counts = experts_forward(
-            normed_two_low, dest, gate_values, route_pairs, inner_low, outer_low, counts, capacity, 8
+        moe_partial, arrived, returned, counts = experts_forward(
+            normed_two_low, dest, gate_columns, route_pairs, inner_low, outer_low, counts, capacity, 8
         )
     else:
-        moe_partial, arrived, hidden_pre, returned = plain_forward(
-            normed_two_low, dest, gate_values, inner_low, outer_low, owners, capacity
+        moe_partial, arrived, returned = plain_forward(
+            normed_two_low, dest, gate_columns, inner_low, outer_low, owners, capacity
         )
         counts = lax.psum(counts, ("dp", "ctx"))
     weight_total = counts[0, 0] + ahead_weight * counts[1, 0]
@@ -1624,7 +1870,6 @@
         4,
         prologue=clear_gain,
     )
-    gate_rows = gate_values.T
     if on_square:
         moe_grad_part, gate_part, inner_grad, outer_grad = experts_backward(
             grad_two_low,
@@ -1633,14 +1878,13 @@
             route_pairs.T,
             returned,
             arrived,
-            hidden_pre,
             inner_low,
             outer_low,
             9,
         )
     else:
         moe_grad_part, gate_part, inner_grad, outer_grad = plain_backward(
-            grad_two_low, dest, gate_rows, returned, arrived, hidden_pre, inner_low, outer_low
+            grad_two_low, dest, gate_rows, returned, arrived, inner_low, outer_low
         )
     gate_part = jnp.concatenate([gate_part, target_sums, jnp.zeros_like(target_sums)], 0)
     gate_block = pltpu.VMEM((3, 4, tokens_here), jnp.float32)
@@ -1665,7 +1909,7 @@
         5,
         prologue=start_router_grad,
         scratch=(gate_block, pltpu.SemaphoreType.DMA((3,)), pltpu.SemaphoreType.DMA((3,))),
-        meets_all=True,
+        opening=send_gate_parts,
     )
     router_grad = jnp.dot(logit_grad, normed_two_low, preferred_element_type=jnp.float32)
     loss_local = jnp.sum(weight_rows[2:3] * logsum_vocab) - jnp.sum(target_total)
@@ -1698,7 +1942,7 @@
     )
     my_units = jnp.take(slot_unit, my_owner, axis=0)
     my_filled = jnp.take(slot_filled, my_owner, axis=0)[:, None, None]
-    outgoing = weight_grads(
+    outgoing, *expert_states = weight_grads(
         unit_slots,
         owners * most_units,
         unit_rows,
@@ -1710,11 +1954,23 @@
         normed_one_low,
         attended,
         grad_one_low,
+        (
+            expert_in[0],
+            expert_in_first[0],
+            expert_in_second[0],
+            inner_grad,
+            expert_out[0],
+            expert_out_first[0],
+            expert_out_second[0],
+            outer_grad,
+        ),
     )
     bias_row = jnp.concatenate([bias_grad.reshape(-1), loss_local[None]])
     bias_row = jnp.pad(bias_row, (0, model_width - bias_row.shape[0]))[None]
     small = jnp.concatenate([gain_grads[:3], router_grad, bias_row], 0)
     small = jnp.pad(small, ((0, -small.shape[0] % 8), (0, 0)))
+    slot_rates = unit_rates(my_units, table_units, query_units, value_units)[:, None, None]
+    states = (master[0, 0], master_first[0, 0], master_second[0, 0])
     if on_square:
         mine, small = own_units(outgoing, small, most_units, 10)
     else:
@@ -1722,21 +1978,11 @@
             outgoing.astype(jnp.float32), ("dp", "ctx"), scatter_dimension=0, tiled=True
         )
         small = lax.psum(small, ("dp", "ctx"))
-    mine = jnp.where(my_filled, mine, 0.0)
+    states = adam_update(*states, jnp.where(my_filled, mine, 0.0), slot_rates, decay_rate)
     gains_grad = small[:3]
     router_grad = small[3 : 3 + experts].T
     bias_grad = small[3 + experts, : rel_bias.size].reshape(rel_bias.shape)
     loss_totals = jnp.stack([small[3 + experts, rel_bias.size], weight_total])
-    slot_rates = unit_rates(my_units, table_units, query_units, value_units)[:, None, None]
-    master_new, master_first_new, master_second_new = adam_update(
-        master[0, 0], master_first[0, 0], master_second[0, 0], mine, slot_rates, decay_rate
-    )
-    inner_new, inner_first_new, inner_second_new = adam_update(
-        expert_in, expert_in_first, expert_in_second, inner_grad[None], rate_inner, decay_rate
-    )
-    outer_new, outer_first_new, outer_second_new = adam_update(
-        expert_out, expert_out_first, expert_out_second, outer_grad[None], rate_outer, decay_rate
-    )
     gains_new, gains_first_new, gains_second_new = adam_update(
         norm_gains, norm_gains_first, norm_gains_second, gains_grad, rate_gains, 0.0
     )
@@ -1748,15 +1994,8 @@
     )
     return (
         loss_totals,
-        master_new[None, None],
-        master_first_new[None, None],
-        master_second_new[None, None],
-        inner_new,
-        inner_first_new,
-        inner_second_new,
-        outer_new,
-        outer_first_new,
-        outer_second_new,
+        *(state[None, None] for state in states),
+        *(state[None] for state in expert_states),
         gains_new,
         gains_first_new,
         gains_second_new,

time: 958 us -> 918 us (0.958)
  Pallas kernels: 729 us -> 807 us
  waiting for transfers between devices: 79.3 us -> 5.16 us
  other arithmetic: 66.7 us -> 42.2 us
  between operations: 17.9 us -> 4.45 us
    all_gather x1 -> x0, waiting for transfers between devices: 79.3 us -> none  [on_device(): lax.all_gather(master[0, 0].astype(jnp.bfloat16), ('dp', 'ctx'), axis=0,...]
    pallas_call x6 -> x7, Pallas kernels: 283 us -> 360 us  [the longest x5 258 us: sum_line(): pl.pallas_call(functools.partial(sum_line_kernel, rows, count, opening, p...]
    unnamed x2 -> x1, other arithmetic: 15.4 us -> 0.76 us
    sub x5 -> x3, other arithmetic: 15.5 us -> 3.41 us  [adam_update(): weight - step_rate * (moment_hat / (jnp.sqrt(square_hat) + adam_epsilon)...]
    gather x1 -> x0, local copies, waits for them, and re-layouts: 11.4 us -> none  [on_device(): jnp.take(weights_low, clipped_ids, axis=0)]
    unnamed x112 -> x108, local copies, waits for them, and re-layouts: 19 us -> 22.9 us
  transfers between devices with their start and end apart: 6 -> 5, of which waited for: 1 -> 1; matrix products, arithmetic and copies ran while one was open for 4% -> 2% of each run, Pallas kernels for 5% -> 7%
where the time goes in v5:
time: 918 us; the launch traced here: 908 us
  Pallas kernels  807 us (88%)
  other arithmetic  42.2 us (5%)
  local copies, waits for them, and re-layouts  34.1 us (4%)
  starting transfers between devices  9.38 us (1%)
    pallas_call x5, Pallas kernels, sum_line(): pl.pallas_call(functools.partial(sum_line_kernel, rows, count, opening, p...  258 us
    pallas_call x1, Pallas kernels, gather_units(): pl.pallas_call(functools.partial(gather_units_kernel, chunks), out_shape=...  97.5 us
    pallas_call x1, Pallas kernels, experts_forward(): pl.pallas_call(experts_kernel, out_shape=[jax.ShapeDtypeStruct((tokens, w...  94.2 us
    pallas_call x1, Pallas kernels, experts_backward(): pl.pallas_call(experts_back_kernel, out_shape=[jax.ShapeDtypeStruct((toke...  93.1 us
    pallas_call x1, Pallas kernels, own_units(): pl.pallas_call(functools.partial(own_units_kernel, chunks), out_shape=[ja...  86.5 us
    pallas_call x1, Pallas kernels, head_back(): pl.pallas_call(functools.partial(head_back_kernel, tile), grid=(vocab //...  44 us
    pallas_call x1, Pallas kernels, weight_grads(): pl.pallas_call(functools.partial(weight_grads_kernel, tile // unit_rows,...  41.9 us
    pallas_call x1, Pallas kernels, gather_line(): pl.pallas_call(functools.partial(gather_line_kernel, count), out_shape=[j...  28.9 us
  transfers between devices with their start and end apart: 5, of which 1 were waited for; matrix products, arithmetic and copies ran while one was open for 2% of the time, Pallas kernels for 7%

profile of v5, /device:TPU:0, one launch (start us, length us, event | category | flops | bytes accessed | tf_op | source)
XLA Modules:
  0.0 908.4 jit_solution(6639120796624556248)
XLA Ops:
  2.9 3.4 convert_reduce_fusion
  9.7 3.8 bitcast_convert_fusion.mine_ref
  14.5 97.5 %shard_map.384 = (bf16[137,64,768]{2,1,0:T(8,128)(2,1)}, bf16[1024,768]{1,0:T(8,128)(2,1)}) custom-call(s32[137]{0:T(256)} %copy-done.39, bf16[21,64,768]{2,1,0:T(8,128)(2,1)} %bitcast_convert_fusion.mine_ref, s32[1024,1]{1,0:T(8,128)} %fusion.10.rows_ref), custom_call_target="tpu_custom_call" | custom-call | tf_op jit(solution)/shard_map/pallas_call | solution.py:586
  114.8 2.6 collective-permute-start.2
  120.0 59.9 %shard_map.385.embedded_ref.refs_0_ = bf16[1024,768]{1,0:T(8,128)(2,1)S(1)} custom-call(bf16[1024,768]{1,0:T(8,128)(2,1)S(1)} %copy-done.12), custom_call_target="tpu_custom_call" | custom-call | tf_op jit(solution)/shard_map/pallas_call | solution.py:184
  183.0 2.4 collective-permute-start
  197.0 13.2 %shard_map.386 = (bf16[192,1024]{1,0:T(8,128)(2,1)S(1)}, f32[3,1024,1]{2,1,0:T(8,128)S(1)}) custom-call(f32[3,8]{1,0:T(4,128)S(1)} %copy-done.20, bf16[576,1024]{1,0:T(8,128)(2,1)S(1)} %convolution_convert_fusion.own_ref, bf16[384,1024]{1,0:T(8,128)(2,1)} %collective-permute-done.before_ref), custom_call_target="tpu_custom_call" | custom-call | tf_op jit(solution)/shard_map/pallas_call | solution.py:710
  210.3 28.9 %shard_map.387 = bf16[4,192,1024]{2,1,0:T(8,128)(2,1)S(1)} custom-call(bf16[192,1024]{1,0:T(8,128)(2,1)S(1)} %get-tuple-element.80.refs_0_.attended_ref), custom_call_target="tpu_custom_call" | custom-call | tf_op jit(solution)/shard_map/pallas_call | solution.py:377
  239.2 4.4 shard_map.388
  248.4 94.2 %shard_map.389 = (f32[1024,768]{1,0:T(8,128)}, bf16[8,288,768]{2,1,0:T(8,128)(2,1)}, bf16[8,288,768]{2,1,0:T(8,128)(2,1)}, f32[8,128]{1,0:T(8,128)}) custom-call(bf16[1024,768]{1,0:T(8,128)(2,1)} %copy-done.3, s32[2,1024]{1,0:T(2,128)} %copy-done.29, s32[1024,2]{1,0:T(8,128)} %copy.76.dest_columns, f32[1024,8]{1,0:T(8,128)} %copy-done.14, ...), custom_call_target="tpu_custom_call" | custom-call | tf_op jit(solution)/shard_map/pallas_call | solution.py:1324
  345.4 55.6 %shard_map.390 = (bf16[1024,768]{1,0:T(8,128)(2,1)S(1)}, f32[1024,768]{1,0:T(8,128)S(1)}) custom-call(f32[1024,768]{1,0:T(8,128)} %get-tuple-element.84.part_ref, f32[1024,768]{1,0:T(8,128)} %copy-done.1, f32[1,768]{1,0:T(1,128)S(1)} %get-tuple-element.164.refs_1_), custom_call_target="tpu_custom_call" | custom-call | tf_op jit(solution)/shard_map/pallas_call | solution.py:184
  403.8 23.3 %shard_map.391.stats_ref = f32[2,1024]{1,0:T(2,128)} custom-call(bf16[8768,768]{1,0:T(8,128)(2,1)} %bitcast.111, bf16[1024,768]{1,0:T(8,128)(2,1)} %copy-done), custom_call_target="tpu_custom_call" | custom-call | tf_op jit(solution)/shard_map/pallas_call | solution.py:894
  427.1 6.8 shard_map.392.logsum_ref
  435.9 44.0 %shard_map.393 = (bf16[8000,1024]{1,0:T(8,128)(2,1)}, f32[1024,768]{1,0:T(8,128)}, f32[1,1024]{1,0:T(1,128)}) custom-call(bf16[8768,768]{1,0:T(8,128)(2,1)} %bitcast.112, bf16[1024,768]{1,0:T(8,128)(2,1)} %copy-done, f32[1,1024]{1,0:T(1,128)} %shard_map.392.logsum_ref, s32[2,1024]{1,0:T(2,128)} %subtract_bitcast_fusion.wanted_ref, ...), custom_call_target="tpu_custom_call" | custom-call | tf_op jit(solution)/shard_map/pallas_call | solution.py:986
  479.9 45.9 %shard_map.394 = (bf16[1024,768]{1,0:T(8,128)(2,1)S(1)}, f32[1024,768]{1,0:T(8,128)S(1)}, f32[1,768]{1,0:T(1,128)S(1)}) custom-call(f32[1024,768]{1,0:T(8,128)} %get-tuple-element.90.part_ref, f32[1024,768]{1,0:T(8,128)} %copy-done.5, f32[1,768]{1,0:T(1,128)S(1)} %get-tuple-element.164.refs_1_), custom_call_target="tpu_custom_call" | custom-call | tf_op jit(solution)/shard_map/pallas_call | solution.py:184
  528.6 93.1 %shard_map.395 = (f32[1024,768]{1,0:T(8,128)}, f32[2,1024]{1,0:T(2,128)}, f32[768,768]{1,0:T(8,128)}, f32[768,768]{1,0:T(8,128)}) custom-call(bf16[1024,768]{1,0:T(8,128)(2,1)} %copy-done.9, s32[2,1024]{1,0:T(2,128)} %copy-done.29, s32[1024,2]{1,0:T(8,128)} %copy.76.dest_columns, f32[2,1024]{1,0:T(2,128)} %copy-done.17, s32[2,1024]{1,0:T(2,128)} %bitcast.107, ...), custom_call_target="tpu_custom_call" | custom-call | tf_op jit(solution)/shard_map/pallas_call | solution.py:1466
  622.5 51.4 %shard_map.396 = (bf16[1024,768]{1,0:T(8,128)(2,1)S(1)}, f32[1024,768]{1,0:T(8,128)S(1)}, bf16[8,1024]{1,0:T(8,128)(2,1)S(1)}, f32[1,1024]{1,0:T(1,128)S(1)}, f32[1,768]{1,0:T(1,128)S(1)}) custom-call(f32[1024,768]{1,0:T(8,128)} %get-tuple-element.96.part_ref, f32[1024,768]{1,0:T(8,128)} %copy-done.1, f32[1,768]{1,0:T(1,128)S(1)} %get-tuple-element.163.gain_ref.refs_1_, ...), custom_call_target="tpu_custom_call" | custom-call | tf_op jit(solution)/shard_map/pallas_call | solution.py:184
  677.9 15.4 %shard_map.397 = (bf16[192,1024]{1,0:T(8,128)(2,1)S(1)}, f32[384,1024]{1,0:T(8,128)S(1)}, bf16[384,1024]{1,0:T(8,128)(2,1)}, f32[24,256]{1,0:T(8,128)S(1)}) custom-call(f32[3,8]{1,0:T(4,128)S(1)} %copy-done.20, bf16[576,1024]{1,0:T(8,128)(2,1)S(1)} %convolution_convert_fusion.own_ref, bf16[384,1024]{1,0:T(8,128)(2,1)} %collective-permute-done.before_ref, ...), custom_call_target="tpu_custom_call" | custom-call | tf_op jit(solution)/shard_map/pallas_call | solution.py:849
  704.6 5.2 collective-permute-done.4
  712.4 3.1 fusion.20.part_ref
  715.5 45.1 %shard_map.398 = (bf16[1024,768]{1,0:T(8,128)(2,1)S(1)}, f32[8,768]{1,0:T(8,128)S(1)}) custom-call(f32[1024,768]{1,0:T(8,128)} %fusion.20.part_ref, bf16[1024,768]{1,0:T(8,128)(2,1)S(1)} %shard_map.385.embedded_ref.refs_0_, f32[1,768]{1,0:T(1,128)S(1)} %get-tuple-element.161.refs_1_, f32[1024,768]{1,0:T(8,128)} %copy-done.4, f32[1,768]{1,0:T(1,128)S(1)} %copy-done.23, ...), custom_call_target="tpu_custom_call" | custom-call | tf_op jit(solution)/shard_map/pallas_call | solution.py:184
  762.3 41.9 %shard_map.399 = (bf16[168,64,768]{2,1,0:T(8,128)(2,1)}, f32[768,768]{1,0:T(8,128)}, f32[768,768]{1,0:T(8,128)}, f32[768,768]{1,0:T(8,128)}, f32[768,768]{1,0:T(...) custom-call(s32[137]{0:T(256)} %copy-done.39, bf16[8000,1024]{1,0:T(8,128)(2,1)} %get-tuple-element.88.slope_ref, ...), custom_call_target="tpu_custom_call" | custom-call | tf_op jit(solution)/shard_map/pallas_call | solution.py:1077
  804.3 86.5 %shard_map.400 = (f32[21,64,768]{2,1,0:T(8,128)}, f32[16,768]{1,0:T(8,128)}) custom-call(bf16[168,64,768]{2,1,0:T(8,128)(2,1)} %get-tuple-element.110.parts_ref, f32[16,768]{1,0:T(8,128)} %select_maximum_fusion.small_ref), custom_call_target="tpu_custom_call" | custom-call | tf_op jit(solution)/shard_map/pallas_call | solution.py:1634
  897.6 10.4 %fusion.19 = (f32[1,1,21,64,768]{4,3,2,1,0:T(8,128)}, f32[1,1,21,64,768]{4,3,2,1,0:T(8,128)}, f32[1,1,21,64,768]{4,3,2,1,0:T(8,128)}) fusion(f32[21,64,768]{2,1,0:T(8,128)} %get-tuple-element.116, pred[21]{0:T(512)(128)(4,1)S(1)} %copy-done.46, f32[1,1,21,64,768]{4,3,2,1,0:T(8,128)} %param.35, f32[1,1,21,64,768]{4,3,2,1,0:T(8,128)} %param.34, ...), kind=kLoop, calls=%fused_computation.95 | loop fusion | flops 16515072 | bytes 28901480 | tf_op jit(solution)/shard_map/broadcast_in_dim | solution.py:1997
  (181 shorter events, 66.1 us)
Async XLA Ops:
  8.7 180.0 %copy-start.29 = (s32[2,1024]{1,0:T(2,128)}, s32[2,1024]{1,0:T(2,128)S(1)}, u32[]{:S(2)}) copy-start(s32[2,1024]{1,0:T(2,128)S(1)} %add_select_fusion.1.dest_rows) | copy-start | bytes 24580
  14.5 105.5 %copy-start.34 = (f32[3,768]{1,0:T(4,128)S(1)}, f32[3,768]{1,0:T(4,128)}, u32[]{:S(2)}) copy-start(f32[3,768]{1,0:T(4,128)} %param.42) | copy-start | bytes 27652
  113.1 79.8 %collective-permute-start.3 = (bf16[192,768]{1,0:T(8,128)(2,1)S(1)}, bf16[192,768]{1,0:T(8,128)(2,1)}, u32[]{:S(2)}, u32[]{:S(2)}) collective-permute-start(bf16[192,768]{1,0:T(8,128)(2,1)S(1)} %bitcast.99), channel_id=1, source_target_pairs={{0,1},{1,2},{2,3},{3,0},{4,5},{5,6},{6,7},{7,4},{8,9},{9,10},{10,1... | collective-permute-start | bytes 884744 | tf_op jit(solution)/shard_map/ppermute | solution.py:1809
  114.8 77.1 %collective-permute-start.2 = (bf16[192,768]{1,0:T(8,128)(2,1)S(1)}, bf16[192,768]{1,0:T(8,128)(2,1)}, u32[]{:S(2)}, u32[]{:S(2)}) collective-permute-start(bf16[192,768]{1,0:T(8,128)(2,1)S(1)} %bitcast.100), channel_id=1, source_target_pairs={{0,2},{1,3},{2,0},{3,1},{4,6},{5,7},{6,4},{7,5},{8,10},{9,11},{10,... | collective-permute-start | bytes 884744 | tf_op jit(solution)/shard_map/ppermute | solution.py:1809
  117.3 73.6 %collective-permute-start.1 = (bf16[192,768]{1,0:T(8,128)(2,1)S(1)}, bf16[192,768]{1,0:T(8,128)(2,1)}, u32[]{:S(2)}, u32[]{:S(2)}) collective-permute-start(bf16[192,768]{1,0:T(8,128)(2,1)S(1)} %bitcast.101), channel_id=1, source_target_pairs={{0,3},{1,0},{2,1},{3,2},{4,7},{5,4},{6,5},{7,6},{8,11},{9,8},{10,9... | collective-permute-start | bytes 884744 | tf_op jit(solution)/shard_map/ppermute | solution.py:1809
  119.9 60.9 %copy-start.27 = (bf16[9,64,768]{2,1,0:T(8,128)(2,1)}, bf16[9,64,768]{2,1,0:T(8,128)(2,1)S(1)}, u32[]{:S(2)}) copy-start(bf16[9,64,768]{2,1,0:T(8,128)(2,1)S(1)} %slice.68) | copy-start | bytes 2654212
  183.0 14.1 %collective-permute-start = (bf16[384,1024]{1,0:T(8,128)(2,1)}, bf16[384,1024]{1,0:T(8,128)(2,1)}, u32[]{:S(2)}, u32[]{:S(2)}) collective-permute-start(bf16[384,1024]{1,0:T(8,128)(2,1)} %slice.99), channel_id=1, source_target_pairs={{0,4},{1,5},{2,6},{3,7},{8,12},{9,13},{10,14},{11,15},{16,20},{17,... | collective-permute-start | bytes 2359304 | tf_op jit(solution)/shard_map/ppermute | solution.py:38
  210.3 28.9 %copy-start.7 = (bf16[192,1024]{1,0:T(8,128)(2,1)}, bf16[192,1024]{1,0:T(8,128)(2,1)S(1)}, u32[]{:S(2)}) copy-start(bf16[192,1024]{1,0:T(8,128)(2,1)S(1)} %get-tuple-element.80.refs_0_.attended_ref) | copy-start | bytes 1179652
  210.3 28.9 %copy-start.13 = (f32[3,1024,1]{2,1,0:T(8,128)}, f32[3,1024,1]{2,1,0:T(8,128)S(1)}, u32[]{:S(2)}) copy-start(f32[3,1024,1]{2,1,0:T(8,128)S(1)} %get-tuple-element.89.logsum_ref) | copy-start | bytes 36868
  528.6 93.1 %copy-start.44 = (f32[1,1024]{1,0:T(1,128)S(1)}, f32[1,1024]{1,0:T(1,128)}, u32[]{:S(2)}) copy-start(f32[1,1024]{1,0:T(1,128)} %get-tuple-element.99) | copy-start | bytes 12292
  528.6 93.9 %copy-start.16 = (s32[1,1024,2]{1,2,0:T(2,128)S(1)}, s32[1,1024,2]{1,2,0:T(2,128)}, u32[]{:S(2)}) copy-start(s32[1,1024,2]{1,2,0:T(2,128)} %param.30) | copy-start | bytes 24580
  528.6 93.9 %copy-start.18 = (f32[2,1024]{1,0:T(2,128)S(1)}, f32[2,1024]{1,0:T(2,128)}, u32[]{:S(2)}) copy-start(f32[2,1024]{1,0:T(2,128)} %copy-done.17) | copy-start | bytes 24580
  677.9 18.6 %copy-start.33 = (pred[21,137]{1,0:T(8,128)(4,1)S(1)}, pred[21,137]{1,0:T(8,128)(4,1)}, u32[]{:S(2)}) copy-start(pred[21,137]{1,0:T(8,128)(4,1)} %iota_compare_fusion.3) | copy-start | bytes 8635
  695.0 14.7 %collective-permute-start.4 = (bf16[384,1024]{1,0:T(8,128)(2,1)}, bf16[384,1024]{1,0:T(8,128)(2,1)}, u32[]{:S(2)}, u32[]{:S(2)}) collective-permute-start(bf16[384,1024]{1,0:T(8,128)(2,1)} %get-tuple-element.103), channel_id=1, source_target_pairs={{4,0},{5,1},{6,2},{7,3},{12,8},{13,9},{14,10},{15,11},{20,16},{21,... | collective-permute-start | bytes 2359304 | tf_op jit(solution)/shard_map/ppermute | solution.py:38
  804.2 89.9 %copy-start.35 = (f32[3,768]{1,0:T(4,128)S(1)}, f32[3,768]{1,0:T(4,128)}, u32[]{:S(2)}) copy-start(f32[3,768]{1,0:T(4,128)} %param.42) | copy-start | bytes 27652
  804.2 89.9 %copy-start.41 = (f32[3,768]{1,0:T(4,128)S(1)}, f32[3,768]{1,0:T(4,128)}, u32[]{:S(2)}) copy-start(f32[3,768]{1,0:T(4,128)} %param.43) | copy-start | bytes 27652
  804.2 89.9 %copy-start.42 = (f32[3,768]{1,0:T(4,128)S(1)}, f32[3,768]{1,0:T(4,128)}, u32[]{:S(2)}) copy-start(f32[3,768]{1,0:T(4,128)} %param.44) | copy-start | bytes 27652
  804.3 91.2 %copy-start.31 = (f32[768,8]{0,1:T(8,128)S(1)}, f32[768,8]{0,1:T(8,128)}, u32[]{:S(2)}) copy-start(f32[768,8]{0,1:T(8,128)} %param.45) | copy-start | bytes 73732
  804.3 91.2 %copy-start.37 = (f32[768,8]{0,1:T(8,128)S(1)}, f32[768,8]{0,1:T(8,128)}, u32[]{:S(2)}) copy-start(f32[768,8]{0,1:T(8,128)} %param.46) | copy-start | bytes 73732
  804.3 91.2 %copy-start.38 = (f32[768,8]{0,1:T(8,128)S(1)}, f32[768,8]{0,1:T(8,128)}, u32[]{:S(2)}) copy-start(f32[768,8]{0,1:T(8,128)} %param.47) | copy-start | bytes 73732
  804.3 92.7 %copy-start.47 = (f32[3,8]{1,0:T(4,128)S(1)}, f32[3,8]{1,0:T(4,128)}, u32[]{:S(2)}) copy-start(f32[3,8]{1,0:T(4,128)} %param.49) | copy-start | bytes 292
  804.3 92.6 %copy-start.48 = (f32[3,8]{1,0:T(4,128)S(1)}, f32[3,8]{1,0:T(4,128)}, u32[]{:S(2)}) copy-start(f32[3,8]{1,0:T(4,128)} %param.50) | copy-start | bytes 292
  804.3 93.2 %copy-start.45 = (f32[21]{0:T(128)S(1)}, f32[21]{0:T(128)}, u32[]{:S(2)}) copy-start(f32[21]{0:T(128)} %select_reduce_fusion.1) | copy-start | bytes 256
  804.3 93.2 %copy-start.46 = (pred[21]{0:T(512)(128)(4,1)S(1)}, pred[21]{0:T(512)(128)(4,1)}, u32[]{:S(2)}) copy-start(pred[21]{0:T(512)(128)(4,1)} %select_reduce_fusion.2) | copy-start | bytes 67
  (31 other events, 112.5 us)

commit v6 on v5

--- a/solution.py
+++ b/solution.py
@@ -214,13 +214,6 @@
     return lax.rsqrt(jnp.mean(values * values, -1, keepdims=True) + norm_epsilon)
 
 
-def finish_mixture(total, span, rank, extras, aux, scratch):
-    stream_one, gain = extras
-    stream_two = stream_one[span] + total
-    aux[0][span] = stream_two
-    return (stream_two * inverse_rms(stream_two) * gain[...]).astype(jnp.bfloat16)
-
-
 def norm_back_rows(values, gain, upstream):
     inverse = inverse_rms(values)
     normed = values * inverse
@@ -257,14 +250,6 @@
     @pl.when(jnp.logical_not(inner))
     def _():
         copy.wait_recv()
-
-
-def finish_head_grad(total, span, rank, extras, aux, scratch):
-    stream_two, gain = extras
-    grad_two, gain_grad = norm_back_rows(stream_two[span], gain[...], total)
-    aux[0][span] = grad_two
-    aux[1][...] += gain_grad
-    return grad_two.astype(jnp.bfloat16)
 
 
 def gate_copies(rank, extras, scratch):
@@ -391,9 +376,17 @@
 
 
 def middle_kernel(
-    attended_ref, project_ref, embedded_ref, gain_ref, router_ref, routes_ref,
-    stream_ref, normed_ref, rows_ref, columns_ref,
+    attended_ref, embedded_ref, gain_ref, router_ref, routes_ref, *refs
 ):
+    rolled, (stream_ref, normed_ref, rows_ref, columns_ref, project_ref) = refs[:4], refs[4:]
+
+    @pl.when(pl.program_id(0) == 0)
+    def _():
+        for step in range(4):
+            lines = rolled[step].shape[0]
+            owner = lax.rem(lax.axis_index("tensor") + 4 - step, 4)
+            project_ref[pl.ds(pl.multiple_of(owner * lines, lines), lines)] = rolled[step][...]
+
     scale = math.sqrt(embedded_ref.shape[1])
     stream = embedded_ref[...].astype(jnp.float32) * scale + lax.dot_general(
         attended_ref[...], project_ref[...], (((0,), (0,)), ((), ())), preferred_element_type=jnp.float32
@@ -417,7 +410,7 @@
     columns_ref[...] = jnp.concatenate([gates, jnp.zeros((6, gates.shape[1]), jnp.float32)], 0).T
 
 
-def middle(attended, project, embedded, gain, router, routes):
+def middle(attended, rolled, embedded, gain, router, routes):
     tokens, width = embedded.shape
     tile = 256
     fixed = lambda k: (0, 0)
@@ -433,10 +426,12 @@
             jax.ShapeDtypeStruct((2, tokens), jnp.float32),
             jax.ShapeDtypeStruct((tokens, 8), jnp.float32),
         ],
-        in_specs=[along(width), whole(project), down(width), whole(gain), whole(router), along(2)],
+        in_specs=[along(width), down(width), whole(gain), whole(router), along(2)]
+        + [whole(x) for x in rolled],
         out_specs=[down(width), down(width), along(2), down(8)],
+        scratch_shapes=[pltpu.VMEM((width, width), jnp.bfloat16)],
         compiler_params=pltpu.CompilerParams(vmem_limit_bytes=40 << 20),
-    )(attended, project, embedded, gain, router, routes)
+    )(attended, embedded, gain, router, routes, *rolled)
 
 
 def gather_units_kernel(
@@ -498,22 +493,15 @@
     lax.fori_loop(0, chunks, start_core, 0)
     total[...] = jnp.zeros_like(total)
 
-    def look(place, which, first, count):
-        lines = count * unit_rows
-        begin = (place * 2 + which) * slots + first
+    def look(place, which):
+        begin = (place * 2 + which) * slots
+        lines = slots * unit_rows
         column = lax.broadcasted_iota(jnp.int32, (tokens, lines), 1) + begin * unit_rows
         hit = jnp.where(column == rows_ref[...], 1.0, 0.0).astype(jnp.bfloat16)
-        block = held[pl.ds(begin, count)].reshape(lines, width)
+        block = held[pl.ds(begin, slots)].reshape(lines, width)
         total[...] += jnp.dot(hit, block, preferred_element_type=jnp.float32)
 
-    def look_block(place, which):
-        def one(q, carry):
-            look(place, which, q * size, size)
-            return carry
-
-        lax.fori_loop(0, chunks, one, 0)
-
-    look_block(chip, core)
+    look(chip, core)
 
     def relay(i, carry):
         to_beside(i).wait_recv()
@@ -532,31 +520,31 @@
 
         to_core(2, j).start()
         to_core(0, i).wait_recv()
-        look(chip, 1 - core, i * size, size)
         return carry
 
     lax.fori_loop(0, chunks, relay, 0)
-    look_block(beside, core)
-    look_block(across, core)
+    look(chip, 1 - core)
+    look(beside, core)
+    look(across, core)
 
     def last(q, carry):
         passed_on(q, opposite, opposite).wait_recv()
         to_core(3, q).start()
         to_core(1, q).wait_recv()
-        look(beside, 1 - core, q * size, size)
         to_core(2, q).wait_recv()
-        look(across, 1 - core, q * size, size)
-        look(opposite, core, q * size, size)
         return carry
 
     lax.fori_loop(0, chunks, last, 0)
+    for source in (beside, across):
+        look(source, 1 - core)
+    look(opposite, core)
 
     def ending(q, carry):
         to_core(3, q).wait_recv()
-        look(opposite, 1 - core, q * size, size)
         return carry
 
     lax.fori_loop(0, chunks, ending, 0)
+    look(opposite, 1 - core)
     looked_ref[...] = total[...].astype(jnp.bfloat16)
 
     def place_unit(u, carry):
@@ -868,144 +856,321 @@
     )(biases, own, before, logsum, grad, project)
 
 
-def head_sums_kernel(table_ref, rows_ref, stats_ref, turned):
-    @pl.when(pl.program_id(0) == 0)
-    def _():
-        turned[...] = rows_ref[...].astype(jnp.float32).T.astype(jnp.bfloat16)
-        stats_ref[0:1, :] = jnp.full_like(stats_ref[0:1, :], masked_score)
-        stats_ref[1:2, :] = jnp.zeros_like(stats_ref[1:2, :])
-
-    logits = jnp.dot(table_ref[...], turned[...], preferred_element_type=jnp.float32)
-    before = stats_ref[0:1, :]
-    top = jnp.maximum(before, jnp.max(logits, 0, keepdims=True))
-    stats_ref[1:2, :] = stats_ref[1:2, :] * jnp.exp(before - top) + jnp.sum(
-        jnp.exp(logits - top), 0, keepdims=True
-    )
-    stats_ref[0:1, :] = top
-
-
 def vocab_tile(vocab):
     return max(k for k in range(16, 1601, 16) if vocab % k == 0)
 
 
-def head_sums(weights, rows, vocab):
-    tokens, width = rows.shape
-    tile = vocab_tile(vocab)
-    return pl.pallas_call(
-        head_sums_kernel,
-        grid=(vocab // tile,),
-        out_shape=jax.ShapeDtypeStruct((2, tokens), jnp.float32),
-        in_specs=[pl.BlockSpec((tile, width), lambda k: (k, 0)), pl.BlockSpec((tokens, width), lambda k: (0, 0))],
-        out_specs=pl.BlockSpec((2, tokens), lambda k: (0, 0)),
-        scratch_shapes=[pltpu.VMEM((width, tokens), jnp.bfloat16)],
-        compiler_params=pltpu.CompilerParams(vmem_limit_bytes=56 << 20),
-    )(weights, rows)
-
-
-def join_sums_kernel(stats_ref, logsum_ref, landed, send_sem, recv_sem):
+def head_line_kernel(
+    tile, part_ref, stream_ref, gain_ref, table_ref, wanted_ref, weight_ref,
+    low_ref, grad_low_ref, grad_ref, gain_grad, logsum_ref, picked_ref, slopes_ref,
+    table, stage, from_end, from_mid, own, turned, stats, landed, slope_tiles, total,
+    load_sem, send_sem, end_sem, mid_sem, back_sem, back_recv, stat_send, stat_recv, store_sem,
+):
     rank = lax.axis_index("tensor")
+    inner = (rank == 1) | (rank == 2)
+    end_peer = jnp.where(rank < 2, 1 - rank, 5 - rank)
+    mid_peer = 3 - rank
+    count, rows = stage.shape[:2]
+    columns = turned.shape[1]
+    pieces = table.shape[0] // tile
+    group = columns // rows
+    tiles = count // group
+    units = tiles * pieces
+    vocab = table.shape[0]
+    load = pltpu.make_async_copy(table_ref.at[pl.ds(0, vocab)], table, load_sem)
+    load.start()
     barrier = pltpu.get_barrier_semaphore()
     for step in (1, 2, 3):
         other = lax.rem(rank + step, 4)
         pl.semaphore_signal(barrier, inc=1, device_id={"tensor": other}, device_id_type=MESH_ID)
     pl.semaphore_wait(barrier, 3)
-    copies = []
-    for step in (1, 2, 3):
-        copy = pltpu.make_async_remote_copy(
-            src_ref=stats_ref,
-            dst_ref=landed.at[step - 1],
-            send_sem=send_sem.at[step - 1],
-            recv_sem=recv_sem.at[step - 1],
-            device_id={"tensor": lax.rem(rank + step, 4)},
+
+    def span(i):
+        return pl.ds(pl.multiple_of(i * rows, rows), rows)
+
+    def over(t):
+        return pl.ds(pl.multiple_of(t * columns, columns), columns)
+
+    def line_copy(source, target, send, recv, peer):
+        return pltpu.make_async_remote_copy(
+            src_ref=source,
+            dst_ref=target,
+            send_sem=send,
+            recv_sem=recv,
+            device_id={"tensor": peer},
             device_id_type=MESH_ID,
         )
+
+    def to_inner(i):
+        return line_copy(stage.at[i], from_end.at[i], send_sem.at[i], end_sem.at[i], end_peer)
+
+    def to_middle(i):
+        return line_copy(stage.at[i], from_mid.at[i], send_sem.at[i], mid_sem.at[i], mid_peer)
+
+    def to_end(ref, i):
+        rows_of = ref.at[span(i)]
+        return line_copy(rows_of, rows_of, back_sem.at[i], back_recv.at[i], end_peer)
+
+    def repeat(first, last, body):
+        def step(i, carry):
+            body(i)
+            return carry
+
+        lax.fori_loop(first, last, step, 0)
+
+    def turn(t):
+        turned[...] = low_ref[over(t)].astype(jnp.float32).T.astype(jnp.bfloat16)
+
+    def table_rows(k):
+        return table[pl.ds(pl.multiple_of(k * tile, tile), tile)]
+
+    def sums_unit(n):
+        t, k = n // pieces, lax.rem(n, pieces)
+
+        @pl.when(k == 0)
+        def _():
+            turn(t)
+
+        logits = jnp.dot(table_rows(k), turned[...], preferred_element_type=jnp.float32)
+        before = stats[0:1, over(t)]
+        top = jnp.maximum(before, jnp.max(logits, 0, keepdims=True))
+        stats[1:2, over(t)] = stats[1:2, over(t)] * jnp.exp(before - top) + jnp.sum(
+            jnp.exp(logits - top), 0, keepdims=True
+        )
+        stats[0:1, over(t)] = top
+
+    stats[0:1, :] = jnp.full_like(stats[0:1, :], masked_score)
+    stats[1:2, :] = jnp.zeros_like(stats[1:2, :])
+
+    @pl.when(jnp.logical_not(inner))
+    def _():
+        def push(i):
+            stage[i] = part_ref[span(i)].astype(jnp.bfloat16)
+            to_inner(i).start()
+
+        repeat(0, count, push)
+        load.wait()
+
+        def forward(t):
+            repeat(0, group, lambda c: to_end(low_ref, t * group + c).wait_recv())
+            repeat(0, pieces, lambda k: sums_unit(t * pieces + k))
+
+        repeat(0, tiles, forward)
+        repeat(0, count, lambda i: to_inner(i).wait_send())
+
+    @pl.when(inner)
+    def _():
+        gain_grad[...] = jnp.zeros_like(gain_grad)
+        load.wait()
+        ahead = group + line_lag
+
+        def step(i):
+            @pl.when(i < count)
+            def _():
+                to_inner(i).wait_recv()
+                mine = part_ref[span(i)] + from_end[i].astype(jnp.float32)
+                stage[i] = mine.astype(jnp.bfloat16)
+                to_middle(i).start()
+
+            @pl.when(i >= line_lag)
+            def _():
+                j = i - line_lag
+                to_middle(j).wait_recv()
+                stream_two = stream_ref[span(j)] + (
+                    stage[j].astype(jnp.float32) + from_mid[j].astype(jnp.float32)
+                )
+                grad_ref[span(j)] = stream_two
+                low_ref[span(j)] = (stream_two * inverse_rms(stream_two) * gain_ref[...]).astype(
+                    jnp.bfloat16
+                )
+                to_end(low_ref, j).start()
+
+            @pl.when(i >= ahead)
+            def _():
+                sums_unit(i - ahead)
+
+        repeat(0, count + line_lag, step)
+        repeat(count + line_lag - ahead, units, sums_unit)
+
+        def drain(i):
+            to_middle(i).wait_send()
+            to_end(low_ref, i).wait_send()
+
+        repeat(0, count, drain)
+
+    copies = [
+        line_copy(
+            stats, landed.at[step - 1], stat_send.at[step - 1], stat_recv.at[step - 1], lax.rem(rank + step, 4)
+        )
+        for step in (1, 2, 3)
+    ]
+    for copy in copies:
         copy.start()
-        copies.append(copy)
     for copy in copies:
         copy.wait()
     tops, sums = [], []
     for source in range(4):
-        piece = stats_ref[...]
+        piece = stats[...]
         for step in (1, 2, 3):
             piece = jnp.where(lax.rem(source + step, 4) == rank, landed[step - 1], piece)
         tops.append(piece[0:1])
         sums.append(piece[1:2])
     top = jnp.maximum(jnp.maximum(tops[0], tops[1]), jnp.maximum(tops[2], tops[3]))
-    total = sums[0] * jnp.exp(tops[0] - top)
+    whole = sums[0] * jnp.exp(tops[0] - top)
     for source in (1, 2, 3):
-        total = total + sums[source] * jnp.exp(tops[source] - top)
-    logsum_ref[...] = top + jnp.log(total)
-
-
-def join_sums(stats, collective_id):
-    tokens = stats.shape[1]
+        whole = whole + sums[source] * jnp.exp(tops[source] - top)
+    logsum_ref[...] = top + jnp.log(whole)
+    picked_ref[...] = jnp.zeros_like(picked_ref)
+
+    def store(t):
+        return pltpu.make_async_copy(
+            slope_tiles.at[lax.rem(t, 2)], slopes_ref.at[:, over(t)], store_sem.at[lax.rem(t, 2)]
+        )
+
+    def back_unit(n):
+        t, k = n // pieces, lax.rem(n, pieces)
+
+        @pl.when(k == 0)
+        def _():
+            turn(t)
+            total[...] = jnp.zeros_like(total)
+
+            @pl.when(t >= 2)
+            def _():
+                store(t - 2).wait()
+
+        lines = table_rows(k)
+        logits = jnp.dot(lines, turned[...], preferred_element_type=jnp.float32)
+        row = lax.broadcasted_iota(jnp.int32, logits.shape, 0)
+        base = k * tile
+        hits = jnp.where(row == wanted_ref[0:1, over(t)] - base, weight_ref[0:1, over(t)], 0.0)
+        hits = hits + jnp.where(
+            row == wanted_ref[1:2, over(t)] - base, weight_ref[1:2, over(t)], 0.0
+        )
+        picked_ref[:, over(t)] += jnp.sum(hits * logits, 0, keepdims=True)
+        softmax = jnp.exp(logits - logsum_ref[:, over(t)])
+        slope = (
+            (weight_ref[2:3, over(t)] * softmax - hits) * weight_ref[3:4, over(t)]
+        ).astype(jnp.bfloat16)
+        slope_tiles[lax.rem(t, 2), pl.ds(pl.multiple_of(base, tile), tile)] = slope
+        total[...] += lax.dot_general(
+            slope, lines, (((0,), (0,)), ((), ())), preferred_element_type=jnp.float32
+        )
+
+        @pl.when(k == pieces - 1)
+        def _():
+            store(t).start()
+
+    @pl.when(jnp.logical_not(inner))
+    def _():
+        def unit(n):
+            back_unit(n)
+
+            @pl.when(lax.rem(n, pieces) == pieces - 1)
+            def _():
+                first = (n // pieces) * group
+
+                def push(c):
+                    stage[first + c] = total[span(c)].astype(jnp.bfloat16)
+                    to_inner(first + c).start()
+
+                repeat(0, group, push)
+
+        repeat(0, units, unit)
+
+        def finish(i):
+            to_end(grad_low_ref, i).wait_recv()
+            to_inner(i).wait_send()
+
+        repeat(0, count, finish)
+
+    @pl.when(inner)
+    def _():
+        def settle(j):
+            to_middle(j).wait_recv()
+            upstream = stage[j].astype(jnp.float32) + from_mid[j].astype(jnp.float32)
+            grad_two, gain_part = norm_back_rows(grad_ref[span(j)], gain_ref[...], upstream)
+            grad_ref[span(j)] = grad_two
+            gain_grad[...] += gain_part
+            grad_low_ref[span(j)] = grad_two.astype(jnp.bfloat16)
+            to_end(grad_low_ref, j).start()
+
+        def exchange(i):
+            to_inner(i).wait_recv()
+            stage[i] = (own[span(i)] + from_end[i].astype(jnp.float32)).astype(jnp.bfloat16)
+            to_middle(i).start()
+
+            @pl.when(i >= line_lag)
+            def _():
+                settle(i - line_lag)
+
+        def unit(n):
+            back_unit(n)
+            t, k = n // pieces, lax.rem(n, pieces)
+
+            @pl.when(k == pieces - 1)
+            def _():
+                own[over(t)] = total[...]
+
+            @pl.when((t >= 1) & (k >= pieces - group))
+            def _():
+                exchange((t - 1) * group + k - (pieces - group))
+
+        repeat(0, units, unit)
+        repeat(count - group, count, exchange)
+        repeat(count - line_lag, count, settle)
+
+        def drain(i):
+            to_middle(i).wait_send()
+            to_end(grad_low_ref, i).wait_send()
+
+        repeat(0, count, drain)
+
+    store(tiles - 2).wait()
+    store(tiles - 1).wait()
+
+
+def head_line(part, stream, gain, weights, wanted, weight_rows, vocab, collective_id):
+    tokens, width = part.shape
+    rows, columns = 64, 256
+    count = tokens // rows
+    chunks = pltpu.VMEM((count, rows, width), jnp.bfloat16)
+    rows_low = jax.ShapeDtypeStruct((tokens, width), jnp.bfloat16)
+    along = jax.ShapeDtypeStruct((1, tokens), jnp.float32)
+    line_sems = pltpu.SemaphoreType.DMA((count,))
     return pl.pallas_call(
-        join_sums_kernel,
-        out_shape=jax.ShapeDtypeStruct((1, tokens), jnp.float32),
-        in_specs=[whole_vmem],
-        out_specs=whole_vmem,
+        functools.partial(head_line_kernel, vocab_tile(vocab)),
+        out_shape=[
+            rows_low,
+            rows_low,
+            jax.ShapeDtypeStruct((tokens, width), jnp.float32),
+            jax.ShapeDtypeStruct((1, width), jnp.float32),
+            along,
+            along,
+            jax.ShapeDtypeStruct((vocab, tokens), jnp.bfloat16),
+        ],
+        in_specs=[whole_vmem] * 3 + [whole_any] + [whole_vmem] * 2,
+        out_specs=[whole_vmem] * 6 + [whole_any],
         scratch_shapes=[
+            pltpu.VMEM((vocab, width), jnp.bfloat16),
+            chunks,
+            chunks,
+            chunks,
+            pltpu.VMEM((tokens, width), jnp.float32),
+            pltpu.VMEM((width, columns), jnp.bfloat16),
+            pltpu.VMEM((2, tokens), jnp.float32),
             pltpu.VMEM((3, 2, tokens), jnp.float32),
-            pltpu.SemaphoreType.DMA((3,)),
-            pltpu.SemaphoreType.DMA((3,)),
-        ],
-        compiler_params=pltpu.CompilerParams(collective_id=collective_id, has_side_effects=True),
-    )(stats)
-
-
-def head_back_kernel(
-    tile, table_ref, rows_ref, logsum_ref, wanted_ref, weight_ref, slope_ref, grad_ref, picked_ref, turned
-):
-    step = pl.program_id(0)
-
-    @pl.when(step == 0)
-    def _():
-        turned[...] = rows_ref[...].astype(jnp.float32).T.astype(jnp.bfloat16)
-        picked_ref[...] = jnp.zeros_like(picked_ref)
-        grad_ref[...] = jnp.zeros_like(grad_ref)
-
-    logits = jnp.dot(table_ref[...], turned[...], preferred_element_type=jnp.float32)
-    row = lax.broadcasted_iota(jnp.int32, logits.shape, 0)
-    base = step * tile
-    hits = jnp.where(row == wanted_ref[0:1, :] - base, weight_ref[0:1, :], 0.0) + jnp.where(
-        row == wanted_ref[1:2, :] - base, weight_ref[1:2, :], 0.0
-    )
-    picked_ref[...] += jnp.sum(hits * logits, 0, keepdims=True)
-    softmax = jnp.exp(logits - logsum_ref[...])
-    slope = ((weight_ref[2:3, :] * softmax - hits) * weight_ref[3:4, :]).astype(jnp.bfloat16)
-    slope_ref[...] = slope
-    grad_ref[...] += lax.dot_general(
-        slope, table_ref[...], (((0,), (0,)), ((), ())), preferred_element_type=jnp.float32
-    )
-
-
-def head_back(weights, rows, logsum, wanted, weight_rows, vocab):
-    tokens, width = rows.shape
-    tile = vocab_tile(vocab)
-    fixed = lambda k: (0, 0)
-    return pl.pallas_call(
-        functools.partial(head_back_kernel, tile),
-        grid=(vocab // tile,),
-        out_shape=[
-            jax.ShapeDtypeStruct((vocab, tokens), jnp.bfloat16),
-            jax.ShapeDtypeStruct((tokens, width), jnp.float32),
-            jax.ShapeDtypeStruct((1, tokens), jnp.float32),
-        ],
-        in_specs=[
-            pl.BlockSpec((tile, width), lambda k: (k, 0)),
-            pl.BlockSpec((tokens, width), fixed),
-            pl.BlockSpec((1, tokens), fixed),
-            pl.BlockSpec((2, tokens), fixed),
-            pl.BlockSpec((4, tokens), fixed),
-        ],
-        out_specs=[
-            pl.BlockSpec((tile, tokens), lambda k: (k, 0)),
-            pl.BlockSpec((tokens, width), fixed),
-            pl.BlockSpec((1, tokens), fixed),
-        ],
-        scratch_shapes=[pltpu.VMEM((width, tokens), jnp.bfloat16)],
-        compiler_params=pltpu.CompilerParams(vmem_limit_bytes=60 << 20),
-    )(weights, rows, logsum, wanted, weight_rows)
+            pltpu.VMEM((2, vocab, columns), jnp.bfloat16),
+            pltpu.VMEM((columns, width), jnp.float32),
+            pltpu.SemaphoreType.DMA,
+        ]
+        + [line_sems] * 5
+        + [pltpu.SemaphoreType.DMA((3,))] * 2
+        + [pltpu.SemaphoreType.DMA((2,))],
+        compiler_params=pltpu.CompilerParams(
+            collective_id=collective_id, has_side_effects=True, vmem_limit_bytes=62 << 20
+        ),
+    )(part, stream, gain, weights, wanted, weight_rows)
 
 
 def weight_grads_kernel(
@@ -1809,9 +1974,6 @@
         lax.ppermute(project_low, "tensor", [(source, (source + step) % 4) for source in range(4)])
         for step in (1, 2, 3)
     ]
-    project_full = lax.dynamic_slice_in_dim(
-        jnp.concatenate(rolled[::-1] + rolled[::-1], 0), (3 - my_rank) * hidden_here, model_width, 0
-    )
     gain_rows = [norm_gains[k : k + 1] for k in range(3)]
     stream_shape = jax.ShapeDtypeStruct((tokens_here, model_width), jnp.float32)
     gain_shape = jax.ShapeDtypeStruct((1, model_width), jnp.float32)
@@ -1827,7 +1989,7 @@
     router_low = router.astype(jnp.bfloat16)
     stream_one, normed_two_low, gate_rows, gate_columns = middle(
         attended_all.reshape(model_width, tokens_here),
-        project_full,
+        rolled,
         embedded,
         gain_rows[1],
         router_low.T,
@@ -1845,11 +2007,6 @@
         )
         counts = lax.psum(counts, ("dp", "ctx"))
     weight_total = counts[0, 0] + ahead_weight * counts[1, 0]
-    head_low, stream_two = sum_line(
-        moe_partial, [stream_one, gain_rows[2]], [stream_shape], finish_mixture, 3
-    )
-    stats = head_sums(weights_low, head_low, vocab_here)
-    logsum_vocab = join_sums(stats, 7)
     local_targets = targets.reshape(tokens_here, 2).T - my_rank * vocab_here
     weight_rows = jnp.concatenate(
         [
@@ -1859,16 +2016,8 @@
         ],
         0,
     )
-    slopes, grad_head, target_sums = head_back(
-        weights_low, head_low, logsum_vocab, local_targets, weight_rows, vocab_here
-    )
-    grad_two_low, grad_two, gain_grad_three = sum_line(
-        grad_head,
-        [stream_two, gain_rows[2]],
-        [stream_shape, gain_shape],
-        finish_head_grad,
-        4,
-        prologue=clear_gain,
+    head_low, grad_two_low, grad_two, gain_grad_three, logsum_vocab, target_sums, slopes = head_line(
+        moe_partial, stream_one, gain_rows[2], weights_low, local_targets, weight_rows, vocab_here, 3
     )
     if on_square:
         moe_grad_part, gate_part, inner_grad, outer_grad = experts_backward(

time: 918 us -> 881 us (0.960)
  Pallas kernels: 807 us -> 783 us
  local copies, waits for them, and re-layouts: 34.1 us -> 23.4 us
    pallas_call x5 -> x3, Pallas kernels: 258 us -> 160 us  [sum_line(): pl.pallas_call(functools.partial(sum_line_kernel, rows, count, opening, p...]
    pallas_call x3 -> x1, Pallas kernels: 74.1 us -> 149 us  [head_line(): pl.pallas_call(functools.partial(head_line_kernel, vocab_tile(vocab)), ou...]
    unnamed x108 -> x83, local copies, waits for them, and re-layouts: 22.9 us -> 11.6 us
  transfers between devices with their start and end apart: 5 -> 5, of which waited for: 1 -> 1; matrix products, arithmetic and copies ran while one was open for 2% -> 2% of each run, Pallas kernels for 7% -> 12%
where the time goes in v6:
time: 881 us; the launch traced here: 873 us
  Pallas kernels  783 us (89%)
  other arithmetic  40.8 us (5%)
  local copies, waits for them, and re-layouts  23.4 us (3%)
    pallas_call x3, Pallas kernels, sum_line(): pl.pallas_call(functools.partial(sum_line_kernel, rows, count, opening, p...  160 us
    pallas_call x1, Pallas kernels, head_line(): pl.pallas_call(functools.partial(head_line_kernel, vocab_tile(vocab)), ou...  149 us
    pallas_call x1, Pallas kernels, gather_units(): pl.pallas_call(functools.partial(gather_units_kernel, chunks), out_shape=...  98 us
    pallas_call x1, Pallas kernels, experts_backward(): pl.pallas_call(experts_back_kernel, out_shape=[jax.ShapeDtypeStruct((toke...  93.2 us
    pallas_call x1, Pallas kernels, experts_forward(): pl.pallas_call(experts_kernel, out_shape=[jax.ShapeDtypeStruct((tokens, w...  92.7 us
    pallas_call x1, Pallas kernels, own_units(): pl.pallas_call(functools.partial(own_units_kernel, chunks), out_shape=[ja...  83.6 us
    pallas_call x1, Pallas kernels, weight_grads(): pl.pallas_call(functools.partial(weight_grads_kernel, tile // unit_rows,...  41.8 us
    pallas_call x1, Pallas kernels, gather_line(): pl.pallas_call(functools.partial(gather_line_kernel, count), out_shape=[j...  30.7 us
  transfers between devices with their start and end apart: 5, of which 1 were waited for; matrix products, arithmetic and copies ran while one was open for 2% of the time, Pallas kernels for 12%

profile of v6, /device:TPU:0, one launch (start us, length us, event | category | flops | bytes accessed | tf_op | source)
XLA Modules:
  0.0 872.9 jit_solution(10689595092180711577)
XLA Ops:
  2.9 3.4 convert_reduce_fusion
  9.7 3.8 bitcast_convert_fusion.mine_ref
  14.5 98.0 %shard_map.384 = (bf16[137,64,768]{2,1,0:T(8,128)(2,1)}, bf16[1024,768]{1,0:T(8,128)(2,1)}) custom-call(s32[137]{0:T(256)} %copy-done.31, bf16[21,64,768]{2,1,0:T(8,128)(2,1)} %bitcast_convert_fusion.mine_ref, s32[1024,1]{1,0:T(8,128)} %fusion.10.rows_ref), custom_call_target="tpu_custom_call" | custom-call | tf_op jit(solution)/shard_map/pallas_call | solution.py:574
  113.6 3.7 collective-permute-start.3
  120.2 59.9 %shard_map.385.embedded_ref.refs_0_ = bf16[1024,768]{1,0:T(8,128)(2,1)S(1)} custom-call(bf16[1024,768]{1,0:T(8,128)(2,1)S(1)} %copy-done.11), custom_call_target="tpu_custom_call" | custom-call | tf_op jit(solution)/shard_map/pallas_call | solution.py:184
  183.3 2.2 collective-permute-start
  188.0 4.0 bitcast_convert_fusion.1
  192.8 13.0 %shard_map.386 = (bf16[192,1024]{1,0:T(8,128)(2,1)S(1)}, f32[3,1024,1]{2,1,0:T(8,128)S(1)}) custom-call(f32[3,8]{1,0:T(4,128)S(1)} %copy-done.18, bf16[576,1024]{1,0:T(8,128)(2,1)S(1)} %convolution_convert_fusion.own_ref, bf16[384,1024]{1,0:T(8,128)(2,1)} %collective-permute-done.before_ref), custom_call_target="tpu_custom_call" | custom-call | tf_op jit(solution)/shard_map/pallas_call | solution.py:698
  207.0 30.7 %shard_map.387 = bf16[4,192,1024]{2,1,0:T(8,128)(2,1)S(1)} custom-call(bf16[192,1024]{1,0:T(8,128)(2,1)S(1)} %get-tuple-element.79.refs_0_.attended_ref), custom_call_target="tpu_custom_call" | custom-call | tf_op jit(solution)/shard_map/pallas_call | solution.py:362
  237.7 5.6 shard_map.388
  248.2 92.7 %shard_map.389 = (f32[1024,768]{1,0:T(8,128)}, bf16[8,288,768]{2,1,0:T(8,128)(2,1)}, bf16[8,288,768]{2,1,0:T(8,128)(2,1)}, f32[8,128]{1,0:T(8,128)}) custom-call(bf16[1024,768]{1,0:T(8,128)(2,1)} %copy-done.4, s32[2,1024]{1,0:T(2,128)} %copy-done.24, s32[1024,2]{1,0:T(8,128)} %copy.76.dest_columns, f32[1024,8]{1,0:T(8,128)} %copy-done.13, ...), custom_call_target="tpu_custom_call" | custom-call | tf_op jit(solution)/shard_map/pallas_call | solution.py:1489
  344.3 149.1 %shard_map.390 = (bf16[1024,768]{1,0:T(8,128)(2,1)}, bf16[1024,768]{1,0:T(8,128)(2,1)}, f32[1024,768]{1,0:T(8,128)}, f32[1,768]{1,0:T(1,128)}, f32[1,1024]{1,0:T...) custom-call(f32[1024,768]{1,0:T(8,128)} %get-tuple-element.83.part_ref, f32[1024,768]{1,0:T(8,128)} %copy-done, ...), custom_call_target="tpu_custom_call" | custom-call | tf_op jit(solution)/shard_map/pallas_call | solution.py:1141
  493.5 93.2 %shard_map.391 = (f32[1024,768]{1,0:T(8,128)}, f32[2,1024]{1,0:T(2,128)}, f32[768,768]{1,0:T(8,128)}, f32[768,768]{1,0:T(8,128)}) custom-call(bf16[1024,768]{1,0:T(8,128)(2,1)} %get-tuple-element.89.rows_ref, s32[2,1024]{1,0:T(2,128)} %copy-done.24, s32[1024,2]{1,0:T(8,128)} %copy.76.dest_columns, f32[2,1024]{1,0:T(2,128)} %copy-done.16, ...), custom_call_target="tpu_custom_call" | custom-call | tf_op jit(solution)/shard_map/pallas_call | solution.py:1631
  587.5 51.6 %shard_map.392 = (bf16[1024,768]{1,0:T(8,128)(2,1)S(1)}, f32[1024,768]{1,0:T(8,128)S(1)}, bf16[8,1024]{1,0:T(8,128)(2,1)S(1)}, f32[1,1024]{1,0:T(1,128)S(1)}, f32[1,768]{1,0:T(1,128)S(1)}) custom-call(f32[1024,768]{1,0:T(8,128)} %get-tuple-element.93.part_ref, f32[1024,768]{1,0:T(8,128)} %copy-done, f32[1,768]{1,0:T(1,128)S(1)} %get-tuple-element.159.gain_ref.refs_1_, ...), custom_call_target="tpu_custom_call" | custom-call | tf_op jit(solution)/shard_map/pallas_call | solution.py:184
  640.2 1.7 copy-done.5
  641.9 15.2 %shard_map.393 = (bf16[192,1024]{1,0:T(8,128)(2,1)S(1)}, f32[384,1024]{1,0:T(8,128)S(1)}, bf16[384,1024]{1,0:T(8,128)(2,1)}, f32[24,256]{1,0:T(8,128)S(1)}) custom-call(f32[3,8]{1,0:T(4,128)S(1)} %copy-done.18, bf16[576,1024]{1,0:T(8,128)(2,1)S(1)} %copy-done.2, bf16[384,1024]{1,0:T(8,128)(2,1)} %collective-permute-done.before_ref, ...), custom_call_target="tpu_custom_call" | custom-call | tf_op jit(solution)/shard_map/pallas_call | solution.py:837
  663.5 1.7 fusion.27
  665.2 7.6 collective-permute-done.4
  673.7 1.9 add_convert_fusion
  676.8 3.1 fusion.20.part_ref
  679.9 48.2 %shard_map.394 = (bf16[1024,768]{1,0:T(8,128)(2,1)S(1)}, f32[8,768]{1,0:T(8,128)S(1)}) custom-call(f32[1024,768]{1,0:T(8,128)} %fusion.20.part_ref, bf16[1024,768]{1,0:T(8,128)(2,1)S(1)} %shard_map.385.embedded_ref.refs_0_, f32[1,768]{1,0:T(1,128)S(1)} %get-tuple-element.157.refs_1_, f32[1024,768]{1,0:T(8,128)} %copy-done.5, ...), custom_call_target="tpu_custom_call" | custom-call | tf_op jit(solution)/shard_map/pallas_call | solution.py:184
  729.8 41.8 %shard_map.395 = (bf16[168,64,768]{2,1,0:T(8,128)(2,1)}, f32[768,768]{1,0:T(8,128)}, f32[768,768]{1,0:T(8,128)}, f32[768,768]{1,0:T(8,128)}, f32[768,768]{1,0:T(...) custom-call(s32[137]{0:T(256)} %copy-done.31, bf16[8000,1024]{1,0:T(8,128)(2,1)} %get-tuple-element.86.slope_ref, ...), custom_call_target="tpu_custom_call" | custom-call | tf_op jit(solution)/shard_map/pallas_call | solution.py:1242
  771.8 83.6 %shard_map.396 = (f32[21,64,768]{2,1,0:T(8,128)}, f32[16,768]{1,0:T(8,128)}) custom-call(bf16[168,64,768]{2,1,0:T(8,128)(2,1)} %get-tuple-element.107.parts_ref, f32[16,768]{1,0:T(8,128)} %select_maximum_fusion.small_ref), custom_call_target="tpu_custom_call" | custom-call | tf_op jit(solution)/shard_map/pallas_call | solution.py:1799
  862.1 10.4 %fusion.19 = (f32[1,1,21,64,768]{4,3,2,1,0:T(8,128)}, f32[1,1,21,64,768]{4,3,2,1,0:T(8,128)}, f32[1,1,21,64,768]{4,3,2,1,0:T(8,128)}) fusion(f32[21,64,768]{2,1,0:T(8,128)} %get-tuple-element.114, pred[21]{0:T(512)(128)(4,1)S(1)} %select_reduce_fusion.2, f32[1,1,21,64,768]{4,3,2,1,0:T(8,128)} %param.35, f32[1,1,21,64,768]{4,3,2,1,0:T(8,128)} %param.34, ...), kind=kLoop, calls=%fused_computation.86 | loop fusion | flops 16515072 | bytes 28901480 | tf_op jit(solution)/shard_map/broadcast_in_dim | solution.py:2146
  (151 shorter events, 42.5 us)
Async XLA Ops:
  1.4 12.0 %copy-start.26 = (s32[1,1024]{1,0:T(1,128)}, s32[1,1024]{1,0:T(1,128)S(1)}, u32[]{:S(2)}) copy-start(s32[1,1024]{1,0:T(1,128)S(1)} %get-tuple-element.153.ids_ref) | copy-start | bytes 12292
  8.7 177.1 %copy-start.24 = (s32[2,1024]{1,0:T(2,128)}, s32[2,1024]{1,0:T(2,128)S(1)}, u32[]{:S(2)}) copy-start(s32[2,1024]{1,0:T(2,128)S(1)} %add_select_fusion.1.dest_rows) | copy-start | bytes 24580
  13.4 106.1 %copy-start.27 = (f32[3,768]{1,0:T(4,128)S(1)}, f32[3,768]{1,0:T(4,128)}, u32[]{:S(2)}) copy-start(f32[3,768]{1,0:T(4,128)} %param.42) | copy-start | bytes 27652
  113.6 124.1 %collective-permute-start.3 = (bf16[192,768]{1,0:T(8,128)(2,1)S(1)}, bf16[192,768]{1,0:T(8,128)(2,1)}, u32[]{:S(2)}, u32[]{:S(2)}) collective-permute-start(bf16[192,768]{1,0:T(8,128)(2,1)S(1)} %bitcast.99), channel_id=1, source_target_pairs={{0,3},{1,0},{2,1},{3,2},{4,7},{5,4},{6,5},{7,6},{8,11},{9,8},{10,9... | collective-permute-start | bytes 884744 | tf_op jit(solution)/shard_map/ppermute | solution.py:1974
  117.3 120.4 %collective-permute-start.2 = (bf16[192,768]{1,0:T(8,128)(2,1)S(1)}, bf16[192,768]{1,0:T(8,128)(2,1)}, u32[]{:S(2)}, u32[]{:S(2)}) collective-permute-start(bf16[192,768]{1,0:T(8,128)(2,1)S(1)} %bitcast.100), channel_id=1, source_target_pairs={{0,2},{1,3},{2,0},{3,1},{4,6},{5,7},{6,4},{7,5},{8,10},{9,11},{10,... | collective-permute-start | bytes 884744 | tf_op jit(solution)/shard_map/ppermute | solution.py:1974
  117.3 120.4 %collective-permute-start.1 = (bf16[192,768]{1,0:T(8,128)(2,1)S(1)}, bf16[192,768]{1,0:T(8,128)(2,1)}, u32[]{:S(2)}, u32[]{:S(2)}) collective-permute-start(bf16[192,768]{1,0:T(8,128)(2,1)S(1)} %bitcast.101), channel_id=1, source_target_pairs={{0,1},{1,2},{2,3},{3,0},{4,5},{5,6},{6,7},{7,4},{8,9},{9,10},{10,1... | collective-permute-start | bytes 884744 | tf_op jit(solution)/shard_map/ppermute | solution.py:1974
  119.5 61.5 %copy-start.21 = (bf16[9,64,768]{2,1,0:T(8,128)(2,1)}, bf16[9,64,768]{2,1,0:T(8,128)(2,1)S(1)}, u32[]{:S(2)}) copy-start(bf16[9,64,768]{2,1,0:T(8,128)(2,1)S(1)} %slice.68) | copy-start | bytes 2654212
  183.3 9.6 %collective-permute-start = (bf16[384,1024]{1,0:T(8,128)(2,1)}, bf16[384,1024]{1,0:T(8,128)(2,1)}, u32[]{:S(2)}, u32[]{:S(2)}) collective-permute-start(bf16[384,1024]{1,0:T(8,128)(2,1)} %slice.99), channel_id=1, source_target_pairs={{0,4},{1,5},{2,6},{3,7},{8,12},{9,13},{10,14},{11,15},{16,20},{17,... | collective-permute-start | bytes 2359304 | tf_op jit(solution)/shard_map/ppermute | solution.py:38
  207.0 30.7 %copy-start.8 = (bf16[192,1024]{1,0:T(8,128)(2,1)}, bf16[192,1024]{1,0:T(8,128)(2,1)S(1)}, u32[]{:S(2)}) copy-start(bf16[192,1024]{1,0:T(8,128)(2,1)S(1)} %get-tuple-element.79.refs_0_.attended_ref) | copy-start | bytes 1179652
  493.4 93.3 %copy-start.37 = (f32[1,1024]{1,0:T(1,128)S(1)}, f32[1,1024]{1,0:T(1,128)}, u32[]{:S(2)}) copy-start(f32[1,1024]{1,0:T(1,128)} %get-tuple-element.96) | copy-start | bytes 12292
  493.4 94.0 %copy-start.7 = (bf16[768,8]{1,0:T(8,128)(2,1)S(1)}, bf16[768,8]{1,0:T(8,128)(2,1)}, u32[]{:S(2)}) copy-start(bf16[768,8]{1,0:T(8,128)(2,1)} %copy-done.6) | copy-start | bytes 36868
  493.5 94.0 %copy-start.15 = (s32[1,1024,2]{1,2,0:T(2,128)S(1)}, s32[1,1024,2]{1,2,0:T(2,128)}, u32[]{:S(2)}) copy-start(s32[1,1024,2]{1,2,0:T(2,128)} %param.30) | copy-start | bytes 24580
  493.5 94.0 %copy-start.17 = (f32[2,1024]{1,0:T(2,128)S(1)}, f32[2,1024]{1,0:T(2,128)}, u32[]{:S(2)}) copy-start(f32[2,1024]{1,0:T(2,128)} %copy-done.16) | copy-start | bytes 24580
  587.5 54.4 %copy-start.2 = (bf16[576,1024]{1,0:T(8,128)(2,1)S(1)}, bf16[576,1024]{1,0:T(8,128)(2,1)}, u32[]{:S(2)}) copy-start(bf16[576,1024]{1,0:T(8,128)(2,1)} %copy-done.1) | copy-start | bytes 3538948
  641.9 17.6 %copy-start.32 = (s32[137,1]{0,1:T(1,128)S(1)}, s32[137,1]{0,1:T(1,128)}, u32[]{:S(2)}) copy-start(s32[137,1]{0,1:T(1,128)} %param.32) | copy-start | bytes 1648
  641.9 19.7 %copy-start.36 = (f32[1,1024]{1,0:T(1,128)S(1)}, f32[1,1024]{1,0:T(1,128)}, u32[]{:S(2)}) copy-start(f32[1,1024]{1,0:T(1,128)} %get-tuple-element.111) | copy-start | bytes 12292
  658.2 14.6 %collective-permute-start.4 = (bf16[384,1024]{1,0:T(8,128)(2,1)}, bf16[384,1024]{1,0:T(8,128)(2,1)S(1)}, u32[]{:S(2)}, u32[]{:S(2)}) collective-permute-start(bf16[384,1024]{1,0:T(8,128)(2,1)} %get-tuple-element.100), channel_id=1, source_target_pairs={{4,0},{5,1},{6,2},{7,3},{12,8},{13,9},{14,10},{15,11},{20,16},{21,... | collective-permute-start | bytes 2359304 | tf_op jit(solution)/shard_map/ppermute | solution.py:38
  665.2 11.5 %copy-start.22 = (bf16[9,64,768]{2,1,0:T(8,128)(2,1)S(1)}, bf16[9,64,768]{2,1,0:T(8,128)(2,1)}, u32[]{:S(2)}) copy-start(bf16[9,64,768]{2,1,0:T(8,128)(2,1)} %copy-done.21) | copy-start | bytes 2654212
  771.7 87.0 %copy-start.33 = (f32[3,768]{1,0:T(4,128)S(1)}, f32[3,768]{1,0:T(4,128)}, u32[]{:S(2)}) copy-start(f32[3,768]{1,0:T(4,128)} %param.43) | copy-start | bytes 27652
  771.7 87.0 %copy-start.34 = (f32[3,768]{1,0:T(4,128)S(1)}, f32[3,768]{1,0:T(4,128)}, u32[]{:S(2)}) copy-start(f32[3,768]{1,0:T(4,128)} %param.44) | copy-start | bytes 27652
  771.7 88.3 %copy-start.29 = (f32[768,8]{0,1:T(8,128)S(1)}, f32[768,8]{0,1:T(8,128)}, u32[]{:S(2)}) copy-start(f32[768,8]{0,1:T(8,128)} %param.46) | copy-start | bytes 73732
  771.7 88.3 %copy-start.30 = (f32[768,8]{0,1:T(8,128)S(1)}, f32[768,8]{0,1:T(8,128)}, u32[]{:S(2)}) copy-start(f32[768,8]{0,1:T(8,128)} %param.47) | copy-start | bytes 73732
  771.7 89.7 %copy-start.38 = (f32[3,8]{1,0:T(4,128)S(1)}, f32[3,8]{1,0:T(4,128)}, u32[]{:S(2)}) copy-start(f32[3,8]{1,0:T(4,128)} %param.49) | copy-start | bytes 292
  771.7 89.7 %copy-start.39 = (f32[3,8]{1,0:T(4,128)S(1)}, f32[3,8]{1,0:T(4,128)}, u32[]{:S(2)}) copy-start(f32[3,8]{1,0:T(4,128)} %param.50) | copy-start | bytes 292
  (22 other events, 73.7 us)

commit v7 on v6

--- a/solution.py
+++ b/solution.py
@@ -434,159 +434,262 @@
     )(attended, embedded, gain, router, routes, *rolled)
 
 
-def gather_units_kernel(
-    chunks, slots_ref, mine_ref, rows_ref, units_ref, looked_ref,
-    held, total, send_x, recv_x, send_y, recv_y, send_z, recv_z, send_core, recv_core,
-):
+def embed_kernel(chunks, slots_ref, mine_ref, rows_ref, units_ref, embedded_ref, *refs):
+    held, total, stage, from_end, from_mid = refs[:5]
+    send_x, recv_x, send_y, recv_y, send_z, recv_z, send_core, recv_core = refs[5:13]
+    send_sem, end_sem, mid_sem, back_sem, back_recv = refs[13:]
     chip, core = lax.axis_index("dp"), lax.axis_index("ctx")
     beside = chip + 1 - 2 * lax.rem(chip, 2)
     across = lax.rem(chip + 2, 4)
     opposite = across + 1 - 2 * lax.rem(across, 2)
     places = (chip, beside, across, opposite)
-    slots, unit_rows, width = mine_ref.shape
+    rank = lax.axis_index("tensor")
+    inner = (rank == 1) | (rank == 2)
+    end_peer = jnp.where(rank < 2, 1 - rank, 5 - rank)
+    mid_peer = 3 - rank
+    slots, unit_rows = mine_ref.shape[:2]
+    width = total.shape[2]
     size = slots // chunks
     split = (chunks + 1) // 2
     tokens = rows_ref.shape[0]
+    count, rows = stage.shape[1:3]
+
+    def repeat(first, last, body):
+        def step(i, carry):
+            body(i)
+            return carry
+
+        lax.fori_loop(first, last, step, 0)
+
+    def columns(h):
+        return slice(h * width, (h + 1) * width)
+
+    own = (chip * 2 + core) * slots
+    for h in range(2):
+        held[h, pl.ds(own, slots)] = mine_ref[:, :, columns(h)].astype(jnp.bfloat16)
     barrier = pltpu.get_barrier_semaphore()
-    for place in ({"ctx": 1 - core}, {"dp": beside}, {"dp": across}):
+    for place in ({"ctx": 1 - core}, {"dp": beside}, {"dp": across}, {"tensor": end_peer}):
         pl.semaphore_signal(barrier, inc=1, device_id=place, device_id_type=MESH_ID)
-    pl.semaphore_wait(barrier, 3)
-
-    def piece(place, which, q):
-        return held.at[pl.ds((place * 2 + which) * slots + q * size, size)]
-
-    def copy(place, q, send, recv, target):
+
+    @pl.when(inner)
+    def _():
+        pl.semaphore_signal(barrier, inc=1, device_id={"tensor": mid_peer}, device_id_type=MESH_ID)
+        pl.semaphore_wait(barrier, 5)
+
+    @pl.when(jnp.logical_not(inner))
+    def _():
+        pl.semaphore_wait(barrier, 4)
+
+    def remote(source, target, send, recv, place):
         return pltpu.make_async_remote_copy(
-            src_ref=piece(place, core, q),
-            dst_ref=piece(place, core, q),
+            src_ref=source,
+            dst_ref=target,
             send_sem=send,
             recv_sem=recv,
-            device_id=target,
+            device_id=place,
             device_id_type=MESH_ID,
         )
 
-    def to_beside(q):
-        return copy(chip, q, send_x.at[q], recv_x.at[q], {"dp": beside})
-
-    def to_across(q):
-        return copy(chip, q, send_y.at[q], recv_y.at[q], {"dp": across})
-
-    def passed_on(q, source, target):
-        return copy(source, q, send_z.at[q], recv_z.at[q], {"dp": target})
-
-    def to_core(k, q):
-        return copy(places[k], q, send_core.at[k, q], recv_core.at[k, q], {"ctx": 1 - core})
-
-    held[pl.ds((chip * 2 + core) * slots, slots)] = mine_ref[...]
-
-    def start(i, carry):
-        to_beside(i).start()
-        to_across(lax.rem(i + split, chunks)).start()
-        return carry
-
-    lax.fori_loop(0, chunks, start, 0)
-
-    def start_core(q, carry):
-        to_core(0, q).start()
-        return carry
-
-    lax.fori_loop(0, chunks, start_core, 0)
-    total[...] = jnp.zeros_like(total)
-
-    def look(place, which):
+    def copy(h, place, q, send, recv, target):
+        piece = held.at[h, pl.ds((place * 2 + core) * slots + q * size, size)]
+        return remote(piece, piece, send, recv, target)
+
+    def to_beside(h, q):
+        return copy(h, chip, q, send_x.at[h, q], recv_x.at[h, q], {"dp": beside})
+
+    def to_across(h, q):
+        return copy(h, chip, q, send_y.at[h, q], recv_y.at[h, q], {"dp": across})
+
+    def passed_on(h, q, source, target):
+        return copy(h, source, q, send_z.at[h, q], recv_z.at[h, q], {"dp": target})
+
+    def to_core(h, k, q):
+        return copy(h, places[k], q, send_core.at[h, k, q], recv_core.at[h, k, q], {"ctx": 1 - core})
+
+    def start(h):
+        def both(i):
+            to_beside(h, i).start()
+            to_across(h, lax.rem(i + split, chunks)).start()
+
+        repeat(0, chunks, both)
+        repeat(0, chunks, lambda q: to_core(h, 0, q).start())
+
+    def look(h, place, which):
         begin = (place * 2 + which) * slots
         lines = slots * unit_rows
         column = lax.broadcasted_iota(jnp.int32, (tokens, lines), 1) + begin * unit_rows
         hit = jnp.where(column == rows_ref[...], 1.0, 0.0).astype(jnp.bfloat16)
-        block = held[pl.ds(begin, slots)].reshape(lines, width)
-        total[...] += jnp.dot(hit, block, preferred_element_type=jnp.float32)
-
-    look(chip, core)
-
-    def relay(i, carry):
-        to_beside(i).wait_recv()
+        block = held[h, pl.ds(begin, slots)].reshape(lines, width)
+        total[h] += jnp.dot(hit, block, preferred_element_type=jnp.float32)
+
+    def relay(h, i):
+        to_beside(h, i).wait_recv()
 
         @pl.when(i < split)
         def _():
-            passed_on(i, beside, across).start()
-
-        to_core(1, i).start()
+            passed_on(h, i, beside, across).start()
+
+        to_core(h, 1, i).start()
         j = lax.rem(i + split, chunks)
-        to_across(j).wait_recv()
+        to_across(h, j).wait_recv()
 
         @pl.when(j >= split)
         def _():
-            passed_on(j, across, beside).start()
-
-        to_core(2, j).start()
-        to_core(0, i).wait_recv()
-        return carry
-
-    lax.fori_loop(0, chunks, relay, 0)
-    look(chip, 1 - core)
-    look(beside, core)
-    look(across, core)
-
-    def last(q, carry):
-        passed_on(q, opposite, opposite).wait_recv()
-        to_core(3, q).start()
-        to_core(1, q).wait_recv()
-        to_core(2, q).wait_recv()
-        return carry
-
-    lax.fori_loop(0, chunks, last, 0)
-    for source in (beside, across):
-        look(source, 1 - core)
-    look(opposite, core)
-
-    def ending(q, carry):
-        to_core(3, q).wait_recv()
-        return carry
-
-    lax.fori_loop(0, chunks, ending, 0)
-    look(opposite, 1 - core)
-    looked_ref[...] = total[...].astype(jnp.bfloat16)
-
-    def place_unit(u, carry):
-        units_ref[u] = held[slots_ref[u]]
-        return carry
-
-    lax.fori_loop(0, units_ref.shape[0], place_unit, 0)
-
-    def finish(q, carry):
-        to_beside(q).wait_send()
-        to_across(q).wait_send()
-        for k in range(4):
-            to_core(k, q).wait_send()
-        passed_on(q, opposite, opposite).wait_send()
-        return carry
-
-    lax.fori_loop(0, chunks, finish, 0)
-
-
-def gather_units(unit_slots, mine, slot_rows, collective_id):
-    slots = mine.shape[0]
-    unit = mine.shape[1:]
+            passed_on(h, j, across, beside).start()
+
+        to_core(h, 2, j).start()
+
+    def rest(h):
+        repeat(0, chunks, lambda q: to_core(h, 0, q).wait_recv())
+        look(h, chip, 1 - core)
+        look(h, beside, core)
+        look(h, across, core)
+
+        def last(q):
+            passed_on(h, q, opposite, opposite).wait_recv()
+            to_core(h, 3, q).start()
+            to_core(h, 1, q).wait_recv()
+            to_core(h, 2, q).wait_recv()
+
+        repeat(0, chunks, last)
+        look(h, beside, 1 - core)
+        look(h, across, 1 - core)
+        look(h, opposite, core)
+        repeat(0, chunks, lambda q: to_core(h, 3, q).wait_recv())
+        look(h, opposite, 1 - core)
+
+    def span(i):
+        return pl.ds(pl.multiple_of(i * rows, rows), rows)
+
+    def to_inner(h, i):
+        return remote(
+            stage.at[h, i], from_end.at[h, i], send_sem.at[h, i], end_sem.at[h, i], {"tensor": end_peer}
+        )
+
+    def to_middle(h, i):
+        return remote(
+            stage.at[h, i], from_mid.at[h, i], send_sem.at[h, i], mid_sem.at[h, i], {"tensor": mid_peer}
+        )
+
+    def to_end(h, i):
+        piece = embedded_ref.at[span(i), columns(h)]
+        return remote(piece, piece, back_sem.at[h, i], back_recv.at[h, i], {"tensor": end_peer})
+
+    def push(h):
+        @pl.when(jnp.logical_not(inner))
+        def _():
+            def one(i):
+                stage[h, i] = total[h, span(i)].astype(jnp.bfloat16)
+                to_inner(h, i).start()
+
+            repeat(0, count, one)
+
+    def exchange(h, i):
+        @pl.when(inner & (i < count))
+        def _():
+            to_inner(h, i).wait_recv()
+            stage[h, i] = (total[h, span(i)] + from_end[h, i].astype(jnp.float32)).astype(jnp.bfloat16)
+            to_middle(h, i).start()
+
+        @pl.when(inner & (i >= line_lag))
+        def _():
+            j = i - line_lag
+            to_middle(h, j).wait_recv()
+            both = stage[h, j].astype(jnp.float32) + from_mid[h, j].astype(jnp.float32)
+            embedded_ref[span(j), columns(h)] = both.astype(jnp.bfloat16)
+            to_end(h, j).start()
+
+    total[...] = jnp.zeros_like(total)
+    start(0)
+    look(0, chip, core)
+    repeat(0, chunks, lambda i: relay(0, i))
+    start(1)
+    rest(0)
+    push(0)
+    look(1, chip, core)
+
+    def between(i):
+        exchange(0, i)
+
+        @pl.when(i < chunks)
+        def _():
+            relay(1, i)
+
+    repeat(0, count + line_lag, between)
+    rest(1)
+    push(1)
+
+    def place_unit(u):
+        for h in range(2):
+            units_ref[u, :, columns(h)] = held[h, slots_ref[u]]
+
+    @pl.when(jnp.logical_not(inner))
+    def _():
+        repeat(0, units_ref.shape[0], place_unit)
+
+    repeat(0, count + line_lag, lambda i: exchange(1, i))
+
+    @pl.when(inner)
+    def _():
+        repeat(0, units_ref.shape[0], place_unit)
+
+    def finish(q):
+        for h in range(2):
+            to_beside(h, q).wait_send()
+            to_across(h, q).wait_send()
+            for k in range(4):
+                to_core(h, k, q).wait_send()
+            passed_on(h, q, opposite, opposite).wait_send()
+
+    repeat(0, chunks, finish)
+
+    @pl.when(inner)
+    def _():
+        def drain(i):
+            for h in range(2):
+                to_middle(h, i).wait_send()
+                to_end(h, i).wait_send()
+
+        repeat(0, count, drain)
+
+    @pl.when(jnp.logical_not(inner))
+    def _():
+        def drain(i):
+            for h in range(2):
+                to_end(h, i).wait_recv()
+                to_inner(h, i).wait_send()
+
+        repeat(0, count, drain)
+
+
+def embed(unit_slots, mine, slot_rows, collective_id):
+    slots, unit_rows, width = mine.shape
     tokens = slot_rows.shape[0]
     chunks = max(k for k in range(1, 8) if slots % k == 0)
-    sems = pltpu.SemaphoreType.DMA((chunks,))
-    core_sems = pltpu.SemaphoreType.DMA((4, chunks))
+    rows = 128
+    half = width // 2
+    sems = pltpu.SemaphoreType.DMA((2, chunks))
+    line = pltpu.VMEM((2, tokens // rows, rows, half), jnp.bfloat16)
     return pl.pallas_call(
-        functools.partial(gather_units_kernel, chunks),
+        functools.partial(embed_kernel, chunks),
         out_shape=[
-            jax.ShapeDtypeStruct((unit_slots.shape[0],) + unit, jnp.bfloat16),
-            jax.ShapeDtypeStruct((tokens, unit[1]), jnp.bfloat16),
+            jax.ShapeDtypeStruct((unit_slots.shape[0], unit_rows, width), jnp.bfloat16),
+            jax.ShapeDtypeStruct((tokens, width), jnp.bfloat16),
         ],
         in_specs=[pl.BlockSpec(memory_space=pltpu.SMEM), whole_vmem, whole_vmem],
         out_specs=[whole_vmem] * 2,
         scratch_shapes=[
-            pltpu.VMEM((8 * slots,) + unit, jnp.bfloat16),
-            pltpu.VMEM((tokens, unit[1]), jnp.float32),
+            pltpu.VMEM((2, 8 * slots, unit_rows, half), jnp.bfloat16),
+            pltpu.VMEM((2, tokens, half), jnp.float32),
+            line,
+            line,
+            line,
         ]
         + [sems] * 6
-        + [core_sems] * 2,
+        + [pltpu.SemaphoreType.DMA((2, 4, chunks))] * 2
+        + [pltpu.SemaphoreType.DMA((2, tokens // rows))] * 5,
         compiler_params=pltpu.CompilerParams(
-            collective_id=collective_id, has_side_effects=True, vmem_limit_bytes=56 << 20
+            collective_id=collective_id, has_side_effects=True, vmem_limit_bytes=60 << 20
         ),
     )(unit_slots, mine, slot_rows)
 
@@ -1948,7 +2051,6 @@
     local_ids = token_ids.reshape(-1) - my_rank * vocab_here
     inside = (local_ids >= 0) & (local_ids < vocab_here)
     clipped_ids = jnp.clip(local_ids, 0, vocab_here - 1)
-    master_low = master[0, 0].astype(jnp.bfloat16)
     unit_starts = jnp.sum(
         jnp.where(
             (clipped_ids // unit_rows)[None, :] == jnp.arange(unit_slots.shape[0])[:, None],
@@ -1960,14 +2062,15 @@
     slot_rows = unit_starts + clipped_ids % unit_rows
     if on_square:
         slot_rows = jnp.where(inside, slot_rows, -1)[:, None]
-        weights_low, looked = gather_units(unit_slots, master_low, slot_rows, 11)
+        weights_low, embedded = embed(unit_slots, master[0, 0], slot_rows, 11)
     else:
+        master_low = master[0, 0].astype(jnp.bfloat16)
         gathered = lax.all_gather(master_low, ("dp", "ctx"), axis=0, tiled=True)
         looked = jnp.take(gathered.reshape(-1, model_width), slot_rows, axis=0)
         looked = jnp.where(inside[:, None], looked, 0)
         weights_low = pull_units([gathered], unit_slots)
+        (embedded,) = sum_line(looked, [], [], keep_total, 1)
     weights_low = weights_low.reshape(-1, model_width)
-    (embedded,) = sum_line(looked, [], [], keep_total, 1)
     joint_low = weights_low[vocab_here : vocab_here + 3 * hidden_here]
     project_low = weights_low[vocab_here + 3 * hidden_here :]
     rolled = [project_low] + [

time: 881 us -> 839 us (0.952)
  Pallas kernels: 783 us -> 744 us
    pallas_call x3 -> x2, Pallas kernels: 160 us -> 99.5 us  [sum_line(): pl.pallas_call(functools.partial(sum_line_kernel, rows, count, opening, p...]
    pallas_call x1, Pallas kernels: 98 us -> 120 us  [embed(): pl.pallas_call(functools.partial(embed_kernel, chunks), out_shape=[jax.Sh...]
  transfers between devices with their start and end apart: 5 -> 5, of which waited for: 1 -> 1; matrix products, arithmetic and copies ran while one was open for 2% -> 2% of each run, Pallas kernels for 12% -> 5%
where the time goes in v7:
time: 839 us; the launch traced here: 829 us
  Pallas kernels  744 us (89%)
  other arithmetic  37.1 us (4%)
  local copies, waits for them, and re-layouts  23.4 us (3%)
    pallas_call x1, Pallas kernels, head_line(): pl.pallas_call(functools.partial(head_line_kernel, vocab_tile(vocab)), ou...  148 us
    pallas_call x1, Pallas kernels, embed(): pl.pallas_call(functools.partial(embed_kernel, chunks), out_shape=[jax.Sh...  120 us
    pallas_call x2, Pallas kernels, sum_line(): pl.pallas_call(functools.partial(sum_line_kernel, rows, count, opening, p...  99.5 us
    pallas_call x1, Pallas kernels, experts_forward(): pl.pallas_call(experts_kernel, out_shape=[jax.ShapeDtypeStruct((tokens, w...  94.2 us
    pallas_call x1, Pallas kernels, experts_backward(): pl.pallas_call(experts_back_kernel, out_shape=[jax.ShapeDtypeStruct((toke...  93.2 us
    pallas_call x1, Pallas kernels, own_units(): pl.pallas_call(functools.partial(own_units_kernel, chunks), out_shape=[ja...  83.6 us
    pallas_call x1, Pallas kernels, weight_grads(): pl.pallas_call(functools.partial(weight_grads_kernel, tile // unit_rows,...  41.8 us
    pallas_call x1, Pallas kernels, gather_line(): pl.pallas_call(functools.partial(gather_line_kernel, count), out_shape=[j...  30.2 us
  transfers between devices with their start and end apart: 5, of which 1 were waited for; matrix products, arithmetic and copies ran while one was open for 2% of the time, Pallas kernels for 5%

profile of v7, /device:TPU:0, one launch (start us, length us, event | category | flops | bytes accessed | tf_op | source)
XLA Modules:
  0.0 828.8 jit_solution(15126843857308752579)
XLA Ops:
  2.9 3.4 convert_reduce_fusion
  10.7 119.7 %shard_map.384 = (bf16[137,64,768]{2,1,0:T(8,128)(2,1)}, bf16[1024,768]{1,0:T(8,128)(2,1)}) custom-call(s32[137]{0:T(256)} %copy-done.31, f32[21,64,768]{2,1,0:T(8,128)} %bitcast.100, s32[1024,1]{1,0:T(8,128)} %fusion.7.rows_ref), custom_call_target="tpu_custom_call" | custom-call | tf_op jit(solution)/shard_map/pallas_call | solution.py:673
  131.5 2.1 collective-permute-start.3
  139.7 2.2 collective-permute-start
  144.4 4.0 bitcast_convert_fusion
  149.2 12.8 %shard_map.385 = (bf16[192,1024]{1,0:T(8,128)(2,1)S(1)}, f32[3,1024,1]{2,1,0:T(8,128)S(1)}) custom-call(f32[3,8]{1,0:T(4,128)S(1)} %copy-done.18, bf16[576,1024]{1,0:T(8,128)(2,1)S(1)} %convolution_convert_fusion.own_ref, bf16[384,1024]{1,0:T(8,128)(2,1)} %collective-permute-done.before_ref), custom_call_target="tpu_custom_call" | custom-call | tf_op jit(solution)/shard_map/pallas_call | solution.py:801
  163.2 30.2 %shard_map.386 = bf16[4,192,1024]{2,1,0:T(8,128)(2,1)S(1)} custom-call(bf16[192,1024]{1,0:T(8,128)(2,1)S(1)} %get-tuple-element.79.refs_0_.attended_ref), custom_call_target="tpu_custom_call" | custom-call | tf_op jit(solution)/shard_map/pallas_call | solution.py:362
  193.4 5.6 shard_map.387
  199.1 1.7 copy-done.1
  203.9 94.2 %shard_map.388 = (f32[1024,768]{1,0:T(8,128)}, bf16[8,288,768]{2,1,0:T(8,128)(2,1)}, bf16[8,288,768]{2,1,0:T(8,128)(2,1)}, f32[8,128]{1,0:T(8,128)}) custom-call(bf16[1024,768]{1,0:T(8,128)(2,1)} %copy-done.5, s32[2,1024]{1,0:T(2,128)} %copy-done.24, s32[1024,2]{1,0:T(8,128)} %copy.76.dest_columns, f32[1024,8]{1,0:T(8,128)} %copy-done.13, ...), custom_call_target="tpu_custom_call" | custom-call | tf_op jit(solution)/shard_map/pallas_call | solution.py:1592
  301.5 148.0 %shard_map.389 = (bf16[1024,768]{1,0:T(8,128)(2,1)}, bf16[1024,768]{1,0:T(8,128)(2,1)}, f32[1024,768]{1,0:T(8,128)}, f32[1,768]{1,0:T(1,128)}, f32[1,1024]{1,0:T...) custom-call(f32[1024,768]{1,0:T(8,128)} %get-tuple-element.83.part_ref, f32[1024,768]{1,0:T(8,128)} %copy-done.1, ...), custom_call_target="tpu_custom_call" | custom-call | tf_op jit(solution)/shard_map/pallas_call | solution.py:1244
  449.5 93.2 %shard_map.390 = (f32[1024,768]{1,0:T(8,128)}, f32[2,1024]{1,0:T(2,128)}, f32[768,768]{1,0:T(8,128)}, f32[768,768]{1,0:T(8,128)}) custom-call(bf16[1024,768]{1,0:T(8,128)(2,1)} %get-tuple-element.89.rows_ref, s32[2,1024]{1,0:T(2,128)} %copy-done.24, s32[1024,2]{1,0:T(8,128)} %copy.76.dest_columns, f32[2,1024]{1,0:T(2,128)} %copy-done.16, ...), custom_call_target="tpu_custom_call" | custom-call | tf_op jit(solution)/shard_map/pallas_call | solution.py:1734
  543.5 51.6 %shard_map.391 = (bf16[1024,768]{1,0:T(8,128)(2,1)S(1)}, f32[1024,768]{1,0:T(8,128)S(1)}, bf16[8,1024]{1,0:T(8,128)(2,1)S(1)}, f32[1,1024]{1,0:T(1,128)S(1)}, f32[1,768]{1,0:T(1,128)S(1)}) custom-call(f32[1024,768]{1,0:T(8,128)} %get-tuple-element.93.part_ref, f32[1024,768]{1,0:T(8,128)} %copy-done.1, f32[1,768]{1,0:T(1,128)S(1)} %get-tuple-element.159.gain_ref.refs_1_, ...), custom_call_target="tpu_custom_call" | custom-call | tf_op jit(solution)/shard_map/pallas_call | solution.py:184
  596.2 1.7 copy-done.6
  597.9 15.4 %shard_map.392 = (bf16[192,1024]{1,0:T(8,128)(2,1)S(1)}, f32[384,1024]{1,0:T(8,128)S(1)}, bf16[384,1024]{1,0:T(8,128)(2,1)}, f32[24,256]{1,0:T(8,128)S(1)}) custom-call(f32[3,8]{1,0:T(4,128)S(1)} %copy-done.18, bf16[576,1024]{1,0:T(8,128)(2,1)S(1)} %copy-done.3, bf16[384,1024]{1,0:T(8,128)(2,1)} %collective-permute-done.before_ref, ...), custom_call_target="tpu_custom_call" | custom-call | tf_op jit(solution)/shard_map/pallas_call | solution.py:940
  619.7 1.7 fusion.24
  621.4 7.6 collective-permute-done.4
  629.9 1.9 add_convert_fusion
  632.9 3.1 fusion.17.part_ref
  636.0 47.9 %shard_map.393 = (bf16[1024,768]{1,0:T(8,128)(2,1)S(1)}, f32[8,768]{1,0:T(8,128)S(1)}) custom-call(f32[1024,768]{1,0:T(8,128)} %fusion.17.part_ref, bf16[1024,768]{1,0:T(8,128)(2,1)S(1)} %copy-done, f32[1,768]{1,0:T(1,128)S(1)} %get-tuple-element.157.refs_1_, f32[1024,768]{1,0:T(8,128)} %copy-done.6, f32[1,768]{1,0:T(1,128)S(1)} %get-tuple-element.102.refs_3_, ...), custom_call_target="tpu_custom_call" | custom-call | tf_op jit(solution)/shard_map/pallas_call | solution.py:184
  685.8 41.8 %shard_map.394 = (bf16[168,64,768]{2,1,0:T(8,128)(2,1)}, f32[768,768]{1,0:T(8,128)}, f32[768,768]{1,0:T(8,128)}, f32[768,768]{1,0:T(8,128)}, f32[768,768]{1,0:T(...) custom-call(s32[137]{0:T(256)} %copy-done.31, bf16[8000,1024]{1,0:T(8,128)(2,1)} %get-tuple-element.86.slope_ref, ...), custom_call_target="tpu_custom_call" | custom-call | tf_op jit(solution)/shard_map/pallas_call | solution.py:1345
  727.7 83.6 %shard_map.395 = (f32[21,64,768]{2,1,0:T(8,128)}, f32[16,768]{1,0:T(8,128)}) custom-call(bf16[168,64,768]{2,1,0:T(8,128)(2,1)} %get-tuple-element.107.parts_ref, f32[16,768]{1,0:T(8,128)} %select_maximum_fusion.small_ref), custom_call_target="tpu_custom_call" | custom-call | tf_op jit(solution)/shard_map/pallas_call | solution.py:1902
  815.9 1.4 multiply_subtract_fusion
  818.0 10.4 %fusion.16 = (f32[1,1,21,64,768]{4,3,2,1,0:T(8,128)}, f32[1,1,21,64,768]{4,3,2,1,0:T(8,128)}, f32[1,1,21,64,768]{4,3,2,1,0:T(8,128)}) fusion(f32[21,64,768]{2,1,0:T(8,128)} %get-tuple-element.114, pred[21]{0:T(512)(128)(4,1)S(1)} %select_reduce_fusion.2, f32[1,1,21,64,768]{4,3,2,1,0:T(8,128)} %param.35, f32[1,1,21,64,768]{4,3,2,1,0:T(8,128)} %param.34, ...), kind=kLoop, calls=%fused_computation.81 | loop fusion | flops 16515072 | bytes 28901480 | tf_op jit(solution)/shard_map/broadcast_in_dim | solution.py:2249
  (149 shorter events, 39.5 us)
Async XLA Ops:
  1.4 129.0 %copy-start.26 = (s32[1,1024]{1,0:T(1,128)}, s32[1,1024]{1,0:T(1,128)S(1)}, u32[]{:S(2)}) copy-start(s32[1,1024]{1,0:T(1,128)S(1)} %get-tuple-element.153.ids_ref) | copy-start | bytes 12292
  8.7 133.5 %copy-start.24 = (s32[2,1024]{1,0:T(2,128)}, s32[2,1024]{1,0:T(2,128)S(1)}, u32[]{:S(2)}) copy-start(s32[2,1024]{1,0:T(2,128)S(1)} %add_select_fusion.1.dest_rows) | copy-start | bytes 24580
  10.7 125.1 %copy-start.27 = (f32[3,768]{1,0:T(4,128)S(1)}, f32[3,768]{1,0:T(4,128)}, u32[]{:S(2)}) copy-start(f32[3,768]{1,0:T(4,128)} %param.42) | copy-start | bytes 27652
  131.5 61.8 %collective-permute-start.3 = (bf16[192,768]{1,0:T(8,128)(2,1)S(1)}, bf16[192,768]{1,0:T(8,128)(2,1)}, u32[]{:S(2)}, u32[]{:S(2)}) collective-permute-start(bf16[192,768]{1,0:T(8,128)(2,1)S(1)} %bitcast.89), channel_id=1, source_target_pairs={{0,3},{1,0},{2,1},{3,2},{4,7},{5,4},{6,5},{7,6},{8,11},{9,8},{10,9... | collective-permute-start | bytes 884744 | tf_op jit(solution)/shard_map/ppermute | solution.py:2077
  133.6 59.8 %collective-permute-start.2 = (bf16[192,768]{1,0:T(8,128)(2,1)S(1)}, bf16[192,768]{1,0:T(8,128)(2,1)}, u32[]{:S(2)}, u32[]{:S(2)}) collective-permute-start(bf16[192,768]{1,0:T(8,128)(2,1)S(1)} %bitcast.90), channel_id=1, source_target_pairs={{0,2},{1,3},{2,0},{3,1},{4,6},{5,7},{6,4},{7,5},{8,10},{9,11},{10,... | collective-permute-start | bytes 884744 | tf_op jit(solution)/shard_map/ppermute | solution.py:2077
  133.6 59.8 %collective-permute-start.1 = (bf16[192,768]{1,0:T(8,128)(2,1)S(1)}, bf16[192,768]{1,0:T(8,128)(2,1)}, u32[]{:S(2)}, u32[]{:S(2)}) collective-permute-start(bf16[192,768]{1,0:T(8,128)(2,1)S(1)} %bitcast.91), channel_id=1, source_target_pairs={{0,1},{1,2},{2,3},{3,0},{4,5},{5,6},{6,7},{7,4},{8,9},{9,10},{10,1... | collective-permute-start | bytes 884744 | tf_op jit(solution)/shard_map/ppermute | solution.py:2077
  138.6 10.6 %copy-start.2 = (bf16[576,1024]{1,0:T(8,128)(2,1)}, bf16[576,1024]{1,0:T(8,128)(2,1)S(1)}, u32[]{:S(2)}) copy-start(bf16[576,1024]{1,0:T(8,128)(2,1)S(1)} %convolution_convert_fusion.own_ref) | copy-start | bytes 3538948
  139.7 9.6 %collective-permute-start = (bf16[384,1024]{1,0:T(8,128)(2,1)}, bf16[384,1024]{1,0:T(8,128)(2,1)}, u32[]{:S(2)}, u32[]{:S(2)}) collective-permute-start(bf16[384,1024]{1,0:T(8,128)(2,1)} %slice.99), channel_id=1, source_target_pairs={{0,4},{1,5},{2,6},{3,7},{8,12},{9,13},{10,14},{11,15},{16,20},{17,... | collective-permute-start | bytes 2359304 | tf_op jit(solution)/shard_map/ppermute | solution.py:38
  163.2 30.2 %copy-start.9 = (bf16[192,1024]{1,0:T(8,128)(2,1)}, bf16[192,1024]{1,0:T(8,128)(2,1)S(1)}, u32[]{:S(2)}) copy-start(bf16[192,1024]{1,0:T(8,128)(2,1)S(1)} %get-tuple-element.79.refs_0_.attended_ref) | copy-start | bytes 1179652
  449.4 93.2 %copy-start.37 = (f32[1,1024]{1,0:T(1,128)S(1)}, f32[1,1024]{1,0:T(1,128)}, u32[]{:S(2)}) copy-start(f32[1,1024]{1,0:T(1,128)} %get-tuple-element.96) | copy-start | bytes 12292
  449.4 94.0 %copy-start.8 = (bf16[768,8]{1,0:T(8,128)(2,1)S(1)}, bf16[768,8]{1,0:T(8,128)(2,1)}, u32[]{:S(2)}) copy-start(bf16[768,8]{1,0:T(8,128)(2,1)} %copy-done.7) | copy-start | bytes 36868
  449.4 94.0 %copy-start.15 = (s32[1,1024,2]{1,2,0:T(2,128)S(1)}, s32[1,1024,2]{1,2,0:T(2,128)}, u32[]{:S(2)}) copy-start(s32[1,1024,2]{1,2,0:T(2,128)} %param.30) | copy-start | bytes 24580
  449.5 94.0 %copy-start.17 = (f32[2,1024]{1,0:T(2,128)S(1)}, f32[2,1024]{1,0:T(2,128)}, u32[]{:S(2)}) copy-start(f32[2,1024]{1,0:T(2,128)} %copy-done.16) | copy-start | bytes 24580
  543.5 54.4 %copy-start.3 = (bf16[576,1024]{1,0:T(8,128)(2,1)S(1)}, bf16[576,1024]{1,0:T(8,128)(2,1)}, u32[]{:S(2)}) copy-start(bf16[576,1024]{1,0:T(8,128)(2,1)} %copy-done.2) | copy-start | bytes 3538948
  597.8 17.8 %copy-start.32 = (s32[137,1]{0,1:T(1,128)S(1)}, s32[137,1]{0,1:T(1,128)}, u32[]{:S(2)}) copy-start(s32[137,1]{0,1:T(1,128)} %param.32) | copy-start | bytes 1648
  597.8 19.9 %copy-start.36 = (f32[1,1024]{1,0:T(1,128)S(1)}, f32[1,1024]{1,0:T(1,128)}, u32[]{:S(2)}) copy-start(f32[1,1024]{1,0:T(1,128)} %get-tuple-element.111) | copy-start | bytes 12292
  614.3 14.6 %collective-permute-start.4 = (bf16[384,1024]{1,0:T(8,128)(2,1)}, bf16[384,1024]{1,0:T(8,128)(2,1)S(1)}, u32[]{:S(2)}, u32[]{:S(2)}) collective-permute-start(bf16[384,1024]{1,0:T(8,128)(2,1)} %get-tuple-element.100), channel_id=1, source_target_pairs={{4,0},{5,1},{6,2},{7,3},{12,8},{13,9},{14,10},{15,11},{20,16},{21,... | collective-permute-start | bytes 2359304 | tf_op jit(solution)/shard_map/ppermute | solution.py:38
  621.4 11.5 %copy-start.22 = (bf16[9,64,768]{2,1,0:T(8,128)(2,1)S(1)}, bf16[9,64,768]{2,1,0:T(8,128)(2,1)}, u32[]{:S(2)}) copy-start(bf16[9,64,768]{2,1,0:T(8,128)(2,1)} %copy-done.21) | copy-start | bytes 2654212
  727.6 87.0 %copy-start.33 = (f32[3,768]{1,0:T(4,128)S(1)}, f32[3,768]{1,0:T(4,128)}, u32[]{:S(2)}) copy-start(f32[3,768]{1,0:T(4,128)} %param.43) | copy-start | bytes 27652
  727.6 87.0 %copy-start.34 = (f32[3,768]{1,0:T(4,128)S(1)}, f32[3,768]{1,0:T(4,128)}, u32[]{:S(2)}) copy-start(f32[3,768]{1,0:T(4,128)} %param.44) | copy-start | bytes 27652
  727.6 88.3 %copy-start.29 = (f32[768,8]{0,1:T(8,128)S(1)}, f32[768,8]{0,1:T(8,128)}, u32[]{:S(2)}) copy-start(f32[768,8]{0,1:T(8,128)} %param.46) | copy-start | bytes 73732
  727.6 88.3 %copy-start.30 = (f32[768,8]{0,1:T(8,128)S(1)}, f32[768,8]{0,1:T(8,128)}, u32[]{:S(2)}) copy-start(f32[768,8]{0,1:T(8,128)} %param.47) | copy-start | bytes 73732
  727.7 89.7 %copy-start.38 = (f32[3,8]{1,0:T(4,128)S(1)}, f32[3,8]{1,0:T(4,128)}, u32[]{:S(2)}) copy-start(f32[3,8]{1,0:T(4,128)} %param.49) | copy-start | bytes 292
  727.7 89.7 %copy-start.39 = (f32[3,8]{1,0:T(4,128)S(1)}, f32[3,8]{1,0:T(4,128)}, u32[]{:S(2)}) copy-start(f32[3,8]{1,0:T(4,128)} %param.50) | copy-start | bytes 292
  (22 other events, 61.6 us)

commit v8 on v7

--- a/solution.py
+++ b/solution.py
@@ -817,8 +817,28 @@
 
 def attention_back_kernel(
     heads, size, bias_ref, own_ref, before_ref, logsum_ref, grad_ref, project_ref,
-    query_out, own_out, before_out, bias_out, probs, slopes, inner, query_sum, own_sum, before_sum,
+    *refs
 ):
+    states, (query_out, own_out, before_out, bias_out) = refs[:8], refs[8:12]
+    updated, (probs, slopes, inner, query_sum, own_sum, before_sum) = refs[12:18], refs[18:24]
+    held, load_sem, store_sem = refs[24:]
+    loads = [pltpu.make_async_copy(states[k], held.at[k], load_sem.at[k]) for k in range(8)]
+    stores = [
+        pltpu.make_async_copy(held.at[4 * (k // 3) + k % 3], updated[k], store_sem.at[k])
+        for k in range(6)
+    ]
+    for load in loads:
+        load.start()
+
+    def update(i, carry):
+        lines = held.shape[1] // 16
+        span = pl.ds(pl.multiple_of(i * lines, lines), lines)
+        for k, rate in enumerate((rate_inner, rate_outer)):
+            fresh = adam_update(*(held[4 * k + n, span] for n in range(4)), rate, decay_rate)
+            for n in range(3):
+                held[4 * k + n, span] = fresh[n]
+        return carry
+
     tokens = own_ref.shape[1]
     blocks = tokens // BLOCK
     hidden = heads * size
@@ -929,12 +949,22 @@
             before_out[span, :] = (before_sum[:size, :] * size**-0.5).astype(jnp.bfloat16)
             before_out[value_span, :] = before_sum[size:, :].astype(jnp.bfloat16)
 
+        if head == 0:
+            for load in loads:
+                load.wait()
+            lax.fori_loop(0, 16, update, 0)
+            for store in stores:
+                store.start()
+
     @pl.when(jnp.logical_not(later))
     def _():
         before_out[...] = jnp.zeros_like(before_out)
 
-
-def attention_back(biases, own, before, logsum, grad, project, heads, size):
+    for store in stores:
+        store.wait()
+
+
+def attention_back(biases, own, before, logsum, grad, project, states, heads, size):
     tokens = own.shape[1]
     hidden = heads * size
     return pl.pallas_call(
@@ -944,9 +974,10 @@
             jax.ShapeDtypeStruct((2 * hidden, tokens), jnp.float32),
             jax.ShapeDtypeStruct((2 * hidden, tokens), jnp.bfloat16),
             jax.ShapeDtypeStruct((heads * 2 * (tokens // BLOCK), BLOCK), jnp.float32),
-        ],
-        in_specs=[pl.BlockSpec(memory_space=pltpu.SMEM)] + [whole_vmem] * 5,
-        out_specs=[whole_vmem] * 4,
+        ]
+        + [jax.ShapeDtypeStruct(states[0].shape, jnp.float32)] * 6,
+        in_specs=[pl.BlockSpec(memory_space=pltpu.SMEM)] + [whole_vmem] * 5 + [whole_any] * 8,
+        out_specs=[whole_vmem] * 4 + [whole_any] * 6,
         scratch_shapes=[
             pltpu.VMEM((BLOCK, tokens), jnp.float32),
             pltpu.VMEM((BLOCK, tokens), jnp.float32),
@@ -954,9 +985,12 @@
             pltpu.VMEM((BLOCK, size), jnp.float32),
             pltpu.VMEM((2 * size, tokens), jnp.float32),
             pltpu.VMEM((2 * size, tokens), jnp.float32),
+            pltpu.VMEM((8,) + states[0].shape, jnp.float32),
+            pltpu.SemaphoreType.DMA((8,)),
+            pltpu.SemaphoreType.DMA((6,)),
         ],
         compiler_params=pltpu.CompilerParams(vmem_limit_bytes=48 << 20),
-    )(biases, own, before, logsum, grad, project)
+    )(biases, own, before, logsum, grad, project, *states)
 
 
 def vocab_tile(vocab):
@@ -1278,14 +1312,9 @@
 
 def weight_grads_kernel(
     tile_units, tiles, place_ref, slope_ref, rows_ref, ids_ref, zero_ref, joint_ref, normed_ref,
-    attended_ref, grad_ref, *refs
+    attended_ref, grad_ref, out_ref, made, sem,
 ):
-    states, (out_ref, *updated), (made, sem) = refs[:8], refs[8:15], refs[15:]
     step = pl.program_id(0)
-    for k, rate in enumerate((rate_inner, rate_outer)):
-        fresh = adam_update(*(state[...] for state in states[4 * k : 4 * k + 4]), rate, decay_rate)
-        for n in range(3):
-            updated[3 * k + n][...] = fresh[n]
     unit_rows = out_ref.shape[1]
     buffer = lax.rem(step, 2)
     last_units = joint_ref.shape[0] // unit_rows + attended_ref.shape[0] // unit_rows
@@ -1332,34 +1361,29 @@
         settle(buffer, last_units)
 
 
-def weight_grads(
-    place, slots, unit_rows, slope, rows, ids, zero, joint, normed, attended, grad, states
-):
+def weight_grads(place, slots, unit_rows, slope, rows, ids, zero, joint, normed, attended, grad):
     vocab, tokens = slope.shape
     width = rows.shape[1]
     tile = vocab_tile(vocab)
     tiles = vocab // tile
     fixed = lambda k: (0, 0)
     whole = lambda x: pl.BlockSpec(x.shape, fixed)
-    piece = pl.BlockSpec((states[0].shape[0] // (tiles + 1), states[0].shape[1]), lambda k: (k, 0))
     return pl.pallas_call(
         functools.partial(weight_grads_kernel, tile // unit_rows, tiles),
         grid=(tiles + 1,),
-        out_shape=[jax.ShapeDtypeStruct((slots, unit_rows, width), jnp.bfloat16)]
-        + [jax.ShapeDtypeStruct(states[0].shape, jnp.float32)] * 6,
+        out_shape=jax.ShapeDtypeStruct((slots, unit_rows, width), jnp.bfloat16),
         in_specs=[
             pl.BlockSpec(memory_space=pltpu.SMEM),
             pl.BlockSpec((tile, tokens), lambda k: (jnp.minimum(k, tiles - 1), 0)),
         ]
-        + [whole(x) for x in (rows, ids, zero, joint, normed, attended, grad)]
-        + [piece] * 8,
-        out_specs=[whole_any] + [piece] * 6,
+        + [whole(x) for x in (rows, ids, zero, joint, normed, attended, grad)],
+        out_specs=whole_any,
         scratch_shapes=[
             pltpu.VMEM((2, tile // unit_rows, unit_rows, width), jnp.bfloat16),
             pltpu.SemaphoreType.DMA((2,)),
         ],
         compiler_params=pltpu.CompilerParams(vmem_limit_bytes=60 << 20),
-    )(place, slope, rows, ids, zero, joint, normed, attended, grad, *states)
+    )(place, slope, rows, ids, zero, joint, normed, attended, grad)
 
 
 def adam_update(weight, moment_one, moment_two, gradient, step_rate, decay_factor):
@@ -1482,9 +1506,9 @@
 
 
 def experts_kernel(
-    rows_ref, dest_rows, dest_columns, gates, routes, inner_ref, outer_ref, counts_ref,
+    rows_ref, dest_rows, dest_columns, gates, routes, inner_full, outer_full, counts_ref,
     mix_ref, arrived, returned, totals_ref,
-    outgoing, results, counts, send_one, recv_one, send_two, recv_two, send_count, recv_count,
+    inner_ref, outer_ref, outgoing, results, counts, send_one, recv_one, send_two, recv_two, send_count, recv_count,
 ):
     capacity = arrived.shape[1]
     tokens = rows_ref.shape[0]
@@ -1580,6 +1604,8 @@
 
     lax.fori_loop(0, 8, dispatch, 0)
     lax.fori_loop(1, 8, send_counts, 0)
+    inner_ref[...] = inner_full[...].astype(jnp.bfloat16)
+    outer_ref[...] = outer_full[...].astype(jnp.bfloat16)
     lax.fori_loop(0, 8, work, 0)
     lax.fori_loop(0, 8, combine, 0)
     lax.fori_loop(1, 8, finish, 0)
@@ -1599,7 +1625,8 @@
         ],
         in_specs=[whole_vmem] * 8,
         out_specs=[whole_vmem] * 4,
-        scratch_shapes=[buffer, buffer, pltpu.VMEM((8,) + counts.shape, jnp.float32)]
+        scratch_shapes=[pltpu.VMEM(w.shape, jnp.bfloat16) for w in (inner, outer)]
+        + [buffer, buffer, pltpu.VMEM((8,) + counts.shape, jnp.float32)]
         + [pltpu.SemaphoreType.DMA((8,))] * 6,
         compiler_params=pltpu.CompilerParams(
             collective_id=collective_id, has_side_effects=True, vmem_limit_bytes=60 << 20
@@ -1610,9 +1637,9 @@
 def experts_back_kernel(
     rows_ref, dest_rows, dest_columns, gates, routes, returned, arrived, *refs
 ):
-    inner_ref, outer_ref, grad_ref, gate_ref, inner_grad, outer_grad = refs[:6]
-    outgoing, landed, results, landed_two, active, slopes = refs[6:12]
-    send_one, recv_one, send_two, recv_two = refs[12:]
+    inner_full, outer_full, grad_ref, gate_ref, inner_grad, outer_grad, inner_ref, outer_ref = refs[:8]
+    outgoing, landed, results, landed_two, active, slopes = refs[8:14]
+    send_one, recv_one, send_two, recv_two = refs[14:]
     capacity = arrived.shape[1]
     tokens = rows_ref.shape[0]
     greet_plane()
@@ -1719,6 +1746,8 @@
         return carry
 
     lax.fori_loop(0, 8, dispatch, 0)
+    inner_ref[...] = inner_full[...].astype(jnp.bfloat16)
+    outer_ref[...] = outer_full[...].astype(jnp.bfloat16)
     lax.fori_loop(0, 8, work, 0)
     lax.fori_loop(0, 8, weigh, 0)
     lax.fori_loop(0, 8, combine, 0)
@@ -1741,7 +1770,10 @@
         ],
         in_specs=[whole_vmem] * 9,
         out_specs=[whole_vmem] * 4,
-        scratch_shapes=[buffer] * 4 + [inside_buffer] * 2 + [pltpu.SemaphoreType.DMA((8,))] * 4,
+        scratch_shapes=[pltpu.VMEM(w.shape, jnp.bfloat16) for w in (inner, outer)]
+        + [buffer] * 4
+        + [inside_buffer] * 2
+        + [pltpu.SemaphoreType.DMA((8,))] * 4,
         compiler_params=pltpu.CompilerParams(
             collective_id=collective_id, has_side_effects=True, vmem_limit_bytes=60 << 20
         ),
@@ -1749,171 +1781,225 @@
 
 
 def own_units_kernel(
-    chunks, parts_ref, small_ref, grads_ref, small_out,
-    own, other, relay, landed, small_landed,
-    own_sem, other_send, other_recv, relay_send, relay_recv, landed_send, landed_recv, small_send, small_recv,
+    chunks, units_of, slopes_ref, rows_ref, ids_ref, zero_ref, joint_ref, normed_ref, attended_ref,
+    grad_ref, small_ref, grads_ref, small_out, *refs
 ):
+    slopes, late, mixed, made, passing, own, other, relay, landed, small_landed, ready = refs[:11]
+    other_send, other_recv, relay_send, relay_recv, landed_send, landed_recv = refs[11:17]
+    small_send, small_recv, load_sem, store_sem = refs[17:]
     chip, core = lax.axis_index("dp"), lax.axis_index("ctx")
     beside = chip + 1 - 2 * lax.rem(chip, 2)
     across = lax.rem(chip + 2, 4)
     opposite = across + 1 - 2 * lax.rem(across, 2)
     places = (opposite, beside, across, chip)
-    slots = grads_ref.shape[0]
+    slots, unit_rows = own.shape[1:3]
+    table_units = slopes.shape[0]
+    tokens = rows_ref.shape[0]
     size = slots // chunks
     split = (chunks + 1) // 2
+    load = pltpu.make_async_copy(slopes_ref, slopes, load_sem)
+    load.start()
     greet_plane()
+
+    def repeat(first, last, body):
+        def step(i, carry):
+            body(i)
+            return carry
+
+        lax.fori_loop(first, last, step, 0)
 
     def span(q):
         return pl.ds(q * size, size)
 
-    def fetch(k):
-        first = (places[k] * 2 + core) * slots
-        return pltpu.make_async_copy(parts_ref.at[pl.ds(first, slots)], own.at[k], own_sem.at[k])
+    def remote(source, target, send, recv, place):
+        return pltpu.make_async_remote_copy(
+            src_ref=source,
+            dst_ref=target,
+            send_sem=send,
+            recv_sem=recv,
+            device_id=place,
+            device_id_type=MESH_ID,
+        )
 
     def pass_over(k, q):
-        first = (places[k] * 2 + 1 - core) * slots + q * size
-        return pltpu.make_async_remote_copy(
-            src_ref=parts_ref.at[pl.ds(first, size)],
-            dst_ref=other.at[k, span(q)],
-            send_sem=other_send.at[k, q],
-            recv_sem=other_recv.at[k, q],
-            device_id={"ctx": 1 - core},
-            device_id_type=MESH_ID,
+        return remote(
+            passing.at[k % 2, span(q)],
+            other.at[k, span(q)],
+            other_send.at[k, q],
+            other_recv.at[k, q],
+            {"ctx": 1 - core},
         )
 
     def to_relay(q, place):
-        return pltpu.make_async_remote_copy(
-            src_ref=own.at[0, span(q)],
-            dst_ref=relay.at[span(q)],
-            send_sem=relay_send.at[q],
-            recv_sem=relay_recv.at[q],
-            device_id={"dp": place},
-            device_id_type=MESH_ID,
-        )
+        return remote(own.at[0, span(q)], relay.at[span(q)], relay_send.at[q], relay_recv.at[q], {"dp": place})
 
     def to_owner(k, q):
-        return pltpu.make_async_remote_copy(
-            src_ref=own.at[k, span(q)],
-            dst_ref=landed.at[k - 1, span(q)],
-            send_sem=landed_send.at[k - 1, q],
-            recv_sem=landed_recv.at[k - 1, q],
-            device_id={"dp": places[k]},
-            device_id_type=MESH_ID,
+        return remote(
+            own.at[k, span(q)],
+            landed.at[k - 1, span(q)],
+            landed_send.at[k - 1, q],
+            landed_recv.at[k - 1, q],
+            {"dp": places[k]},
         )
 
     def small_copy(step):
         place, _ = plane_peer(step)
-        return pltpu.make_async_remote_copy(
-            src_ref=small_ref,
-            dst_ref=small_landed.at[chip * 2 + core],
-            send_sem=small_send.at[step],
-            recv_sem=small_recv.at[step],
-            device_id=place,
-            device_id_type=MESH_ID,
-        )
-
-    for k in range(4):
-        fetch(k).start()
-
-        def start(q, carry):
-            pass_over(k, q).start()
-            return carry
-
-        lax.fori_loop(0, chunks, start, 0)
+        return remote(
+            small_ref, small_landed.at[chip * 2 + core], small_send.at[step], small_recv.at[step], place
+        )
+
+    joint_units = joint_ref.shape[0] // unit_rows
+    late[pl.ds(0, joint_units)] = jnp.dot(
+        joint_ref[...], normed_ref[...], preferred_element_type=jnp.float32
+    ).reshape(joint_units, unit_rows, -1)
+    last_units = attended_ref.shape[0] // unit_rows
+    late[pl.ds(joint_units, last_units)] = jnp.dot(
+        attended_ref[...], grad_ref[...], preferred_element_type=jnp.float32
+    ).reshape(last_units, unit_rows, -1)
+    load.wait()
+    group = made.shape[0] // unit_rows
+
+    def form(owner, target):
+        def some(g):
+            first = owner * slots + g * group
+
+            def fill(s):
+                unit = units_of[first + s]
+                lines = pl.ds(pl.multiple_of(s * unit_rows, unit_rows), unit_rows)
+                mixed[lines, :tokens] = slopes[jnp.minimum(unit, table_units - 1)]
+                row = lax.broadcasted_iota(jnp.int32, (unit_rows, tokens), 0) + unit * unit_rows
+                mixed[lines, tokens:] = jnp.where(row == ids_ref[...], 1.0, 0.0).astype(jnp.bfloat16)
+
+            repeat(0, group, fill)
+            made[...] = jnp.dot(
+                mixed[:, :tokens], rows_ref[...], preferred_element_type=jnp.float32
+            ) + jnp.dot(mixed[:, tokens:], zero_ref[...], preferred_element_type=jnp.float32)
+
+            def put(s):
+                unit = units_of[first + s]
+                table_piece = made[pl.ds(pl.multiple_of(s * unit_rows, unit_rows), unit_rows)]
+                late_piece = late[jnp.clip(unit - table_units, 0, late.shape[0] - 1)]
+                marks = jnp.zeros(table_piece.shape, jnp.int32) + unit
+                piece = jnp.where(marks < table_units, table_piece, late_piece)
+                target[g * group + s] = piece.astype(jnp.bfloat16)
+
+            repeat(0, group, put)
+
+        repeat(0, slots // group, some)
 
     def joined(k, q):
         pass_over(k, q).wait_recv()
         return own[k, span(q)].astype(jnp.float32) + other[k, span(q)].astype(jnp.float32)
 
-    fetch(0).wait()
-
     def first_leg(place):
-        def leg(q, carry):
+        def leg(q):
             own[0, span(q)] = joined(0, q).astype(jnp.bfloat16)
             to_relay(q, place).start()
-            return carry
 
         return leg
 
-    lax.fori_loop(0, split, first_leg(beside), 0)
-    lax.fori_loop(split, chunks, first_leg(across), 0)
-    lax.fori_loop(1, 8, lambda step, carry: (small_copy(step).start(), carry)[1], 0)
-    small_landed[chip * 2 + core] = small_ref[...]
-    fetch(1).wait()
-    fetch(2).wait()
-
     def direct(k):
-        def leg(q, carry):
+        def leg(q):
             own[k, span(q)] = joined(k, q).astype(jnp.bfloat16)
             to_owner(k, q).start()
-            return carry
 
         return leg
 
     def relayed(k, place):
-        def leg(q, carry):
+        def leg(q):
             to_relay(q, place).wait_recv()
             total = joined(k, q) + relay[span(q)].astype(jnp.float32)
             own[k, span(q)] = total.astype(jnp.bfloat16)
             to_owner(k, q).start()
-            return carry
 
         return leg
 
-    lax.fori_loop(0, split, direct(1), 0)
-    lax.fori_loop(split, chunks, direct(2), 0)
-    lax.fori_loop(0, split, relayed(2, beside), 0)
-    lax.fori_loop(split, chunks, relayed(1, across), 0)
-    fetch(3).wait()
-
-    def keep(q, carry):
+    def form_pair(k):
+        if k >= 2:
+            repeat(0, chunks, lambda q: pass_over(k - 2, q).wait_send())
+        form(places[k] * 2 + 1 - core, passing.at[k % 2])
+        repeat(0, chunks, lambda q: pass_over(k, q).start())
+        form(places[k] * 2 + core, own.at[k])
+
+    form_pair(0)
+    repeat(0, split, first_leg(beside))
+    repeat(split, chunks, first_leg(across))
+    repeat(1, 8, lambda step: small_copy(step).start())
+    small_landed[chip * 2 + core] = small_ref[...]
+    form_pair(1)
+    repeat(0, split, direct(1))
+    form_pair(2)
+    repeat(split, chunks, direct(2))
+    repeat(0, split, relayed(2, beside))
+    repeat(split, chunks, relayed(1, across))
+    form_pair(3)
+
+    def store(q):
+        return pltpu.make_async_copy(
+            ready.at[lax.rem(q, 2)], grads_ref.at[span(q)], store_sem.at[lax.rem(q, 2)]
+        )
+
+    def keep(q):
         total = joined(3, q)
         to_owner(1, q).wait_recv()
         to_owner(2, q).wait_recv()
-        grads_ref[span(q)] = (
+
+        @pl.when(q >= 2)
+        def _():
+            store(q - 2).wait()
+
+        ready[lax.rem(q, 2)] = (
             total + landed[0, span(q)].astype(jnp.float32) + landed[1, span(q)].astype(jnp.float32)
         )
-        return carry
-
-    lax.fori_loop(0, split, keep, 0)
-    lax.fori_loop(split, chunks, keep, 0)
-
-    def finish(q, carry):
-        for k in range(4):
+        store(q).start()
+
+    repeat(0, chunks, keep)
+
+    def finish(q):
+        for k in (2, 3):
             pass_over(k, q).wait_send()
         to_owner(1, q).wait_send()
         to_owner(2, q).wait_send()
-        return carry
-
-    lax.fori_loop(0, chunks, finish, 0)
-    lax.fori_loop(0, split, lambda q, carry: (to_relay(q, beside).wait_send(), carry)[1], 0)
-    lax.fori_loop(split, chunks, lambda q, carry: (to_relay(q, across).wait_send(), carry)[1], 0)
-    lax.fori_loop(1, 8, lambda step, carry: (small_copy(step).wait(), carry)[1], 0)
+
+    repeat(0, chunks, finish)
+    repeat(0, split, lambda q: to_relay(q, beside).wait_send())
+    repeat(split, chunks, lambda q: to_relay(q, across).wait_send())
+    repeat(1, 8, lambda step: small_copy(step).wait())
     total = small_landed[0]
     for source in range(1, 8):
         total = total + small_landed[source]
     small_out[...] = total
-
-
-def own_units(parts, small, slots, collective_id):
-    unit = parts.shape[1:]
+    for q in range(max(0, chunks - 2), chunks):
+        store(q).wait()
+
+
+def own_units(units_of, slots, unit_rows, slopes, rows, ids, zero, joint, normed, attended, grad, small, collective_id):
+    tokens, width = rows.shape
+    unit = (unit_rows, width)
     chunks = max(k for k in range(1, 8) if slots % k == 0)
-    block = pltpu.VMEM((4, slots) + unit, jnp.bfloat16)
+    group = max(k for k in range(1, 8) if slots % k == 0)
+    late = (joint.shape[0] + attended.shape[0]) // unit_rows
+    slopes = slopes.reshape(-1, unit_rows, tokens)
     return pl.pallas_call(
         functools.partial(own_units_kernel, chunks),
         out_shape=[
             jax.ShapeDtypeStruct((slots,) + unit, jnp.float32),
             jax.ShapeDtypeStruct(small.shape, jnp.float32),
         ],
-        in_specs=[whole_any, whole_vmem],
-        out_specs=[whole_vmem] * 2,
+        in_specs=[pl.BlockSpec(memory_space=pltpu.SMEM), whole_any] + [whole_vmem] * 8,
+        out_specs=[whole_any, whole_vmem],
         scratch_shapes=[
-            block,
-            block,
+            pltpu.VMEM(slopes.shape, jnp.bfloat16),
+            pltpu.VMEM((late,) + unit, jnp.float32),
+            pltpu.VMEM((group * unit_rows, 2 * tokens), jnp.bfloat16),
+            pltpu.VMEM((group * unit_rows, width), jnp.float32),
+            pltpu.VMEM((2, slots) + unit, jnp.bfloat16),
+            pltpu.VMEM((4, slots) + unit, jnp.bfloat16),
+            pltpu.VMEM((4, slots) + unit, jnp.bfloat16),
             pltpu.VMEM((slots,) + unit, jnp.bfloat16),
             pltpu.VMEM((2, slots) + unit, jnp.bfloat16),
             pltpu.VMEM((8,) + small.shape, jnp.float32),
-            pltpu.SemaphoreType.DMA((4,)),
+            pltpu.VMEM((2, slots // chunks) + unit, jnp.float32),
             pltpu.SemaphoreType.DMA((4, chunks)),
             pltpu.SemaphoreType.DMA((4, chunks)),
             pltpu.SemaphoreType.DMA((chunks,)),
@@ -1922,11 +2008,13 @@
             pltpu.SemaphoreType.DMA((2, chunks)),
             pltpu.SemaphoreType.DMA((8,)),
             pltpu.SemaphoreType.DMA((8,)),
+            pltpu.SemaphoreType.DMA,
+            pltpu.SemaphoreType.DMA((2,)),
         ],
         compiler_params=pltpu.CompilerParams(
-            collective_id=collective_id, has_side_effects=True, vmem_limit_bytes=56 << 20
+            collective_id=collective_id, has_side_effects=True, vmem_limit_bytes=63 << 20
         ),
-    )(parts, small)
+    )(units_of, slopes, rows, ids, zero, joint, normed, attended, grad, small)
 
 
 def to_plane(buffer):
@@ -2098,13 +2186,12 @@
         router_low.T,
         route_pairs.T,
     )
-    inner_low = expert_in[0].astype(jnp.bfloat16)
-    outer_low = expert_out[0].astype(jnp.bfloat16)
     if on_square:
         moe_partial, arrived, returned, counts = experts_forward(
-            normed_two_low, dest, gate_columns, route_pairs, inner_low, outer_low, counts, capacity, 8
+            normed_two_low, dest, gate_columns, route_pairs, expert_in[0], expert_out[0], counts, capacity, 8
         )
     else:
+        inner_low, outer_low = expert_in[0].astype(jnp.bfloat16), expert_out[0].astype(jnp.bfloat16)
         moe_partial, arrived, returned = plain_forward(
             normed_two_low, dest, gate_columns, inner_low, outer_low, owners, capacity
         )
@@ -2130,8 +2217,8 @@
             route_pairs.T,
             returned,
             arrived,
-            inner_low,
-            outer_low,
+            expert_in[0],
+            expert_out[0],
             9,
         )
     else:
@@ -2165,13 +2252,23 @@
     )
     router_grad = jnp.dot(logit_grad, normed_two_low, preferred_element_type=jnp.float32)
     loss_local = jnp.sum(weight_rows[2:3] * logsum_vocab) - jnp.sum(target_total)
-    query_grad, pair_grad, before_grad, bias_lines = attention_back(
+    query_grad, pair_grad, before_grad, bias_lines, *expert_states = attention_back(
         rel_bias,
         joint,
         pairs_before,
         logsum_rows,
         grad_one_low,
         project_low,
+        (
+            expert_in[0],
+            expert_in_first[0],
+            expert_in_second[0],
+            inner_grad,
+            expert_out[0],
+            expert_out_first[0],
+            expert_out_second[0],
+            outer_grad,
+        ),
         heads_here,
         head_size,
     )
@@ -2194,10 +2291,13 @@
     )
     my_units = jnp.take(slot_unit, my_owner, axis=0)
     my_filled = jnp.take(slot_filled, my_owner, axis=0)[:, None, None]
-    outgoing, *expert_states = weight_grads(
-        unit_slots,
-        owners * most_units,
-        unit_rows,
+    bias_row = jnp.concatenate([bias_grad.reshape(-1), loss_local[None]])
+    bias_row = jnp.pad(bias_row, (0, model_width - bias_row.shape[0]))[None]
+    small = jnp.concatenate([gain_grads[:3], router_grad, bias_row], 0)
+    small = jnp.pad(small, ((0, -small.shape[0] % 8), (0, 0)))
+    slot_rates = unit_rates(my_units, table_units, query_units, value_units)[:, None, None]
+    states = (master[0, 0], master_first[0, 0], master_second[0, 0])
+    grad_rows = (
         slopes,
         head_low,
         local_ids[None, :],
@@ -2206,26 +2306,11 @@
         normed_one_low,
         attended,
         grad_one_low,
-        (
-            expert_in[0],
-            expert_in_first[0],
-            expert_in_second[0],
-            inner_grad,
-            expert_out[0],
-            expert_out_first[0],
-            expert_out_second[0],
-            outer_grad,
-        ),
-    )
-    bias_row = jnp.concatenate([bias_grad.reshape(-1), loss_local[None]])
-    bias_row = jnp.pad(bias_row, (0, model_width - bias_row.shape[0]))[None]
-    small = jnp.concatenate([gain_grads[:3], router_grad, bias_row], 0)
-    small = jnp.pad(small, ((0, -small.shape[0] % 8), (0, 0)))
-    slot_rates = unit_rates(my_units, table_units, query_units, value_units)[:, None, None]
-    states = (master[0, 0], master_first[0, 0], master_second[0, 0])
+    )
     if on_square:
-        mine, small = own_units(outgoing, small, most_units, 10)
+        mine, small = own_units(slot_unit.reshape(-1), most_units, unit_rows, *grad_rows, small, 10)
     else:
+        outgoing = weight_grads(unit_slots, owners * most_units, unit_rows, *grad_rows)
         mine = lax.psum_scatter(
             outgoing.astype(jnp.float32), ("dp", "ctx"), scatter_dimension=0, tiled=True
         )

time: 839 us -> 809 us (0.964)
  Pallas kernels: 744 us -> 720 us
    pallas_call x1 -> x0, Pallas kernels: 41.8 us -> none  [weight_grads(): pl.pallas_call(functools.partial(weight_grads_kernel, tile // unit_rows,...]
    pallas_call x1, Pallas kernels: 83.6 us -> 97.2 us  [own_units(): pl.pallas_call(functools.partial(own_units_kernel, chunks), out_shape=[ja...]
where the time goes in v8:
time: 809 us; the launch traced here: 798 us
  Pallas kernels  720 us (89%)
  other arithmetic  32.9 us (4%)
  local copies, waits for them, and re-layouts  22.7 us (3%)
    pallas_call x1, Pallas kernels, head_line(): pl.pallas_call(functools.partial(head_line_kernel, vocab_tile(vocab)), ou...  148 us
    pallas_call x1, Pallas kernels, embed(): pl.pallas_call(functools.partial(embed_kernel, chunks), out_shape=[jax.Sh...  120 us
    pallas_call x2, Pallas kernels, sum_line(): pl.pallas_call(functools.partial(sum_line_kernel, rows, count, opening, p...  97.9 us
    pallas_call x1, Pallas kernels, own_units(): pl.pallas_call(functools.partial(own_units_kernel, chunks), out_shape=[ja...  97.2 us
    pallas_call x1, Pallas kernels, experts_forward(): pl.pallas_call(experts_kernel, out_shape=[jax.ShapeDtypeStruct((tokens, w...  95 us
    pallas_call x1, Pallas kernels, experts_backward(): pl.pallas_call(experts_back_kernel, out_shape=[jax.ShapeDtypeStruct((toke...  93.8 us
    pallas_call x1, Pallas kernels, gather_line(): pl.pallas_call(functools.partial(gather_line_kernel, count), out_shape=[j...  28.9 us
    pallas_call x1, Pallas kernels, attention_back(): pl.pallas_call(functools.partial(attention_back_kernel, heads, size), out...  21.1 us
  transfers between devices with their start and end apart: 5, of which 1 were waited for; matrix products, arithmetic and copies ran while one was open for 2% of the time, Pallas kernels for 5%

profile of v8, /device:TPU:0, one launch (start us, length us, event | category | flops | bytes accessed | tf_op | source)
XLA Modules:
  0.0 798.0 jit_solution(14464387716614353364)
XLA Ops:
  2.1 3.4 convert_reduce_fusion
  10.7 119.8 %shard_map.384 = (bf16[137,64,768]{2,1,0:T(8,128)(2,1)}, bf16[1024,768]{1,0:T(8,128)(2,1)}) custom-call(s32[137]{0:T(256)} %copy-done.33, f32[21,64,768]{2,1,0:T(8,128)} %bitcast.105, s32[1024,1]{1,0:T(8,128)} %fusion.7.rows_ref), custom_call_target="tpu_custom_call" | custom-call | tf_op jit(solution)/shard_map/pallas_call | solution.py:673
  131.7 2.5 collective-permute-start.2
  134.2 1.7 collective-permute-start.3
  140.9 2.2 collective-permute-start
  147.0 12.8 %shard_map.385 = (bf16[192,1024]{1,0:T(8,128)(2,1)S(1)}, f32[3,1024,1]{2,1,0:T(8,128)S(1)}) custom-call(f32[3,8]{1,0:T(4,128)S(1)} %copy-done.18, bf16[576,1024]{1,0:T(8,128)(2,1)S(1)} %convolution_convert_fusion.own_ref, bf16[384,1024]{1,0:T(8,128)(2,1)} %collective-permute-done.before_ref), custom_call_target="tpu_custom_call" | custom-call | tf_op jit(solution)/shard_map/pallas_call | solution.py:801
  159.8 28.9 %shard_map.386 = bf16[4,192,1024]{2,1,0:T(8,128)(2,1)S(1)} custom-call(bf16[192,1024]{1,0:T(8,128)(2,1)S(1)} %get-tuple-element.78.refs_0_.attended_ref), custom_call_target="tpu_custom_call" | custom-call | tf_op jit(solution)/shard_map/pallas_call | solution.py:362
  188.8 5.6 shard_map.387
  194.4 1.7 copy-done.1
  199.3 95.0 %shard_map.388 = (f32[1024,768]{1,0:T(8,128)}, bf16[8,288,768]{2,1,0:T(8,128)(2,1)}, bf16[8,288,768]{2,1,0:T(8,128)(2,1)}, f32[8,128]{1,0:T(8,128)}) custom-call(bf16[1024,768]{1,0:T(8,128)(2,1)} %copy-done.5, s32[2,1024]{1,0:T(2,128)} %copy-done.23, s32[1024,2]{1,0:T(8,128)} %copy.77.dest_columns, f32[1024,8]{1,0:T(8,128)} %copy-done.13, ...), custom_call_target="tpu_custom_call" | custom-call | tf_op jit(solution)/shard_map/pallas_call | solution.py:1618
  297.6 148.2 %shard_map.389 = (bf16[1024,768]{1,0:T(8,128)(2,1)}, bf16[1024,768]{1,0:T(8,128)(2,1)}, f32[1024,768]{1,0:T(8,128)}, f32[1,768]{1,0:T(1,128)}, f32[1,1024]{1,0:T...) custom-call(f32[1024,768]{1,0:T(8,128)} %get-tuple-element.82.part_ref, f32[1024,768]{1,0:T(8,128)} %copy-done.1, ...), custom_call_target="tpu_custom_call" | custom-call | tf_op jit(solution)/shard_map/pallas_call | solution.py:1278
  445.9 93.8 %shard_map.390 = (f32[1024,768]{1,0:T(8,128)}, f32[2,1024]{1,0:T(2,128)}, f32[768,768]{1,0:T(8,128)}, f32[768,768]{1,0:T(8,128)}) custom-call(bf16[1024,768]{1,0:T(8,128)(2,1)} %get-tuple-element.88.rows_ref, s32[2,1024]{1,0:T(2,128)} %copy-done.23, s32[1024,2]{1,0:T(8,128)} %copy.77.dest_columns, f32[2,1024]{1,0:T(2,128)} %copy-done.16, ...), custom_call_target="tpu_custom_call" | custom-call | tf_op jit(solution)/shard_map/pallas_call | solution.py:1763
  540.5 51.6 %shard_map.391 = (bf16[1024,768]{1,0:T(8,128)(2,1)S(1)}, f32[1024,768]{1,0:T(8,128)S(1)}, bf16[8,1024]{1,0:T(8,128)(2,1)S(1)}, f32[1,1024]{1,0:T(1,128)S(1)}, f32[1,768]{1,0:T(1,128)S(1)}) custom-call(f32[1024,768]{1,0:T(8,128)} %get-tuple-element.92.part_ref, f32[1024,768]{1,0:T(8,128)} %copy-done.1, f32[1,768]{1,0:T(1,128)S(1)} %get-tuple-element.157.gain_ref.refs_1_, ...), custom_call_target="tpu_custom_call" | custom-call | tf_op jit(solution)/shard_map/pallas_call | solution.py:184
  593.3 1.7 copy-done.6
  594.9 21.1 %shard_map.392 = (bf16[192,1024]{1,0:T(8,128)(2,1)S(1)}, f32[384,1024]{1,0:T(8,128)S(1)}, bf16[384,1024]{1,0:T(8,128)(2,1)S(1)}, f32[24,256]{1,0:T(8,128)S(1)}, ...) custom-call(f32[3,8]{1,0:T(4,128)S(1)} %copy-done.18, ...), custom_call_target="tpu_custom_call" | custom-call | tf_op jit(solution)/shard_map/pallas_call | solution.py:970
  623.3 1.8 fusion.24
  625.1 4.0 collective-permute-done.4
  629.0 1.9 add_convert_fusion
  630.9 3.1 fusion.17.part_ref
  635.1 46.3 %shard_map.393 = (bf16[1024,768]{1,0:T(8,128)(2,1)S(1)}, f32[8,768]{1,0:T(8,128)S(1)}) custom-call(f32[1024,768]{1,0:T(8,128)} %fusion.17.part_ref, bf16[1024,768]{1,0:T(8,128)(2,1)S(1)} %copy-done, f32[1,768]{1,0:T(1,128)S(1)} %get-tuple-element.155.refs_1_, f32[1024,768]{1,0:T(8,128)} %copy-done.6, f32[1,768]{1,0:T(1,128)S(1)} %get-tuple-element.103.refs_3_, ...), custom_call_target="tpu_custom_call" | custom-call | tf_op jit(solution)/shard_map/pallas_call | solution.py:184
  683.3 97.2 %shard_map.394 = (f32[21,64,768]{2,1,0:T(8,128)}, f32[16,768]{1,0:T(8,128)}) custom-call(s32[168]{0:T(256)} %reshape.285.units_of, bf16[125,64,1024]{2,1,0:T(8,128)(2,1)} %bitcast.106, bf16[1024,768]{1,0:T(8,128)(2,1)} %get-tuple-element.86.rows_ref, s32[1,1024]{1,0:T(1,128)} %copy-done.25, bf16[1024,768]{1,0:T(8,128)(2,1)} %copy-done.10, ...), custom_call_target="tpu_custom_call" | custom-call | tf_op jit(solution)/shard_map/pallas_call | solution.py:1983
  782.6 1.4 multiply_subtract_fusion
  784.0 1.4 multiply_subtract_fusion.1
  787.2 10.4 %fusion.16 = (f32[1,1,21,64,768]{4,3,2,1,0:T(8,128)}, f32[1,1,21,64,768]{4,3,2,1,0:T(8,128)}, f32[1,1,21,64,768]{4,3,2,1,0:T(8,128)}) fusion(f32[21,64,768]{2,1,0:T(8,128)} %get-tuple-element.112, pred[21]{0:T(512)(128)(4,1)S(1)} %select_reduce_fusion.2, f32[1,1,21,64,768]{4,3,2,1,0:T(8,128)} %param.35, f32[1,1,21,64,768]{4,3,2,1,0:T(8,128)} %param.34, ...), kind=kLoop, calls=%fused_computation.79 | loop fusion | flops 16515072 | bytes 28901480 | tf_op jit(solution)/shard_map/broadcast_in_dim | solution.py:2334
  (147 shorter events, 36.4 us)
Async XLA Ops:
  6.3 124.2 %copy-start.25 = (s32[1,1024]{1,0:T(1,128)}, s32[1,1024]{1,0:T(1,128)S(1)}, u32[]{:S(2)}) copy-start(s32[1,1024]{1,0:T(1,128)S(1)} %get-tuple-element.151.ids_ref) | copy-start | bytes 12292
  8.7 135.3 %copy-start.23 = (s32[2,1024]{1,0:T(2,128)}, s32[2,1024]{1,0:T(2,128)S(1)}, u32[]{:S(2)}) copy-start(s32[2,1024]{1,0:T(2,128)S(1)} %add_select_fusion.1.dest_rows) | copy-start | bytes 24580
  10.7 126.9 %copy-start.26 = (f32[3,768]{1,0:T(4,128)S(1)}, f32[3,768]{1,0:T(4,128)}, u32[]{:S(2)}) copy-start(f32[3,768]{1,0:T(4,128)} %param.42) | copy-start | bytes 27652
  131.6 57.1 %collective-permute-start.1 = (bf16[192,768]{1,0:T(8,128)(2,1)S(1)}, bf16[192,768]{1,0:T(8,128)(2,1)}, u32[]{:S(2)}, u32[]{:S(2)}) collective-permute-start(bf16[192,768]{1,0:T(8,128)(2,1)S(1)} %bitcast.88), channel_id=1, source_target_pairs={{0,1},{1,2},{2,3},{3,0},{4,5},{5,6},{6,7},{7,4},{8,9},{9,10},{10,1... | collective-permute-start | bytes 884744 | tf_op jit(solution)/shard_map/ppermute | solution.py:2165
  131.7 57.0 %collective-permute-start.2 = (bf16[192,768]{1,0:T(8,128)(2,1)S(1)}, bf16[192,768]{1,0:T(8,128)(2,1)}, u32[]{:S(2)}, u32[]{:S(2)}) collective-permute-start(bf16[192,768]{1,0:T(8,128)(2,1)S(1)} %bitcast.89), channel_id=1, source_target_pairs={{0,2},{1,3},{2,0},{3,1},{4,6},{5,7},{6,4},{7,5},{8,10},{9,11},{10,... | collective-permute-start | bytes 884744 | tf_op jit(solution)/shard_map/ppermute | solution.py:2165
  134.2 54.5 %collective-permute-start.3 = (bf16[192,768]{1,0:T(8,128)(2,1)S(1)}, bf16[192,768]{1,0:T(8,128)(2,1)}, u32[]{:S(2)}, u32[]{:S(2)}) collective-permute-start(bf16[192,768]{1,0:T(8,128)(2,1)S(1)} %bitcast.90), channel_id=1, source_target_pairs={{0,3},{1,0},{2,1},{3,2},{4,7},{5,4},{6,5},{7,6},{8,11},{9,8},{10,9... | collective-permute-start | bytes 884744 | tf_op jit(solution)/shard_map/ppermute | solution.py:2165
  139.9 48.8 %copy-start.2 = (bf16[576,1024]{1,0:T(8,128)(2,1)}, bf16[576,1024]{1,0:T(8,128)(2,1)S(1)}, u32[]{:S(2)}) copy-start(bf16[576,1024]{1,0:T(8,128)(2,1)S(1)} %convolution_convert_fusion.own_ref) | copy-start | bytes 3538948
  140.9 6.1 collective-permute-start
  159.8 28.9 %copy-start.9 = (f32[3,1024,1]{2,1,0:T(8,128)}, f32[3,1024,1]{2,1,0:T(8,128)S(1)}, u32[]{:S(2)}) copy-start(f32[3,1024,1]{2,1,0:T(8,128)S(1)} %get-tuple-element.87.logsum_ref) | copy-start | bytes 36868
  159.8 28.9 %copy-start.12 = (bf16[192,1024]{1,0:T(8,128)(2,1)}, bf16[192,1024]{1,0:T(8,128)(2,1)S(1)}, u32[]{:S(2)}) copy-start(bf16[192,1024]{1,0:T(8,128)(2,1)S(1)} %get-tuple-element.78.refs_0_.attended_ref) | copy-start | bytes 1179652
  445.8 93.9 %copy-start.36 = (f32[1,1024]{1,0:T(1,128)S(1)}, f32[1,1024]{1,0:T(1,128)}, u32[]{:S(2)}) copy-start(f32[1,1024]{1,0:T(1,128)} %get-tuple-element.95) | copy-start | bytes 12292
  445.8 94.6 %copy-start.8 = (bf16[768,8]{1,0:T(8,128)(2,1)S(1)}, bf16[768,8]{1,0:T(8,128)(2,1)}, u32[]{:S(2)}) copy-start(bf16[768,8]{1,0:T(8,128)(2,1)} %copy-done.7) | copy-start | bytes 36868
  445.8 94.6 %copy-start.15 = (s32[1,1024,2]{1,2,0:T(2,128)S(1)}, s32[1,1024,2]{1,2,0:T(2,128)}, u32[]{:S(2)}) copy-start(s32[1,1024,2]{1,2,0:T(2,128)} %param.30) | copy-start | bytes 24580
  445.8 94.6 %copy-start.17 = (f32[2,1024]{1,0:T(2,128)S(1)}, f32[2,1024]{1,0:T(2,128)}, u32[]{:S(2)}) copy-start(f32[2,1024]{1,0:T(2,128)} %copy-done.16) | copy-start | bytes 24580
  540.5 54.5 %copy-start.3 = (bf16[576,1024]{1,0:T(8,128)(2,1)S(1)}, bf16[576,1024]{1,0:T(8,128)(2,1)}, u32[]{:S(2)}) copy-start(bf16[576,1024]{1,0:T(8,128)(2,1)} %copy-done.2) | copy-start | bytes 3538948
  594.9 23.6 %copy-start.30 = (s32[137,1]{0,1:T(1,128)S(1)}, s32[137,1]{0,1:T(1,128)}, u32[]{:S(2)}) copy-start(s32[137,1]{0,1:T(1,128)} %param.32) | copy-start | bytes 1648
  594.9 26.3 %copy-start.35 = (f32[1,1024]{1,0:T(1,128)S(1)}, f32[1,1024]{1,0:T(1,128)}, u32[]{:S(2)}) copy-start(f32[1,1024]{1,0:T(1,128)} %get-tuple-element.109) | copy-start | bytes 12292
  617.2 11.8 %collective-permute-start.4 = (bf16[384,1024]{1,0:T(8,128)(2,1)S(1)}, bf16[384,1024]{1,0:T(8,128)(2,1)}, u32[]{:S(2)}, u32[]{:S(2)}) collective-permute-start(bf16[384,1024]{1,0:T(8,128)(2,1)S(1)} %get-tuple-element.101), channel_id=1, source_target_pairs={{4,0},{5,1},{6,2},{7,3},{12,8},{13,9},{14,10},{15,11},{20,16},{21,... | collective-permute-start | bytes 2359304 | tf_op jit(solution)/shard_map/ppermute | solution.py:38
  683.3 99.3 %copy-start.28 = (f32[768,8]{0,1:T(8,128)S(1)}, f32[768,8]{0,1:T(8,128)}, u32[]{:S(2)}) copy-start(f32[768,8]{0,1:T(8,128)} %param.46) | copy-start | bytes 73732
  683.3 99.3 %copy-start.29 = (f32[768,8]{0,1:T(8,128)S(1)}, f32[768,8]{0,1:T(8,128)}, u32[]{:S(2)}) copy-start(f32[768,8]{0,1:T(8,128)} %param.47) | copy-start | bytes 73732
  683.3 100.7 %copy-start.31 = (f32[3,768]{1,0:T(4,128)S(1)}, f32[3,768]{1,0:T(4,128)}, u32[]{:S(2)}) copy-start(f32[3,768]{1,0:T(4,128)} %param.43) | copy-start | bytes 27652
  683.3 100.7 %copy-start.32 = (f32[3,768]{1,0:T(4,128)S(1)}, f32[3,768]{1,0:T(4,128)}, u32[]{:S(2)}) copy-start(f32[3,768]{1,0:T(4,128)} %param.44) | copy-start | bytes 27652
  683.3 103.3 %copy-start.37 = (f32[3,8]{1,0:T(4,128)S(1)}, f32[3,8]{1,0:T(4,128)}, u32[]{:S(2)}) copy-start(f32[3,8]{1,0:T(4,128)} %param.49) | copy-start | bytes 292
  683.3 103.3 %copy-start.38 = (f32[3,8]{1,0:T(4,128)S(1)}, f32[3,8]{1,0:T(4,128)}, u32[]{:S(2)}) copy-start(f32[3,8]{1,0:T(4,128)} %param.50) | copy-start | bytes 292
  (21 other events, 76.9 us)

commit v9 on v8

--- a/solution.py
+++ b/solution.py
@@ -327,54 +327,6 @@
     return ((grad_one[span] + part) * scale).astype(jnp.bfloat16)
 
 
-def gather_line_kernel(count, *refs):
-    ins = refs[:count]
-    outs = refs[count : 2 * count]
-    local_sem, send_sem, recv_sem = refs[2 * count :]
-    rank = lax.axis_index("tensor")
-    barrier = pltpu.get_barrier_semaphore()
-    for step in (1, 2, 3):
-        other = lax.rem(rank + step, 4)
-        pl.semaphore_signal(barrier, inc=1, device_id={"tensor": other}, device_id_type=MESH_ID)
-    pl.semaphore_wait(barrier, 3)
-    copies = []
-    for k in range(count):
-        for step in (1, 2, 3):
-            copy = pltpu.make_async_remote_copy(
-                src_ref=ins[k],
-                dst_ref=outs[k].at[rank],
-                send_sem=send_sem.at[k, step - 1],
-                recv_sem=recv_sem.at[k, step - 1],
-                device_id={"tensor": lax.rem(rank + step, 4)},
-                device_id_type=MESH_ID,
-            )
-            copy.start()
-            copies.append(copy)
-        own = pltpu.make_async_copy(ins[k], outs[k].at[rank], local_sem.at[k])
-        own.start()
-        own.wait()
-    for copy in copies:
-        copy.wait()
-
-
-def gather_line(arrays, collective_id):
-    count = len(arrays)
-    return pl.pallas_call(
-        functools.partial(gather_line_kernel, count),
-        out_shape=[jax.ShapeDtypeStruct((4,) + x.shape, x.dtype) for x in arrays],
-        in_specs=[whole_vmem] * count,
-        out_specs=[whole_vmem] * count,
-        scratch_shapes=[
-            pltpu.SemaphoreType.DMA((count,)),
-            pltpu.SemaphoreType.DMA((count, 3)),
-            pltpu.SemaphoreType.DMA((count, 3)),
-        ],
-        compiler_params=pltpu.CompilerParams(
-            collective_id=collective_id, has_side_effects=True, vmem_limit_bytes=40 << 20
-        ),
-    )(*arrays)
-
-
 def middle_kernel(
     attended_ref, embedded_ref, gain_ref, router_ref, routes_ref, *refs
 ):
@@ -434,7 +386,9 @@
     )(attended, embedded, gain, router, routes, *rolled)
 
 
-def embed_kernel(chunks, slots_ref, mine_ref, rows_ref, units_ref, embedded_ref, *refs):
+def embed_kernel(
+    chunks, first_unit, slots_ref, mine_ref, rows_ref, gain_ref, units_ref, embedded_ref, normed_ref, joint_ref, *refs
+):
     held, total, stage, from_end, from_mid = refs[:5]
     send_x, recv_x, send_y, recv_y, send_z, recv_z, send_core, recv_core = refs[5:13]
     send_sem, end_sem, mid_sem, back_sem, back_recv = refs[13:]
@@ -661,8 +615,17 @@
 
         repeat(0, count, drain)
 
-
-def embed(unit_slots, mine, slot_rows, collective_id):
+    stream = embedded_ref[...].astype(jnp.float32) * math.sqrt(2 * width)
+    normed = (stream * inverse_rms(stream) * gain_ref[...]).astype(jnp.bfloat16)
+    normed_ref[...] = normed
+    lines = joint_ref.shape[0]
+    weights = units_ref[first_unit : first_unit + lines // unit_rows].reshape(lines, 2 * width)
+    joint_ref[...] = lax.dot_general(
+        weights, normed, (((1,), (1,)), ((), ())), preferred_element_type=jnp.float32
+    ).astype(jnp.bfloat16)
+
+
+def embed(unit_slots, mine, slot_rows, gain, first_unit, lines, collective_id):
     slots, unit_rows, width = mine.shape
     tokens = slot_rows.shape[0]
     chunks = max(k for k in range(1, 8) if slots % k == 0)
@@ -671,13 +634,15 @@
     sems = pltpu.SemaphoreType.DMA((2, chunks))
     line = pltpu.VMEM((2, tokens // rows, rows, half), jnp.bfloat16)
     return pl.pallas_call(
-        functools.partial(embed_kernel, chunks),
+        functools.partial(embed_kernel, chunks, first_unit),
         out_shape=[
             jax.ShapeDtypeStruct((unit_slots.shape[0], unit_rows, width), jnp.bfloat16),
             jax.ShapeDtypeStruct((tokens, width), jnp.bfloat16),
+            jax.ShapeDtypeStruct((tokens, width), jnp.bfloat16),
+            jax.ShapeDtypeStruct((lines, tokens), jnp.bfloat16),
         ],
-        in_specs=[pl.BlockSpec(memory_space=pltpu.SMEM), whole_vmem, whole_vmem],
-        out_specs=[whole_vmem] * 2,
+        in_specs=[pl.BlockSpec(memory_space=pltpu.SMEM)] + [whole_vmem] * 3,
+        out_specs=[whole_vmem] * 4,
         scratch_shapes=[
             pltpu.VMEM((2, 8 * slots, unit_rows, half), jnp.bfloat16),
             pltpu.VMEM((2, tokens, half), jnp.float32),
@@ -691,7 +656,7 @@
         compiler_params=pltpu.CompilerParams(
             collective_id=collective_id, has_side_effects=True, vmem_limit_bytes=60 << 20
         ),
-    )(unit_slots, mine, slot_rows)
+    )(unit_slots, mine, slot_rows, gain)
 
 
 def pull_units_kernel(parts, slots_ref, *refs):
@@ -724,23 +689,70 @@
     )(slots, *sources)
 
 
-def attention_kernel(heads, size, bias_ref, own_ref, before_ref, out_ref, logsum_ref, scores, peak, total):
+def attention_kernel(
+    heads, size, bias_ref, own_ref, out_ref, logsum_ref, before_ref,
+    queries, own_values, old_values, scores, peak, total, keys_sem, send_sem, recv_sem,
+):
     tokens = own_ref.shape[1]
     blocks = tokens // BLOCK
     hidden = heads * size
     later = lax.axis_index("ctx") > 0
+    rank = lax.axis_index("tensor")
+    barrier = pltpu.get_barrier_semaphore()
+    other_core = {"ctx": 1 - lax.axis_index("ctx")}
+    pl.semaphore_signal(barrier, inc=1, device_id=other_core, device_id_type=MESH_ID)
+    for step in (1, 2, 3):
+        other = lax.rem(rank + step, 4)
+        pl.semaphore_signal(barrier, inc=1, device_id={"tensor": other}, device_id_type=MESH_ID)
+    pl.semaphore_wait(barrier, 4)
+    pairs = pltpu.make_async_remote_copy(
+        src_ref=own_ref.at[pl.ds(hidden, 2 * hidden)],
+        dst_ref=before_ref,
+        send_sem=keys_sem.at[0],
+        recv_sem=keys_sem.at[1],
+        device_id=other_core,
+        device_id_type=MESH_ID,
+    )
+
+    @pl.when(jnp.logical_not(later))
+    def _():
+        pairs.start()
+        before_ref[...] = jnp.zeros_like(before_ref)
+
+    def flipped(rows):
+        return rows.astype(jnp.float32).T.astype(jnp.bfloat16)
 
     for head in range(heads):
-        query = own_ref[head * size : (head + 1) * size, :].astype(jnp.float32).T * size**-0.5
-        query = query.astype(jnp.bfloat16)
-        own_keys = own_ref[hidden + head * size : hidden + (head + 1) * size, :]
-        old_keys = before_ref[head * size : (head + 1) * size, :]
-        own_values = own_ref[2 * hidden + head * size : 2 * hidden + (head + 1) * size, :]
-        own_values = own_values.astype(jnp.float32).T.astype(jnp.bfloat16)
-        old_values = before_ref[hidden + head * size : hidden + (head + 1) * size, :]
-        old_values = old_values.astype(jnp.float32).T.astype(jnp.bfloat16)
-        for block in range(blocks):
-            rows = query[block * BLOCK : (block + 1) * BLOCK]
+        span = slice(head * size, (head + 1) * size)
+        queries[head] = flipped(own_ref[span, :]) * jnp.bfloat16(size**-0.5)
+        own_values[head] = flipped(
+            own_ref[2 * hidden + head * size : 2 * hidden + (head + 1) * size, :]
+        )
+
+    @pl.when(later)
+    def _():
+        pairs.wait_recv()
+        for head in range(heads):
+            old_values[head] = flipped(
+                before_ref[hidden + head * size : hidden + (head + 1) * size, :]
+            )
+
+    def sent(block, step):
+        piece = out_ref.at[rank, :, pl.ds(block * BLOCK, BLOCK)]
+        return pltpu.make_async_remote_copy(
+            src_ref=piece,
+            dst_ref=piece,
+            send_sem=send_sem.at[block, step - 1],
+            recv_sem=recv_sem.at[block, step - 1],
+            device_id={"tensor": lax.rem(rank + step, 4)},
+            device_id_type=MESH_ID,
+        )
+
+    for block in range(blocks):
+        for head in range(heads):
+            span = slice(head * size, (head + 1) * size)
+            rows = queries[head, block * BLOCK : (block + 1) * BLOCK]
+            own_keys = own_ref[hidden + head * size : hidden + (head + 1) * size, :]
             width = (block + 1) * BLOCK
             mine = jnp.dot(rows, own_keys[:, :width], preferred_element_type=jnp.float32)
             top = None
@@ -754,7 +766,7 @@
 
             @pl.when(later)
             def _():
-                old = jnp.dot(rows, old_keys, preferred_element_type=jnp.float32)
+                old = jnp.dot(rows, before_ref[span, :], preferred_element_type=jnp.float32)
                 top_old = None
                 for k in range(blocks):
                     part = old[:, k * BLOCK : (k + 1) * BLOCK] + bias_ref[head, block + blocks - k]
@@ -780,39 +792,60 @@
             full = total[...]
             inverse = 1.0 / full
             low = jnp.concatenate([(part * inverse).astype(jnp.bfloat16) for part in parts], 1)
-            result = jnp.dot(low, own_values[:width], preferred_element_type=jnp.float32)
-            peak[...] = top + jnp.log(full)
-            logsum_ref[head, block * BLOCK : (block + 1) * BLOCK, :] = peak[...]
-            place = (slice(head * size, (head + 1) * size), slice(block * BLOCK, (block + 1) * BLOCK))
+            result = jnp.dot(low, own_values[head, :width], preferred_element_type=jnp.float32)
+            logsum_ref[head, block * BLOCK : (block + 1) * BLOCK, :] = top + jnp.log(full)
+            place = (rank, span, slice(block * BLOCK, (block + 1) * BLOCK))
 
             @pl.when(later)
             def _():
                 low_old = (scores[...] * inverse).astype(jnp.bfloat16)
-                both = result + jnp.dot(low_old, old_values, preferred_element_type=jnp.float32)
+                both = result + jnp.dot(low_old, old_values[head], preferred_element_type=jnp.float32)
                 out_ref[place] = both.T.astype(jnp.bfloat16)
 
             @pl.when(jnp.logical_not(later))
             def _():
                 out_ref[place] = result.T.astype(jnp.bfloat16)
 
-
-def attention(biases, own, before, heads, size):
+        for step in (1, 2, 3):
+            sent(block, step).start()
+
+    for block in range(blocks):
+        for step in (1, 2, 3):
+            sent(block, step).wait()
+
+    @pl.when(jnp.logical_not(later))
+    def _():
+        pairs.wait_send()
+
+
+def attention(biases, own, heads, size, collective_id):
     tokens = own.shape[1]
+    blocks = tokens // BLOCK
+    flat = pltpu.VMEM((heads, tokens, size), jnp.bfloat16)
     return pl.pallas_call(
         functools.partial(attention_kernel, heads, size),
         out_shape=[
-            jax.ShapeDtypeStruct((heads * size, tokens), jnp.bfloat16),
+            jax.ShapeDtypeStruct((4, heads * size, tokens), jnp.bfloat16),
             jax.ShapeDtypeStruct((heads, tokens, 1), jnp.float32),
+            jax.ShapeDtypeStruct((2 * heads * size, tokens), jnp.bfloat16),
         ],
-        in_specs=[pl.BlockSpec(memory_space=pltpu.SMEM), whole_vmem, whole_vmem],
-        out_specs=[whole_vmem, whole_vmem],
+        in_specs=[pl.BlockSpec(memory_space=pltpu.SMEM), whole_vmem],
+        out_specs=[whole_vmem] * 3,
         scratch_shapes=[
+            flat,
+            flat,
+            flat,
             pltpu.VMEM((BLOCK, tokens), jnp.float32),
             pltpu.VMEM((BLOCK, 1), jnp.float32),
             pltpu.VMEM((BLOCK, 1), jnp.float32),
+            pltpu.SemaphoreType.DMA((2,)),
+            pltpu.SemaphoreType.DMA((blocks, 3)),
+            pltpu.SemaphoreType.DMA((blocks, 3)),
         ],
-        compiler_params=pltpu.CompilerParams(vmem_limit_bytes=40 << 20),
-    )(biases, own, before)
+        compiler_params=pltpu.CompilerParams(
+            collective_id=collective_id, has_side_effects=True, vmem_limit_bytes=40 << 20
+        ),
+    )(biases, own)
 
 
 def attention_back_kernel(
@@ -1000,7 +1033,7 @@
 def head_line_kernel(
     tile, part_ref, stream_ref, gain_ref, table_ref, wanted_ref, weight_ref,
     low_ref, grad_low_ref, grad_ref, gain_grad, logsum_ref, picked_ref, slopes_ref,
-    table, stage, from_end, from_mid, own, turned, stats, landed, slope_tiles, total,
+    logits, table, stage, from_end, from_mid, own, turned, stats, landed, slope_tiles, total,
     load_sem, send_sem, end_sem, mid_sem, back_sem, back_recv, stat_send, stat_recv, store_sem,
 ):
     rank = lax.axis_index("tensor")
@@ -1012,7 +1045,6 @@
     pieces = table.shape[0] // tile
     group = columns // rows
     tiles = count // group
-    units = tiles * pieces
     vocab = table.shape[0]
     load = pltpu.make_async_copy(table_ref.at[pl.ds(0, vocab)], table, load_sem)
     load.start()
@@ -1059,22 +1091,31 @@
         turned[...] = low_ref[over(t)].astype(jnp.float32).T.astype(jnp.bfloat16)
 
     def table_rows(k):
-        return table[pl.ds(pl.multiple_of(k * tile, tile), tile)]
-
-    def sums_unit(n):
-        t, k = n // pieces, lax.rem(n, pieces)
-
-        @pl.when(k == 0)
-        def _():
-            turn(t)
-
-        logits = jnp.dot(table_rows(k), turned[...], preferred_element_type=jnp.float32)
+        return table[k * tile : (k + 1) * tile]
+
+    def first_logits(t):
+        turn(t)
+        logits[0] = jnp.dot(table_rows(0), turned[...], preferred_element_type=jnp.float32)
+
+    def next_logits(k):
+        if k + 1 < pieces:
+            logits[(k + 1) % 2] = jnp.dot(
+                table_rows(k + 1), turned[...], preferred_element_type=jnp.float32
+            )
+
+    def sums_unit(t, k):
+        next_logits(k)
         before = stats[0:1, over(t)]
-        top = jnp.maximum(before, jnp.max(logits, 0, keepdims=True))
+        top = jnp.maximum(before, jnp.max(logits[k % 2], 0, keepdims=True))
         stats[1:2, over(t)] = stats[1:2, over(t)] * jnp.exp(before - top) + jnp.sum(
-            jnp.exp(logits - top), 0, keepdims=True
+            jnp.exp(logits[k % 2] - top), 0, keepdims=True
         )
         stats[0:1, over(t)] = top
+
+    def sums_tile(t):
+        first_logits(t)
+        for k in range(pieces):
+            sums_unit(t, k)
 
     stats[0:1, :] = jnp.full_like(stats[0:1, :], masked_score)
     stats[1:2, :] = jnp.zeros_like(stats[1:2, :])
@@ -1090,7 +1131,7 @@
 
         def forward(t):
             repeat(0, group, lambda c: to_end(low_ref, t * group + c).wait_recv())
-            repeat(0, pieces, lambda k: sums_unit(t * pieces + k))
+            sums_tile(t)
 
         repeat(0, tiles, forward)
         repeat(0, count, lambda i: to_inner(i).wait_send())
@@ -1099,35 +1140,47 @@
     def _():
         gain_grad[...] = jnp.zeros_like(gain_grad)
         load.wait()
-        ahead = group + line_lag
-
-        def step(i):
-            @pl.when(i < count)
-            def _():
-                to_inner(i).wait_recv()
-                mine = part_ref[span(i)] + from_end[i].astype(jnp.float32)
-                stage[i] = mine.astype(jnp.bfloat16)
-                to_middle(i).start()
-
-            @pl.when(i >= line_lag)
-            def _():
-                j = i - line_lag
-                to_middle(j).wait_recv()
-                stream_two = stream_ref[span(j)] + (
-                    stage[j].astype(jnp.float32) + from_mid[j].astype(jnp.float32)
-                )
-                grad_ref[span(j)] = stream_two
-                low_ref[span(j)] = (stream_two * inverse_rms(stream_two) * gain_ref[...]).astype(
-                    jnp.bfloat16
-                )
-                to_end(low_ref, j).start()
-
-            @pl.when(i >= ahead)
-            def _():
-                sums_unit(i - ahead)
-
-        repeat(0, count + line_lag, step)
-        repeat(count + line_lag - ahead, units, sums_unit)
+
+        def gather(i):
+            to_inner(i).wait_recv()
+            mine = part_ref[span(i)] + from_end[i].astype(jnp.float32)
+            stage[i] = mine.astype(jnp.bfloat16)
+            to_middle(i).start()
+
+        def settle_rows(j):
+            to_middle(j).wait_recv()
+            stream_two = stream_ref[span(j)] + (
+                stage[j].astype(jnp.float32) + from_mid[j].astype(jnp.float32)
+            )
+            grad_ref[span(j)] = stream_two
+            low_ref[span(j)] = (stream_two * inverse_rms(stream_two) * gain_ref[...]).astype(
+                jnp.bfloat16
+            )
+            to_end(low_ref, j).start()
+
+        turns = [[k for k in range(pieces) if k * (group - 1) // pieces == c - 1] for c in range(group)]
+
+        def advance(t):
+            for c in range(group):
+                i = t * group + c
+                gather(i)
+
+                @pl.when(i >= line_lag)
+                def _():
+                    settle_rows(i - line_lag)
+
+                if turns[c]:
+
+                    @pl.when(t >= 1)
+                    def _():
+                        if c == 1:
+                            first_logits(t - 1)
+                        for k in turns[c]:
+                            sums_unit(t - 1, k)
+
+        repeat(0, tiles, advance)
+        repeat(count - line_lag, count, settle_rows)
+        sums_tile(tiles - 1)
 
         def drain(i):
             to_middle(i).wait_send()
@@ -1164,57 +1217,83 @@
             slope_tiles.at[lax.rem(t, 2)], slopes_ref.at[:, over(t)], store_sem.at[lax.rem(t, 2)]
         )
 
-    def back_unit(n):
-        t, k = n // pieces, lax.rem(n, pieces)
-
-        @pl.when(k == 0)
-        def _():
-            turn(t)
-            total[...] = jnp.zeros_like(total)
-
-            @pl.when(t >= 2)
-            def _():
-                store(t - 2).wait()
-
-        lines = table_rows(k)
-        logits = jnp.dot(lines, turned[...], preferred_element_type=jnp.float32)
-        row = lax.broadcasted_iota(jnp.int32, logits.shape, 0)
+    def slope_unit(t, k):
+        values = logits[k % 2]
+        row = lax.broadcasted_iota(jnp.int32, values.shape, 0)
         base = k * tile
         hits = jnp.where(row == wanted_ref[0:1, over(t)] - base, weight_ref[0:1, over(t)], 0.0)
         hits = hits + jnp.where(
             row == wanted_ref[1:2, over(t)] - base, weight_ref[1:2, over(t)], 0.0
         )
-        picked_ref[:, over(t)] += jnp.sum(hits * logits, 0, keepdims=True)
-        softmax = jnp.exp(logits - logsum_ref[:, over(t)])
-        slope = (
+        picked_ref[:, over(t)] += jnp.sum(hits * values, 0, keepdims=True)
+        softmax = jnp.exp(values - logsum_ref[:, over(t)])
+        slope_tiles[lax.rem(t, 2), base : base + tile] = (
             (weight_ref[2:3, over(t)] * softmax - hits) * weight_ref[3:4, over(t)]
         ).astype(jnp.bfloat16)
-        slope_tiles[lax.rem(t, 2), pl.ds(pl.multiple_of(base, tile), tile)] = slope
+
+    def add_rows(t, k):
         total[...] += lax.dot_general(
-            slope, lines, (((0,), (0,)), ((), ())), preferred_element_type=jnp.float32
-        )
-
-        @pl.when(k == pieces - 1)
-        def _():
-            store(t).start()
+            slope_tiles[lax.rem(t, 2), k * tile : (k + 1) * tile],
+            table_rows(k),
+            (((0,), (0,)), ((), ())),
+            preferred_element_type=jnp.float32,
+        )
+
+    def settle(j):
+        to_middle(j).wait_recv()
+        upstream = stage[j].astype(jnp.float32) + from_mid[j].astype(jnp.float32)
+        grad_two, gain_part = norm_back_rows(grad_ref[span(j)], gain_ref[...], upstream)
+        grad_ref[span(j)] = grad_two
+        gain_grad[...] += gain_part
+        grad_low_ref[span(j)] = grad_two.astype(jnp.bfloat16)
+        to_end(grad_low_ref, j).start()
+
+    def exchange(i):
+        to_inner(i).wait_recv()
+        stage[i] = (own[span(i)] + from_end[i].astype(jnp.float32)).astype(jnp.bfloat16)
+        to_middle(i).start()
+
+        @pl.when(i >= line_lag)
+        def _():
+            settle(i - line_lag)
+
+    def back_tile(t):
+        @pl.when(t >= 2)
+        def _():
+            store(t - 2).wait()
+
+        total[...] = jnp.zeros_like(total)
+        first_logits(t)
+        for k in range(pieces):
+            next_logits(k)
+            slope_unit(t, k)
+            if k >= 1:
+                add_rows(t, k - 1)
+            if k >= pieces - group:
+
+                @pl.when(inner & (t >= 1))
+                def _():
+                    exchange((t - 1) * group + k - (pieces - group))
+
+        add_rows(t, pieces - 1)
+        store(t).start()
+
+        @pl.when(inner)
+        def _():
+            own[over(t)] = total[...]
+
+        @pl.when(jnp.logical_not(inner))
+        def _():
+            def push(c):
+                stage[t * group + c] = total[span(c)].astype(jnp.bfloat16)
+                to_inner(t * group + c).start()
+
+            repeat(0, group, push)
+
+    repeat(0, tiles, back_tile)
 
     @pl.when(jnp.logical_not(inner))
     def _():
-        def unit(n):
-            back_unit(n)
-
-            @pl.when(lax.rem(n, pieces) == pieces - 1)
-            def _():
-                first = (n // pieces) * group
-
-                def push(c):
-                    stage[first + c] = total[span(c)].astype(jnp.bfloat16)
-                    to_inner(first + c).start()
-
-                repeat(0, group, push)
-
-        repeat(0, units, unit)
-
         def finish(i):
             to_end(grad_low_ref, i).wait_recv()
             to_inner(i).wait_send()
@@ -1223,37 +1302,6 @@
 
     @pl.when(inner)
     def _():
-        def settle(j):
-            to_middle(j).wait_recv()
-            upstream = stage[j].astype(jnp.float32) + from_mid[j].astype(jnp.float32)
-            grad_two, gain_part = norm_back_rows(grad_ref[span(j)], gain_ref[...], upstream)
-            grad_ref[span(j)] = grad_two
-            gain_grad[...] += gain_part
-            grad_low_ref[span(j)] = grad_two.astype(jnp.bfloat16)
-            to_end(grad_low_ref, j).start()
-
-        def exchange(i):
-            to_inner(i).wait_recv()
-            stage[i] = (own[span(i)] + from_end[i].astype(jnp.float32)).astype(jnp.bfloat16)
-            to_middle(i).start()
-
-            @pl.when(i >= line_lag)
-            def _():
-                settle(i - line_lag)
-
-        def unit(n):
-            back_unit(n)
-            t, k = n // pieces, lax.rem(n, pieces)
-
-            @pl.when(k == pieces - 1)
-            def _():
-                own[over(t)] = total[...]
-
-            @pl.when((t >= 1) & (k >= pieces - group))
-            def _():
-                exchange((t - 1) * group + k - (pieces - group))
-
-        repeat(0, units, unit)
         repeat(count - group, count, exchange)
         repeat(count - line_lag, count, settle)
 
@@ -1289,6 +1337,7 @@
         in_specs=[whole_vmem] * 3 + [whole_any] + [whole_vmem] * 2,
         out_specs=[whole_vmem] * 6 + [whole_any],
         scratch_shapes=[
+            pltpu.VMEM((2, vocab_tile(vocab), columns), jnp.float32),
             pltpu.VMEM((vocab, width), jnp.bfloat16),
             chunks,
             chunks,
@@ -2150,7 +2199,15 @@
     slot_rows = unit_starts + clipped_ids % unit_rows
     if on_square:
         slot_rows = jnp.where(inside, slot_rows, -1)[:, None]
-        weights_low, embedded = embed(unit_slots, master[0, 0], slot_rows, 11)
+        weights_low, embedded, normed_one_low, joint = embed(
+            unit_slots,
+            master[0, 0],
+            slot_rows,
+            norm_gains[0:1],
+            table_units,
+            3 * hidden_here,
+            11,
+        )
     else:
         master_low = master[0, 0].astype(jnp.bfloat16)
         gathered = lax.all_gather(master_low, ("dp", "ctx"), axis=0, tiled=True)
@@ -2168,15 +2225,14 @@
     gain_rows = [norm_gains[k : k + 1] for k in range(3)]
     stream_shape = jax.ShapeDtypeStruct((tokens_here, model_width), jnp.float32)
     gain_shape = jax.ShapeDtypeStruct((1, model_width), jnp.float32)
-    stream_zero = embedded.astype(jnp.float32) * embed_scale
-    first_normalized = norm_forward(stream_zero, norm_gains[0])
-    normed_one_low = first_normalized.astype(jnp.bfloat16)
-    joint = lax.dot_general(
-        joint_low, normed_one_low, (((1,), (1,)), ((), ())), preferred_element_type=jnp.float32
-    ).astype(jnp.bfloat16)
-    pairs_before = passed_along(joint[hidden_here:], "ctx", 1)
-    attended, logsum_rows = attention(rel_bias, joint, pairs_before, heads_here, head_size)
-    (attended_all,) = gather_line([attended], 2)
+    if not on_square:
+        stream_zero = embedded.astype(jnp.float32) * embed_scale
+        normed_one_low = norm_forward(stream_zero, norm_gains[0]).astype(jnp.bfloat16)
+        joint = lax.dot_general(
+            joint_low, normed_one_low, (((1,), (1,)), ((), ())), preferred_element_type=jnp.float32
+        ).astype(jnp.bfloat16)
+    attended_all, logsum_rows, pairs_before = attention(rel_bias, joint, heads_here, head_size, 2)
+    attended = lax.dynamic_index_in_dim(attended_all, my_rank, 0, keepdims=False)
     router_low = router.astype(jnp.bfloat16)
     stream_one, normed_two_low, gate_rows, gate_columns = middle(
         attended_all.reshape(model_width, tokens_here),

time: 809 us -> 795 us (0.983)
    pallas_call x1, Pallas kernels: 12.8 us -> 51.1 us  [attention(): pl.pallas_call(functools.partial(attention_kernel, heads, size), out_shap...]
    pallas_call x2 -> x1, Pallas kernels: 149 us -> 121 us  [embed(): pl.pallas_call(functools.partial(embed_kernel, chunks, first_unit), out_s...]
    pallas_call x1, Pallas kernels: 148 us -> 134 us  [head_line(): pl.pallas_call(functools.partial(head_line_kernel, vocab_tile(vocab)), ou...]
  transfers between devices with their start and end apart: 5 -> 4, of which waited for: 1 -> 1; matrix products, arithmetic and copies ran while one was open for 2% -> 2% of each run, Pallas kernels for 5% -> 6%
where the time goes in v9:
time: 795 us; the launch traced here: 790 us
  Pallas kernels  715 us (90%)
  other arithmetic  32.1 us (4%)
  local copies, waits for them, and re-layouts  29.5 us (4%)
    pallas_call x1, Pallas kernels, head_line(): pl.pallas_call(functools.partial(head_line_kernel, vocab_tile(vocab)), ou...  134 us
    pallas_call x1, Pallas kernels, embed(): pl.pallas_call(functools.partial(embed_kernel, chunks, first_unit), out_s...  121 us
    pallas_call x1, Pallas kernels, own_units(): pl.pallas_call(functools.partial(own_units_kernel, chunks), out_shape=[ja...  100 us
    pallas_call x2, Pallas kernels, sum_line(): pl.pallas_call(functools.partial(sum_line_kernel, rows, count, opening, p...  95.5 us
    pallas_call x1, Pallas kernels, experts_backward(): pl.pallas_call(experts_back_kernel, out_shape=[jax.ShapeDtypeStruct((toke...  93.9 us
    pallas_call x1, Pallas kernels, experts_forward(): pl.pallas_call(experts_kernel, out_shape=[jax.ShapeDtypeStruct((tokens, w...  93.5 us
    pallas_call x1, Pallas kernels, attention(): pl.pallas_call(functools.partial(attention_kernel, heads, size), out_shap...  51.1 us
    pallas_call x1, Pallas kernels, attention_back(): pl.pallas_call(functools.partial(attention_back_kernel, heads, size), out...  22 us
  transfers between devices with their start and end apart: 4, of which 1 were waited for; matrix products, arithmetic and copies ran while one was open for 2% of the time, Pallas kernels for 6%

profile of v9, /device:TPU:0, one launch (start us, length us, event | category | flops | bytes accessed | tf_op | source)
XLA Modules:
  0.0 790.1 jit_solution(5943908564410557508)
XLA Ops:
  2.9 3.4 convert_reduce_fusion
  8.7 1.4 fusion.18
  12.2 121.0 %shard_map.384 = (bf16[137,64,768]{2,1,0:T(8,128)(2,1)}, bf16[1024,768]{1,0:T(8,128)(2,1)}, bf16[1024,768]{1,0:T(8,128)(2,1)}, bf16[576,1024]{1,0:T(8,128)(2,1)}) custom-call(s32[137]{0:T(256)} %copy-done.36, f32[21,64,768]{2,1,0:T(8,128)} %bitcast.105, s32[1024,1]{1,0:T(8,128)} %fusion.3.rows_ref, f32[1,768]{1,0:T(1,128)} %get-tuple-element.163.gain_ref.refs_1_), custom_call_target="tpu_custom_call" | custom-call | tf_op jit(solution)/shard_map/pallas_call | solution.py:636
  134.3 2.1 collective-permute-start.2
  141.0 51.1 %shard_map.385 = (bf16[4,192,1024]{2,1,0:T(8,128)(2,1)S(1)}, f32[3,1024,1]{2,1,0:T(8,128)S(1)}, bf16[384,1024]{1,0:T(8,128)(2,1)S(1)}) custom-call(f32[3,8]{1,0:T(4,128)S(1)} %copy-done.23, bf16[576,1024]{1,0:T(8,128)(2,1)S(1)} %copy-done.4), custom_call_target="tpu_custom_call" | custom-call | tf_op jit(solution)/shard_map/pallas_call | solution.py:825
  196.5 4.5 shard_map.386
  201.1 1.7 copy-done
  205.9 93.5 %shard_map.387 = (f32[1024,768]{1,0:T(8,128)}, bf16[8,288,768]{2,1,0:T(8,128)(2,1)}, bf16[8,288,768]{2,1,0:T(8,128)(2,1)}, f32[8,128]{1,0:T(8,128)}) custom-call(bf16[1024,768]{1,0:T(8,128)(2,1)} %copy-done.3, s32[2,1024]{1,0:T(2,128)} %copy-done.26, s32[1024,2]{1,0:T(8,128)} %copy.77.dest_columns, f32[1024,8]{1,0:T(8,128)} %copy-done.15, ...), custom_call_target="tpu_custom_call" | custom-call | tf_op jit(solution)/shard_map/pallas_call | solution.py:1667
  302.8 133.6 %shard_map.388 = (bf16[1024,768]{1,0:T(8,128)(2,1)}, bf16[1024,768]{1,0:T(8,128)(2,1)}, f32[1024,768]{1,0:T(8,128)}, f32[1,768]{1,0:T(1,128)}, f32[1,1024]{1,0:T...) custom-call(f32[1024,768]{1,0:T(8,128)} %get-tuple-element.86.part_ref, f32[1024,768]{1,0:T(8,128)} %copy-done, ...), custom_call_target="tpu_custom_call" | custom-call | tf_op jit(solution)/shard_map/pallas_call | solution.py:1326
  436.5 93.9 %shard_map.389 = (f32[1024,768]{1,0:T(8,128)}, f32[2,1024]{1,0:T(2,128)}, f32[768,768]{1,0:T(8,128)}, f32[768,768]{1,0:T(8,128)}) custom-call(bf16[1024,768]{1,0:T(8,128)(2,1)} %get-tuple-element.93.rows_ref, s32[2,1024]{1,0:T(2,128)} %copy-done.26, s32[1024,2]{1,0:T(8,128)} %copy.77.dest_columns, f32[2,1024]{1,0:T(2,128)} %copy-done.20, ...), custom_call_target="tpu_custom_call" | custom-call | tf_op jit(solution)/shard_map/pallas_call | solution.py:1812
  531.2 51.5 %shard_map.390 = (bf16[1024,768]{1,0:T(8,128)(2,1)S(1)}, f32[1024,768]{1,0:T(8,128)S(1)}, bf16[8,1024]{1,0:T(8,128)(2,1)S(1)}, f32[1,1024]{1,0:T(1,128)S(1)}, f32[1,768]{1,0:T(1,128)S(1)}) custom-call(f32[1024,768]{1,0:T(8,128)} %get-tuple-element.97.part_ref, f32[1024,768]{1,0:T(8,128)} %copy-done, f32[1,768]{1,0:T(1,128)S(1)} %get-tuple-element.162.gain_ref.refs_1_, ...), custom_call_target="tpu_custom_call" | custom-call | tf_op jit(solution)/shard_map/pallas_call | solution.py:184
  583.9 1.7 copy-done.6
  585.6 22.0 %shard_map.391 = (bf16[192,1024]{1,0:T(8,128)(2,1)S(1)}, f32[384,1024]{1,0:T(8,128)S(1)}, bf16[384,1024]{1,0:T(8,128)(2,1)}, f32[24,256]{1,0:T(8,128)S(1)}, f32[...) custom-call(f32[3,8]{1,0:T(4,128)S(1)} %copy-done.23, ...), custom_call_target="tpu_custom_call" | custom-call | tf_op jit(solution)/shard_map/pallas_call | solution.py:1003
  608.7 1.3 collective-permute-start.3
  610.4 2.2 slice.74
  614.1 1.8 dynamic-slice_bitcast_fusion.attended_ref
  618.6 1.7 fusion.20
  620.7 1.9 add_convert_fusion
  623.6 3.1 fusion.13.part_ref
  626.8 44.0 %shard_map.392 = (bf16[1024,768]{1,0:T(8,128)(2,1)S(1)}, f32[8,768]{1,0:T(8,128)S(1)}) custom-call(f32[1024,768]{1,0:T(8,128)} %fusion.13.part_ref, bf16[1024,768]{1,0:T(8,128)(2,1)S(1)} %copy-done.2, f32[1,768]{1,0:T(1,128)S(1)} %copy-done.22, f32[1024,768]{1,0:T(8,128)} %copy-done.6, f32[1,768]{1,0:T(1,128)S(1)} %get-tuple-element.108.refs_3_, ...), custom_call_target="tpu_custom_call" | custom-call | tf_op jit(solution)/shard_map/pallas_call | solution.py:184
  672.6 100.2 %shard_map.393 = (f32[21,64,768]{2,1,0:T(8,128)}, f32[16,768]{1,0:T(8,128)}) custom-call(s32[168]{0:T(256)} %reshape.277.units_of, bf16[125,64,1024]{2,1,0:T(8,128)(2,1)} %bitcast.106, bf16[1024,768]{1,0:T(8,128)(2,1)} %get-tuple-element.90.rows_ref, s32[1,1024]{1,0:T(1,128)} %copy-done.28, bf16[1024,768]{1,0:T(8,128)(2,1)} %copy-done.11, ...), custom_call_target="tpu_custom_call" | custom-call | tf_op jit(solution)/shard_map/pallas_call | solution.py:2032
  776.1 1.4 multiply_subtract_fusion.1
  777.5 1.4 multiply_subtract_fusion
  779.5 10.4 %fusion.12 = (f32[1,1,21,64,768]{4,3,2,1,0:T(8,128)}, f32[1,1,21,64,768]{4,3,2,1,0:T(8,128)}, f32[1,1,21,64,768]{4,3,2,1,0:T(8,128)}) fusion(f32[21,64,768]{2,1,0:T(8,128)} %get-tuple-element.118, pred[21]{0:T(512)(128)(4,1)S(1)} %select_reduce_fusion.2, f32[1,1,21,64,768]{4,3,2,1,0:T(8,128)} %param.35, f32[1,1,21,64,768]{4,3,2,1,0:T(8,128)} %param.34, ...), kind=kLoop, calls=%fused_computation.72 | loop fusion | flops 16515072 | bytes 28901480 | tf_op jit(solution)/shard_map/broadcast_in_dim | solution.py:2390
  (146 shorter events, 35.4 us)
Async XLA Ops:
  1.4 131.8 %copy-start.28 = (s32[1,1024]{1,0:T(1,128)}, s32[1,1024]{1,0:T(1,128)S(1)}, u32[]{:S(2)}) copy-start(s32[1,1024]{1,0:T(1,128)S(1)} %get-tuple-element.157.ids_ref) | copy-start | bytes 12292
  8.7 128.7 %copy-start.26 = (s32[2,1024]{1,0:T(2,128)}, s32[2,1024]{1,0:T(2,128)S(1)}, u32[]{:S(2)}) copy-start(s32[2,1024]{1,0:T(2,128)S(1)} %add_select_fusion.1.dest_rows) | copy-start | bytes 24580
  11.1 125.9 %copy-start.33 = (s32[137,1]{0,1:T(1,128)S(1)}, s32[137,1]{0,1:T(1,128)}, u32[]{:S(2)}) copy-start(s32[137,1]{0,1:T(1,128)} %param.32) | copy-start | bytes 1648
  11.1 125.9 %copy-start.30 = (s32[1,1024,2]{1,2,0:T(2,128)S(1)}, s32[1,1024,2]{1,2,0:T(2,128)}, u32[]{:S(2)}) copy-start(s32[1,1024,2]{1,2,0:T(2,128)} %param.29) | copy-start | bytes 24580
  11.1 125.9 %copy-start.42 = (f32[2]{0:T(128)S(1)}, f32[2]{0:T(128)}, u32[]{:S(2)}) copy-start(f32[2]{0:T(128)} %constant.253) | copy-start | bytes 28
  11.1 126.0 %copy-start.27 = (f32[768,8]{0,1:T(8,128)S(1)}, f32[768,8]{0,1:T(8,128)}, u32[]{:S(2)}) copy-start(f32[768,8]{0,1:T(8,128)} %param.45) | copy-start | bytes 73732
  12.2 126.3 %copy-start.18 = (s32[1,1024,2]{1,2,0:T(2,128)S(1)}, s32[1,1024,2]{1,2,0:T(2,128)}, u32[]{:S(2)}) copy-start(s32[1,1024,2]{1,2,0:T(2,128)} %param.30) | copy-start | bytes 24580
  12.2 127.5 %copy-start.23 = (f32[3,8]{1,0:T(4,128)S(1)}, f32[3,8]{1,0:T(4,128)}, u32[]{:S(2)}) copy-start(f32[3,8]{1,0:T(4,128)} %bias_ref.3) | copy-start | bytes 292
  12.2 182.0 %copy-start.37 = (s32[1,1024,2]{1,2,0:T(2,128)S(1)}, s32[1,1024,2]{1,2,0:T(2,128)}, u32[]{:S(2)}) copy-start(s32[1,1024,2]{1,2,0:T(2,128)} %param.28) | copy-start | bytes 24580
  134.3 60.5 %collective-permute-start.2 = (bf16[192,768]{1,0:T(8,128)(2,1)S(1)}, bf16[192,768]{1,0:T(8,128)(2,1)S(1)}, u32[]{:S(2)}, u32[]{:S(2)}) collective-permute-start(bf16[192,768]{1,0:T(8,128)(2,1)S(1)} %bitcast.87), channel_id=1, source_target_pairs={{0,3},{1,0},{2,1},{3,2},{4,7},{5,4},{6,5},{7,6},{8,11},{9,8},{10,9... | collective-permute-start | bytes 884744 | tf_op jit(solution)/shard_map/ppermute | solution.py:2222
  136.4 58.5 %collective-permute-start.1 = (bf16[192,768]{1,0:T(8,128)(2,1)S(1)}, bf16[192,768]{1,0:T(8,128)(2,1)S(1)}, u32[]{:S(2)}, u32[]{:S(2)}) collective-permute-start(bf16[192,768]{1,0:T(8,128)(2,1)S(1)} %bitcast.88), channel_id=1, source_target_pairs={{0,2},{1,3},{2,0},{3,1},{4,6},{5,7},{6,4},{7,5},{8,10},{9,11},{10,... | collective-permute-start | bytes 884744 | tf_op jit(solution)/shard_map/ppermute | solution.py:2222
  136.4 58.5 %collective-permute-start = (bf16[192,768]{1,0:T(8,128)(2,1)S(1)}, bf16[192,768]{1,0:T(8,128)(2,1)S(1)}, u32[]{:S(2)}, u32[]{:S(2)}) collective-permute-start(bf16[192,768]{1,0:T(8,128)(2,1)S(1)} %bitcast.89), channel_id=1, source_target_pairs={{0,1},{1,2},{2,3},{3,0},{4,5},{5,6},{6,7},{7,4},{8,9},{9,10},{10,1... | collective-permute-start | bytes 884744 | tf_op jit(solution)/shard_map/ppermute | solution.py:2222
  436.4 94.0 %copy-start.39 = (f32[1,1024]{1,0:T(1,128)S(1)}, f32[1,1024]{1,0:T(1,128)}, u32[]{:S(2)}) copy-start(f32[1,1024]{1,0:T(1,128)} %get-tuple-element.100) | copy-start | bytes 12292
  436.4 94.7 %copy-start.9 = (bf16[768,8]{1,0:T(8,128)(2,1)S(1)}, bf16[768,8]{1,0:T(8,128)(2,1)}, u32[]{:S(2)}) copy-start(bf16[768,8]{1,0:T(8,128)(2,1)} %copy-done.8) | copy-start | bytes 36868
  436.4 94.7 %copy-start.19 = (s32[1,1024,2]{1,2,0:T(2,128)S(1)}, s32[1,1024,2]{1,2,0:T(2,128)}, u32[]{:S(2)}) copy-start(s32[1,1024,2]{1,2,0:T(2,128)} %param.30) | copy-start | bytes 24580
  436.4 94.7 %copy-start.21 = (f32[2,1024]{1,0:T(2,128)S(1)}, f32[2,1024]{1,0:T(2,128)}, u32[]{:S(2)}) copy-start(f32[2,1024]{1,0:T(2,128)} %copy-done.20) | copy-start | bytes 24580
  608.7 12.0 %collective-permute-start.3 = (bf16[384,1024]{1,0:T(8,128)(2,1)}, bf16[384,1024]{1,0:T(8,128)(2,1)}, u32[]{:S(2)}, u32[]{:S(2)}) collective-permute-start(bf16[384,1024]{1,0:T(8,128)(2,1)} %get-tuple-element.106), channel_id=1, source_target_pairs={{4,0},{5,1},{6,2},{7,3},{12,8},{13,9},{14,10},{15,11},{20,16},{21,... | collective-permute-start | bytes 2359304 | tf_op jit(solution)/shard_map/ppermute | solution.py:38
  672.5 103.6 %copy-start.29 = (f32[3,768]{1,0:T(4,128)S(1)}, f32[3,768]{1,0:T(4,128)}, u32[]{:S(2)}) copy-start(f32[3,768]{1,0:T(4,128)} %param.42) | copy-start | bytes 27652
  672.5 103.6 %copy-start.34 = (f32[3,768]{1,0:T(4,128)S(1)}, f32[3,768]{1,0:T(4,128)}, u32[]{:S(2)}) copy-start(f32[3,768]{1,0:T(4,128)} %param.43) | copy-start | bytes 27652
  672.5 103.6 %copy-start.35 = (f32[3,768]{1,0:T(4,128)S(1)}, f32[3,768]{1,0:T(4,128)}, u32[]{:S(2)}) copy-start(f32[3,768]{1,0:T(4,128)} %param.44) | copy-start | bytes 27652
  672.5 104.9 %copy-start.31 = (f32[768,8]{0,1:T(8,128)S(1)}, f32[768,8]{0,1:T(8,128)}, u32[]{:S(2)}) copy-start(f32[768,8]{0,1:T(8,128)} %param.46) | copy-start | bytes 73732
  672.5 104.9 %copy-start.32 = (f32[768,8]{0,1:T(8,128)S(1)}, f32[768,8]{0,1:T(8,128)}, u32[]{:S(2)}) copy-start(f32[768,8]{0,1:T(8,128)} %param.47) | copy-start | bytes 73732
  672.6 106.4 %copy-start.40 = (f32[3,8]{1,0:T(4,128)S(1)}, f32[3,8]{1,0:T(4,128)}, u32[]{:S(2)}) copy-start(f32[3,8]{1,0:T(4,128)} %param.49) | copy-start | bytes 292
  672.6 106.3 %copy-start.41 = (f32[3,8]{1,0:T(4,128)S(1)}, f32[3,8]{1,0:T(4,128)}, u32[]{:S(2)}) copy-start(f32[3,8]{1,0:T(4,128)} %param.50) | copy-start | bytes 292
  (23 other events, 305.0 us)

commit v10 on v9

--- a/solution.py
+++ b/solution.py
@@ -32,11 +32,6 @@
 decay_rate = 0.1
 
 
-def passed_along(value, axis, steps):
-    count = lax.axis_size(axis)
-    initial, last = (max(0, -steps), min(count, count - steps))
-    return lax.ppermute(value, axis, [(source, source + steps) for source in range(initial, last)])
-
 MESH_ID = pl.DeviceIdType.MESH
 whole_vmem = pl.BlockSpec(memory_space=pltpu.VMEM)
 whole_any = pl.BlockSpec(memory_space=pl.ANY)
@@ -44,32 +39,37 @@
 
 
 def sum_line_kernel(
-    rows, count, opening, prologue, epilogue, ending, n_extra, n_aux, n_scratch, part_ref, *refs
+    rows, count, opening, with_core, prologue, epilogue, ending, n_extra, n_aux, n_scratch, *refs
 ):
     extras = refs[:n_extra]
     out_ref = refs[n_extra]
     aux = refs[n_extra + 1 : n_extra + 1 + n_aux]
     rest = refs[n_extra + 1 + n_aux :]
     scratch = rest[:n_scratch]
+    part_ref = scratch[-1] if with_core else extras[0]
+    extras = extras if with_core else extras[1:]
     stage, from_end, from_mid, send_sem, end_sem, mid_sem, back_sem, back_recv = rest[n_scratch:]
     rank = lax.axis_index("tensor")
     inner = (rank == 1) | (rank == 2)
     end_peer = jnp.where(rank < 2, 1 - rank, 5 - rank)
     mid_peer = 3 - rank
     barrier = pltpu.get_barrier_semaphore()
-    if opening is None:
+    if opening is None or with_core:
         pl.semaphore_signal(barrier, inc=1, device_id={"tensor": end_peer}, device_id_type=MESH_ID)
+        if with_core:
+            other_core = {"ctx": 1 - lax.axis_index("ctx")}
+            pl.semaphore_signal(barrier, inc=1, device_id=other_core, device_id_type=MESH_ID)
 
         @pl.when(inner)
         def _():
             pl.semaphore_signal(
                 barrier, inc=1, device_id={"tensor": mid_peer}, device_id_type=MESH_ID
             )
-            pl.semaphore_wait(barrier, 2)
+            pl.semaphore_wait(barrier, 2 + with_core)
 
         @pl.when(jnp.logical_not(inner))
         def _():
-            pl.semaphore_wait(barrier, 1)
+            pl.semaphore_wait(barrier, 1 + with_core)
     else:
         for step in (1, 2, 3):
             other = lax.rem(rank + step, 4)
@@ -110,7 +110,7 @@
         )
 
     if opening is not None:
-        opening(rank, extras, scratch)
+        opening(rank, extras, aux, scratch)
 
     @pl.when(jnp.logical_not(inner))
     def _():
@@ -178,7 +178,8 @@
     ending=None,
     rows=64,
 ):
-    tokens, width = part.shape
+    tokens, width = scratch[-1].shape if part is None else part.shape
+    inputs = list(extras) if part is None else [part, *extras]
     count = tokens // rows
     chunks = pltpu.VMEM((count, rows, width), jnp.bfloat16)
     return pl.pallas_call(
@@ -187,15 +188,16 @@
             rows,
             count,
             opening,
+            part is None,
             prologue,
             epilogue,
             ending,
-            len(extras),
+            len(inputs),
             len(aux_shapes),
             len(scratch),
         ),
         out_shape=[jax.ShapeDtypeStruct((tokens, width), jnp.bfloat16)] + list(aux_shapes),
-        in_specs=[whole_vmem] * (1 + len(extras)),
+        in_specs=[whole_vmem] * len(inputs),
         out_specs=[whole_vmem] * (1 + len(aux_shapes)),
         scratch_shapes=list(scratch)
         + [chunks, chunks, chunks]
@@ -203,7 +205,7 @@
         compiler_params=pltpu.CompilerParams(
             collective_id=collective_id, has_side_effects=True, vmem_limit_bytes=48 << 20
         ),
-    )(part, *extras)
+    )(*inputs)
 
 
 def keep_total(total, span, rank, extras, aux, scratch):
@@ -230,7 +232,7 @@
 
 
 def share_gains(inner, end_peer, extras, aux, scratch):
-    gains = aux[0]
+    gains = aux[-1]
     copy = pltpu.make_async_remote_copy(
         src_ref=gains,
         dst_ref=gains,
@@ -268,7 +270,7 @@
     ]
 
 
-def send_gate_parts(rank, extras, scratch):
+def send_gate_parts(rank, extras, aux, scratch):
     for copy in gate_copies(rank, extras, scratch):
         copy.start()
 
@@ -319,18 +321,57 @@
     return result.astype(jnp.bfloat16)
 
 
+def form_joint_grad(rank, extras, aux, scratch):
+    query_grad, pair_grad, before_grad, joint_weights = extras[5:]
+    joint_grad = aux[0]
+    landed, pair_sem, part = scratch[2:]
+    hidden = query_grad.shape[0]
+    later = lax.axis_index("ctx") > 0
+    copy = pltpu.make_async_remote_copy(
+        src_ref=before_grad,
+        dst_ref=landed,
+        send_sem=pair_sem.at[0],
+        recv_sem=pair_sem.at[1],
+        device_id={"ctx": 1 - lax.axis_index("ctx")},
+        device_id_type=MESH_ID,
+    )
+    joint_grad[0:hidden, :] = query_grad[...]
+
+    @pl.when(later)
+    def _():
+        copy.start()
+        joint_grad[hidden:, :] = pair_grad[...].astype(jnp.bfloat16)
+
+    @pl.when(jnp.logical_not(later))
+    def _():
+        copy.wait_recv()
+        both = pair_grad[...] + landed[...].astype(jnp.float32)
+        joint_grad[hidden:, :] = both.astype(jnp.bfloat16)
+
+    part[...] = lax.dot_general(
+        joint_grad[...], joint_weights[...], (((0,), (0,)), ((), ())), preferred_element_type=jnp.float32
+    )
+
+    @pl.when(later)
+    def _():
+        copy.wait_send()
+
+
 def finish_input_grad(scale, total, span, rank, extras, aux, scratch):
     embedded, gain, grad_one = extras[:3]
     stream_zero = embedded[span].astype(jnp.float32) * scale
     part, gain_part = norm_back_rows(stream_zero, gain[...], total)
-    aux[0][0:1, :] += gain_part
+    aux[-1][0:1, :] += gain_part
     return ((grad_one[span] + part) * scale).astype(jnp.bfloat16)
 
 
 def middle_kernel(
-    attended_ref, embedded_ref, gain_ref, router_ref, routes_ref, *refs
+    attended_ref, embedded_ref, gain_ref, router_ref, routes_ref, dest_ref, *refs
 ):
-    rolled, (stream_ref, normed_ref, rows_ref, columns_ref, project_ref) = refs[:4], refs[4:]
+    rolled, (stream_ref, normed_ref, rows_ref, columns_ref, places_ref, project_ref) = (
+        refs[:4],
+        refs[4:],
+    )
 
     @pl.when(pl.program_id(0) == 0)
     def _():
@@ -359,10 +400,13 @@
     total = first + second
     gates = jnp.concatenate([first / total, second / total], 0)
     rows_ref[...] = gates
-    columns_ref[...] = jnp.concatenate([gates, jnp.zeros((6, gates.shape[1]), jnp.float32)], 0).T
-
-
-def middle(attended, rolled, embedded, gain, router, routes):
+    places = jnp.concatenate([routes_ref[...], dest_ref[...]], 0).astype(jnp.float32)
+    turned = jnp.concatenate([gates, places, jnp.zeros_like(gates)], 0).T
+    columns_ref[...] = turned
+    places_ref[...] = turned.astype(jnp.int32)
+
+
+def middle(attended, rolled, embedded, gain, router, routes, dest):
     tokens, width = embedded.shape
     tile = 256
     fixed = lambda k: (0, 0)
@@ -377,17 +421,19 @@
             jax.ShapeDtypeStruct((tokens, width), jnp.bfloat16),
             jax.ShapeDtypeStruct((2, tokens), jnp.float32),
             jax.ShapeDtypeStruct((tokens, 8), jnp.float32),
+            jax.ShapeDtypeStruct((tokens, 8), jnp.int32),
         ],
-        in_specs=[along(width), down(width), whole(gain), whole(router), along(2)]
+        in_specs=[along(width), down(width), whole(gain), whole(router), along(2), along(2)]
         + [whole(x) for x in rolled],
-        out_specs=[down(width), down(width), along(2), down(8)],
+        out_specs=[down(width), down(width), along(2), down(8), down(8)],
         scratch_shapes=[pltpu.VMEM((width, width), jnp.bfloat16)],
         compiler_params=pltpu.CompilerParams(vmem_limit_bytes=40 << 20),
-    )(attended, embedded, gain, router, routes, *rolled)
+    )(attended, embedded, gain, router, routes, dest, *rolled)
 
 
 def embed_kernel(
-    chunks, first_unit, slots_ref, mine_ref, rows_ref, gain_ref, units_ref, embedded_ref, normed_ref, joint_ref, *refs
+    chunks, first_unit, slots_ref, mine_ref, rows_ref, gain_ref, units_ref, embedded_ref, normed_ref, joint_ref,
+    joint_weights, project_weights, *refs
 ):
     held, total, stage, from_end, from_mid = refs[:5]
     send_x, recv_x, send_y, recv_y, send_z, recv_z, send_core, recv_core = refs[5:13]
@@ -620,6 +666,10 @@
     normed_ref[...] = normed
     lines = joint_ref.shape[0]
     weights = units_ref[first_unit : first_unit + lines // unit_rows].reshape(lines, 2 * width)
+    joint_weights[...] = weights
+    project_weights[...] = units_ref[first_unit + lines // unit_rows :].reshape(
+        project_weights.shape
+    )
     joint_ref[...] = lax.dot_general(
         weights, normed, (((1,), (1,)), ((), ())), preferred_element_type=jnp.float32
     ).astype(jnp.bfloat16)
@@ -640,9 +690,11 @@
             jax.ShapeDtypeStruct((tokens, width), jnp.bfloat16),
             jax.ShapeDtypeStruct((tokens, width), jnp.bfloat16),
             jax.ShapeDtypeStruct((lines, tokens), jnp.bfloat16),
+            jax.ShapeDtypeStruct((lines, width), jnp.bfloat16),
+            jax.ShapeDtypeStruct((lines // 3, width), jnp.bfloat16),
         ],
         in_specs=[pl.BlockSpec(memory_space=pltpu.SMEM)] + [whole_vmem] * 3,
-        out_specs=[whole_vmem] * 4,
+        out_specs=[whole_vmem] * 6,
         scratch_shapes=[
             pltpu.VMEM((2, 8 * slots, unit_rows, half), jnp.bfloat16),
             pltpu.VMEM((2, tokens, half), jnp.float32),
@@ -690,7 +742,7 @@
 
 
 def attention_kernel(
-    heads, size, bias_ref, own_ref, out_ref, logsum_ref, before_ref,
+    heads, size, bias_ref, own_ref, out_ref, logsum_ref, before_ref, mine_ref,
     queries, own_values, old_values, scores, peak, total, keys_sem, send_sem, recv_sem,
 ):
     tokens = own_ref.shape[1]
@@ -801,10 +853,12 @@
                 low_old = (scores[...] * inverse).astype(jnp.bfloat16)
                 both = result + jnp.dot(low_old, old_values[head], preferred_element_type=jnp.float32)
                 out_ref[place] = both.T.astype(jnp.bfloat16)
+                mine_ref[place[1:]] = both.T.astype(jnp.bfloat16)
 
             @pl.when(jnp.logical_not(later))
             def _():
                 out_ref[place] = result.T.astype(jnp.bfloat16)
+                mine_ref[place[1:]] = result.T.astype(jnp.bfloat16)
 
         for step in (1, 2, 3):
             sent(block, step).start()
@@ -828,9 +882,10 @@
             jax.ShapeDtypeStruct((4, heads * size, tokens), jnp.bfloat16),
             jax.ShapeDtypeStruct((heads, tokens, 1), jnp.float32),
             jax.ShapeDtypeStruct((2 * heads * size, tokens), jnp.bfloat16),
+            jax.ShapeDtypeStruct((heads * size, tokens), jnp.bfloat16),
         ],
         in_specs=[pl.BlockSpec(memory_space=pltpu.SMEM), whole_vmem],
-        out_specs=[whole_vmem] * 3,
+        out_specs=[whole_vmem] * 4,
         scratch_shapes=[
             flat,
             flat,
@@ -1537,16 +1592,21 @@
     return (slot == dest_rows[0:1, :]) | (slot == dest_rows[1:2, :])
 
 
-def token_hits(dest_columns, expert, capacity, tokens):
+def token_hits(places, expert, capacity, tokens):
     slot = lax.broadcasted_iota(jnp.int32, (tokens, capacity), 1) + expert * capacity
-    hit = (slot == dest_columns[:, 0:1]) | (slot == dest_columns[:, 1:2])
+    hit = (slot == places[:, 4:5]) | (slot == places[:, 5:6])
     return jnp.where(hit, 1.0, 0.0).astype(jnp.bfloat16)
 
 
-def gate_of(routes, gates, expert, axis):
-    pick = (lambda a, k: a[k : k + 1, :]) if axis == 0 else (lambda a, k: a[:, k : k + 1])
-    return jnp.where(pick(routes, 0) == expert, pick(gates, 0), 0.0) + jnp.where(
-        pick(routes, 1) == expert, pick(gates, 1), 0.0
+def gate_of_rows(routes, gates, expert):
+    return jnp.where(routes[0:1, :] == expert, gates[0:1, :], 0.0) + jnp.where(
+        routes[1:2, :] == expert, gates[1:2, :], 0.0
+    )
+
+
+def gate_of_columns(places, gates, expert):
+    return jnp.where(places[:, 2:3] == expert, gates[:, 0:1], 0.0) + jnp.where(
+        places[:, 3:4] == expert, gates[:, 1:2], 0.0
     )
 
 
@@ -1555,7 +1615,7 @@
 
 
 def experts_kernel(
-    rows_ref, dest_rows, dest_columns, gates, routes, inner_full, outer_full, counts_ref,
+    rows_ref, dest_rows, places, gates, inner_full, outer_full, counts_ref,
     mix_ref, arrived, returned, totals_ref,
     inner_ref, outer_ref, outgoing, results, counts, send_one, recv_one, send_two, recv_two, send_count, recv_count,
 ):
@@ -1618,8 +1678,8 @@
     def combine(i, carry):
         step = arrival(i)
         _, expert = plane_peer(step)
-        hit = token_hits(dest_columns, expert, capacity, tokens)
-        gate = gate_of(routes, gates, expert, 1)
+        hit = token_hits(places, expert, capacity, tokens)
+        gate = gate_of_columns(places, gates, expert)
 
         @pl.when(step > 0)
         def _():
@@ -1661,7 +1721,7 @@
     totals_ref[...] = jnp.sum(counts[...], 0)
 
 
-def experts_forward(rows, dest, gates, routes, inner, outer, counts, capacity, collective_id):
+def experts_forward(rows, dest, places, gates, inner, outer, counts, capacity, collective_id):
     tokens, width = rows.shape
     buffer = pltpu.VMEM((8, capacity, width), jnp.bfloat16)
     return pl.pallas_call(
@@ -1672,7 +1732,7 @@
             jax.ShapeDtypeStruct((8, capacity, width), jnp.bfloat16),
             jax.ShapeDtypeStruct(counts.shape, jnp.float32),
         ],
-        in_specs=[whole_vmem] * 8,
+        in_specs=[whole_vmem] * 7,
         out_specs=[whole_vmem] * 4,
         scratch_shapes=[pltpu.VMEM(w.shape, jnp.bfloat16) for w in (inner, outer)]
         + [buffer, buffer, pltpu.VMEM((8,) + counts.shape, jnp.float32)]
@@ -1680,11 +1740,11 @@
         compiler_params=pltpu.CompilerParams(
             collective_id=collective_id, has_side_effects=True, vmem_limit_bytes=60 << 20
         ),
-    )(rows, dest, dest.T, gates, routes, inner, outer, counts)
+    )(rows, dest, places, gates, inner, outer, counts)
 
 
 def experts_back_kernel(
-    rows_ref, dest_rows, dest_columns, gates, routes, returned, arrived, *refs
+    rows_ref, dest_rows, places, gates, routes, returned, arrived, *refs
 ):
     inner_full, outer_full, grad_ref, gate_ref, inner_grad, outer_grad, inner_ref, outer_ref = refs[:8]
     outgoing, landed, results, landed_two, active, slopes = refs[8:14]
@@ -1701,7 +1761,7 @@
         rows = jnp.dot(
             jnp.where(hit, 1.0, 0.0).astype(jnp.bfloat16), rows_ref[...], preferred_element_type=jnp.float32
         )
-        scale = jnp.sum(jnp.where(hit, gate_of(routes, gates, expert, 0), 0.0), 1, keepdims=True)
+        scale = jnp.sum(jnp.where(hit, gate_of_rows(routes, gates, expert), 0.0), 1, keepdims=True)
         sent = (rows * scale).astype(jnp.bfloat16)
 
         @pl.when(step > 0)
@@ -1771,7 +1831,7 @@
     def combine(i, carry):
         step = arrival(i)
         _, expert = plane_peer(step)
-        hit = token_hits(dest_columns, expert, capacity, tokens)
+        hit = token_hits(places, expert, capacity, tokens)
 
         @pl.when(step > 0)
         def _():
@@ -1803,7 +1863,9 @@
     lax.fori_loop(1, 8, finish, 0)
 
 
-def experts_backward(rows, dest, gates, routes, returned, arrived, inner, outer, collective_id):
+def experts_backward(
+    rows, dest, places, gates, routes, returned, arrived, inner, outer, collective_id
+):
     tokens, width = rows.shape
     capacity = arrived.shape[1]
     inside = inner.shape[1]
@@ -1826,7 +1888,7 @@
         compiler_params=pltpu.CompilerParams(
             collective_id=collective_id, has_side_effects=True, vmem_limit_bytes=60 << 20
         ),
-    )(rows, dest, dest.T, gates, routes, returned, arrived, inner, outer)
+    )(rows, dest, places, gates, routes, returned, arrived, inner, outer)
 
 
 def own_units_kernel(
@@ -2064,6 +2126,53 @@
             collective_id=collective_id, has_side_effects=True, vmem_limit_bytes=63 << 20
         ),
     )(units_of, slopes, rows, ids, zero, joint, normed, attended, grad, small)
+
+
+def update_kernel(rates_ref, filled_ref, grad_ref, small_ref, *refs):
+    states, shared = refs[:3], refs[3:12]
+    updated, renewed = refs[12:15], refs[15:]
+    step = pl.program_id(0)
+    size = grad_ref.shape[0]
+    for n in range(size):
+        slot = step * size + n
+        marks = jnp.zeros(grad_ref.shape[1:], jnp.int32) + filled_ref[slot]
+        gradient = jnp.where(marks > 0, grad_ref[n], 0.0)
+        fresh = adam_update(*(state[n] for state in states), gradient, rates_ref[slot], decay_rate)
+        for k in range(3):
+            updated[k][n] = fresh[k]
+
+    @pl.when(step == 0)
+    def _():
+        experts = shared[3].shape[1]
+        heads, buckets = shared[6].shape
+        line = small_ref[3 + experts : 4 + experts, :]
+        biases = [line[:, h * buckets : (h + 1) * buckets] for h in range(heads)]
+        gradients = (
+            small_ref[0:3, :],
+            small_ref[3 : 3 + experts, :].T,
+            jnp.concatenate(biases, 0),
+        )
+        rates = ((rate_gains, 0.0), (rate_router, decay_rate), (rate_biases, 0.0))
+        for j in range(3):
+            fresh = adam_update(*(x[...] for x in shared[3 * j : 3 * j + 3]), gradients[j], *rates[j])
+            for k in range(3):
+                renewed[3 * j + k][...] = fresh[k]
+
+
+def update_all(rates, filled, grad, small, states, shared):
+    slots = grad.shape[0]
+    size = max(k for k in range(1, 5) if slots % k == 0)
+    block = pl.BlockSpec((size,) + grad.shape[1:], lambda k: (k, 0, 0))
+    whole = lambda x: pl.BlockSpec(x.shape, lambda k: (0,) * x.ndim)
+    scalars = pl.BlockSpec(memory_space=pltpu.SMEM)
+    return pl.pallas_call(
+        update_kernel,
+        grid=(slots // size,),
+        out_shape=[jax.ShapeDtypeStruct(x.shape, jnp.float32) for x in (*states, *shared)],
+        in_specs=[scalars] * 2 + [block, whole(small)] + [block] * 3 + [whole(x) for x in shared],
+        out_specs=[block] * 3 + [whole(x) for x in shared],
+        compiler_params=pltpu.CompilerParams(vmem_limit_bytes=40 << 20),
+    )(rates, filled, grad, small, *states, *shared)
 
 
 def to_plane(buffer):
@@ -2199,7 +2308,7 @@
     slot_rows = unit_starts + clipped_ids % unit_rows
     if on_square:
         slot_rows = jnp.where(inside, slot_rows, -1)[:, None]
-        weights_low, embedded, normed_one_low, joint = embed(
+        weights_low, embedded, normed_one_low, joint, joint_low, project_low = embed(
             unit_slots,
             master[0, 0],
             slot_rows,
@@ -2216,8 +2325,9 @@
         weights_low = pull_units([gathered], unit_slots)
         (embedded,) = sum_line(looked, [], [], keep_total, 1)
     weights_low = weights_low.reshape(-1, model_width)
-    joint_low = weights_low[vocab_here : vocab_here + 3 * hidden_here]
-    project_low = weights_low[vocab_here + 3 * hidden_here :]
+    if not on_square:
+        joint_low = weights_low[vocab_here : vocab_here + 3 * hidden_here]
+        project_low = weights_low[vocab_here + 3 * hidden_here :]
     rolled = [project_low] + [
         lax.ppermute(project_low, "tensor", [(source, (source + step) % 4) for source in range(4)])
         for step in (1, 2, 3)
@@ -2231,20 +2341,22 @@
         joint = lax.dot_general(
             joint_low, normed_one_low, (((1,), (1,)), ((), ())), preferred_element_type=jnp.float32
         ).astype(jnp.bfloat16)
-    attended_all, logsum_rows, pairs_before = attention(rel_bias, joint, heads_here, head_size, 2)
-    attended = lax.dynamic_index_in_dim(attended_all, my_rank, 0, keepdims=False)
+    attended_all, logsum_rows, pairs_before, attended = attention(
+        rel_bias, joint, heads_here, head_size, 2
+    )
     router_low = router.astype(jnp.bfloat16)
-    stream_one, normed_two_low, gate_rows, gate_columns = middle(
+    stream_one, normed_two_low, gate_rows, gate_columns, places = middle(
         attended_all.reshape(model_width, tokens_here),
         rolled,
         embedded,
         gain_rows[1],
         router_low.T,
         route_pairs.T,
+        dest,
     )
     if on_square:
         moe_partial, arrived, returned, counts = experts_forward(
-            normed_two_low, dest, gate_columns, route_pairs, expert_in[0], expert_out[0], counts, capacity, 8
+            normed_two_low, dest, places, gate_columns, expert_in[0], expert_out[0], counts, capacity, 8
         )
     else:
         inner_low, outer_low = expert_in[0].astype(jnp.bfloat16), expert_out[0].astype(jnp.bfloat16)
@@ -2269,6 +2381,7 @@
         moe_grad_part, gate_part, inner_grad, outer_grad = experts_backward(
             grad_two_low,
             dest,
+            places,
             gate_rows,
             route_pairs.T,
             returned,
@@ -2328,30 +2441,46 @@
         heads_here,
         head_size,
     )
-    grad_after = passed_along(before_grad, "ctx", -1)
-    pair_grad_low = (pair_grad + grad_after.astype(jnp.float32)).astype(jnp.bfloat16)
-    joint_grad = jnp.concatenate([query_grad, pair_grad_low], 0)
     distances = 2 * (half_length // BLOCK)
     bias_grad = jnp.sum(bias_lines, 1).reshape(heads_here, distances)
-    zero_grad_low, gain_grads = sum_line(
-        lax.dot_general(
-            joint_grad, joint_low, (((0,), (0,)), ((), ())), preferred_element_type=jnp.float32
-        ),
-        [embedded, gain_rows[0], grad_one, gain_grad_two, gain_grad_three],
-        [jax.ShapeDtypeStruct((8, model_width), jnp.float32)],
+    pair_shape = pltpu.VMEM((2 * hidden_here, tokens_here), jnp.bfloat16)
+    zero_grad_low, joint_grad, gain_grads = sum_line(
+        None,
+        [
+            embedded,
+            gain_rows[0],
+            grad_one,
+            gain_grad_two,
+            gain_grad_three,
+            query_grad,
+            pair_grad,
+            before_grad,
+            joint_low,
+        ],
+        [
+            jax.ShapeDtypeStruct((3 * hidden_here, tokens_here), jnp.bfloat16),
+            jax.ShapeDtypeStruct((8, model_width), jnp.float32),
+        ],
         functools.partial(finish_input_grad, embed_scale),
         6,
         prologue=clear_gain,
-        scratch=(pltpu.SemaphoreType.DMA, pltpu.SemaphoreType.DMA),
+        scratch=(
+            pltpu.SemaphoreType.DMA,
+            pltpu.SemaphoreType.DMA,
+            pair_shape,
+            pltpu.SemaphoreType.DMA((2,)),
+            pltpu.VMEM((tokens_here, model_width), jnp.float32),
+        ),
+        opening=form_joint_grad,
         ending=share_gains,
     )
     my_units = jnp.take(slot_unit, my_owner, axis=0)
-    my_filled = jnp.take(slot_filled, my_owner, axis=0)[:, None, None]
+    my_filled = jnp.take(slot_filled, my_owner, axis=0).astype(jnp.int32)
     bias_row = jnp.concatenate([bias_grad.reshape(-1), loss_local[None]])
     bias_row = jnp.pad(bias_row, (0, model_width - bias_row.shape[0]))[None]
     small = jnp.concatenate([gain_grads[:3], router_grad, bias_row], 0)
     small = jnp.pad(small, ((0, -small.shape[0] % 8), (0, 0)))
-    slot_rates = unit_rates(my_units, table_units, query_units, value_units)[:, None, None]
+    slot_rates = unit_rates(my_units, table_units, query_units, value_units)
     states = (master[0, 0], master_first[0, 0], master_second[0, 0])
     grad_rows = (
         slopes,
@@ -2371,33 +2500,25 @@
             outgoing.astype(jnp.float32), ("dp", "ctx"), scatter_dimension=0, tiled=True
         )
         small = lax.psum(small, ("dp", "ctx"))
-    states = adam_update(*states, jnp.where(my_filled, mine, 0.0), slot_rates, decay_rate)
-    gains_grad = small[:3]
-    router_grad = small[3 : 3 + experts].T
-    bias_grad = small[3 + experts, : rel_bias.size].reshape(rel_bias.shape)
+    shared = (
+        norm_gains,
+        norm_gains_first,
+        norm_gains_second,
+        router,
+        router_first,
+        router_second,
+        rel_bias,
+        rel_bias_first,
+        rel_bias_second,
+    )
+    fresh = update_all(slot_rates, my_filled, mine, small, states, shared)
+    states, shared = fresh[:3], fresh[3:]
     loss_totals = jnp.stack([small[3 + experts, rel_bias.size], weight_total])
-    gains_new, gains_first_new, gains_second_new = adam_update(
-        norm_gains, norm_gains_first, norm_gains_second, gains_grad, rate_gains, 0.0
-    )
-    router_new, router_first_new, router_second_new = adam_update(
-        router, router_first, router_second, router_grad, rate_router, decay_rate
-    )
-    biases_new, biases_first_new, biases_second_new = adam_update(
-        rel_bias, rel_bias_first, rel_bias_second, bias_grad, rate_biases, 0.0
-    )
     return (
         loss_totals,
         *(state[None, None] for state in states),
         *(state[None] for state in expert_states),
-        gains_new,
-        gains_first_new,
-        gains_second_new,
-        router_new,
-        router_first_new,
-        router_second_new,
-        biases_new,
-        biases_first_new,
-        biases_second_new,
+        *shared,
     )
 
 

time: 795 us -> 809 us (1.018)
  Pallas kernels: 715 us -> 743 us
  other arithmetic: 32.1 us -> 16.7 us
    pallas_call x2, Pallas kernels: 95.5 us -> 112 us  [sum_line(): pl.pallas_call(functools.partial(sum_line_kernel, rows, count, opening, p...]
    unnamed x87 -> x106, local copies, waits for them, and re-layouts: 14.6 us -> 29.3 us
    pallas_call x0 -> x1, Pallas kernels: none -> 11.4 us  [update_all(): pl.pallas_call(update_kernel, grid=(slots // size,), out_shape=[jax.Shape...]
    broadcast_in_dim x1 -> x0, other arithmetic: 10.4 us -> none  [on_device(): state[None, None]]
  transfers between devices with their start and end apart: 4 -> 3, of which waited for: 1 -> 0; matrix products, arithmetic and copies ran while one was open for 2% -> 1% of each run, Pallas kernels for 6% -> 6%
where the time goes in v10:
time: 809 us; the launch traced here: 805 us
  Pallas kernels  743 us (92%)
  local copies, waits for them, and re-layouts  37.4 us (5%)
  other arithmetic  16.7 us (2%)
    pallas_call x1, Pallas kernels, head_line(): pl.pallas_call(functools.partial(head_line_kernel, vocab_tile(vocab)), ou...  140 us
    pallas_call x1, Pallas kernels, embed(): pl.pallas_call(functools.partial(embed_kernel, chunks, first_unit), out_s...  121 us
    pallas_call x2, Pallas kernels, sum_line(): pl.pallas_call(functools.partial(sum_line_kernel, rows, count, opening, p...  112 us
    pallas_call x1, Pallas kernels, own_units(): pl.pallas_call(functools.partial(own_units_kernel, chunks), out_shape=[ja...  96.3 us
    pallas_call x1, Pallas kernels, experts_backward(): pl.pallas_call(experts_back_kernel, out_shape=[jax.ShapeDtypeStruct((toke...  93.8 us
    pallas_call x1, Pallas kernels, experts_forward(): pl.pallas_call(experts_kernel, out_shape=[jax.ShapeDtypeStruct((tokens, w...  93.5 us
    pallas_call x1, Pallas kernels, attention(): pl.pallas_call(functools.partial(attention_kernel, heads, size), out_shap...  48.3 us
    unnamed x106, local copies, waits for them, and re-layouts  29.3 us
  transfers between devices with their start and end apart: 3, of which 0 were waited for; matrix products, arithmetic and copies ran while one was open for 1% of the time, Pallas kernels for 6%

profile of v10, /device:TPU:0, one launch (start us, length us, event | category | flops | bytes accessed | tf_op | source)
XLA Modules:
  0.0 805.3 jit_solution(2714401743100504760)
XLA Ops:
  2.1 3.4 convert_reduce_fusion
  9.7 1.4 fusion.6
  12.2 121.4 %shard_map.384 = (bf16[137,64,768]{2,1,0:T(8,128)(2,1)}, bf16[1024,768]{1,0:T(8,128)(2,1)}, bf16[1024,768]{1,0:T(8,128)(2,1)}, bf16[576,1024]{1,0:T(8,128)(2,1)}...) custom-call(s32[137]{0:T(256)} %copy-done.45, f32[21,64,768]{2,1,0:T(8,128)} %bitcast.61, s32[1024,1]{1,0:T(8,128)} %fusion.2.rows_ref, ...), custom_call_target="tpu_custom_call" | custom-call | tf_op jit(solution)/shard_map/pallas_call | solution.py:686
  133.7 2.6 collective-permute-start.1
  136.3 1.3 collective-permute-start.2
  141.6 1.7 copy.87.refs_7_
  143.2 1.6 copy.88.refs_8_
  144.9 48.3 %shard_map.385 = (bf16[4,192,1024]{2,1,0:T(8,128)(2,1)S(1)}, f32[3,1024,1]{2,1,0:T(8,128)S(1)}, bf16[384,1024]{1,0:T(8,128)(2,1)S(1)}, bf16[192,1024]{1,0:T(8,128)(2,1)S(1)}) custom-call(f32[3,8]{1,0:T(4,128)S(1)} %copy-done.35, bf16[576,1024]{1,0:T(8,128)(2,1)S(1)} %copy-done.6), custom_call_target="tpu_custom_call" | custom-call | tf_op jit(solution)/shard_map/pallas_call | solution.py:879
  198.7 1.4 copy-done.15
  200.1 5.6 shard_map.386
  205.7 1.7 copy-done.1
  211.4 93.5 %shard_map.387 = (f32[1024,768]{1,0:T(8,128)}, bf16[8,288,768]{2,1,0:T(8,128)(2,1)}, bf16[8,288,768]{2,1,0:T(8,128)(2,1)}, f32[8,128]{1,0:T(8,128)}) custom-call(bf16[1024,768]{1,0:T(8,128)(2,1)} %copy-done.4, s32[2,1024]{1,0:T(2,128)} %copy-done.29, s32[1024,8]{1,0:T(8,128)} %copy-done.10, f32[1024,8]{1,0:T(8,128)} %copy-done.25, f32[768,768]{1,0:T(8,128)} %bitcast.68, ...), custom_call_target="tpu_custom_call" | custom-call | tf_op jit(solution)/shard_map/pallas_call | solution.py:1727
  304.9 1.3 fusion.7
  308.3 139.6 %shard_map.388 = (bf16[1024,768]{1,0:T(8,128)(2,1)}, bf16[1024,768]{1,0:T(8,128)(2,1)}, f32[1024,768]{1,0:T(8,128)}, f32[1,768]{1,0:T(1,128)}, f32[1,1024]{1,0:T...) custom-call(f32[1024,768]{1,0:T(8,128)} %get-tuple-element.104.part_ref, f32[1024,768]{1,0:T(8,128)} %copy-done.1, ...), custom_call_target="tpu_custom_call" | custom-call | tf_op jit(solution)/shard_map/pallas_call | solution.py:1381
  447.9 93.8 %shard_map.389 = (f32[1024,768]{1,0:T(8,128)}, f32[2,1024]{1,0:T(2,128)}, f32[768,768]{1,0:T(8,128)}, f32[768,768]{1,0:T(8,128)}) custom-call(bf16[1024,768]{1,0:T(8,128)(2,1)} %get-tuple-element.110.rows_ref, s32[2,1024]{1,0:T(2,128)} %copy-done.29, s32[1024,8]{1,0:T(8,128)} %copy-done.10, f32[2,1024]{1,0:T(2,128)} %copy-done.32, s32[2,1024]{1,0:T(2,128)} %bitcast.65, ...), custom_call_target="tpu_custom_call" | custom-call | tf_op jit(solution)/shard_map/pallas_call | solution.py:1874
  542.6 52.0 %shard_map.390 = (bf16[1024,768]{1,0:T(8,128)(2,1)S(1)}, f32[1024,768]{1,0:T(8,128)S(1)}, bf16[8,1024]{1,0:T(8,128)(2,1)S(1)}, f32[1,1024]{1,0:T(1,128)S(1)}, f32[1,768]{1,0:T(1,128)S(1)}) custom-call(f32[1024,768]{1,0:T(8,128)} %get-tuple-element.114.refs_0_, f32[1024,768]{1,0:T(8,128)} %copy-done.1, f32[1,768]{1,0:T(1,128)S(1)} %get-tuple-element.260.gain_ref.refs_2_, ...), custom_call_target="tpu_custom_call" | custom-call | tf_op jit(solution)/shard_map/pallas_call | solution.py:185
  595.8 1.7 copy-done.9
  598.7 20.9 %shard_map.391 = (bf16[192,1024]{1,0:T(8,128)(2,1)S(1)}, f32[384,1024]{1,0:T(8,128)S(1)}, bf16[384,1024]{1,0:T(8,128)(2,1)S(1)}, f32[24,256]{1,0:T(8,128)S(1)}, ...) custom-call(f32[3,8]{1,0:T(4,128)S(1)} %copy-done.35, ...), custom_call_target="tpu_custom_call" | custom-call | tf_op jit(solution)/shard_map/pallas_call | solution.py:1058
  620.8 60.0 %shard_map.392 = (bf16[1024,768]{1,0:T(8,128)(2,1)S(1)}, bf16[576,1024]{1,0:T(8,128)(2,1)S(1)}, f32[8,768]{1,0:T(8,128)S(1)}) custom-call(bf16[1024,768]{1,0:T(8,128)(2,1)} %get-tuple-element.98.embedded_ref.refs_0_, f32[1,768]{1,0:T(1,128)S(1)} %copy-done.34, f32[1024,768]{1,0:T(8,128)} %copy-done.9, f32[1,768]{1,0:T(1,128)S(1)} %get-tuple-element.119.refs_3_, ...), custom_call_target="tpu_custom_call" | custom-call | tf_op jit(solution)/shard_map/pallas_call | solution.py:185
  686.4 96.3 %shard_map.393 = (f32[21,64,768]{2,1,0:T(8,128)}, f32[16,768]{1,0:T(8,128)}) custom-call(s32[168]{0:T(256)} %reshape.259.units_of, bf16[125,64,1024]{2,1,0:T(8,128)(2,1)} %bitcast.74, bf16[1024,768]{1,0:T(8,128)(2,1)} %get-tuple-element.109.rows_ref, s32[1,1024]{1,0:T(1,128)} %copy-done.41, bf16[1024,768]{1,0:T(8,128)(2,1)} %copy-done.12, ...), custom_call_target="tpu_custom_call" | custom-call | tf_op jit(solution)/shard_map/pallas_call | solution.py:2094
  782.6 1.3 slice.52
  784.0 2.2 copy-done
  786.2 2.2 copy-done.8
  790.1 11.4 %shard_map.394 = (f32[21,64,768]{2,1,0:T(8,128)}, f32[21,64,768]{2,1,0:T(8,128)}, f32[21,64,768]{2,1,0:T(8,128)}, f32[3,768]{1,0:T(4,128)}, f32[3,768]{1,0:T(4,1...) custom-call(f32[21]{0:T(128)S(1)} %select_reduce_fusion.1.rates_ref,, ...), custom_call_target="tpu_custom_call" | custom-call | tf_op jit(solution)/shard_map/pallas_call | solution.py:2168
  (152 shorter events, 34.6 us)
Async XLA Ops:
  6.3 127.3 %copy-start.41 = (s32[1,1024]{1,0:T(1,128)}, s32[1,1024]{1,0:T(1,128)S(1)}, u32[]{:S(2)}) copy-start(s32[1,1024]{1,0:T(1,128)S(1)} %get-tuple-element.258.ids_ref) | copy-start | bytes 12292
  8.7 190.0 %copy-start.29 = (s32[2,1024]{1,0:T(2,128)}, s32[2,1024]{1,0:T(2,128)S(1)}, u32[]{:S(2)}) copy-start(s32[2,1024]{1,0:T(2,128)S(1)} %add_select_fusion.1.dest_ref.dest_rows) | copy-start | bytes 24580
  12.1 125.4 %copy-start.43 = (f32[768,8]{0,1:T(8,128)S(1)}, f32[768,8]{0,1:T(8,128)}, u32[]{:S(2)}) copy-start(f32[768,8]{0,1:T(8,128)} %param.45) | copy-start | bytes 73732
  12.1 127.0 %copy-start.44 = (s32[137,1]{0,1:T(1,128)S(1)}, s32[137,1]{0,1:T(1,128)}, u32[]{:S(2)}) copy-start(s32[137,1]{0,1:T(1,128)} %param.32) | copy-start | bytes 1648
  12.1 128.0 %copy-start.42 = (s32[1,1024,2]{1,2,0:T(2,128)S(1)}, s32[1,1024,2]{1,2,0:T(2,128)}, u32[]{:S(2)}) copy-start(s32[1,1024,2]{1,2,0:T(2,128)} %param.29) | copy-start | bytes 24580
  12.1 128.1 %copy-start.49 = (f32[2]{0:T(128)S(1)}, f32[2]{0:T(128)}, u32[]{:S(2)}) copy-start(f32[2]{0:T(128)} %constant.203) | copy-start | bytes 28
  12.2 132.7 %copy-start.35 = (f32[3,8]{1,0:T(4,128)S(1)}, f32[3,8]{1,0:T(4,128)}, u32[]{:S(2)}) copy-start(f32[3,8]{1,0:T(4,128)} %refs_9_.1) | copy-start | bytes 292
  133.6 64.4 %copy-start.46 = (s32[1,1024,2]{1,2,0:T(2,128)S(1)}, s32[1,1024,2]{1,2,0:T(2,128)}, u32[]{:S(2)}) copy-start(s32[1,1024,2]{1,2,0:T(2,128)} %param.28) | copy-start | bytes 24580
  133.6 65.1 %copy-start.3 = (bf16[1024,768]{1,0:T(8,128)(2,1)S(1)}, bf16[1024,768]{1,0:T(8,128)(2,1)}, u32[]{:S(2)}) copy-start(bf16[1024,768]{1,0:T(8,128)(2,1)} %get-tuple-element.98.embedded_ref.refs_0_) | copy-start | bytes 4718596
  133.6 65.1 %copy-start.19 = (bf16[192,768]{1,0:T(8,128)(2,1)S(1)}, bf16[192,768]{1,0:T(8,128)(2,1)}, u32[]{:S(2)}) copy-start(bf16[192,768]{1,0:T(8,128)(2,1)} %get-tuple-element.100.refs_0_.project_ref) | copy-start | bytes 884740
  133.6 65.1 %copy-start.27 = (s32[1,1024,2]{1,2,0:T(2,128)S(1)}, s32[1,1024,2]{1,2,0:T(2,128)}, u32[]{:S(2)}) copy-start(s32[1,1024,2]{1,2,0:T(2,128)} %param.30) | copy-start | bytes 24580
  133.7 65.0 %collective-permute-start = (bf16[192,768]{1,0:T(8,128)(2,1)}, bf16[192,768]{1,0:T(8,128)(2,1)}, u32[]{:S(2)}, u32[]{:S(2)}) collective-permute-start(bf16[192,768]{1,0:T(8,128)(2,1)} %get-tuple-element.100.refs_0_.project_ref), channel_id=1, source_target_pairs={{0,1},{1,2},{2,3},{3,0},{4,5},{5,6},{6,7},{7,4},{8,9},{9,10},{10,1... | collective-permute-start | bytes 884744 | tf_op jit(solution)/shard_map/ppermute | solution.py:2332
  133.7 65.0 %collective-permute-start.1 = (bf16[192,768]{1,0:T(8,128)(2,1)}, bf16[192,768]{1,0:T(8,128)(2,1)}, u32[]{:S(2)}, u32[]{:S(2)}) collective-permute-start(bf16[192,768]{1,0:T(8,128)(2,1)} %get-tuple-element.100.refs_0_.project_ref), channel_id=1, source_target_pairs={{0,2},{1,3},{2,0},{3,1},{4,6},{5,7},{6,4},{7,5},{8,10},{9,11},{10,... | collective-permute-start | bytes 884744 | tf_op jit(solution)/shard_map/ppermute | solution.py:2332
  136.3 62.4 %collective-permute-start.2 = (bf16[192,768]{1,0:T(8,128)(2,1)}, bf16[192,768]{1,0:T(8,128)(2,1)}, u32[]{:S(2)}, u32[]{:S(2)}) collective-permute-start(bf16[192,768]{1,0:T(8,128)(2,1)} %get-tuple-element.100.refs_0_.project_ref), channel_id=1, source_target_pairs={{0,3},{1,0},{2,1},{3,2},{4,7},{5,4},{6,5},{7,6},{8,11},{9,8},{10,9... | collective-permute-start | bytes 884744 | tf_op jit(solution)/shard_map/ppermute | solution.py:2332
  447.9 93.8 %copy-start.48 = (f32[1,1024]{1,0:T(1,128)S(1)}, f32[1,1024]{1,0:T(1,128)}, u32[]{:S(2)}) copy-start(f32[1,1024]{1,0:T(1,128)} %get-tuple-element.117) | copy-start | bytes 12292
  447.9 94.6 %copy-start.24 = (bf16[768,8]{1,0:T(8,128)(2,1)S(1)}, bf16[768,8]{1,0:T(8,128)(2,1)}, u32[]{:S(2)}) copy-start(bf16[768,8]{1,0:T(8,128)(2,1)} %convert_element_type.25.refs_7_) | copy-start | bytes 36868
  447.9 94.6 %copy-start.28 = (s32[1,1024,2]{1,2,0:T(2,128)S(1)}, s32[1,1024,2]{1,2,0:T(2,128)}, u32[]{:S(2)}) copy-start(s32[1,1024,2]{1,2,0:T(2,128)} %param.30) | copy-start | bytes 24580
  447.9 94.6 %copy-start.33 = (f32[2,1024]{1,0:T(2,128)S(1)}, f32[2,1024]{1,0:T(2,128)}, u32[]{:S(2)}) copy-start(f32[2,1024]{1,0:T(2,128)} %copy-done.32) | copy-start | bytes 24580
  686.3 97.6 %copy-start.16 = (f32[768,8]{1,0:T(8,128)S(1)}, f32[768,8]{1,0:T(8,128)}, u32[]{:S(2)}) copy-start(f32[768,8]{1,0:T(8,128)} %copy.87.refs_7_) | copy-start | bytes 73732
  686.3 97.6 %copy-start.31 = (f32[3,768]{1,0:T(4,128)S(1)}, f32[3,768]{1,0:T(4,128)}, u32[]{:S(2)}) copy-start(f32[3,768]{1,0:T(4,128)} %refs_3_.1) | copy-start | bytes 27652
  686.3 97.6 %copy-start.36 = (f32[3,768]{1,0:T(4,128)S(1)}, f32[3,768]{1,0:T(4,128)}, u32[]{:S(2)}) copy-start(f32[3,768]{1,0:T(4,128)} %refs_4_.1) | copy-start | bytes 27652
  686.3 97.6 %copy-start.37 = (f32[3,768]{1,0:T(4,128)S(1)}, f32[3,768]{1,0:T(4,128)}, u32[]{:S(2)}) copy-start(f32[3,768]{1,0:T(4,128)} %refs_5_.1) | copy-start | bytes 27652
  686.3 97.6 %copy-start.39 = (f32[3,8]{1,0:T(4,128)S(1)}, f32[3,8]{1,0:T(4,128)}, u32[]{:S(2)}) copy-start(f32[3,8]{1,0:T(4,128)} %refs_10_.1) | copy-start | bytes 292
  686.4 97.6 %copy-start.40 = (f32[3,8]{1,0:T(4,128)S(1)}, f32[3,8]{1,0:T(4,128)}, u32[]{:S(2)}) copy-start(f32[3,8]{1,0:T(4,128)} %refs_11_.1) | copy-start | bytes 292
  (29 other events, 333.6 us)

commit v11 on v9

--- a/solution.py
+++ b/solution.py
@@ -32,11 +32,6 @@
 decay_rate = 0.1
 
 
-def passed_along(value, axis, steps):
-    count = lax.axis_size(axis)
-    initial, last = (max(0, -steps), min(count, count - steps))
-    return lax.ppermute(value, axis, [(source, source + steps) for source in range(initial, last)])
-
 MESH_ID = pl.DeviceIdType.MESH
 whole_vmem = pl.BlockSpec(memory_space=pltpu.VMEM)
 whole_any = pl.BlockSpec(memory_space=pl.ANY)
@@ -44,32 +39,37 @@
 
 
 def sum_line_kernel(
-    rows, count, opening, prologue, epilogue, ending, n_extra, n_aux, n_scratch, part_ref, *refs
+    rows, count, opening, with_core, prologue, epilogue, ending, n_extra, n_aux, n_scratch, *refs
 ):
     extras = refs[:n_extra]
     out_ref = refs[n_extra]
     aux = refs[n_extra + 1 : n_extra + 1 + n_aux]
     rest = refs[n_extra + 1 + n_aux :]
     scratch = rest[:n_scratch]
+    part_ref = scratch[-1] if with_core else extras[0]
+    extras = extras if with_core else extras[1:]
     stage, from_end, from_mid, send_sem, end_sem, mid_sem, back_sem, back_recv = rest[n_scratch:]
     rank = lax.axis_index("tensor")
     inner = (rank == 1) | (rank == 2)
     end_peer = jnp.where(rank < 2, 1 - rank, 5 - rank)
     mid_peer = 3 - rank
     barrier = pltpu.get_barrier_semaphore()
-    if opening is None:
+    if opening is None or with_core:
         pl.semaphore_signal(barrier, inc=1, device_id={"tensor": end_peer}, device_id_type=MESH_ID)
+        if with_core:
+            other_core = {"ctx": 1 - lax.axis_index("ctx")}
+            pl.semaphore_signal(barrier, inc=1, device_id=other_core, device_id_type=MESH_ID)
 
         @pl.when(inner)
         def _():
             pl.semaphore_signal(
                 barrier, inc=1, device_id={"tensor": mid_peer}, device_id_type=MESH_ID
             )
-            pl.semaphore_wait(barrier, 2)
+            pl.semaphore_wait(barrier, 2 + with_core)
 
         @pl.when(jnp.logical_not(inner))
         def _():
-            pl.semaphore_wait(barrier, 1)
+            pl.semaphore_wait(barrier, 1 + with_core)
     else:
         for step in (1, 2, 3):
             other = lax.rem(rank + step, 4)
@@ -110,7 +110,7 @@
         )
 
     if opening is not None:
-        opening(rank, extras, scratch)
+        opening(rank, extras, aux, scratch)
 
     @pl.when(jnp.logical_not(inner))
     def _():
@@ -178,7 +178,8 @@
     ending=None,
     rows=64,
 ):
-    tokens, width = part.shape
+    tokens, width = scratch[-1].shape if part is None else part.shape
+    inputs = list(extras) if part is None else [part, *extras]
     count = tokens // rows
     chunks = pltpu.VMEM((count, rows, width), jnp.bfloat16)
     return pl.pallas_call(
@@ -187,15 +188,16 @@
             rows,
             count,
             opening,
+            part is None,
             prologue,
             epilogue,
             ending,
-            len(extras),
+            len(inputs),
             len(aux_shapes),
             len(scratch),
         ),
         out_shape=[jax.ShapeDtypeStruct((tokens, width), jnp.bfloat16)] + list(aux_shapes),
-        in_specs=[whole_vmem] * (1 + len(extras)),
+        in_specs=[whole_vmem] * len(inputs),
         out_specs=[whole_vmem] * (1 + len(aux_shapes)),
         scratch_shapes=list(scratch)
         + [chunks, chunks, chunks]
@@ -203,7 +205,7 @@
         compiler_params=pltpu.CompilerParams(
             collective_id=collective_id, has_side_effects=True, vmem_limit_bytes=48 << 20
         ),
-    )(part, *extras)
+    )(*inputs)
 
 
 def keep_total(total, span, rank, extras, aux, scratch):
@@ -230,7 +232,7 @@
 
 
 def share_gains(inner, end_peer, extras, aux, scratch):
-    gains = aux[0]
+    gains = aux[-1]
     copy = pltpu.make_async_remote_copy(
         src_ref=gains,
         dst_ref=gains,
@@ -268,7 +270,7 @@
     ]
 
 
-def send_gate_parts(rank, extras, scratch):
+def send_gate_parts(rank, extras, aux, scratch):
     for copy in gate_copies(rank, extras, scratch):
         copy.start()
 
@@ -319,11 +321,47 @@
     return result.astype(jnp.bfloat16)
 
 
+def form_joint_grad(rank, extras, aux, scratch):
+    query_grad, pair_grad, before_grad, joint_weights = extras[5:]
+    joint_grad = aux[0]
+    landed, pair_sem, part = scratch[2:]
+    hidden = query_grad.shape[0]
+    later = lax.axis_index("ctx") > 0
+    copy = pltpu.make_async_remote_copy(
+        src_ref=before_grad,
+        dst_ref=landed,
+        send_sem=pair_sem.at[0],
+        recv_sem=pair_sem.at[1],
+        device_id={"ctx": 1 - lax.axis_index("ctx")},
+        device_id_type=MESH_ID,
+    )
+    joint_grad[0:hidden, :] = query_grad[...]
+
+    @pl.when(later)
+    def _():
+        copy.start()
+        joint_grad[hidden:, :] = pair_grad[...].astype(jnp.bfloat16)
+
+    @pl.when(jnp.logical_not(later))
+    def _():
+        copy.wait_recv()
+        both = pair_grad[...] + landed[...].astype(jnp.float32)
+        joint_grad[hidden:, :] = both.astype(jnp.bfloat16)
+
+    part[...] = lax.dot_general(
+        joint_grad[...], joint_weights[...], (((0,), (0,)), ((), ())), preferred_element_type=jnp.float32
+    )
+
+    @pl.when(later)
+    def _():
+        copy.wait_send()
+
+
 def finish_input_grad(scale, total, span, rank, extras, aux, scratch):
     embedded, gain, grad_one = extras[:3]
     stream_zero = embedded[span].astype(jnp.float32) * scale
     part, gain_part = norm_back_rows(stream_zero, gain[...], total)
-    aux[0][0:1, :] += gain_part
+    aux[-1][0:1, :] += gain_part
     return ((grad_one[span] + part) * scale).astype(jnp.bfloat16)
 
 
@@ -387,7 +425,8 @@
 
 
 def embed_kernel(
-    chunks, first_unit, slots_ref, mine_ref, rows_ref, gain_ref, units_ref, embedded_ref, normed_ref, joint_ref, *refs
+    chunks, first_unit, slots_ref, mine_ref, rows_ref, gain_ref, units_ref, embedded_ref, normed_ref, joint_ref,
+    joint_weights, project_weights, *refs
 ):
     held, total, stage, from_end, from_mid = refs[:5]
     send_x, recv_x, send_y, recv_y, send_z, recv_z, send_core, recv_core = refs[5:13]
@@ -620,6 +659,10 @@
     normed_ref[...] = normed
     lines = joint_ref.shape[0]
     weights = units_ref[first_unit : first_unit + lines // unit_rows].reshape(lines, 2 * width)
+    joint_weights[...] = weights
+    project_weights[...] = units_ref[first_unit + lines // unit_rows :].reshape(
+        project_weights.shape
+    )
     joint_ref[...] = lax.dot_general(
         weights, normed, (((1,), (1,)), ((), ())), preferred_element_type=jnp.float32
     ).astype(jnp.bfloat16)
@@ -640,9 +683,11 @@
             jax.ShapeDtypeStruct((tokens, width), jnp.bfloat16),
             jax.ShapeDtypeStruct((tokens, width), jnp.bfloat16),
             jax.ShapeDtypeStruct((lines, tokens), jnp.bfloat16),
+            jax.ShapeDtypeStruct((lines, width), jnp.bfloat16),
+            jax.ShapeDtypeStruct((lines // 3, width), jnp.bfloat16),
         ],
         in_specs=[pl.BlockSpec(memory_space=pltpu.SMEM)] + [whole_vmem] * 3,
-        out_specs=[whole_vmem] * 4,
+        out_specs=[whole_vmem] * 6,
         scratch_shapes=[
             pltpu.VMEM((2, 8 * slots, unit_rows, half), jnp.bfloat16),
             pltpu.VMEM((2, tokens, half), jnp.float32),
@@ -690,7 +735,7 @@
 
 
 def attention_kernel(
-    heads, size, bias_ref, own_ref, out_ref, logsum_ref, before_ref,
+    heads, size, bias_ref, own_ref, out_ref, logsum_ref, before_ref, mine_ref,
     queries, own_values, old_values, scores, peak, total, keys_sem, send_sem, recv_sem,
 ):
     tokens = own_ref.shape[1]
@@ -698,13 +743,25 @@
     hidden = heads * size
     later = lax.axis_index("ctx") > 0
     rank = lax.axis_index("tensor")
+    inner = (rank == 1) | (rank == 2)
+    end_peer = jnp.where(rank < 2, 1 - rank, 5 - rank)
+    mid_peer = 3 - rank
+    mid_owner = jnp.where(inner, mid_peer, 3 - end_peer)
+    far_owner = jnp.where(inner, 3 - end_peer, 3 - rank)
+    other_core = {"ctx": 1 - lax.axis_index("ctx")}
     barrier = pltpu.get_barrier_semaphore()
-    other_core = {"ctx": 1 - lax.axis_index("ctx")}
-    pl.semaphore_signal(barrier, inc=1, device_id=other_core, device_id_type=MESH_ID)
-    for step in (1, 2, 3):
-        other = lax.rem(rank + step, 4)
-        pl.semaphore_signal(barrier, inc=1, device_id={"tensor": other}, device_id_type=MESH_ID)
-    pl.semaphore_wait(barrier, 4)
+    for place in (other_core, {"tensor": end_peer}):
+        pl.semaphore_signal(barrier, inc=1, device_id=place, device_id_type=MESH_ID)
+
+    @pl.when(inner)
+    def _():
+        pl.semaphore_signal(barrier, inc=1, device_id={"tensor": mid_peer}, device_id_type=MESH_ID)
+        pl.semaphore_wait(barrier, 3)
+
+    @pl.when(jnp.logical_not(inner))
+    def _():
+        pl.semaphore_wait(barrier, 2)
+
     pairs = pltpu.make_async_remote_copy(
         src_ref=own_ref.at[pl.ds(hidden, 2 * hidden)],
         dst_ref=before_ref,
@@ -737,16 +794,46 @@
                 before_ref[hidden + head * size : hidden + (head + 1) * size, :]
             )
 
-    def sent(block, step):
-        piece = out_ref.at[rank, :, pl.ds(block * BLOCK, BLOCK)]
+    def sent(owner, block, peer, send, recv):
+        piece = out_ref.at[owner, :, pl.ds(block * BLOCK, BLOCK)]
         return pltpu.make_async_remote_copy(
             src_ref=piece,
             dst_ref=piece,
-            send_sem=send_sem.at[block, step - 1],
-            recv_sem=recv_sem.at[block, step - 1],
-            device_id={"tensor": lax.rem(rank + step, 4)},
+            send_sem=send_sem.at[block, send],
+            recv_sem=recv_sem.at[block, recv],
+            device_id={"tensor": peer},
             device_id_type=MESH_ID,
         )
+
+    def own_to_end(block):
+        return sent(rank, block, end_peer, 0, 0)
+
+    def from_end(block):
+        return sent(end_peer, block, end_peer, 0, 0)
+
+    def own_to_middle(block):
+        return sent(rank, block, mid_peer, 1, 1)
+
+    def end_to_middle(block):
+        return sent(end_peer, block, mid_peer, 2, 2)
+
+    def middle_to_end(block):
+        return sent(mid_owner, block, end_peer, 3, 1)
+
+    def far_to_end(block):
+        return sent(far_owner, block, end_peer, 4, 2)
+
+    def hand_on(block, stages):
+        @pl.when(inner)
+        def _():
+            if 0 in stages:
+                from_end(block).wait_recv()
+                end_to_middle(block).start()
+                middle_to_end(block).wait_recv()
+                middle_to_end(block).start()
+            if 1 in stages:
+                far_to_end(block).wait_recv()
+                far_to_end(block).start()
 
     for block in range(blocks):
         for head in range(heads):
@@ -801,17 +888,40 @@
                 low_old = (scores[...] * inverse).astype(jnp.bfloat16)
                 both = result + jnp.dot(low_old, old_values[head], preferred_element_type=jnp.float32)
                 out_ref[place] = both.T.astype(jnp.bfloat16)
+                mine_ref[place[1:]] = both.T.astype(jnp.bfloat16)
 
             @pl.when(jnp.logical_not(later))
             def _():
                 out_ref[place] = result.T.astype(jnp.bfloat16)
-
-        for step in (1, 2, 3):
-            sent(block, step).start()
-
+                mine_ref[place[1:]] = result.T.astype(jnp.bfloat16)
+
+        own_to_end(block).start()
+
+        @pl.when(inner)
+        def _():
+            own_to_middle(block).start()
+
+        if block >= 1:
+            hand_on(block - 1, (0,))
+        if block >= 2:
+            hand_on(block - 2, (1,))
+
+    hand_on(blocks - 1, (0,))
+    hand_on(blocks - 2, (1,))
+    hand_on(blocks - 1, (1,))
     for block in range(blocks):
-        for step in (1, 2, 3):
-            sent(block, step).wait()
+        own_to_end(block).wait_send()
+
+        @pl.when(inner)
+        def _():
+            for copy in (own_to_middle, end_to_middle, middle_to_end, far_to_end):
+                copy(block).wait_send()
+
+        @pl.when(jnp.logical_not(inner))
+        def _():
+            from_end(block).wait_recv()
+            middle_to_end(block).wait_recv()
+            far_to_end(block).wait_recv()
 
     @pl.when(jnp.logical_not(later))
     def _():
@@ -828,9 +938,10 @@
             jax.ShapeDtypeStruct((4, heads * size, tokens), jnp.bfloat16),
             jax.ShapeDtypeStruct((heads, tokens, 1), jnp.float32),
             jax.ShapeDtypeStruct((2 * heads * size, tokens), jnp.bfloat16),
+            jax.ShapeDtypeStruct((heads * size, tokens), jnp.bfloat16),
         ],
         in_specs=[pl.BlockSpec(memory_space=pltpu.SMEM), whole_vmem],
-        out_specs=[whole_vmem] * 3,
+        out_specs=[whole_vmem] * 4,
         scratch_shapes=[
             flat,
             flat,
@@ -839,7 +950,7 @@
             pltpu.VMEM((BLOCK, 1), jnp.float32),
             pltpu.VMEM((BLOCK, 1), jnp.float32),
             pltpu.SemaphoreType.DMA((2,)),
-            pltpu.SemaphoreType.DMA((blocks, 3)),
+            pltpu.SemaphoreType.DMA((blocks, 5)),
             pltpu.SemaphoreType.DMA((blocks, 3)),
         ],
         compiler_params=pltpu.CompilerParams(
@@ -2199,7 +2310,7 @@
     slot_rows = unit_starts + clipped_ids % unit_rows
     if on_square:
         slot_rows = jnp.where(inside, slot_rows, -1)[:, None]
-        weights_low, embedded, normed_one_low, joint = embed(
+        weights_low, embedded, normed_one_low, joint, joint_low, project_low = embed(
             unit_slots,
             master[0, 0],
             slot_rows,
@@ -2216,8 +2327,9 @@
         weights_low = pull_units([gathered], unit_slots)
         (embedded,) = sum_line(looked, [], [], keep_total, 1)
     weights_low = weights_low.reshape(-1, model_width)
-    joint_low = weights_low[vocab_here : vocab_here + 3 * hidden_here]
-    project_low = weights_low[vocab_here + 3 * hidden_here :]
+    if not on_square:
+        joint_low = weights_low[vocab_here : vocab_here + 3 * hidden_here]
+        project_low = weights_low[vocab_here + 3 * hidden_here :]
     rolled = [project_low] + [
         lax.ppermute(project_low, "tensor", [(source, (source + step) % 4) for source in range(4)])
         for step in (1, 2, 3)
@@ -2231,8 +2343,9 @@
         joint = lax.dot_general(
             joint_low, normed_one_low, (((1,), (1,)), ((), ())), preferred_element_type=jnp.float32
         ).astype(jnp.bfloat16)
-    attended_all, logsum_rows, pairs_before = attention(rel_bias, joint, heads_here, head_size, 2)
-    attended = lax.dynamic_index_in_dim(attended_all, my_rank, 0, keepdims=False)
+    attended_all, logsum_rows, pairs_before, attended = attention(
+        rel_bias, joint, heads_here, head_size, 2
+    )
     router_low = router.astype(jnp.bfloat16)
     stream_one, normed_two_low, gate_rows, gate_columns = middle(
         attended_all.reshape(model_width, tokens_here),
@@ -2328,21 +2441,37 @@
         heads_here,
         head_size,
     )
-    grad_after = passed_along(before_grad, "ctx", -1)
-    pair_grad_low = (pair_grad + grad_after.astype(jnp.float32)).astype(jnp.bfloat16)
-    joint_grad = jnp.concatenate([query_grad, pair_grad_low], 0)
     distances = 2 * (half_length // BLOCK)
     bias_grad = jnp.sum(bias_lines, 1).reshape(heads_here, distances)
-    zero_grad_low, gain_grads = sum_line(
-        lax.dot_general(
-            joint_grad, joint_low, (((0,), (0,)), ((), ())), preferred_element_type=jnp.float32
-        ),
-        [embedded, gain_rows[0], grad_one, gain_grad_two, gain_grad_three],
-        [jax.ShapeDtypeStruct((8, model_width), jnp.float32)],
+    pair_shape = pltpu.VMEM((2 * hidden_here, tokens_here), jnp.bfloat16)
+    zero_grad_low, joint_grad, gain_grads = sum_line(
+        None,
+        [
+            embedded,
+            gain_rows[0],
+            grad_one,
+            gain_grad_two,
+            gain_grad_three,
+            query_grad,
+            pair_grad,
+            before_grad,
+            joint_low,
+        ],
+        [
+            jax.ShapeDtypeStruct((3 * hidden_here, tokens_here), jnp.bfloat16),
+            jax.ShapeDtypeStruct((8, model_width), jnp.float32),
+        ],
         functools.partial(finish_input_grad, embed_scale),
         6,
         prologue=clear_gain,
-        scratch=(pltpu.SemaphoreType.DMA, pltpu.SemaphoreType.DMA),
+        scratch=(
+            pltpu.SemaphoreType.DMA,
+            pltpu.SemaphoreType.DMA,
+            pair_shape,
+            pltpu.SemaphoreType.DMA((2,)),
+            pltpu.VMEM((tokens_here, model_width), jnp.float32),
+        ),
+        opening=form_joint_grad,
         ending=share_gains,
     )
     my_units = jnp.take(slot_unit, my_owner, axis=0)

time: 795 us -> 795 us (level)
  Pallas kernels: 715 us -> 727 us
    pallas_call x2, Pallas kernels: 95.5 us -> 112 us  [sum_line(): pl.pallas_call(functools.partial(sum_line_kernel, rows, count, opening, p...]
  transfers between devices with their start and end apart: 4 -> 3, of which waited for: 1 -> 0; matrix products, arithmetic and copies ran while one was open for 2% -> 1% of each run, Pallas kernels for 6% -> 6%
where the time goes in v11:
time: 795 us; the launch traced here: 792 us
  Pallas kernels  727 us (91%)
  other arithmetic  29.1 us (4%)
  local copies, waits for them, and re-layouts  26.9 us (3%)
    pallas_call x1, Pallas kernels, head_line(): pl.pallas_call(functools.partial(head_line_kernel, vocab_tile(vocab)), ou...  140 us
    pallas_call x1, Pallas kernels, embed(): pl.pallas_call(functools.partial(embed_kernel, chunks, first_unit), out_s...  121 us
    pallas_call x2, Pallas kernels, sum_line(): pl.pallas_call(functools.partial(sum_line_kernel, rows, count, opening, p...  112 us
    pallas_call x1, Pallas kernels, own_units(): pl.pallas_call(functools.partial(own_units_kernel, chunks), out_shape=[ja...  96.2 us
    pallas_call x1, Pallas kernels, experts_backward(): pl.pallas_call(experts_back_kernel, out_shape=[jax.ShapeDtypeStruct((toke...  93.8 us
    pallas_call x1, Pallas kernels, experts_forward(): pl.pallas_call(experts_kernel, out_shape=[jax.ShapeDtypeStruct((tokens, w...  93.4 us
    pallas_call x1, Pallas kernels, attention(): pl.pallas_call(functools.partial(attention_kernel, heads, size), out_shap...  45.4 us
    pallas_call x1, Pallas kernels, attention_back(): pl.pallas_call(functools.partial(attention_back_kernel, heads, size), out...  20.9 us
  transfers between devices with their start and end apart: 3, of which 0 were waited for; matrix products, arithmetic and copies ran while one was open for 1% of the time, Pallas kernels for 6%

profile of v11, /device:TPU:0, one launch (start us, length us, event | category | flops | bytes accessed | tf_op | source)
XLA Modules:
  0.0 791.7 jit_solution(16011136707933876360)
XLA Ops:
  2.1 3.4 convert_reduce_fusion
  9.7 1.4 fusion.17
  12.2 121.4 %shard_map.384 = (bf16[137,64,768]{2,1,0:T(8,128)(2,1)}, bf16[1024,768]{1,0:T(8,128)(2,1)}, bf16[1024,768]{1,0:T(8,128)(2,1)}, bf16[576,1024]{1,0:T(8,128)(2,1)}...) custom-call(s32[137]{0:T(256)} %copy-done.36, f32[21,64,768]{2,1,0:T(8,128)} %bitcast.95, s32[1024,1]{1,0:T(8,128)} %fusion.3.rows_ref, ...), custom_call_target="tpu_custom_call" | custom-call | tf_op jit(solution)/shard_map/pallas_call | solution.py:679
  133.7 2.5 collective-permute-start.1
  136.3 1.3 collective-permute-start.2
  141.4 1.3 copy-done.5
  142.6 45.4 %shard_map.385 = (bf16[4,192,1024]{2,1,0:T(8,128)(2,1)S(1)}, f32[3,1024,1]{2,1,0:T(8,128)S(1)}, bf16[384,1024]{1,0:T(8,128)(2,1)S(1)}, bf16[192,1024]{1,0:T(8,128)(2,1)S(1)}) custom-call(f32[3,8]{1,0:T(4,128)S(1)} %copy-done.24, bf16[576,1024]{1,0:T(8,128)(2,1)S(1)} %copy-done.5), custom_call_target="tpu_custom_call" | custom-call | tf_op jit(solution)/shard_map/pallas_call | solution.py:935
  192.4 1.4 copy-done.2
  194.7 4.5 shard_map.386
  199.3 1.7 copy-done
  204.1 93.4 %shard_map.387 = (f32[1024,768]{1,0:T(8,128)}, bf16[8,288,768]{2,1,0:T(8,128)(2,1)}, bf16[8,288,768]{2,1,0:T(8,128)(2,1)}, f32[8,128]{1,0:T(8,128)}) custom-call(bf16[1024,768]{1,0:T(8,128)(2,1)} %copy-done.3, s32[2,1024]{1,0:T(2,128)} %copy-done.26, s32[1024,2]{1,0:T(8,128)} %copy.77.dest_columns, f32[1024,8]{1,0:T(8,128)} %copy-done.17, ...), custom_call_target="tpu_custom_call" | custom-call | tf_op jit(solution)/shard_map/pallas_call | solution.py:1778
  297.6 1.3 fusion.18
  300.9 139.6 %shard_map.388 = (bf16[1024,768]{1,0:T(8,128)(2,1)}, bf16[1024,768]{1,0:T(8,128)(2,1)}, f32[1024,768]{1,0:T(8,128)}, f32[1,768]{1,0:T(1,128)}, f32[1,1024]{1,0:T...) custom-call(f32[1024,768]{1,0:T(8,128)} %get-tuple-element.90.part_ref, f32[1024,768]{1,0:T(8,128)} %copy-done, ...), custom_call_target="tpu_custom_call" | custom-call | tf_op jit(solution)/shard_map/pallas_call | solution.py:1437
  440.5 93.8 %shard_map.389 = (f32[1024,768]{1,0:T(8,128)}, f32[2,1024]{1,0:T(2,128)}, f32[768,768]{1,0:T(8,128)}, f32[768,768]{1,0:T(8,128)}) custom-call(bf16[1024,768]{1,0:T(8,128)(2,1)} %get-tuple-element.96.rows_ref, s32[2,1024]{1,0:T(2,128)} %copy-done.26, s32[1024,2]{1,0:T(8,128)} %copy.77.dest_columns, f32[2,1024]{1,0:T(2,128)} %copy-done.21, ...), custom_call_target="tpu_custom_call" | custom-call | tf_op jit(solution)/shard_map/pallas_call | solution.py:1923
  535.1 52.1 %shard_map.390 = (bf16[1024,768]{1,0:T(8,128)(2,1)S(1)}, f32[1024,768]{1,0:T(8,128)S(1)}, bf16[8,1024]{1,0:T(8,128)(2,1)S(1)}, f32[1,1024]{1,0:T(1,128)S(1)}, f32[1,768]{1,0:T(1,128)S(1)}) custom-call(f32[1024,768]{1,0:T(8,128)} %get-tuple-element.100.refs_0_, f32[1024,768]{1,0:T(8,128)} %copy-done, f32[1,768]{1,0:T(1,128)S(1)} %get-tuple-element.170.gain_ref.refs_2_, ...), custom_call_target="tpu_custom_call" | custom-call | tf_op jit(solution)/shard_map/pallas_call | solution.py:185
  588.3 1.7 copy-done.7
  590.4 20.9 %shard_map.391 = (bf16[192,1024]{1,0:T(8,128)(2,1)S(1)}, f32[384,1024]{1,0:T(8,128)S(1)}, bf16[384,1024]{1,0:T(8,128)(2,1)S(1)}, f32[24,256]{1,0:T(8,128)S(1)}, ...) custom-call(f32[3,8]{1,0:T(4,128)S(1)} %copy-done.24, ...), custom_call_target="tpu_custom_call" | custom-call | tf_op jit(solution)/shard_map/pallas_call | solution.py:1114
  612.5 60.1 %shard_map.392 = (bf16[1024,768]{1,0:T(8,128)(2,1)S(1)}, bf16[576,1024]{1,0:T(8,128)(2,1)S(1)}, f32[8,768]{1,0:T(8,128)S(1)}) custom-call(bf16[1024,768]{1,0:T(8,128)(2,1)} %get-tuple-element.85.embedded_ref.refs_0_, f32[1,768]{1,0:T(1,128)S(1)} %copy-done.23, f32[1024,768]{1,0:T(8,128)} %copy-done.7, f32[1,768]{1,0:T(1,128)S(1)} %get-tuple-element.105.refs_3_, ...), custom_call_target="tpu_custom_call" | custom-call | tf_op jit(solution)/shard_map/pallas_call | solution.py:185
  678.1 96.2 %shard_map.393 = (f32[21,64,768]{2,1,0:T(8,128)}, f32[16,768]{1,0:T(8,128)}) custom-call(s32[168]{0:T(256)} %reshape.275.units_of, bf16[125,64,1024]{2,1,0:T(8,128)(2,1)} %bitcast.96, bf16[1024,768]{1,0:T(8,128)(2,1)} %get-tuple-element.95.rows_ref, s32[1,1024]{1,0:T(1,128)} %copy-done.28, bf16[1024,768]{1,0:T(8,128)(2,1)} %copy-done.9, ...), custom_call_target="tpu_custom_call" | custom-call | tf_op jit(solution)/shard_map/pallas_call | solution.py:2143
  775.1 1.3 slice.61
  776.4 1.4 multiply_subtract_fusion
  777.9 1.4 multiply_subtract_fusion.1
  779.2 1.2 pad_maximum_fusion
  781.1 10.4 %fusion.12 = (f32[1,1,21,64,768]{4,3,2,1,0:T(8,128)}, f32[1,1,21,64,768]{4,3,2,1,0:T(8,128)}, f32[1,1,21,64,768]{4,3,2,1,0:T(8,128)}) fusion(f32[21,64,768]{2,1,0:T(8,128)} %get-tuple-element.126, pred[21]{0:T(512)(128)(4,1)S(1)} %select_reduce_fusion.2, f32[1,1,21,64,768]{4,3,2,1,0:T(8,128)} %param.35, f32[1,1,21,64,768]{4,3,2,1,0:T(8,128)} %param.34, ...), kind=kLoop, calls=%fused_computation.69 | loop fusion | flops 16515072 | bytes 28901480 | tf_op jit(solution)/shard_map/broadcast_in_dim | solution.py:2519
  (138 shorter events, 28.6 us)
Async XLA Ops:
  0.7 136.9 %copy-start.33 = (s32[137,1]{0,1:T(1,128)S(1)}, s32[137,1]{0,1:T(1,128)}, u32[]{:S(2)}) copy-start(s32[137,1]{0,1:T(1,128)} %param.32) | copy-start | bytes 1648
  0.7 136.9 %copy-start.27 = (f32[768,8]{0,1:T(8,128)S(1)}, f32[768,8]{0,1:T(8,128)}, u32[]{:S(2)}) copy-start(f32[768,8]{0,1:T(8,128)} %param.45) | copy-start | bytes 73732
  6.3 132.6 %copy-start.28 = (s32[1,1024]{1,0:T(1,128)}, s32[1,1024]{1,0:T(1,128)S(1)}, u32[]{:S(2)}) copy-start(s32[1,1024]{1,0:T(1,128)S(1)} %get-tuple-element.165.ids_ref) | copy-start | bytes 12292
  8.8 130.2 %copy-start.26 = (s32[2,1024]{1,0:T(2,128)}, s32[2,1024]{1,0:T(2,128)S(1)}, u32[]{:S(2)}) copy-start(s32[2,1024]{1,0:T(2,128)S(1)} %add_select_fusion.1.dest_rows) | copy-start | bytes 24580
  9.2 129.8 %copy-start.19 = (s32[1,1024,2]{1,2,0:T(2,128)S(1)}, s32[1,1024,2]{1,2,0:T(2,128)}, u32[]{:S(2)}) copy-start(s32[1,1024,2]{1,2,0:T(2,128)} %param.30) | copy-start | bytes 24580
  9.5 130.5 %copy-start.30 = (s32[1,1024,2]{1,2,0:T(2,128)S(1)}, s32[1,1024,2]{1,2,0:T(2,128)}, u32[]{:S(2)}) copy-start(s32[1,1024,2]{1,2,0:T(2,128)} %param.29) | copy-start | bytes 24580
  9.5 130.6 %copy-start.42 = (f32[2]{0:T(128)S(1)}, f32[2]{0:T(128)}, u32[]{:S(2)}) copy-start(f32[2]{0:T(128)} %constant.248) | copy-start | bytes 28
  9.7 131.6 %copy-start.24 = (f32[3,8]{1,0:T(4,128)S(1)}, f32[3,8]{1,0:T(4,128)}, u32[]{:S(2)}) copy-start(f32[3,8]{1,0:T(4,128)} %bias_ref.3) | copy-start | bytes 292
  12.2 179.5 %copy-start.37 = (s32[1,1024,2]{1,2,0:T(2,128)S(1)}, s32[1,1024,2]{1,2,0:T(2,128)}, u32[]{:S(2)}) copy-start(s32[1,1024,2]{1,2,0:T(2,128)} %param.28) | copy-start | bytes 24580
  133.7 58.7 %collective-permute-start = (bf16[192,768]{1,0:T(8,128)(2,1)}, bf16[192,768]{1,0:T(8,128)(2,1)S(1)}, u32[]{:S(2)}, u32[]{:S(2)}) collective-permute-start(bf16[192,768]{1,0:T(8,128)(2,1)} %get-tuple-element.86.refs_0_.project_ref), channel_id=1, source_target_pairs={{0,1},{1,2},{2,3},{3,0},{4,5},{5,6},{6,7},{7,4},{8,9},{9,10},{10,1... | collective-permute-start | bytes 884744 | tf_op jit(solution)/shard_map/ppermute | solution.py:2334
  133.7 58.6 %collective-permute-start.1 = (bf16[192,768]{1,0:T(8,128)(2,1)}, bf16[192,768]{1,0:T(8,128)(2,1)S(1)}, u32[]{:S(2)}, u32[]{:S(2)}) collective-permute-start(bf16[192,768]{1,0:T(8,128)(2,1)} %get-tuple-element.86.refs_0_.project_ref), channel_id=1, source_target_pairs={{0,2},{1,3},{2,0},{3,1},{4,6},{5,7},{6,4},{7,5},{8,10},{9,11},{10,... | collective-permute-start | bytes 884744 | tf_op jit(solution)/shard_map/ppermute | solution.py:2334
  136.3 56.1 %collective-permute-start.2 = (bf16[192,768]{1,0:T(8,128)(2,1)}, bf16[192,768]{1,0:T(8,128)(2,1)S(1)}, u32[]{:S(2)}, u32[]{:S(2)}) collective-permute-start(bf16[192,768]{1,0:T(8,128)(2,1)} %get-tuple-element.86.refs_0_.project_ref), channel_id=1, source_target_pairs={{0,3},{1,0},{2,1},{3,2},{4,7},{5,4},{6,5},{7,6},{8,11},{9,8},{10,9... | collective-permute-start | bytes 884744 | tf_op jit(solution)/shard_map/ppermute | solution.py:2334
  440.5 93.8 %copy-start.39 = (f32[1,1024]{1,0:T(1,128)S(1)}, f32[1,1024]{1,0:T(1,128)}, u32[]{:S(2)}) copy-start(f32[1,1024]{1,0:T(1,128)} %get-tuple-element.103) | copy-start | bytes 12292
  440.5 94.6 %copy-start.20 = (s32[1,1024,2]{1,2,0:T(2,128)S(1)}, s32[1,1024,2]{1,2,0:T(2,128)}, u32[]{:S(2)}) copy-start(s32[1,1024,2]{1,2,0:T(2,128)} %param.30) | copy-start | bytes 24580
  440.5 94.6 %copy-start.22 = (f32[2,1024]{1,0:T(2,128)S(1)}, f32[2,1024]{1,0:T(2,128)}, u32[]{:S(2)}) copy-start(f32[2,1024]{1,0:T(2,128)} %copy-done.21) | copy-start | bytes 24580
  535.1 55.2 %copy-start.6 = (bf16[576,1024]{1,0:T(8,128)(2,1)S(1)}, bf16[576,1024]{1,0:T(8,128)(2,1)}, u32[]{:S(2)}) copy-start(bf16[576,1024]{1,0:T(8,128)(2,1)} %get-tuple-element.83.own_ref) | copy-start | bytes 3538948
  612.5 62.9 %copy-start.38 = (f32[1,1024]{1,0:T(1,128)S(1)}, f32[1,1024]{1,0:T(1,128)}, u32[]{:S(2)}) copy-start(f32[1,1024]{1,0:T(1,128)} %get-tuple-element.123) | copy-start | bytes 12292
  678.1 98.4 %copy-start.31 = (f32[768,8]{0,1:T(8,128)S(1)}, f32[768,8]{0,1:T(8,128)}, u32[]{:S(2)}) copy-start(f32[768,8]{0,1:T(8,128)} %param.46) | copy-start | bytes 73732
  678.1 98.4 %copy-start.32 = (f32[768,8]{0,1:T(8,128)S(1)}, f32[768,8]{0,1:T(8,128)}, u32[]{:S(2)}) copy-start(f32[768,8]{0,1:T(8,128)} %param.47) | copy-start | bytes 73732
  678.1 99.8 %copy-start.29 = (f32[3,768]{1,0:T(4,128)S(1)}, f32[3,768]{1,0:T(4,128)}, u32[]{:S(2)}) copy-start(f32[3,768]{1,0:T(4,128)} %param.42) | copy-start | bytes 27652
  678.1 99.8 %copy-start.34 = (f32[3,768]{1,0:T(4,128)S(1)}, f32[3,768]{1,0:T(4,128)}, u32[]{:S(2)}) copy-start(f32[3,768]{1,0:T(4,128)} %param.43) | copy-start | bytes 27652
  678.1 99.8 %copy-start.35 = (f32[3,768]{1,0:T(4,128)S(1)}, f32[3,768]{1,0:T(4,128)}, u32[]{:S(2)}) copy-start(f32[3,768]{1,0:T(4,128)} %param.44) | copy-start | bytes 27652
  678.1 102.4 %copy-start.40 = (f32[3,8]{1,0:T(4,128)S(1)}, f32[3,8]{1,0:T(4,128)}, u32[]{:S(2)}) copy-start(f32[3,8]{1,0:T(4,128)} %param.49) | copy-start | bytes 292
  678.1 102.4 %copy-start.41 = (f32[3,8]{1,0:T(4,128)S(1)}, f32[3,8]{1,0:T(4,128)}, u32[]{:S(2)}) copy-start(f32[3,8]{1,0:T(4,128)} %param.50) | copy-start | bytes 292
  (22 other events, 252.6 us)

commit v12 on v11

--- a/solution.py
+++ b/solution.py
@@ -428,9 +428,9 @@
     chunks, first_unit, slots_ref, mine_ref, rows_ref, gain_ref, units_ref, embedded_ref, normed_ref, joint_ref,
     joint_weights, project_weights, *refs
 ):
-    held, total, stage, from_end, from_mid = refs[:5]
-    send_x, recv_x, send_y, recv_y, send_z, recv_z, send_core, recv_core = refs[5:13]
-    send_sem, end_sem, mid_sem, back_sem, back_recv = refs[13:]
+    held, total, stage, from_end, from_mid, units, store_sem = refs[:7]
+    send_x, recv_x, send_y, recv_y, send_z, recv_z, send_core, recv_core = refs[7:15]
+    send_sem, end_sem, mid_sem, back_sem, back_recv = refs[15:]
     chip, core = lax.axis_index("dp"), lax.axis_index("ctx")
     beside = chip + 1 - 2 * lax.rem(chip, 2)
     across = lax.rem(chip + 2, 4)
@@ -614,17 +614,18 @@
 
     def place_unit(u):
         for h in range(2):
-            units_ref[u, :, columns(h)] = held[h, slots_ref[u]]
-
-    @pl.when(jnp.logical_not(inner))
-    def _():
-        repeat(0, units_ref.shape[0], place_unit)
-
-    repeat(0, count + line_lag, lambda i: exchange(1, i))
-
-    @pl.when(inner)
-    def _():
-        repeat(0, units_ref.shape[0], place_unit)
+            units[u, :, columns(h)] = held[h, slots_ref[u]]
+
+    turns = count + line_lag
+    share = -(-units.shape[0] // turns)
+
+    def exchange_and_place(i):
+        exchange(1, i)
+        repeat(i * share, jnp.minimum((i + 1) * share, units.shape[0]), place_unit)
+
+    repeat(0, turns, exchange_and_place)
+    store = pltpu.make_async_copy(units, units_ref, store_sem)
+    store.start()
 
     def finish(q):
         for h in range(2):
@@ -658,14 +659,15 @@
     normed = (stream * inverse_rms(stream) * gain_ref[...]).astype(jnp.bfloat16)
     normed_ref[...] = normed
     lines = joint_ref.shape[0]
-    weights = units_ref[first_unit : first_unit + lines // unit_rows].reshape(lines, 2 * width)
+    weights = units[first_unit : first_unit + lines // unit_rows].reshape(lines, 2 * width)
     joint_weights[...] = weights
-    project_weights[...] = units_ref[first_unit + lines // unit_rows :].reshape(
+    project_weights[...] = units[first_unit + lines // unit_rows :].reshape(
         project_weights.shape
     )
     joint_ref[...] = lax.dot_general(
         weights, normed, (((1,), (1,)), ((), ())), preferred_element_type=jnp.float32
     ).astype(jnp.bfloat16)
+    store.wait()
 
 
 def embed(unit_slots, mine, slot_rows, gain, first_unit, lines, collective_id):
@@ -687,13 +689,15 @@
             jax.ShapeDtypeStruct((lines // 3, width), jnp.bfloat16),
         ],
         in_specs=[pl.BlockSpec(memory_space=pltpu.SMEM)] + [whole_vmem] * 3,
-        out_specs=[whole_vmem] * 6,
+        out_specs=[whole_any] + [whole_vmem] * 5,
         scratch_shapes=[
             pltpu.VMEM((2, 8 * slots, unit_rows, half), jnp.bfloat16),
             pltpu.VMEM((2, tokens, half), jnp.float32),
             line,
             line,
             line,
+            pltpu.VMEM((unit_slots.shape[0], unit_rows, width), jnp.bfloat16),
+            pltpu.SemaphoreType.DMA,
         ]
         + [sems] * 6
         + [pltpu.SemaphoreType.DMA((2, 4, chunks))] * 2
@@ -2019,7 +2023,7 @@
     load.wait()
     group = made.shape[0] // unit_rows
 
-    def form(owner, target):
+    def form(owner, target, first_group=0, last_group=slots // group):
         def some(g):
             first = owner * slots + g * group
 
@@ -2045,7 +2049,7 @@
 
             repeat(0, group, put)
 
-        repeat(0, slots // group, some)
+        repeat(first_group, last_group, some)
 
     def joined(k, q):
         pass_over(k, q).wait_recv()
@@ -2081,9 +2085,14 @@
         repeat(0, chunks, lambda q: pass_over(k, q).start())
         form(places[k] * 2 + core, own.at[k])
 
-    form_pair(0)
-    repeat(0, split, first_leg(beside))
-    repeat(split, chunks, first_leg(across))
+    for g in range(slots // group):
+        done = [q for q in range(chunks) if g * group < (q + 1) * size <= (g + 1) * group]
+        form(places[0] * 2 + 1 - core, passing.at[0], g, g + 1)
+        for q in done:
+            pass_over(0, q).start()
+        form(places[0] * 2 + core, own.at[0], g, g + 1)
+        for q in done:
+            first_leg(beside if q < split else across)(q)
     repeat(1, 8, lambda step: small_copy(step).start())
     small_landed[chip * 2 + core] = small_ref[...]
     form_pair(1)

time: 795 us -> 794 us (level)
  no operation moved by 1% of the time
where the time goes in v12:
time: 794 us; the launch traced here: 791 us
  Pallas kernels  727 us (92%)
  other arithmetic  29.1 us (4%)
  local copies, waits for them, and re-layouts  26.9 us (3%)
    pallas_call x1, Pallas kernels, head_line(): pl.pallas_call(functools.partial(head_line_kernel, vocab_tile(vocab)), ou...  140 us
    pallas_call x1, Pallas kernels, embed(): pl.pallas_call(functools.partial(embed_kernel, chunks, first_unit), out_s...  119 us
    pallas_call x2, Pallas kernels, sum_line(): pl.pallas_call(functools.partial(sum_line_kernel, rows, count, opening, p...  112 us
    pallas_call x1, Pallas kernels, own_units(): pl.pallas_call(functools.partial(own_units_kernel, chunks), out_shape=[ja...  97.9 us
    pallas_call x1, Pallas kernels, experts_backward(): pl.pallas_call(experts_back_kernel, out_shape=[jax.ShapeDtypeStruct((toke...  93.8 us
    pallas_call x1, Pallas kernels, experts_forward(): pl.pallas_call(experts_kernel, out_shape=[jax.ShapeDtypeStruct((tokens, w...  93.4 us
    pallas_call x1, Pallas kernels, attention(): pl.pallas_call(functools.partial(attention_kernel, heads, size), out_shap...  45.3 us
    pallas_call x1, Pallas kernels, attention_back(): pl.pallas_call(functools.partial(attention_back_kernel, heads, size), out...  20.9 us
  transfers between devices with their start and end apart: 3, of which 0 were waited for; matrix products, arithmetic and copies ran while one was open for 1% of the time, Pallas kernels for 6%

profile of v12, /device:TPU:0, one launch (start us, length us, event | category | flops | bytes accessed | tf_op | source)
XLA Modules:
  0.0 790.8 jit_solution(5521958134806348260)
XLA Ops:
  2.1 3.4 convert_reduce_fusion
  9.7 1.4 fusion.17
  12.2 119.0 %shard_map.384 = (bf16[137,64,768]{2,1,0:T(8,128)(2,1)}, bf16[1024,768]{1,0:T(8,128)(2,1)}, bf16[1024,768]{1,0:T(8,128)(2,1)}, bf16[576,1024]{1,0:T(8,128)(2,1)}...) custom-call(s32[137]{0:T(256)} %copy-done.36, f32[21,64,768]{2,1,0:T(8,128)} %bitcast.95, s32[1024,1]{1,0:T(8,128)} %fusion.3.rows_ref, ...), custom_call_target="tpu_custom_call" | custom-call | tf_op jit(solution)/shard_map/pallas_call | solution.py:681
  131.3 2.5 collective-permute-start.1
  133.8 1.3 collective-permute-start.2
  138.9 1.3 copy-done.5
  140.2 45.3 %shard_map.385 = (bf16[4,192,1024]{2,1,0:T(8,128)(2,1)S(1)}, f32[3,1024,1]{2,1,0:T(8,128)S(1)}, bf16[384,1024]{1,0:T(8,128)(2,1)S(1)}, bf16[192,1024]{1,0:T(8,128)(2,1)S(1)}) custom-call(f32[3,8]{1,0:T(4,128)S(1)} %copy-done.24, bf16[576,1024]{1,0:T(8,128)(2,1)S(1)} %copy-done.5), custom_call_target="tpu_custom_call" | custom-call | tf_op jit(solution)/shard_map/pallas_call | solution.py:939
  189.8 1.4 copy-done.2
  192.2 4.5 shard_map.386
  196.7 1.7 copy-done
  201.6 93.4 %shard_map.387 = (f32[1024,768]{1,0:T(8,128)}, bf16[8,288,768]{2,1,0:T(8,128)(2,1)}, bf16[8,288,768]{2,1,0:T(8,128)(2,1)}, f32[8,128]{1,0:T(8,128)}) custom-call(bf16[1024,768]{1,0:T(8,128)(2,1)} %copy-done.3, s32[2,1024]{1,0:T(2,128)} %copy-done.26, s32[1024,2]{1,0:T(8,128)} %copy.77.dest_columns, f32[1024,8]{1,0:T(8,128)} %copy-done.17, ...), custom_call_target="tpu_custom_call" | custom-call | tf_op jit(solution)/shard_map/pallas_call | solution.py:1782
  295.0 1.3 fusion.18
  298.4 139.7 %shard_map.388 = (bf16[1024,768]{1,0:T(8,128)(2,1)}, bf16[1024,768]{1,0:T(8,128)(2,1)}, f32[1024,768]{1,0:T(8,128)}, f32[1,768]{1,0:T(1,128)}, f32[1,1024]{1,0:T...) custom-call(f32[1024,768]{1,0:T(8,128)} %get-tuple-element.90.part_ref, f32[1024,768]{1,0:T(8,128)} %copy-done, ...), custom_call_target="tpu_custom_call" | custom-call | tf_op jit(solution)/shard_map/pallas_call | solution.py:1441
  438.1 93.8 %shard_map.389 = (f32[1024,768]{1,0:T(8,128)}, f32[2,1024]{1,0:T(2,128)}, f32[768,768]{1,0:T(8,128)}, f32[768,768]{1,0:T(8,128)}) custom-call(bf16[1024,768]{1,0:T(8,128)(2,1)} %get-tuple-element.96.rows_ref, s32[2,1024]{1,0:T(2,128)} %copy-done.26, s32[1024,2]{1,0:T(8,128)} %copy.77.dest_columns, f32[2,1024]{1,0:T(2,128)} %copy-done.21, ...), custom_call_target="tpu_custom_call" | custom-call | tf_op jit(solution)/shard_map/pallas_call | solution.py:1927
  532.7 52.0 %shard_map.390 = (bf16[1024,768]{1,0:T(8,128)(2,1)S(1)}, f32[1024,768]{1,0:T(8,128)S(1)}, bf16[8,1024]{1,0:T(8,128)(2,1)S(1)}, f32[1,1024]{1,0:T(1,128)S(1)}, f32[1,768]{1,0:T(1,128)S(1)}) custom-call(f32[1024,768]{1,0:T(8,128)} %get-tuple-element.100.refs_0_, f32[1024,768]{1,0:T(8,128)} %copy-done, f32[1,768]{1,0:T(1,128)S(1)} %get-tuple-element.170.gain_ref.refs_2_, ...), custom_call_target="tpu_custom_call" | custom-call | tf_op jit(solution)/shard_map/pallas_call | solution.py:185
  585.8 1.7 copy-done.7
  587.9 20.9 %shard_map.391 = (bf16[192,1024]{1,0:T(8,128)(2,1)S(1)}, f32[384,1024]{1,0:T(8,128)S(1)}, bf16[384,1024]{1,0:T(8,128)(2,1)S(1)}, f32[24,256]{1,0:T(8,128)S(1)}, ...) custom-call(f32[3,8]{1,0:T(4,128)S(1)} %copy-done.24, ...), custom_call_target="tpu_custom_call" | custom-call | tf_op jit(solution)/shard_map/pallas_call | solution.py:1118
  610.0 60.1 %shard_map.392 = (bf16[1024,768]{1,0:T(8,128)(2,1)S(1)}, bf16[576,1024]{1,0:T(8,128)(2,1)S(1)}, f32[8,768]{1,0:T(8,128)S(1)}) custom-call(bf16[1024,768]{1,0:T(8,128)(2,1)} %get-tuple-element.85.embedded_ref.refs_0_, f32[1,768]{1,0:T(1,128)S(1)} %copy-done.23, f32[1024,768]{1,0:T(8,128)} %copy-done.7, f32[1,768]{1,0:T(1,128)S(1)} %get-tuple-element.105.refs_3_, ...), custom_call_target="tpu_custom_call" | custom-call | tf_op jit(solution)/shard_map/pallas_call | solution.py:185
  675.6 97.9 %shard_map.393 = (f32[21,64,768]{2,1,0:T(8,128)}, f32[16,768]{1,0:T(8,128)}) custom-call(s32[168]{0:T(256)} %reshape.275.units_of, bf16[125,64,1024]{2,1,0:T(8,128)(2,1)} %bitcast.96, bf16[1024,768]{1,0:T(8,128)(2,1)} %get-tuple-element.95.rows_ref, s32[1,1024]{1,0:T(1,128)} %copy-done.28, bf16[1024,768]{1,0:T(8,128)(2,1)} %copy-done.9, ...), custom_call_target="tpu_custom_call" | custom-call | tf_op jit(solution)/shard_map/pallas_call | solution.py:2152
  774.3 1.3 slice.61
  775.6 1.4 multiply_subtract_fusion
  777.1 1.4 multiply_subtract_fusion.1
  778.4 1.2 pad_maximum_fusion
  780.3 10.4 %fusion.12 = (f32[1,1,21,64,768]{4,3,2,1,0:T(8,128)}, f32[1,1,21,64,768]{4,3,2,1,0:T(8,128)}, f32[1,1,21,64,768]{4,3,2,1,0:T(8,128)}) fusion(f32[21,64,768]{2,1,0:T(8,128)} %get-tuple-element.126, pred[21]{0:T(512)(128)(4,1)S(1)} %select_reduce_fusion.2, f32[1,1,21,64,768]{4,3,2,1,0:T(8,128)} %param.35, f32[1,1,21,64,768]{4,3,2,1,0:T(8,128)} %param.34, ...), kind=kLoop, calls=%fused_computation.69 | loop fusion | flops 16515072 | bytes 28901480 | tf_op jit(solution)/shard_map/broadcast_in_dim | solution.py:2528
  (138 shorter events, 28.6 us)
Async XLA Ops:
  0.7 134.5 %copy-start.33 = (s32[137,1]{0,1:T(1,128)S(1)}, s32[137,1]{0,1:T(1,128)}, u32[]{:S(2)}) copy-start(s32[137,1]{0,1:T(1,128)} %param.32) | copy-start | bytes 1648
  0.7 134.5 %copy-start.27 = (f32[768,8]{0,1:T(8,128)S(1)}, f32[768,8]{0,1:T(8,128)}, u32[]{:S(2)}) copy-start(f32[768,8]{0,1:T(8,128)} %param.45) | copy-start | bytes 73732
  6.3 130.2 %copy-start.28 = (s32[1,1024]{1,0:T(1,128)}, s32[1,1024]{1,0:T(1,128)S(1)}, u32[]{:S(2)}) copy-start(s32[1,1024]{1,0:T(1,128)S(1)} %get-tuple-element.165.ids_ref) | copy-start | bytes 12292
  8.8 127.8 %copy-start.26 = (s32[2,1024]{1,0:T(2,128)}, s32[2,1024]{1,0:T(2,128)S(1)}, u32[]{:S(2)}) copy-start(s32[2,1024]{1,0:T(2,128)S(1)} %add_select_fusion.1.dest_rows) | copy-start | bytes 24580
  9.2 127.3 %copy-start.19 = (s32[1,1024,2]{1,2,0:T(2,128)S(1)}, s32[1,1024,2]{1,2,0:T(2,128)}, u32[]{:S(2)}) copy-start(s32[1,1024,2]{1,2,0:T(2,128)} %param.30) | copy-start | bytes 24580
  9.5 128.1 %copy-start.30 = (s32[1,1024,2]{1,2,0:T(2,128)S(1)}, s32[1,1024,2]{1,2,0:T(2,128)}, u32[]{:S(2)}) copy-start(s32[1,1024,2]{1,2,0:T(2,128)} %param.29) | copy-start | bytes 24580
  9.5 128.2 %copy-start.42 = (f32[2]{0:T(128)S(1)}, f32[2]{0:T(128)}, u32[]{:S(2)}) copy-start(f32[2]{0:T(128)} %constant.248) | copy-start | bytes 28
  9.7 129.2 %copy-start.24 = (f32[3,8]{1,0:T(4,128)S(1)}, f32[3,8]{1,0:T(4,128)}, u32[]{:S(2)}) copy-start(f32[3,8]{1,0:T(4,128)} %bias_ref.3) | copy-start | bytes 292
  12.2 177.0 %copy-start.37 = (s32[1,1024,2]{1,2,0:T(2,128)S(1)}, s32[1,1024,2]{1,2,0:T(2,128)}, u32[]{:S(2)}) copy-start(s32[1,1024,2]{1,2,0:T(2,128)} %param.28) | copy-start | bytes 24580
  131.2 58.6 %collective-permute-start = (bf16[192,768]{1,0:T(8,128)(2,1)}, bf16[192,768]{1,0:T(8,128)(2,1)S(1)}, u32[]{:S(2)}, u32[]{:S(2)}) collective-permute-start(bf16[192,768]{1,0:T(8,128)(2,1)} %get-tuple-element.86.refs_0_.project_ref), channel_id=1, source_target_pairs={{0,1},{1,2},{2,3},{3,0},{4,5},{5,6},{6,7},{7,4},{8,9},{9,10},{10,1... | collective-permute-start | bytes 884744 | tf_op jit(solution)/shard_map/ppermute | solution.py:2343
  131.3 58.5 %collective-permute-start.1 = (bf16[192,768]{1,0:T(8,128)(2,1)}, bf16[192,768]{1,0:T(8,128)(2,1)S(1)}, u32[]{:S(2)}, u32[]{:S(2)}) collective-permute-start(bf16[192,768]{1,0:T(8,128)(2,1)} %get-tuple-element.86.refs_0_.project_ref), channel_id=1, source_target_pairs={{0,2},{1,3},{2,0},{3,1},{4,6},{5,7},{6,4},{7,5},{8,10},{9,11},{10,... | collective-permute-start | bytes 884744 | tf_op jit(solution)/shard_map/ppermute | solution.py:2343
  133.8 56.0 %collective-permute-start.2 = (bf16[192,768]{1,0:T(8,128)(2,1)}, bf16[192,768]{1,0:T(8,128)(2,1)S(1)}, u32[]{:S(2)}, u32[]{:S(2)}) collective-permute-start(bf16[192,768]{1,0:T(8,128)(2,1)} %get-tuple-element.86.refs_0_.project_ref), channel_id=1, source_target_pairs={{0,3},{1,0},{2,1},{3,2},{4,7},{5,4},{6,5},{7,6},{8,11},{9,8},{10,9... | collective-permute-start | bytes 884744 | tf_op jit(solution)/shard_map/ppermute | solution.py:2343
  438.0 93.8 %copy-start.39 = (f32[1,1024]{1,0:T(1,128)S(1)}, f32[1,1024]{1,0:T(1,128)}, u32[]{:S(2)}) copy-start(f32[1,1024]{1,0:T(1,128)} %get-tuple-element.103) | copy-start | bytes 12292
  438.0 94.6 %copy-start.20 = (s32[1,1024,2]{1,2,0:T(2,128)S(1)}, s32[1,1024,2]{1,2,0:T(2,128)}, u32[]{:S(2)}) copy-start(s32[1,1024,2]{1,2,0:T(2,128)} %param.30) | copy-start | bytes 24580
  438.1 94.6 %copy-start.22 = (f32[2,1024]{1,0:T(2,128)S(1)}, f32[2,1024]{1,0:T(2,128)}, u32[]{:S(2)}) copy-start(f32[2,1024]{1,0:T(2,128)} %copy-done.21) | copy-start | bytes 24580
  532.6 55.2 %copy-start.6 = (bf16[576,1024]{1,0:T(8,128)(2,1)S(1)}, bf16[576,1024]{1,0:T(8,128)(2,1)}, u32[]{:S(2)}) copy-start(bf16[576,1024]{1,0:T(8,128)(2,1)} %get-tuple-element.83.own_ref) | copy-start | bytes 3538948
  610.0 62.9 %copy-start.38 = (f32[1,1024]{1,0:T(1,128)S(1)}, f32[1,1024]{1,0:T(1,128)}, u32[]{:S(2)}) copy-start(f32[1,1024]{1,0:T(1,128)} %get-tuple-element.123) | copy-start | bytes 12292
  675.6 100.1 %copy-start.31 = (f32[768,8]{0,1:T(8,128)S(1)}, f32[768,8]{0,1:T(8,128)}, u32[]{:S(2)}) copy-start(f32[768,8]{0,1:T(8,128)} %param.46) | copy-start | bytes 73732
  675.6 100.1 %copy-start.32 = (f32[768,8]{0,1:T(8,128)S(1)}, f32[768,8]{0,1:T(8,128)}, u32[]{:S(2)}) copy-start(f32[768,8]{0,1:T(8,128)} %param.47) | copy-start | bytes 73732
  675.6 101.5 %copy-start.29 = (f32[3,768]{1,0:T(4,128)S(1)}, f32[3,768]{1,0:T(4,128)}, u32[]{:S(2)}) copy-start(f32[3,768]{1,0:T(4,128)} %param.42) | copy-start | bytes 27652
  675.6 101.5 %copy-start.34 = (f32[3,768]{1,0:T(4,128)S(1)}, f32[3,768]{1,0:T(4,128)}, u32[]{:S(2)}) copy-start(f32[3,768]{1,0:T(4,128)} %param.43) | copy-start | bytes 27652
  675.6 101.5 %copy-start.35 = (f32[3,768]{1,0:T(4,128)S(1)}, f32[3,768]{1,0:T(4,128)}, u32[]{:S(2)}) copy-start(f32[3,768]{1,0:T(4,128)} %param.44) | copy-start | bytes 27652
  675.6 104.1 %copy-start.40 = (f32[3,8]{1,0:T(4,128)S(1)}, f32[3,8]{1,0:T(4,128)}, u32[]{:S(2)}) copy-start(f32[3,8]{1,0:T(4,128)} %param.49) | copy-start | bytes 292
  675.6 104.1 %copy-start.41 = (f32[3,8]{1,0:T(4,128)S(1)}, f32[3,8]{1,0:T(4,128)}, u32[]{:S(2)}) copy-start(f32[3,8]{1,0:T(4,128)} %param.50) | copy-start | bytes 292
  (22 other events, 252.5 us)

commit v13 on v12

--- a/solution.py
+++ b/solution.py
@@ -740,7 +740,7 @@
 
 def attention_kernel(
     heads, size, bias_ref, own_ref, out_ref, logsum_ref, before_ref, mine_ref,
-    queries, own_values, old_values, scores, peak, total, keys_sem, send_sem, recv_sem,
+    scores, peak, total, keys_sem, send_sem, recv_sem,
 ):
     tokens = own_ref.shape[1]
     blocks = tokens // BLOCK
@@ -783,23 +783,12 @@
     def flipped(rows):
         return rows.astype(jnp.float32).T.astype(jnp.bfloat16)
 
-    for head in range(heads):
-        span = slice(head * size, (head + 1) * size)
-        queries[head] = flipped(own_ref[span, :]) * jnp.bfloat16(size**-0.5)
-        own_values[head] = flipped(
-            own_ref[2 * hidden + head * size : 2 * hidden + (head + 1) * size, :]
-        )
-
     @pl.when(later)
     def _():
         pairs.wait_recv()
-        for head in range(heads):
-            old_values[head] = flipped(
-                before_ref[hidden + head * size : hidden + (head + 1) * size, :]
-            )
 
     def sent(owner, block, peer, send, recv):
-        piece = out_ref.at[owner, :, pl.ds(block * BLOCK, BLOCK)]
+        piece = out_ref.at[owner, pl.ds(block * size, size), :]
         return pltpu.make_async_remote_copy(
             src_ref=piece,
             dst_ref=piece,
@@ -839,11 +828,16 @@
                 far_to_end(block).wait_recv()
                 far_to_end(block).start()
 
-    for block in range(blocks):
-        for head in range(heads):
-            span = slice(head * size, (head + 1) * size)
-            rows = queries[head, block * BLOCK : (block + 1) * BLOCK]
-            own_keys = own_ref[hidden + head * size : hidden + (head + 1) * size, :]
+    for head in range(heads):
+        span = slice(head * size, (head + 1) * size)
+        query = flipped(own_ref[span, :]) * jnp.bfloat16(size**-0.5)
+        own_keys = own_ref[hidden + head * size : hidden + (head + 1) * size, :]
+        own_values = flipped(
+            own_ref[2 * hidden + head * size : 2 * hidden + (head + 1) * size, :]
+        )
+        old_values = flipped(before_ref[hidden + head * size : hidden + (head + 1) * size, :])
+        for block in range(blocks):
+            rows = query[block * BLOCK : (block + 1) * BLOCK]
             width = (block + 1) * BLOCK
             mine = jnp.dot(rows, own_keys[:, :width], preferred_element_type=jnp.float32)
             top = None
@@ -883,14 +877,14 @@
             full = total[...]
             inverse = 1.0 / full
             low = jnp.concatenate([(part * inverse).astype(jnp.bfloat16) for part in parts], 1)
-            result = jnp.dot(low, own_values[head, :width], preferred_element_type=jnp.float32)
+            result = jnp.dot(low, own_values[:width], preferred_element_type=jnp.float32)
             logsum_ref[head, block * BLOCK : (block + 1) * BLOCK, :] = top + jnp.log(full)
             place = (rank, span, slice(block * BLOCK, (block + 1) * BLOCK))
 
             @pl.when(later)
             def _():
                 low_old = (scores[...] * inverse).astype(jnp.bfloat16)
-                both = result + jnp.dot(low_old, old_values[head], preferred_element_type=jnp.float32)
+                both = result + jnp.dot(low_old, old_values, preferred_element_type=jnp.float32)
                 out_ref[place] = both.T.astype(jnp.bfloat16)
                 mine_ref[place[1:]] = both.T.astype(jnp.bfloat16)
 
@@ -899,33 +893,33 @@
                 out_ref[place] = result.T.astype(jnp.bfloat16)
                 mine_ref[place[1:]] = result.T.astype(jnp.bfloat16)
 
-        own_to_end(block).start()
+        own_to_end(head).start()
 
         @pl.when(inner)
         def _():
-            own_to_middle(block).start()
-
-        if block >= 1:
-            hand_on(block - 1, (0,))
-        if block >= 2:
-            hand_on(block - 2, (1,))
-
-    hand_on(blocks - 1, (0,))
-    hand_on(blocks - 2, (1,))
-    hand_on(blocks - 1, (1,))
-    for block in range(blocks):
-        own_to_end(block).wait_send()
+            own_to_middle(head).start()
+
+        if head >= 1:
+            hand_on(head - 1, (0,))
+        if head >= 2:
+            hand_on(head - 2, (1,))
+
+    hand_on(heads - 1, (0,))
+    hand_on(heads - 2, (1,))
+    hand_on(heads - 1, (1,))
+    for head in range(heads):
+        own_to_end(head).wait_send()
 
         @pl.when(inner)
         def _():
             for copy in (own_to_middle, end_to_middle, middle_to_end, far_to_end):
-                copy(block).wait_send()
+                copy(head).wait_send()
 
         @pl.when(jnp.logical_not(inner))
         def _():
-            from_end(block).wait_recv()
-            middle_to_end(block).wait_recv()
-            far_to_end(block).wait_recv()
+            from_end(head).wait_recv()
+            middle_to_end(head).wait_recv()
+            far_to_end(head).wait_recv()
 
     @pl.when(jnp.logical_not(later))
     def _():
@@ -935,7 +929,6 @@
 def attention(biases, own, heads, size, collective_id):
     tokens = own.shape[1]
     blocks = tokens // BLOCK
-    flat = pltpu.VMEM((heads, tokens, size), jnp.bfloat16)
     return pl.pallas_call(
         functools.partial(attention_kernel, heads, size),
         out_shape=[
@@ -947,15 +940,12 @@
         in_specs=[pl.BlockSpec(memory_space=pltpu.SMEM), whole_vmem],
         out_specs=[whole_vmem] * 4,
         scratch_shapes=[
-            flat,
-            flat,
-            flat,
             pltpu.VMEM((BLOCK, tokens), jnp.float32),
             pltpu.VMEM((BLOCK, 1), jnp.float32),
             pltpu.VMEM((BLOCK, 1), jnp.float32),
             pltpu.SemaphoreType.DMA((2,)),
-            pltpu.SemaphoreType.DMA((blocks, 5)),
-            pltpu.SemaphoreType.DMA((blocks, 3)),
+            pltpu.SemaphoreType.DMA((heads, 5)),
+            pltpu.SemaphoreType.DMA((heads, 3)),
         ],
         compiler_params=pltpu.CompilerParams(
             collective_id=collective_id, has_side_effects=True, vmem_limit_bytes=40 << 20
@@ -2085,14 +2075,9 @@
         repeat(0, chunks, lambda q: pass_over(k, q).start())
         form(places[k] * 2 + core, own.at[k])
 
-    for g in range(slots // group):
-        done = [q for q in range(chunks) if g * group < (q + 1) * size <= (g + 1) * group]
-        form(places[0] * 2 + 1 - core, passing.at[0], g, g + 1)
-        for q in done:
-            pass_over(0, q).start()
-        form(places[0] * 2 + core, own.at[0], g, g + 1)
-        for q in done:
-            first_leg(beside if q < split else across)(q)
+    form_pair(0)
+    repeat(0, split, first_leg(beside))
+    repeat(split, chunks, first_leg(across))
     repeat(1, 8, lambda step: small_copy(step).start())
     small_landed[chip * 2 + core] = small_ref[...]
     form_pair(1)

time: 794 us -> 790 us (level)
  transfers between devices with their start and end apart: 3 -> 3, of which waited for: 0 -> 0; matrix products, arithmetic and copies ran while one was open for 1% -> 1% of each run, Pallas kernels for 6% -> 5%
where the time goes in v13:
time: 790 us; the launch traced here: 787 us
  Pallas kernels  723 us (92%)
  other arithmetic  29.1 us (4%)
  local copies, waits for them, and re-layouts  26.9 us (3%)
    pallas_call x1, Pallas kernels, head_line(): pl.pallas_call(functools.partial(head_line_kernel, vocab_tile(vocab)), ou...  140 us
    pallas_call x1, Pallas kernels, embed(): pl.pallas_call(functools.partial(embed_kernel, chunks, first_unit), out_s...  119 us
    pallas_call x2, Pallas kernels, sum_line(): pl.pallas_call(functools.partial(sum_line_kernel, rows, count, opening, p...  112 us
    pallas_call x1, Pallas kernels, own_units(): pl.pallas_call(functools.partial(own_units_kernel, chunks), out_shape=[ja...  96.2 us
    pallas_call x1, Pallas kernels, experts_forward(): pl.pallas_call(experts_kernel, out_shape=[jax.ShapeDtypeStruct((tokens, w...  94.4 us
    pallas_call x1, Pallas kernels, experts_backward(): pl.pallas_call(experts_back_kernel, out_shape=[jax.ShapeDtypeStruct((toke...  93.8 us
    pallas_call x1, Pallas kernels, attention(): pl.pallas_call(functools.partial(attention_kernel, heads, size), out_shap...  42.4 us
    pallas_call x1, Pallas kernels, attention_back(): pl.pallas_call(functools.partial(attention_back_kernel, heads, size), out...  20.9 us
  transfers between devices with their start and end apart: 3, of which 0 were waited for; matrix products, arithmetic and copies ran while one was open for 1% of the time, Pallas kernels for 5%

profile of v13, /device:TPU:0, one launch (start us, length us, event | category | flops | bytes accessed | tf_op | source)
XLA Modules:
  0.0 787.2 jit_solution(3689728590843075155)
XLA Ops:
  2.1 3.4 convert_reduce_fusion
  9.7 1.4 fusion.17
  12.2 119.1 %shard_map.384 = (bf16[137,64,768]{2,1,0:T(8,128)(2,1)}, bf16[1024,768]{1,0:T(8,128)(2,1)}, bf16[1024,768]{1,0:T(8,128)(2,1)}, bf16[576,1024]{1,0:T(8,128)(2,1)}...) custom-call(s32[137]{0:T(256)} %copy-done.36, f32[21,64,768]{2,1,0:T(8,128)} %bitcast.95, s32[1024,1]{1,0:T(8,128)} %fusion.3.rows_ref, ...), custom_call_target="tpu_custom_call" | custom-call | tf_op jit(solution)/shard_map/pallas_call | solution.py:681
  131.4 2.5 collective-permute-start.1
  133.9 1.3 collective-permute-start.2
  139.0 1.3 copy-done.5
  140.3 42.4 %shard_map.385 = (bf16[4,192,1024]{2,1,0:T(8,128)(2,1)S(1)}, f32[3,1024,1]{2,1,0:T(8,128)S(1)}, bf16[384,1024]{1,0:T(8,128)(2,1)S(1)}, bf16[192,1024]{1,0:T(8,128)(2,1)S(1)}) custom-call(f32[3,8]{1,0:T(4,128)S(1)} %copy-done.24, bf16[576,1024]{1,0:T(8,128)(2,1)S(1)} %copy-done.5), custom_call_target="tpu_custom_call" | custom-call | tf_op jit(solution)/shard_map/pallas_call | solution.py:932
  187.0 1.4 copy-done.2
  189.3 4.5 shard_map.386
  193.9 1.7 copy-done
  198.7 94.4 %shard_map.387 = (f32[1024,768]{1,0:T(8,128)}, bf16[8,288,768]{2,1,0:T(8,128)(2,1)}, bf16[8,288,768]{2,1,0:T(8,128)(2,1)}, f32[8,128]{1,0:T(8,128)}) custom-call(bf16[1024,768]{1,0:T(8,128)(2,1)} %copy-done.3, s32[2,1024]{1,0:T(2,128)} %copy-done.26, s32[1024,2]{1,0:T(8,128)} %copy.77.dest_columns, f32[1024,8]{1,0:T(8,128)} %copy-done.17, ...), custom_call_target="tpu_custom_call" | custom-call | tf_op jit(solution)/shard_map/pallas_call | solution.py:1772
  293.1 1.3 fusion.18
  296.5 139.6 %shard_map.388 = (bf16[1024,768]{1,0:T(8,128)(2,1)}, bf16[1024,768]{1,0:T(8,128)(2,1)}, f32[1024,768]{1,0:T(8,128)}, f32[1,768]{1,0:T(1,128)}, f32[1,1024]{1,0:T...) custom-call(f32[1024,768]{1,0:T(8,128)} %get-tuple-element.90.part_ref, f32[1024,768]{1,0:T(8,128)} %copy-done, ...), custom_call_target="tpu_custom_call" | custom-call | tf_op jit(solution)/shard_map/pallas_call | solution.py:1431
  436.1 93.8 %shard_map.389 = (f32[1024,768]{1,0:T(8,128)}, f32[2,1024]{1,0:T(2,128)}, f32[768,768]{1,0:T(8,128)}, f32[768,768]{1,0:T(8,128)}) custom-call(bf16[1024,768]{1,0:T(8,128)(2,1)} %get-tuple-element.96.rows_ref, s32[2,1024]{1,0:T(2,128)} %copy-done.26, s32[1024,2]{1,0:T(8,128)} %copy.77.dest_columns, f32[2,1024]{1,0:T(2,128)} %copy-done.21, ...), custom_call_target="tpu_custom_call" | custom-call | tf_op jit(solution)/shard_map/pallas_call | solution.py:1917
  530.7 52.1 %shard_map.390 = (bf16[1024,768]{1,0:T(8,128)(2,1)S(1)}, f32[1024,768]{1,0:T(8,128)S(1)}, bf16[8,1024]{1,0:T(8,128)(2,1)S(1)}, f32[1,1024]{1,0:T(1,128)S(1)}, f32[1,768]{1,0:T(1,128)S(1)}) custom-call(f32[1024,768]{1,0:T(8,128)} %get-tuple-element.100.refs_0_, f32[1024,768]{1,0:T(8,128)} %copy-done, f32[1,768]{1,0:T(1,128)S(1)} %get-tuple-element.170.gain_ref.refs_2_, ...), custom_call_target="tpu_custom_call" | custom-call | tf_op jit(solution)/shard_map/pallas_call | solution.py:185
  583.9 1.7 copy-done.7
  585.9 20.9 %shard_map.391 = (bf16[192,1024]{1,0:T(8,128)(2,1)S(1)}, f32[384,1024]{1,0:T(8,128)S(1)}, bf16[384,1024]{1,0:T(8,128)(2,1)S(1)}, f32[24,256]{1,0:T(8,128)S(1)}, ...) custom-call(f32[3,8]{1,0:T(4,128)S(1)} %copy-done.24, ...), custom_call_target="tpu_custom_call" | custom-call | tf_op jit(solution)/shard_map/pallas_call | solution.py:1108
  608.0 60.1 %shard_map.392 = (bf16[1024,768]{1,0:T(8,128)(2,1)S(1)}, bf16[576,1024]{1,0:T(8,128)(2,1)S(1)}, f32[8,768]{1,0:T(8,128)S(1)}) custom-call(bf16[1024,768]{1,0:T(8,128)(2,1)} %get-tuple-element.85.embedded_ref.refs_0_, f32[1,768]{1,0:T(1,128)S(1)} %copy-done.23, f32[1024,768]{1,0:T(8,128)} %copy-done.7, f32[1,768]{1,0:T(1,128)S(1)} %get-tuple-element.105.refs_3_, ...), custom_call_target="tpu_custom_call" | custom-call | tf_op jit(solution)/shard_map/pallas_call | solution.py:185
  673.7 96.2 %shard_map.393 = (f32[21,64,768]{2,1,0:T(8,128)}, f32[16,768]{1,0:T(8,128)}) custom-call(s32[168]{0:T(256)} %reshape.275.units_of, bf16[125,64,1024]{2,1,0:T(8,128)(2,1)} %bitcast.96, bf16[1024,768]{1,0:T(8,128)(2,1)} %get-tuple-element.95.rows_ref, s32[1,1024]{1,0:T(1,128)} %copy-done.28, bf16[1024,768]{1,0:T(8,128)(2,1)} %copy-done.9, ...), custom_call_target="tpu_custom_call" | custom-call | tf_op jit(solution)/shard_map/pallas_call | solution.py:2137
  770.6 1.3 slice.61
  772.0 1.4 multiply_subtract_fusion
  773.4 1.4 multiply_subtract_fusion.1
  774.8 1.2 pad_maximum_fusion
  776.6 10.4 %fusion.12 = (f32[1,1,21,64,768]{4,3,2,1,0:T(8,128)}, f32[1,1,21,64,768]{4,3,2,1,0:T(8,128)}, f32[1,1,21,64,768]{4,3,2,1,0:T(8,128)}) fusion(f32[21,64,768]{2,1,0:T(8,128)} %get-tuple-element.126, pred[21]{0:T(512)(128)(4,1)S(1)} %select_reduce_fusion.2, f32[1,1,21,64,768]{4,3,2,1,0:T(8,128)} %param.35, f32[1,1,21,64,768]{4,3,2,1,0:T(8,128)} %param.34, ...), kind=kLoop, calls=%fused_computation.69 | loop fusion | flops 16515072 | bytes 28901480 | tf_op jit(solution)/shard_map/broadcast_in_dim | solution.py:2513
  (138 shorter events, 28.6 us)
Async XLA Ops:
  0.7 134.6 %copy-start.33 = (s32[137,1]{0,1:T(1,128)S(1)}, s32[137,1]{0,1:T(1,128)}, u32[]{:S(2)}) copy-start(s32[137,1]{0,1:T(1,128)} %param.32) | copy-start | bytes 1648
  0.7 134.6 %copy-start.27 = (f32[768,8]{0,1:T(8,128)S(1)}, f32[768,8]{0,1:T(8,128)}, u32[]{:S(2)}) copy-start(f32[768,8]{0,1:T(8,128)} %param.45) | copy-start | bytes 73732
  6.3 130.3 %copy-start.28 = (s32[1,1024]{1,0:T(1,128)}, s32[1,1024]{1,0:T(1,128)S(1)}, u32[]{:S(2)}) copy-start(s32[1,1024]{1,0:T(1,128)S(1)} %get-tuple-element.165.ids_ref) | copy-start | bytes 12292
  8.8 127.9 %copy-start.26 = (s32[2,1024]{1,0:T(2,128)}, s32[2,1024]{1,0:T(2,128)S(1)}, u32[]{:S(2)}) copy-start(s32[2,1024]{1,0:T(2,128)S(1)} %add_select_fusion.1.dest_rows) | copy-start | bytes 24580
  9.2 127.5 %copy-start.19 = (s32[1,1024,2]{1,2,0:T(2,128)S(1)}, s32[1,1024,2]{1,2,0:T(2,128)}, u32[]{:S(2)}) copy-start(s32[1,1024,2]{1,2,0:T(2,128)} %param.30) | copy-start | bytes 24580
  9.5 128.2 %copy-start.30 = (s32[1,1024,2]{1,2,0:T(2,128)S(1)}, s32[1,1024,2]{1,2,0:T(2,128)}, u32[]{:S(2)}) copy-start(s32[1,1024,2]{1,2,0:T(2,128)} %param.29) | copy-start | bytes 24580
  9.5 128.3 %copy-start.42 = (f32[2]{0:T(128)S(1)}, f32[2]{0:T(128)}, u32[]{:S(2)}) copy-start(f32[2]{0:T(128)} %constant.248) | copy-start | bytes 28
  9.7 129.3 %copy-start.24 = (f32[3,8]{1,0:T(4,128)S(1)}, f32[3,8]{1,0:T(4,128)}, u32[]{:S(2)}) copy-start(f32[3,8]{1,0:T(4,128)} %bias_ref.3) | copy-start | bytes 292
  12.2 174.1 %copy-start.37 = (s32[1,1024,2]{1,2,0:T(2,128)S(1)}, s32[1,1024,2]{1,2,0:T(2,128)}, u32[]{:S(2)}) copy-start(s32[1,1024,2]{1,2,0:T(2,128)} %param.28) | copy-start | bytes 24580
  131.3 55.6 %collective-permute-start = (bf16[192,768]{1,0:T(8,128)(2,1)}, bf16[192,768]{1,0:T(8,128)(2,1)S(1)}, u32[]{:S(2)}, u32[]{:S(2)}) collective-permute-start(bf16[192,768]{1,0:T(8,128)(2,1)} %get-tuple-element.86.refs_0_.project_ref), channel_id=1, source_target_pairs={{0,1},{1,2},{2,3},{3,0},{4,5},{5,6},{6,7},{7,4},{8,9},{9,10},{10,1... | collective-permute-start | bytes 884744 | tf_op jit(solution)/shard_map/ppermute | solution.py:2328
  131.4 55.6 %collective-permute-start.1 = (bf16[192,768]{1,0:T(8,128)(2,1)}, bf16[192,768]{1,0:T(8,128)(2,1)S(1)}, u32[]{:S(2)}, u32[]{:S(2)}) collective-permute-start(bf16[192,768]{1,0:T(8,128)(2,1)} %get-tuple-element.86.refs_0_.project_ref), channel_id=1, source_target_pairs={{0,2},{1,3},{2,0},{3,1},{4,6},{5,7},{6,4},{7,5},{8,10},{9,11},{10,... | collective-permute-start | bytes 884744 | tf_op jit(solution)/shard_map/ppermute | solution.py:2328
  133.9 53.0 %collective-permute-start.2 = (bf16[192,768]{1,0:T(8,128)(2,1)}, bf16[192,768]{1,0:T(8,128)(2,1)S(1)}, u32[]{:S(2)}, u32[]{:S(2)}) collective-permute-start(bf16[192,768]{1,0:T(8,128)(2,1)} %get-tuple-element.86.refs_0_.project_ref), channel_id=1, source_target_pairs={{0,3},{1,0},{2,1},{3,2},{4,7},{5,4},{6,5},{7,6},{8,11},{9,8},{10,9... | collective-permute-start | bytes 884744 | tf_op jit(solution)/shard_map/ppermute | solution.py:2328
  436.1 93.8 %copy-start.39 = (f32[1,1024]{1,0:T(1,128)S(1)}, f32[1,1024]{1,0:T(1,128)}, u32[]{:S(2)}) copy-start(f32[1,1024]{1,0:T(1,128)} %get-tuple-element.103) | copy-start | bytes 12292
  436.1 94.6 %copy-start.20 = (s32[1,1024,2]{1,2,0:T(2,128)S(1)}, s32[1,1024,2]{1,2,0:T(2,128)}, u32[]{:S(2)}) copy-start(s32[1,1024,2]{1,2,0:T(2,128)} %param.30) | copy-start | bytes 24580
  436.1 94.6 %copy-start.22 = (f32[2,1024]{1,0:T(2,128)S(1)}, f32[2,1024]{1,0:T(2,128)}, u32[]{:S(2)}) copy-start(f32[2,1024]{1,0:T(2,128)} %copy-done.21) | copy-start | bytes 24580
  530.6 55.2 %copy-start.6 = (bf16[576,1024]{1,0:T(8,128)(2,1)S(1)}, bf16[576,1024]{1,0:T(8,128)(2,1)}, u32[]{:S(2)}) copy-start(bf16[576,1024]{1,0:T(8,128)(2,1)} %get-tuple-element.83.own_ref) | copy-start | bytes 3538948
  608.0 62.9 %copy-start.38 = (f32[1,1024]{1,0:T(1,128)S(1)}, f32[1,1024]{1,0:T(1,128)}, u32[]{:S(2)}) copy-start(f32[1,1024]{1,0:T(1,128)} %get-tuple-element.123) | copy-start | bytes 12292
  673.6 98.4 %copy-start.31 = (f32[768,8]{0,1:T(8,128)S(1)}, f32[768,8]{0,1:T(8,128)}, u32[]{:S(2)}) copy-start(f32[768,8]{0,1:T(8,128)} %param.46) | copy-start | bytes 73732
  673.6 98.4 %copy-start.32 = (f32[768,8]{0,1:T(8,128)S(1)}, f32[768,8]{0,1:T(8,128)}, u32[]{:S(2)}) copy-start(f32[768,8]{0,1:T(8,128)} %param.47) | copy-start | bytes 73732
  673.6 99.8 %copy-start.29 = (f32[3,768]{1,0:T(4,128)S(1)}, f32[3,768]{1,0:T(4,128)}, u32[]{:S(2)}) copy-start(f32[3,768]{1,0:T(4,128)} %param.42) | copy-start | bytes 27652
  673.6 99.8 %copy-start.34 = (f32[3,768]{1,0:T(4,128)S(1)}, f32[3,768]{1,0:T(4,128)}, u32[]{:S(2)}) copy-start(f32[3,768]{1,0:T(4,128)} %param.43) | copy-start | bytes 27652
  673.6 99.8 %copy-start.35 = (f32[3,768]{1,0:T(4,128)S(1)}, f32[3,768]{1,0:T(4,128)}, u32[]{:S(2)}) copy-start(f32[3,768]{1,0:T(4,128)} %param.44) | copy-start | bytes 27652
  673.6 102.4 %copy-start.40 = (f32[3,8]{1,0:T(4,128)S(1)}, f32[3,8]{1,0:T(4,128)}, u32[]{:S(2)}) copy-start(f32[3,8]{1,0:T(4,128)} %param.49) | copy-start | bytes 292
  673.6 102.4 %copy-start.41 = (f32[3,8]{1,0:T(4,128)S(1)}, f32[3,8]{1,0:T(4,128)}, u32[]{:S(2)}) copy-start(f32[3,8]{1,0:T(4,128)} %param.50) | copy-start | bytes 292
  (22 other events, 252.6 us)
